TPU v7x, 32 devices: a whole 2x2x4 slice. The times are simulated.
32 devices in a mesh: groups: 2 (over x), shard: 16 (over z, y, core).
Axes of the slice: x: 2, y: 2, z: 4, core: 2. Of those that a mesh axis runs over, the one named last changes fastest.
Arguments:
- query_grads: bfloat16 [256, 8, 4096], P(('groups', 'shard')), parts along dimension 0, may hold values from -6 to 6
- query_routes: int32 [256, 8], P('groups'), parts along dimension 0, may hold values from 0 to 31, all different within a row; in each aligned block of 8 rows (0 to 7, 8 to 15, ...) at most 4 rows name the same one
- train_grads: bfloat16 [4096, 8, 4096], P(('groups', 'shard')), parts along dimension 0, may hold values from -6 to 6
- train_routes: int32 [4096, 8], P(('groups', 'shard')), parts along dimension 0, may hold values from 0 to 31, all different within a row; in each aligned block of 128 rows (0 to 127, 128 to 255, ...) at most 64 rows name the same one
- train_counts: int32 [32], P(('groups', 'shard')), parts along dimension 0, may hold values from 1 to 128, 1536 in all
- owner_slot: int32 [32], replicated, may hold values from 0 to 31, each once
- basis_s: float32 [32, 64, 64], P('shard'), may hold values from -0.75 to 0.75
- basis_a: float32 [32, 64, 64], P('shard'), may hold values from -0.75 to 0.75
- eigenvalues: float32 [32, 64, 64], P('shard'), may hold values from 0.05 to 5
Outputs:
- scores: float32 [256, 2048], P('groups', 'shard'), parts along dimension 0
There are 2 independent parts, one for each index of `groups`. A program takes and returns all parts, laid end to end along the dimension named above; an argument that names none is the same for every part. Nothing has to cross between parts.
Inputs may be any that keep to these rules, and one draw needn't show every extreme that they name: `query_routes`: in each aligned block of 8 query rows no expert is named by more than 4 rows. `train_routes`: in each aligned block of 128 train rows no expert is named by more than 64 rows.
All inputs are finite; a program needn't handle non-finite values. No bound on the sum of `train_counts` on one device may be relied on, other than what follows from the above.
Results may differ from a plain program's by a relative error of at most 0.0029.
Values may be sent and summed in bfloat16 or wider, within the bound.
No kernel may reach another device: no remote copies, remote signals or barrier semaphores. Data moves between devices by JAX's collectives and lax.ppermute only.
A program may use at most 128 MiB of HBM per device.

v0:
```python
import jax
import jax.numpy as jnp
from jax import lax
from jax.sharding import PartitionSpec as P

DAMPING = 0.01


def precondition(grads, basis_s, basis_a, eigenvalues):
    count = grads.shape[0]
    slots = grads.shape[1]
    order = basis_s.shape[-1]
    field = grads.reshape(count, slots, order, order).astype(jnp.float32)
    turned = jnp.einsum("eji,ecjk->ecik", basis_s, field, precision=lax.Precision.HIGHEST)
    turned = jnp.einsum("ecik,ekl->ecil", turned, basis_a, precision=lax.Precision.HIGHEST)
    scaled = turned / (eigenvalues[:, None] + DAMPING)
    back = jnp.einsum("eij,ecjk->ecik", basis_s, scaled, precision=lax.Precision.HIGHEST)
    back = jnp.einsum("ecik,elk->ecil", back, basis_a, precision=lax.Precision.HIGHEST)
    return back.reshape(count, slots, order * order).astype(jnp.bfloat16)


def lookup_slots(routes, owner_slot):
    experts = owner_slot.shape[0]
    hitting = routes[..., None] == jnp.arange(experts, dtype=jnp.int32)
    return (jnp.sum(jnp.where(hitting, owner_slot, 0), axis=-1), hitting)


def place_tiles(total, tiles, query_index, train_index):
    query_hot = (query_index[..., None] == jnp.arange(total.shape[0], dtype=jnp.int32)).astype(
        jnp.float32
    )
    train_hot = (train_index[..., None] == jnp.arange(total.shape[1], dtype=jnp.int32)).astype(
        jnp.float32
    )
    spread = jnp.einsum("ect,etr->ecr", tiles, train_hot, precision=lax.Precision.HIGHEST)
    return jnp.einsum("ecq,ecr->qr", query_hot, spread, precision=lax.Precision.HIGHEST)


def gather_rows(source_table, flat_rows, shape):
    chosen = (source_table[:, None] - 1 == jnp.arange(flat_rows.shape[0], dtype=jnp.int32)).astype(
        jnp.bfloat16
    )
    picked = jnp.dot(chosen, flat_rows, preferred_element_type=jnp.float32).astype(jnp.bfloat16)
    return picked.reshape(shape)


def local(
    query_grads,
    query_routes,
    train_grads,
    train_routes,
    train_counts,
    owner_slot,
    basis_s,
    basis_a,
    eigenvalues,
):
    devices = lax.axis_size("shard")
    my_index = lax.axis_index("shard")
    experts = owner_slot.shape[0]
    queries, top_count = query_routes.shape
    per_device = queries // devices
    grad_width = query_grads.shape[2]
    train_rows_dev = train_grads.shape[0]
    query_most = 2 * per_device * top_count // experts
    query_cap = devices * query_most
    train_most = 2 * train_rows_dev * top_count // experts
    query_slot, query_hit = lookup_slots(query_routes, owner_slot)
    named = jnp.any(query_hit, axis=1).astype(jnp.int32).reshape(devices, per_device, experts)
    rank_table = (jnp.cumsum(named, axis=1) - named).reshape(queries, experts)
    query_rank = jnp.sum(jnp.where(query_hit, rank_table[:, None, :], 0), axis=-1)
    block_of = jnp.arange(queries, dtype=jnp.int32) // per_device
    global_slot = query_slot * query_cap + block_of[:, None] * query_most + query_rank
    query_source = (
        jnp.zeros((experts * query_cap,), jnp.int32)
        .at[global_slot.reshape(-1)]
        .set(jnp.arange(queries * top_count, dtype=jnp.int32) + 1)
    )
    query_index = jnp.where(query_source > 0, (query_source - 1) // top_count, queries)
    query_index = query_index.reshape(experts, query_cap)
    live = jnp.arange(train_rows_dev, dtype=jnp.int32) < train_counts[0]
    train_slot, train_hit = lookup_slots(train_routes, owner_slot)
    train_named = (jnp.any(train_hit, axis=1) & live[:, None]).astype(jnp.int32)
    train_rank_table = jnp.cumsum(train_named, axis=0) - train_named
    train_rank = jnp.sum(jnp.where(train_hit, train_rank_table[:, None, :], 0), axis=-1)
    bucket_id = jnp.where(live[:, None], train_slot * train_most + train_rank, experts * train_most)
    train_source = (
        jnp.zeros((experts * train_most,), jnp.int32)
        .at[bucket_id.reshape(-1)]
        .set(jnp.arange(train_rows_dev * top_count, dtype=jnp.int32) + 1, mode="drop")
    )
    train_buckets = gather_rows(
        train_source,
        train_grads.reshape(train_rows_dev * top_count, grad_width),
        (experts, train_most, grad_width),
    )
    train_index = jnp.where(train_source > 0, (train_source - 1) // top_count, train_rows_dev)
    train_index = train_index.reshape(experts, train_most)
    local_slot = query_slot * query_most + query_rank
    mine = lax.dynamic_slice_in_dim(local_slot, my_index * per_device, per_device, 0)
    send_source = (
        jnp.zeros((experts * query_most,), jnp.int32)
        .at[mine.reshape(-1)]
        .set(jnp.arange(per_device * top_count, dtype=jnp.int32) + 1)
    )
    flat_mine = query_grads.reshape(per_device * top_count, grad_width)
    start_scores = jnp.zeros((queries, train_rows_dev), jnp.float32)
    outgoing = gather_rows(send_source, flat_mine, (experts, query_most, grad_width))
    arrived = lax.all_to_all(outgoing, "shard", split_axis=0, concat_axis=1, tiled=True)
    ready = precondition(arrived, basis_s, basis_a, eigenvalues)
    tiles = jnp.einsum(
        "ecd,etd->ect",
        lax.all_gather(ready, "shard", axis=0, tiled=True),
        train_buckets,
        preferred_element_type=jnp.float32,
    )
    return place_tiles(start_scores, tiles, query_index, train_index)


def solution(mesh):
    placed = (
        P(("groups", "shard"), None, None),
        P("groups", None),
        P(("groups", "shard"), None, None),
        P(("groups", "shard"), None),
        P(("groups", "shard")),
        P(),
        P("shard", None, None),
        P("shard", None, None),
        P("shard", None, None),
    )
    return jax.shard_map(
        local, mesh=mesh, in_specs=placed, out_specs=P("groups", "shard"), check_vma=False
    )
```

profile of v0, /device:TPU:0, one launch (start us, length us, event | category | flops | bytes accessed | tf_op | source)
XLA Modules:
  0.0 223.6 jit_solution(4506542704072328639)
XLA Ops:
  6.5 0.0 copy-start
  6.5 0.0 copy-start.4
  7.3 0.7 fusion.16
  8.0 0.1 copy.47
  8.1 0.1 and_convert_fusion
  8.2 0.2 reduce_window_sum.26
  8.4 0.1 fusion.30
  8.5 0.1 copy.48
  8.5 0.7 fusion.17
  9.3 0.1 copy.38
  9.4 0.1 reduce_window_sum.24
  9.4 0.1 copy.39
  9.5 0.9 select_reduce_fusion.1
  10.4 0.1 constant_dynamic-slice_fusion
  10.4 0.1 copy.41
  10.5 0.1 reshape.219
  10.6 0.8 scatter_custom_fusion.1
  11.4 0.0 copy-done
  11.4 0.5 convolution_convert_fusion.1
  11.9 1.2 reshape.221
  13.1 0.0 copy-start.3
  13.1 7.5 %all-to-all-start = ((bf16[32,4,4096]{2,1,0:T(4,128)(2,1)}), bf16[32,4,4096]{2,1,0:T(4,128)(2,1)S(1)}, u32[]{:S(2)}, u32[]{:S(2)}) async-start(bf16[32,4,4096]{2,1,0:T(4,128)(2,1)} %reshape.221), calls=%async_computation | async-start | bytes 2097152 | tf_op jit(solution)/shard_map/all_to_all | solution.py:109
  20.6 0.0 all-gather.2.cloned.1.call-start
  20.7 0.0 copy-done.4
  20.7 22.9 %all-to-all-done = bf16[32,4,4096]{2,1,0:T(4,128)(2,1)S(1)} async-done(((bf16[32,4,4096]{2,1,0:T(4,128)(2,1)}), bf16[32,4,4096]{2,1,0:T(4,128)(2,1)S(1)}, u32[]{:S(2)}, u32[]{:S(2)}) %all-to-all-start) | async-done | bytes 1048608 | tf_op jit(solution)/shard_map/all_to_all | solution.py:109
  43.6 0.6 copy.42
  44.2 0.0 copy-start.2
  44.2 1.8 reshape.222
  46.1 0.0 copy-done.3
  46.1 2.2 fusion.21
  48.3 0.0 copy-done.2
  48.3 6.7 %fusion.3 = f32[2,64,64,64]{3,2,1,0:T(8,128)S(1)} fusion(f32[2,64,64,64]{3,2,1,0:T(8,128)S(1)} %fusion.21, f32[2,64,64]{2,1,0:T(8,128)S(1)} %copy-done.2), kind=kOutput, calls=%fused_computation.9 | convolution fusion | flops 402653184 | bytes 4227072 | tf_op jit(solution)/shard_map/ecik,ekl->ecil/dot_general | solution.py:15
  55.0 7.0 %fusion.6 = f32[2,64,64,64]{3,2,1,0:T(8,128)S(1)} fusion(f32[2,64,64,64]{3,2,1,0:T(8,128)S(1)} %fusion.3, f32[2,64,64]{2,1,0:T(8,128)S(1)} %broadcast_add_fusion, f32[2,64,64]{2,1,0:T(8,128)S(1)} %copy-done.3), kind=kOutput, calls=%fused_computation.12 | convolution fusion | flops 403177472 | bytes 4259840 | tf_op jit(solution)/shard_map/eij,ecjk->ecik/dot_general | solution.py:17
  62.0 7.1 %fusion.9 = bf16[2,64,64,64]{3,2,1,0:T(8,128)(2,1)S(1)} fusion(f32[2,64,64,64]{3,2,1,0:T(8,128)S(1)} %fusion.6, f32[2,64,64]{2,1,0:T(8,128)S(1)} %copy-done.2), kind=kOutput, calls=%fused_computation.15 | convolution fusion | flops 403177472 | bytes 3178496 | tf_op jit(solution)/shard_map/ecik,elk->ecil/dot_general | solution.py:18
  69.1 2.5 %convert_element_type.46 = bf16[2,64,4096]{2,1,0:T(8,128)(2,1)} reshape(bf16[2,64,64,64]{3,2,1,0:T(8,128)(2,1)S(1)} %fusion.9) | data formatting | bytes 2097152 | tf_op jit(solution)/shard_map/convert_element_type | solution.py:19
  71.6 0.0 all-gather.2.cloned.1.call-update
  71.6 0.1 copy.49
  71.7 0.1 select_n.97
  71.9 4.3 %scatter_custom_fusion.2 = s32[2048]{0:T(1024)S(1)} fusion(s32[1024]{0:T(1024)S(1)} %bitcast.53, s32[1024]{0:T(1024)S(1)} %iota_add_fusion, s32[]{:T(128)} %constant.61.clone.1), kind=kCustom, calls=%fused_computation.65 | custom fusion | bytes 8196 | tf_op jit(solution)/shard_map/scatter | solution.py:90
  76.2 0.1 eq.98
  76.3 0.1 copy.40
  76.4 0.1 add.117
  76.5 4.3 %scatter_custom_fusion = s32[2048]{0:T(1024)S(1)} fusion(s32[1024]{0:T(1024)S(1)} %bitcast.52, s32[1024]{0:T(1024)S(1)} %iota_add_fusion, s32[]{:T(128)} %constant.61.clone.1), kind=kCustom, calls=%fused_computation.67 | custom fusion | bytes 8196 | tf_op jit(solution)/shard_map/scatter | solution.py:77
  80.8 0.1 eq.85
  80.9 24.7 %convolution_convert_fusion = bf16[2048,4096]{1,0:T(8,128)(2,1)} fusion(bf16[128,8,4096]{2,1,0:T(8,128)(2,1)} %param.11, s32[2048]{0:T(1024)S(1)} %get-tuple-element.14), kind=kOutput, calls=%fused_computation.3 | convolution fusion | flops 17190354944 | bytes 25174016 | tf_op jit(solution)/shard_map/dot_general | solution.py:43
  105.6 95.3 %all-gather.2.cloned.1.call-done = bf16[32,64,4096]{2,1,0:T(8,128)(2,1)} async-done(((bf16[2,64,4096]{2,1,0:T(8,128)(2,1)}), bf16[32,64,4096]{2,1,0:T(8,128)(2,1)}) %all-gather.2.cloned.1.call-update) | async-done | bytes 16777232 | tf_op jit(solution)/shard_map/all_gather | solution.py:113
  200.9 0.0 copy-start.1
  200.9 12.9 %fusion.39 = f32[32,64,64]{2,1,0:T(8,128)S(1)} fusion(bf16[32,64,4096]{2,1,0:T(8,128)(2,1)} %all-gather.2.cloned.1.call-done, bf16[32,64,4096]{2,1,0:T(8,128)(2,1)} %bitcast.54), kind=kOutput, calls=%fused_computation.82 | convolution fusion | flops 1073741824 | bytes 34078720 | tf_op jit(solution)/shard_map/ecd,etd->ect/dot_general | solution.py:111
  213.8 1.0 fusion.12
  214.8 2.0 convolution_bitcast_fusion
  216.8 0.0 copy-done.1
  (14 shorter events, 0.1 us)
Async XLA Ops:
  6.5 4.9 %copy-start = (bf16[8,8,4096]{2,1,0:T(8,128)(2,1)S(1)}, bf16[8,8,4096]{2,1,0:T(8,128)(2,1)}, u32[]{:S(2)}) copy-start(bf16[8,8,4096]{2,1,0:T(8,128)(2,1)} %param.9) | copy-start | bytes 1572868
  6.5 14.2 %copy-start.4 = (f32[2,64,64]{2,1,0:T(8,128)S(1)}, f32[2,64,64]{2,1,0:T(8,128)}, u32[]{:S(2)}) copy-start(f32[2,64,64]{2,1,0:T(8,128)} %param.17) | copy-start | bytes 98308
  13.1 32.9 %copy-start.3 = (f32[2,64,64]{2,1,0:T(8,128)S(1)}, f32[2,64,64]{2,1,0:T(8,128)}, u32[]{:S(2)}) copy-start(f32[2,64,64]{2,1,0:T(8,128)} %param.15) | copy-start | bytes 98308
  13.1 30.5 %all-to-all-start = ((bf16[32,4,4096]{2,1,0:T(4,128)(2,1)}), bf16[32,4,4096]{2,1,0:T(4,128)(2,1)S(1)}, u32[]{:S(2)}, u32[]{:S(2)}) async-start(bf16[32,4,4096]{2,1,0:T(4,128)(2,1)} %reshape.221), calls=%async_computation | async-start | bytes 2097152 | tf_op jit(solution)/shard_map/all_to_all | solution.py:109
  20.6 180.2 %all-gather.2.cloned.1.call-start = ((), (), s32[]{:S(2)}) async-start(), calls=%async_computation.1 | async-start | bytes 17825792 | tf_op jit(solution)/shard_map/all_gather | solution.py:113
  44.2 4.1 %copy-start.2 = (f32[2,64,64]{2,1,0:T(8,128)S(1)}, f32[2,64,64]{2,1,0:T(8,128)}, u32[]{:S(2)}) copy-start(f32[2,64,64]{2,1,0:T(8,128)} %param.16) | copy-start | bytes 98308
  200.9 15.9 %copy-start.1 = (bf16[8,8,4096]{2,1,0:T(8,128)(2,1)S(1)}, bf16[8,8,4096]{2,1,0:T(8,128)(2,1)}, u32[]{:S(2)}) copy-start(bf16[8,8,4096]{2,1,0:T(8,128)(2,1)} %param.9) | copy-start | bytes 1572868
Sparse Core Ops, SparseCore 0:
  71.8 129.0 all-gather.1
where the time goes:
time: 224 us
  waiting for transfers between devices  118 us (53%)
  matrix products  64.1 us (29%)
  local copies, waits for them, and re-layouts  16.7 us (7%)
  between operations  14.3 us (6%)
  starting transfers between devices  7.56 us (3%)
  other arithmetic  2.8 us (1%)
    all_gather x1, waiting for transfers between devices, local(): lax.all_gather(ready, 'shard', axis=0, tiled=True)  95.3 us
    dot_general x2, matrix products, gather_rows(): jnp.dot(chosen, flat_rows, preferred_element_type=jnp.float32)  25.2 us
    all_to_all x1, waiting for transfers between devices, local(): lax.all_to_all(outgoing, 'shard', split_axis=0, concat_axis=1, tiled=True)  22.9 us
    dot_general x1, matrix products, local(): jnp.einsum('ecd,etd->ect', lax.all_gather(ready, 'shard', axis=0, tiled=T...  12.9 us
    all_to_all x1, starting transfers between devices, local(): lax.all_to_all(outgoing, 'shard', split_axis=0, concat_axis=1, tiled=True)  7.52 us
    dot_general x1, matrix products, precondition(): jnp.einsum('ecik,elk->ecil', back, basis_a, precision=lax.Precision.HIGHEST)  7.11 us
    dot_general x1, matrix products, precondition(): jnp.einsum('eij,ecjk->ecik', basis_s, scaled, precision=lax.Precision.HIG...  7 us
    dot_general x1, matrix products, precondition(): jnp.einsum('ecik,ekl->ecil', turned, basis_a, precision=lax.Precision.HIG...  6.68 us
  transfers between devices with their start and end apart: 2, of which 2 were waited for; matrix products, arithmetic and copies ran while one was open for 15% of the time, Pallas kernels for 0%

commit v1 on v0

v1 whole, which is shorter than its diff:
```python
import functools

import jax
import jax.numpy as jnp
from jax import lax
from jax.experimental import pallas as pl
from jax.experimental.pallas import tpu as pltpu
from jax.sharding import PartitionSpec as P

DAMPING = 0.01
F32, BF16 = jnp.float32, jnp.bfloat16
RAW_HOPS = 0
STRIDE = 65
GROUP = 32
TILE = 256
MIB = 2**20


def split(x):
    hi = x.astype(BF16)
    return hi, (x - hi.astype(F32)).astype(BF16)


def swap(x):
    return pltpu.roll(x, 64, 1)


def precondition_kernel(chunks, experts, routes, owner, place, devs, mine, sib, *rest):
    raws, outs = rest[:chunks], rest[chunks : 2 * chunks]
    tab_a, tab_at, tab_s, tab_st, scale, xs, ys = rest[2 * chunks :]
    half = experts // 2
    left64 = lax.broadcasted_iota(jnp.int32, (64, 128), 1) < 64
    left = left64[:32]

    def prepare(e, src, at):
        base = pl.multiple_of(e * 96, 32)

        def twice(f):
            r = swap(f)
            return jnp.concatenate([jnp.where(left, f, r), jnp.where(left, r, f)], 0)

        s = twice(src[pl.ds(base, 32), :])
        a = twice(src[pl.ds(base + 32, 32), :])
        scale[at + e] = 1.0 / (twice(src[pl.ds(base + 64, 32), :]) + DAMPING)
        t = jnp.concatenate([s, a], 0).T[:64]
        r = swap(t)
        st, a_t = jnp.where(left64, t, r), jnp.where(left64, r, t)
        for ref, m in ((tab_s, s), (tab_st, st)):
            hi, lo = split(m)
            ref[at + e, :, :128] = hi
            ref[at + e, :, 128:] = lo
        for ref, m in ((tab_a, a), (tab_at, a_t)):
            for w in (0, 1):
                hi, lo = split(jnp.where(left64 if w == 0 else ~left64, m, 0.0))
                ref[at + e, w, :64] = hi
                ref[at + e, w, 64:] = lo

    def both(e, unused):
        prepare(e, mine, 0)
        prepare(e, sib, half)
        return 0

    lax.fori_loop(0, half, both, 0, unroll=2)

    def pair(tab, e1, e2, three):
        hi = [tab[e1, 0, :64], tab[e2, 1, :64]]
        lo = [tab[e1, 0, 64:], tab[e2, 1, 64:]]
        return jnp.concatenate(hi + (hi if three else []) + lo, 0)

    def cross(tab, e1, e2, x):
        hi, lo = split(x)
        o = jnp.dot(
            jnp.concatenate([tab[e1], tab[e2]], 0),
            jnp.concatenate([hi, lo, hi, lo], 0),
            preferred_element_type=F32,
        )
        return jnp.where(left64, o[:64], o[64:])

    for ch in range(chunks):
        raw, out = raws[ch], outs[ch]
        for c in range(32):
            xs[pl.ds(c * STRIDE, 64), :] = raw[:, c * 128 : (c + 1) * 128].astype(F32)

        def group(b, unused):
            es, g, x = [], [], []
            for i in range(GROUP):
                row = b * GROUP + i
                es.append(place[owner[routes[devs[ch] * 8 + row // 8, row % 8]]])
                g.append(xs[pl.ds(row, 32, stride=STRIDE), :])
            n = GROUP // 2
            ee = [(es[2 * p], es[2 * p + 1]) for p in range(n)]
            for p in range(n):
                g1, g2 = g[2 * p], g[2 * p + 1]
                h = [jnp.where(left, g1, swap(g2)), jnp.where(left, swap(g1), g2)]
                h = jnp.concatenate(h, 0).astype(BF16)
                h = jnp.concatenate([h, h], 1)
                x.append(jnp.dot(h, pair(tab_a, *ee[p], False), preferred_element_type=F32))
            x = [
                cross(tab_st, *ee[p], x[p]) * jnp.where(left64, scale[ee[p][0]], scale[ee[p][1]])
                for p in range(n)
            ]
            x = [cross(tab_s, *ee[p], x[p]) for p in range(n)]
            for p in range(n):
                hi, lo = split(x[p])
                h = jnp.concatenate([hi, lo, hi], 1)
                y = jnp.dot(h, pair(tab_at, *ee[p], True), preferred_element_type=F32)
                top, low = y[:32], y[32:]
                for w, v in enumerate((jnp.where(left, top, swap(low)), jnp.where(left, swap(top), low))):
                    row = b * GROUP + 2 * p + w
                    ys[pl.ds((row % 8) * 8 + row // 8, 32, stride=STRIDE), :] = v
            return 0

        lax.fori_loop(0, 64 // GROUP, group, 0)
        for c in range(32):
            out[:, c * 128 : (c + 1) * 128] = ys[pl.ds(c * STRIDE, 64), :].astype(BF16)


def precondition(routes, owner, place, devs, mine, sib, raws):
    experts = owner.shape[0]
    chunks = len(raws)
    sm = pl.BlockSpec(memory_space=pltpu.SMEM)
    vm = pl.BlockSpec(memory_space=pltpu.VMEM)
    return pl.pallas_call(
        functools.partial(precondition_kernel, chunks, experts),
        out_shape=[jax.ShapeDtypeStruct(r.shape, BF16) for r in raws],
        in_specs=[sm] * 4 + [vm] * (2 + chunks),
        out_specs=[vm] * chunks,
        scratch_shapes=[
            pltpu.VMEM((experts, 2, 128, 128), BF16),
            pltpu.VMEM((experts, 2, 128, 128), BF16),
            pltpu.VMEM((experts, 64, 256), BF16),
            pltpu.VMEM((experts, 64, 256), BF16),
            pltpu.VMEM((experts, 64, 128), F32),
            pltpu.VMEM((32 * STRIDE, 128), F32),
            pltpu.VMEM((32 * STRIDE, 128), F32),
        ],
        compiler_params=pltpu.CompilerParams(vmem_limit_bytes=32 * MIB),
        cost_estimate=pl.CostEstimate(
            flops=10**9 * (2 + 3 * chunks), bytes_accessed=10**6 * (1 + chunks), transcendentals=0
        ),
        name="precondition",
    )(routes, owner, place, devs, mine, sib, *raws)


def products_kernel(rows, earlier, tiles, devs, own_route, sib_route, query_route, own_train, sib_train, *rest):
    n_in = len(rows)
    parts, old = rest[:n_in], rest[n_in : n_in + 2 * len(earlier)]
    out_own, out_sib, held, total = rest[n_in + 2 * len(earlier) :]
    step = pl.program_id(0)
    units = sum(rows) // 64
    train_rows = tiles * TILE

    @pl.when(step == 0)
    def _():
        at = 0
        for part, r in zip(parts, rows):
            held[at : at + r, :] = part[...]
            at += r

    def one(train, route, base, i):
        g = lax.dot_general(held[...], train[...], (((1,), (1,)), ((), ())), preferred_element_type=F32)
        column = pl.multiple_of(i * TILE, TILE)
        there = route[:, pl.ds(column, TILE)]
        for u in range(units):
            want = query_route[pl.ds(pl.multiple_of(devs[u] * 64, 64), 64), :]
            want = jnp.concatenate([want] * (TILE // 128), 1)
            hit = jnp.where(want == there, g[u * 64 : (u + 1) * 64], 0.0)
            total[u * 8 : (u + 1) * 8, pl.ds(base + column, TILE)] = jnp.sum(hit.reshape(8, 8, TILE), axis=0)

    @pl.when(step < tiles)
    def _():
        one(own_train, own_route, 0, step)

    @pl.when(step >= tiles)
    def _():
        one(sib_train, sib_route, train_rows, step - tiles)

    @pl.when(step == 2 * tiles - 1)
    def _():
        row = lax.broadcasted_iota(jnp.int32, (train_rows, 128), 0)
        col = lax.broadcasted_iota(jnp.int32, (train_rows, 128), 1)
        fold = (lax.shift_right_logical(row, 3) == col).astype(BF16)

        def folded(x):
            hi = x.astype(BF16)
            left = x - hi.astype(F32)
            mid = left.astype(BF16)
            low = (left - mid.astype(F32)).astype(BF16)
            y = jnp.dot(jnp.concatenate([hi, mid, low], 0), fold, preferred_element_type=F32)
            n = x.shape[0]
            return y[:n] + y[n : 2 * n] + y[2 * n :]

        for k, out in enumerate((out_own, out_sib)):
            now = folded(total[:, k * train_rows : (k + 1) * train_rows])
            if not earlier:
                out[...] = now
                continue
            at = 0
            for j, n_units in enumerate(list(earlier) + [units]):
                for u in range(n_units):
                    dev = devs[units + at] if j < len(earlier) else devs[u]
                    block = (old[2 * j + k] if j < len(earlier) else now)[u * 8 : (u + 1) * 8]
                    out[pl.ds(pl.multiple_of((dev // 2) * 8, 8), 8), :] = block
                    at += 1


def products(devs, own_route, sib_route, query_route, own_train, sib_train, parts, old, chips):
    rows = [p.shape[0] for p in parts]
    units = sum(rows) // 64
    train_rows, width = own_train.shape
    tiles = train_rows // TILE
    earlier = [o[0].shape[0] // 8 for o in old]
    flat_old = [v for o in old for v in o]
    sm = pl.BlockSpec(memory_space=pltpu.SMEM)
    whole = lambda v: pl.BlockSpec(v.shape, lambda i: (0,) * len(v.shape))
    n_out = chips * 8 if old else units * 8
    return pl.pallas_call(
        functools.partial(products_kernel, rows, earlier, tiles),
        grid=(2 * tiles,),
        out_shape=[jax.ShapeDtypeStruct((n_out, 128), F32)] * 2,
        in_specs=[sm, whole(own_route), whole(sib_route), whole(query_route)]
        + [
            pl.BlockSpec((TILE, width), lambda i: (jnp.minimum(i, tiles - 1), 0)),
            pl.BlockSpec((TILE, width), lambda i: (jnp.maximum(i - tiles, 0), 0)),
        ]
        + [whole(v) for v in list(parts) + flat_old],
        out_specs=[pl.BlockSpec((n_out, 128), lambda i: (0, 0))] * 2,
        scratch_shapes=[pltpu.VMEM((sum(rows), width), BF16), pltpu.VMEM((units * 8, 2 * train_rows), F32)],
        compiler_params=pltpu.CompilerParams(vmem_limit_bytes=32 * MIB),
        cost_estimate=pl.CostEstimate(
            flops=4 * 128 * max(1, (units + 1) // 2) * train_rows * width,
            bytes_accessed=4 * train_rows * width,
            transcendentals=0,
        ),
        name="products",
    )(devs, own_route, sib_route, query_route, own_train, sib_train, *parts, *flat_old)


def local(
    query_grads,
    query_routes,
    train_grads,
    train_routes,
    train_counts,
    owner_slot,
    basis_s,
    basis_a,
    eigenvalues,
):
    devices = lax.axis_size("shard")
    me = lax.axis_index("shard")
    experts = owner_slot.shape[0]
    queries, top = query_routes.shape
    width = query_grads.shape[2]
    train_dev = train_grads.shape[0]
    slots = basis_s.shape[0]
    chips = devices // 2
    far = chips // 2
    ring = [2 * z for z in range(far)] + [2 * z + 1 for z in reversed(range(far))]
    spot = [ring.index(c) for c in range(chips)]

    def shift(step):
        return [
            (2 * c + k, 2 * ring[(i + step) % chips] + k) for i, c in enumerate(ring) for k in range(2)
        ]

    ahead, back = shift(1), shift(-1)
    across = [(d, d ^ 1) for d in range(devices)]
    send = lambda v, way: lax.ppermute(v, "shard", way)

    def circulate(own, up, down, first, until=None):
        out = []
        for _ in range(first, far - 1):
            up, down = send(up, ahead), send(down, back)
            out.append((up, down))
        cut = own.shape[0] // 2
        out.append((send(up[:cut], ahead), send(down[cut:], back)))
        return out

    halves = lambda m: jnp.concatenate([m[:, :32], m[:, 32:]], axis=-1)
    pack = jnp.stack([basis_s.reshape(slots, 32, 128), halves(basis_a), halves(eigenvalues)], axis=1)
    pack = pack.reshape(slots * 96, 128)
    steps = circulate(pack, pack, pack, 0)
    mine = jnp.concatenate([pack] + [v for step in steps for v in step], axis=0)
    sib = send(mine, across)

    spots = jnp.asarray(spot, jnp.int32)
    my_spot = jnp.sum(jnp.where(jnp.arange(chips) == me // 2, spots, 0))
    rel = (jnp.repeat(spots, 2 * slots) - my_spot + chips) % chips
    order = jnp.where(rel > far, 2 * (chips - rel) - 1, 2 * rel)
    order = jnp.where(rel == far, chips - 1, order)
    slot = jnp.arange(experts, dtype=jnp.int32)
    core = (slot // slots) % 2
    place = (jnp.where(core == me % 2, 0, chips) + order) * slots + slot % slots

    rings = jnp.asarray(ring, jnp.int32)

    def dev_at(distance):
        at = (my_spot + distance) % chips
        return 2 * jnp.sum(jnp.where(jnp.arange(chips) == at, rings, 0)) + me % 2

    devs_of = lambda ds: jnp.stack([dev_at(d) for d in ds]).astype(jnp.int32)

    live = jnp.arange(train_dev, dtype=jnp.int32) < train_counts[0]
    own_route = jnp.where(live[:, None], train_routes, -1).reshape(1, train_dev * top)
    sib_route = send(own_route, across)
    own_train = train_grads.reshape(train_dev * top, width)
    sib_train = send(own_train, across)
    query_route = query_routes.reshape(devices, 8, top).transpose(0, 2, 1).reshape(queries * top, 1)
    query_route = jnp.broadcast_to(query_route, (queries * top, 128))

    raw = query_grads.reshape(-1, width)
    pre = lambda raws, ds: precondition(query_routes, owner_slot, place, devs_of(ds), mine, sib, raws)
    if RAW_HOPS == 0:
        own = pre([raw], [0])[0]
        steps = circulate(own, own, own, 0)
    else:
        up, down = send(raw, ahead), send(raw, back)
        up, down = pre([up, down], [-1, 1])
        own = pre([raw], [0])[0]
        steps = [(up, down)] + circulate(own, up, down, 1)

    calls = [([own, *steps[0]], [0, -1, 1])]
    for s in range(1, far - 1, 2):
        two = range(s, min(s + 2, far - 1))
        calls.append(([v for t in two for v in steps[t]], [d for t in two for d in (-t - 1, t + 1)]))
    done, ds = [], []
    for parts, distances in calls:
        done.append(
            products(devs_of(distances), own_route, sib_route, query_route, own_train, sib_train, parts, [], chips)
        )
        ds += distances
    here, there = products(
        devs_of([far] + ds), own_route, sib_route, query_route, own_train, sib_train, steps[-1], done, chips
    )
    other = send(there, across)
    here, other = here.reshape(chips, 8, train_dev), other.reshape(chips, 8, train_dev)
    even = me % 2 == 0
    both = jnp.stack([jnp.where(even, here, other), jnp.where(even, other, here)], axis=1)
    return both.reshape(queries, train_dev)


def solution(mesh):
    placed = (
        P(("groups", "shard"), None, None),
        P("groups", None),
        P(("groups", "shard"), None, None),
        P(("groups", "shard"), None),
        P(("groups", "shard")),
        P(),
        P("shard", None, None),
        P("shard", None, None),
        P("shard", None, None),
    )
    return jax.shard_map(
        local, mesh=mesh, in_specs=placed, out_specs=P("groups", "shard"), check_vma=False
    )
```

time: 224 us -> 126 us (0.56)
  waiting for transfers between devices: 118 us -> 42.3 us
  matrix products: 64.1 us -> 0 us
  Pallas kernels: 0 us -> 38 us
  starting transfers between devices: 7.56 us -> 17.6 us
  local copies, waits for them, and re-layouts: 16.7 us -> 9.94 us
    all_gather x1 -> x0, waiting for transfers between devices: 95.3 us -> none  [local(): lax.all_gather(ready, 'shard', axis=0, tiled=True)]
    dot_general x9 -> x0, matrix products: 64.1 us -> none  [the longest x2 25.2 us: gather_rows(): jnp.dot(chosen, flat_rows, preferred_element_type=jnp.float32)]
    ppermute x0 -> x20, waiting for transfers between devices: none -> 42.3 us  [local(): send = lambda v, way: lax.ppermute(v, 'shard', way)]
    pallas_call x0 -> x4, Pallas kernels: none -> 38 us  [the longest x3 30.6 us: products(): pl.pallas_call(functools.partial(products_kernel, rows, earlier, tiles),...]
    all_to_all x1 -> x0, waiting for transfers between devices: 22.9 us -> none  [local(): lax.all_to_all(outgoing, 'shard', split_axis=0, concat_axis=1, tiled=True)]
    ppermute x0 -> x20, starting transfers between devices: none -> 17.6 us  [local(): send = lambda v, way: lax.ppermute(v, 'shard', way)]
    scatter x3 -> x0, local copies, waits for them, and re-layouts: 9.41 us -> none  [the longest x1 4.32 us: local(): train_source = jnp.zeros((experts * train_most,), jnp.int32).at[bucket_id...]
    all_to_all x1 -> x0, starting transfers between devices: 7.52 us -> none  [local(): lax.all_to_all(outgoing, 'shard', split_axis=0, concat_axis=1, tiled=True)]
  transfers between devices with their start and end apart: 2 -> 20, of which waited for: 2 -> 9; matrix products, arithmetic and copies ran while one was open for 15% -> 7% of each run, Pallas kernels for 0% -> 23%
where the time goes in v1:
time: 126 us; the launch traced here: 125 us
  waiting for transfers between devices  42.3 us (34%)
  Pallas kernels  38 us (30%)
  starting transfers between devices  17.6 us (14%)
  between operations  12.4 us (10%)
  local copies, waits for them, and re-layouts  9.94 us (8%)
  other arithmetic  4.37 us (3%)
    ppermute x20, waiting for transfers between devices, local(): send = lambda v, way: lax.ppermute(v, 'shard', way)  42.3 us
    pallas_call x3, Pallas kernels, products(): pl.pallas_call(functools.partial(products_kernel, rows, earlier, tiles),...  30.6 us
    ppermute x20, starting transfers between devices, local(): send = lambda v, way: lax.ppermute(v, 'shard', way)  17.6 us
    pallas_call x1, Pallas kernels, precondition(): pl.pallas_call(functools.partial(precondition_kernel, chunks, experts), o...  7.42 us
    unnamed x21, local copies, waits for them, and re-layouts  5.94 us
  transfers between devices with their start and end apart: 20, of which 9 were waited for; matrix products, arithmetic and copies ran while one was open for 7% of the time, Pallas kernels for 23%

profile of v1, /device:TPU:0, one launch (start us, length us, event | category | flops | bytes accessed | tf_op | source)
XLA Modules:
  0.0 124.6 jit_solution(9824707024234608535)
XLA Ops:
  0.0 0.5 collective-permute-start.1
  0.5 0.9 stack_reshape.3
  1.4 0.8 fusion.13
  2.1 0.8 fusion.14
  2.9 0.1 maximum_bitcast_fusion
  3.1 2.6 %collective-permute-start.2 = (f32[192,128]{1,0:T(8,128)S(1)}, f32[192,128]{1,0:T(8,128)S(1)}, u32[]{:S(2)}, u32[]{:S(2)}) collective-permute-start(f32[192,128]{1,0:T(8,128)S(1)} %bitcast.30), channel_id=1, source_target_pairs={{0,4},{1,5},{4,8},{5,9},{8,12},{9,13},{12,14},{13,15},{14,10},{15,... | collective-permute-start | bytes 294920 | tf_op jit(solution)/shard_map/ppermute | solution.py:269
  5.7 0.0 collective-permute-start.3
  5.7 3.4 %collective-permute-done.2 = f32[192,128]{1,0:T(8,128)S(1)} collective-permute-done((f32[192,128]{1,0:T(8,128)S(1)}, f32[192,128]{1,0:T(8,128)S(1)}, u32[]{:S(2)}, u32[]{:S(2)}) %collective-permute-start.2) | collective-permute-done | bytes 98336 | tf_op jit(solution)/shard_map/ppermute | solution.py:269
  9.1 1.8 %collective-permute-start.4 = (f32[192,128]{1,0:T(8,128)S(1)}, f32[192,128]{1,0:T(8,128)S(1)}, u32[]{:S(2)}, u32[]{:S(2)}) collective-permute-start(f32[192,128]{1,0:T(8,128)S(1)} %collective-permute-done.2), channel_id=1, source_target_pairs={{0,4},{1,5},{4,8},{5,9},{8,12},{9,13},{12,14},{13,15},{14,10},{15,... | collective-permute-start | bytes 294920 | tf_op jit(solution)/shard_map/ppermute | solution.py:269
  10.9 0.0 collective-permute-done.3
  10.9 0.2 collective-permute-start.5
  11.1 2.6 %collective-permute-done.4 = f32[192,128]{1,0:T(8,128)S(1)} collective-permute-done((f32[192,128]{1,0:T(8,128)S(1)}, f32[192,128]{1,0:T(8,128)S(1)}, u32[]{:S(2)}, u32[]{:S(2)}) %collective-permute-start.4) | collective-permute-done | bytes 98336 | tf_op jit(solution)/shard_map/ppermute | solution.py:269
  13.7 1.8 %collective-permute-start.6 = (f32[192,128]{1,0:T(8,128)S(1)}, f32[192,128]{1,0:T(8,128)S(1)}, u32[]{:S(2)}, u32[]{:S(2)}) collective-permute-start(f32[192,128]{1,0:T(8,128)S(1)} %collective-permute-done.4), channel_id=1, source_target_pairs={{0,4},{1,5},{4,8},{5,9},{8,12},{9,13},{12,14},{13,15},{14,10},{15,... | collective-permute-start | bytes 294920 | tf_op jit(solution)/shard_map/ppermute | solution.py:269
  15.5 0.0 collective-permute-done.5
  15.5 0.2 collective-permute-start.7
  15.8 2.6 %collective-permute-done.6 = f32[192,128]{1,0:T(8,128)S(1)} collective-permute-done((f32[192,128]{1,0:T(8,128)S(1)}, f32[192,128]{1,0:T(8,128)S(1)}, u32[]{:S(2)}, u32[]{:S(2)}) %collective-permute-start.6) | collective-permute-done | bytes 98336 | tf_op jit(solution)/shard_map/ppermute | solution.py:269
  18.3 1.8 %collective-permute-start.8 = (f32[96,128]{1,0:T(8,128)S(1)}, f32[96,128]{1,0:T(8,128)S(1)}, u32[]{:S(2)}, u32[]{:S(2)}) collective-permute-start(f32[96,128]{1,0:T(8,128)S(1)} %slice.32), channel_id=1, source_target_pairs={{0,4},{1,5},{4,8},{5,9},{8,12},{9,13},{12,14},{13,15},{14,10},{15,... | collective-permute-start | bytes 147464 | tf_op jit(solution)/shard_map/ppermute | solution.py:269
  20.1 0.0 collective-permute-done.7
  20.1 0.3 collective-permute-start.9
  20.5 2.0 %collective-permute-done.8 = f32[96,128]{1,0:T(8,128)S(1)} collective-permute-done((f32[96,128]{1,0:T(8,128)S(1)}, f32[96,128]{1,0:T(8,128)S(1)}, u32[]{:S(2)}, u32[]{:S(2)}) %collective-permute-start.8) | collective-permute-done | bytes 49184 | tf_op jit(solution)/shard_map/ppermute | solution.py:269
  22.4 1.8 %collective-permute-done.9 = f32[96,128]{1,0:T(8,128)S(1)} collective-permute-done((f32[96,128]{1,0:T(8,128)S(1)}, f32[96,128]{1,0:T(8,128)S(1)}, u32[]{:S(2)}, u32[]{:S(2)}) %collective-permute-start.9) | collective-permute-done | bytes 49184 | tf_op jit(solution)/shard_map/ppermute | solution.py:269
  24.3 1.3 %fusion.1 = s32[]{:T(128)} fusion(s32[8]{0:T(128)} %constant.167.clone, s32[]{:T(128)S(6)} %select_n.197), kind=kLoop, calls=%fused_computation.40 | loop fusion | flops 23 | bytes 40 | tf_op jit(solution)/shard_map/reduce_sum | solution.py:288
  32.2 1.5 %fusion.9 = (s32[]{:T(128)}, s32[]{:T(128)}, s32[]{:T(128)}, s32[]{:T(128)}, s32[]{:T(128)}, /*index=5*/s32[]{:T(128)}, s32[]{:T(128)}, s32[]{:T(128)}) fusion(s32[8]{0:T(128)} %constant.168.clone, s32[]{:T(128)S(6)} %select_n.213, s32[]{:T(128)S(6)} %select_n.209, s32[]{:T(128)S(6)} %select_n.207, s32[]{:T(128)S(6)} %select_n.205, s32[]{:T(128)S(6)} %select_n.203, ...), kind=kLoop, calls=%fused_computation.48 | loop fusion | flops 184 | bytes 96 | tf_op jit(solution)/shard_map/reduce_sum | solution.py:300
  34.2 1.3 %subtract_add_fusion = s32[8]{0:T(128)S(1)} fusion(s32[8]{0:T(128)} %constant.167.clone, s32[]{:T(128)} %fusion.1), kind=kLoop, calls=%fused_computation.54 | loop fusion | flops 16 | bytes 68 | tf_op jit(solution)/shard_map/add | solution.py:289
  35.5 0.1 broadcast_in_dim.60
  35.6 0.1 add.168
  35.7 0.8 copy.19.routes
  36.5 0.0 copy-start.2
  36.5 1.0 copy-done.2
  37.6 0.7 copy-done.3
  38.2 7.4 %precondition.1.rest_0_ = bf16[64,4096]{1,0:T(8,128)(2,1)S(1)} custom-call(s32[128,8]{1,0:T(8,128)S(1)} %copy.19.routes, s32[32]{0:T(128)S(1)} %copy-done.3, s32[32]{0:T(128)S(1)} %fusion.place, s32[1]{0:T(128)} %bitcast.1.devs, f32[1536,128]{1,0:T(8,128)S(1)} %constant_dynamic-update-slice_fusion.mine, f32[1536,128]{1,0:T(8,128)S(1)} %collective-permute-done.10.sib, ...), custom_call_target="tpu_custom_call" | custom-call | flops 5000000000 | bytes 2000000 | tf_op jit(solution)/shard_map/precondition/pallas_call | solution.py:123
  45.6 1.6 %collective-permute-start.11 = (bf16[64,4096]{1,0:T(8,128)(2,1)S(1)}, bf16[64,4096]{1,0:T(8,128)(2,1)S(1)}, u32[]{:S(2)}, u32[]{:S(2)}) collective-permute-start(bf16[64,4096]{1,0:T(8,128)(2,1)S(1)} %precondition.1.rest_0_), channel_id=1, source_target_pairs={{0,4},{1,5},{4,8},{5,9},{8,12},{9,13},{12,14},{13,15},{14,10},{15,... | collective-permute-start | bytes 1572872 | tf_op jit(solution)/shard_map/ppermute | solution.py:269
  47.3 0.5 collective-permute-start.15
  47.7 12.3 %collective-permute-done.11.rest_1_ = bf16[64,4096]{1,0:T(8,128)(2,1)S(1)} collective-permute-done((bf16[64,4096]{1,0:T(8,128)(2,1)S(1)}, bf16[64,4096]{1,0:T(8,128)(2,1)S(1)}, u32[]{:S(2)}, u32[]{:S(2)}) %collective-permute-start.11) | collective-permute-done | bytes 524320 | tf_op jit(solution)/shard_map/ppermute | solution.py:269
  60.0 1.6 %collective-permute-start.12 = (bf16[64,4096]{1,0:T(8,128)(2,1)S(1)}, bf16[64,4096]{1,0:T(8,128)(2,1)S(1)}, u32[]{:S(2)}, u32[]{:S(2)}) collective-permute-start(bf16[64,4096]{1,0:T(8,128)(2,1)S(1)} %collective-permute-done.11.rest_1_), channel_id=1, source_target_pairs={{0,4},{1,5},{4,8},{5,9},{8,12},{9,13},{12,14},{13,15},{14,10},{15,... | collective-permute-start | bytes 1572872 | tf_op jit(solution)/shard_map/ppermute | solution.py:269
  61.6 0.4 collective-permute-start.16
  62.7 10.9 %collective-permute-done.12.rest_0_ = bf16[64,4096]{1,0:T(8,128)(2,1)S(1)} collective-permute-done((bf16[64,4096]{1,0:T(8,128)(2,1)S(1)}, bf16[64,4096]{1,0:T(8,128)(2,1)S(1)}, u32[]{:S(2)}, u32[]{:S(2)}) %collective-permute-start.12) | collective-permute-done | bytes 524320 | tf_op jit(solution)/shard_map/ppermute | solution.py:269
  73.5 1.6 %collective-permute-start.13 = (bf16[64,4096]{1,0:T(8,128)(2,1)S(1)}, bf16[64,4096]{1,0:T(8,128)(2,1)S(1)}, u32[]{:S(2)}, u32[]{:S(2)}) collective-permute-start(bf16[64,4096]{1,0:T(8,128)(2,1)S(1)} %collective-permute-done.12.rest_0_), channel_id=1, source_target_pairs={{0,4},{1,5},{4,8},{5,9},{8,12},{9,13},{12,14},{13,15},{14,10},{15,... | collective-permute-start | bytes 1572872 | tf_op jit(solution)/shard_map/ppermute | solution.py:269
  75.2 0.0 collective-permute-done.16.rest_1_
  75.2 0.4 collective-permute-start.17
  75.6 0.1 copy.16
  75.7 0.1 reshape.69.own_route
  75.8 0.1 collective-permute-start
  79.5 0.1 pad_add_fusion.devs
  79.6 0.1 pad_add_fusion.1.devs
  79.7 0.1 reshape.70
  79.8 0.1 broadcast_in_dim.56
  80.6 0.1 stack.63.devs
  80.7 5.6 %collective-permute-done.13.rest_2_ = bf16[64,4096]{1,0:T(8,128)(2,1)S(1)} collective-permute-done((bf16[64,4096]{1,0:T(8,128)(2,1)S(1)}, bf16[64,4096]{1,0:T(8,128)(2,1)S(1)}, u32[]{:S(2)}, u32[]{:S(2)}) %collective-permute-start.13) | collective-permute-done | bytes 524320 | tf_op jit(solution)/shard_map/ppermute | solution.py:269
  86.3 1.7 %collective-permute-start.14 = (bf16[32,4096]{1,0:T(8,128)(2,1)S(1)}, bf16[32,4096]{1,0:T(8,128)(2,1)S(1)}, u32[]{:S(2)}, u32[]{:S(2)}) collective-permute-start(bf16[32,4096]{1,0:T(8,128)(2,1)S(1)} %slice.34), channel_id=1, source_target_pairs={{0,4},{1,5},{4,8},{5,9},{8,12},{9,13},{12,14},{13,15},{14,10},{15,... | collective-permute-start | bytes 786440 | tf_op jit(solution)/shard_map/ppermute | solution.py:269
  88.0 0.0 collective-permute-done.17.rest_3_
  88.0 0.4 collective-permute-start.18
  88.5 0.0 collective-permute-done.sib_route
  88.5 0.0 collective-permute-done.1.sib_train
  88.5 0.2 broadcast_in_dim.57.query_route
  88.7 0.0 copy-start
  88.7 3.4 %copy-done = bf16[128,8,4096]{2,1,0:T(8,128)(2,1)S(1)} copy-done((bf16[128,8,4096]{2,1,0:T(8,128)(2,1)S(1)}, bf16[128,8,4096]{2,1,0:T(8,128)(2,1)}, u32[]{:S(2)}) %copy-start) | copy-done | bytes 8388632
  92.1 10.2 %products.4 = (f32[32,128]{1,0:T(8,128)S(1)}, f32[32,128]{1,0:T(8,128)S(1)}) custom-call(s32[4]{0:T(128)S(1)} %pad_add_fusion.1.devs, s32[1,1024]{1,0:T(1,128)S(1)} %reshape.69.own_route, s32[1,1024]{1,0:T(1,128)S(1)} %collective-permute-done.sib_route, s32[1024,128]{1,0:T(8,128)S(1)} %broadcast_in_dim.57.query_route, bf16[1024,4096]{1,0:T(8,128)(2,1)S(1)} %bitcast.26, ...), custom_call_target="tpu_custom_call" | custom-call | flops 4294967296 | bytes 16777216 | tf_op jit(solution)/shard_map/products/pallas_call | solution.py:217
  102.2 10.5 %products.3 = (f32[24,128]{1,0:T(8,128)S(1)}, f32[24,128]{1,0:T(8,128)S(1)}) custom-call(s32[3]{0:T(128)S(1)} %pad_add_fusion.devs, s32[1,1024]{1,0:T(1,128)S(1)} %reshape.69.own_route, s32[1,1024]{1,0:T(1,128)S(1)} %collective-permute-done.sib_route, s32[1024,128]{1,0:T(8,128)S(1)} %broadcast_in_dim.57.query_route, bf16[1024,4096]{1,0:T(8,128)(2,1)S(1)} %bitcast.27, ...), custom_call_target="tpu_custom_call" | custom-call | flops 4294967296 | bytes 16777216 | tf_op jit(solution)/shard_map/products/pallas_call | solution.py:217
  112.8 0.0 collective-permute-done.14.rest_0_
  112.8 9.9 %products.5 = (f32[64,128]{1,0:T(8,128)S(1)}, f32[64,128]{1,0:T(8,128)S(1)}) custom-call(s32[8]{0:T(128)S(1)} %stack.63.devs, s32[1,1024]{1,0:T(1,128)S(1)} %reshape.69.own_route, s32[1,1024]{1,0:T(1,128)S(1)} %collective-permute-done.sib_route, s32[1024,128]{1,0:T(8,128)S(1)} %broadcast_in_dim.57.query_route, bf16[1024,4096]{1,0:T(8,128)(2,1)S(1)} %bitcast.28, ...), custom_call_target="tpu_custom_call" | custom-call | flops 2147483648 | bytes 16777216 | tf_op jit(solution)/shard_map/products/pallas_call | solution.py:217
  122.7 0.1 collective-permute-start.19
  122.8 1.2 collective-permute-done.19
  124.0 0.6 copy.20
  (32 shorter events, 0.2 us)
Async XLA Ops:
  0.0 88.5 %collective-permute-start.1 = (bf16[1024,4096]{1,0:T(8,128)(2,1)}, bf16[1024,4096]{1,0:T(8,128)(2,1)}, u32[]{:S(2)}, u32[]{:S(2)}) collective-permute-start(bf16[1024,4096]{1,0:T(8,128)(2,1)} %bitcast.25), channel_id=1, source_target_pairs={{0,1},{1,0},{2,3},{3,2},{4,5},{5,4},{6,7},{7,6},{8,9},{9,8},{10,11... | collective-permute-start | bytes 25165832 | tf_op jit(solution)/shard_map/ppermute | solution.py:269
  3.1 6.0 %collective-permute-start.2 = (f32[192,128]{1,0:T(8,128)S(1)}, f32[192,128]{1,0:T(8,128)S(1)}, u32[]{:S(2)}, u32[]{:S(2)}) collective-permute-start(f32[192,128]{1,0:T(8,128)S(1)} %bitcast.30), channel_id=1, source_target_pairs={{0,4},{1,5},{4,8},{5,9},{8,12},{9,13},{12,14},{13,15},{14,10},{15,... | collective-permute-start | bytes 294920 | tf_op jit(solution)/shard_map/ppermute | solution.py:269
  5.7 5.2 %collective-permute-start.3 = (f32[192,128]{1,0:T(8,128)S(1)}, f32[192,128]{1,0:T(8,128)S(1)}, u32[]{:S(2)}, u32[]{:S(2)}) collective-permute-start(f32[192,128]{1,0:T(8,128)S(1)} %bitcast.31), channel_id=1, source_target_pairs={{0,2},{1,3},{4,0},{5,1},{8,4},{9,5},{12,8},{13,9},{14,12},{15,13},... | collective-permute-start | bytes 294920 | tf_op jit(solution)/shard_map/ppermute | solution.py:269
  9.1 4.6 %collective-permute-start.4 = (f32[192,128]{1,0:T(8,128)S(1)}, f32[192,128]{1,0:T(8,128)S(1)}, u32[]{:S(2)}, u32[]{:S(2)}) collective-permute-start(f32[192,128]{1,0:T(8,128)S(1)} %collective-permute-done.2), channel_id=1, source_target_pairs={{0,4},{1,5},{4,8},{5,9},{8,12},{9,13},{12,14},{13,15},{14,10},{15,... | collective-permute-start | bytes 294920 | tf_op jit(solution)/shard_map/ppermute | solution.py:269
  10.9 4.6 %collective-permute-start.5 = (f32[192,128]{1,0:T(8,128)S(1)}, f32[192,128]{1,0:T(8,128)S(1)}, u32[]{:S(2)}, u32[]{:S(2)}) collective-permute-start(f32[192,128]{1,0:T(8,128)S(1)} %collective-permute-done.3), channel_id=1, source_target_pairs={{0,2},{1,3},{4,0},{5,1},{8,4},{9,5},{12,8},{13,9},{14,12},{15,13},... | collective-permute-start | bytes 294920 | tf_op jit(solution)/shard_map/ppermute | solution.py:269
  13.7 4.6 %collective-permute-start.6 = (f32[192,128]{1,0:T(8,128)S(1)}, f32[192,128]{1,0:T(8,128)S(1)}, u32[]{:S(2)}, u32[]{:S(2)}) collective-permute-start(f32[192,128]{1,0:T(8,128)S(1)} %collective-permute-done.4), channel_id=1, source_target_pairs={{0,4},{1,5},{4,8},{5,9},{8,12},{9,13},{12,14},{13,15},{14,10},{15,... | collective-permute-start | bytes 294920 | tf_op jit(solution)/shard_map/ppermute | solution.py:269
  15.5 4.6 %collective-permute-start.7 = (f32[192,128]{1,0:T(8,128)S(1)}, f32[192,128]{1,0:T(8,128)S(1)}, u32[]{:S(2)}, u32[]{:S(2)}) collective-permute-start(f32[192,128]{1,0:T(8,128)S(1)} %collective-permute-done.5), channel_id=1, source_target_pairs={{0,2},{1,3},{4,0},{5,1},{8,4},{9,5},{12,8},{13,9},{14,12},{15,13},... | collective-permute-start | bytes 294920 | tf_op jit(solution)/shard_map/ppermute | solution.py:269
  18.3 4.1 %collective-permute-start.8 = (f32[96,128]{1,0:T(8,128)S(1)}, f32[96,128]{1,0:T(8,128)S(1)}, u32[]{:S(2)}, u32[]{:S(2)}) collective-permute-start(f32[96,128]{1,0:T(8,128)S(1)} %slice.32), channel_id=1, source_target_pairs={{0,4},{1,5},{4,8},{5,9},{8,12},{9,13},{12,14},{13,15},{14,10},{15,... | collective-permute-start | bytes 147464 | tf_op jit(solution)/shard_map/ppermute | solution.py:269
  20.1 4.1 %collective-permute-start.9 = (f32[96,128]{1,0:T(8,128)S(1)}, f32[96,128]{1,0:T(8,128)S(1)}, u32[]{:S(2)}, u32[]{:S(2)}) collective-permute-start(f32[96,128]{1,0:T(8,128)S(1)} %slice.33), channel_id=1, source_target_pairs={{0,2},{1,3},{4,0},{5,1},{8,4},{9,5},{12,8},{13,9},{14,12},{15,13},... | collective-permute-start | bytes 147464 | tf_op jit(solution)/shard_map/ppermute | solution.py:269
  24.3 12.2 %collective-permute-start.10 = (f32[1536,128]{1,0:T(8,128)S(1)}, f32[1536,128]{1,0:T(8,128)S(1)}, u32[]{:S(2)}, u32[]{:S(2)}) collective-permute-start(f32[1536,128]{1,0:T(8,128)S(1)} %constant_dynamic-update-slice_fusion.mine), channel_id=1, source_target_pairs={{0,1},{1,0},{2,3},{3,2},{4,5},{5,4},{6,7},{7,6},{8,9},{9,8},{10,11... | collective-permute-start | bytes 2359304 | tf_op jit(solution)/shard_map/ppermute | solution.py:269
  36.5 1.0 copy-start.2
  37.6 0.7 copy-start.3
  38.2 37.4 %copy-start.5 = (s32[128,8]{0,1:T(8,128)S(1)}, s32[128,8]{0,1:T(8,128)}, u32[]{:S(2)}) copy-start(s32[128,8]{0,1:T(8,128)} %param.14) | copy-start | bytes 12292
  38.2 41.5 %copy-start.4 = (s32[128,8]{0,1:T(8,128)S(1)}, s32[128,8]{0,1:T(8,128)}, u32[]{:S(2)}) copy-start(s32[128,8]{0,1:T(8,128)} %param.12) | copy-start | bytes 12292
  45.6 14.4 %collective-permute-start.11 = (bf16[64,4096]{1,0:T(8,128)(2,1)S(1)}, bf16[64,4096]{1,0:T(8,128)(2,1)S(1)}, u32[]{:S(2)}, u32[]{:S(2)}) collective-permute-start(bf16[64,4096]{1,0:T(8,128)(2,1)S(1)} %precondition.1.rest_0_), channel_id=1, source_target_pairs={{0,4},{1,5},{4,8},{5,9},{8,12},{9,13},{12,14},{13,15},{14,10},{15,... | collective-permute-start | bytes 1572872 | tf_op jit(solution)/shard_map/ppermute | solution.py:269
  47.3 14.3 %collective-permute-start.15 = (bf16[64,4096]{1,0:T(8,128)(2,1)S(1)}, bf16[64,4096]{1,0:T(8,128)(2,1)S(1)}, u32[]{:S(2)}, u32[]{:S(2)}) collective-permute-start(bf16[64,4096]{1,0:T(8,128)(2,1)S(1)} %precondition.1.rest_0_), channel_id=1, source_target_pairs={{0,2},{1,3},{4,0},{5,1},{8,4},{9,5},{12,8},{13,9},{14,12},{15,13},... | collective-permute-start | bytes 1572872 | tf_op jit(solution)/shard_map/ppermute | solution.py:269
  60.0 13.5 %collective-permute-start.12 = (bf16[64,4096]{1,0:T(8,128)(2,1)S(1)}, bf16[64,4096]{1,0:T(8,128)(2,1)S(1)}, u32[]{:S(2)}, u32[]{:S(2)}) collective-permute-start(bf16[64,4096]{1,0:T(8,128)(2,1)S(1)} %collective-permute-done.11.rest_1_), channel_id=1, source_target_pairs={{0,4},{1,5},{4,8},{5,9},{8,12},{9,13},{12,14},{13,15},{14,10},{15,... | collective-permute-start | bytes 1572872 | tf_op jit(solution)/shard_map/ppermute | solution.py:269
  61.6 13.6 %collective-permute-start.16 = (bf16[64,4096]{1,0:T(8,128)(2,1)S(1)}, bf16[64,4096]{1,0:T(8,128)(2,1)}, u32[]{:S(2)}, u32[]{:S(2)}) collective-permute-start(bf16[64,4096]{1,0:T(8,128)(2,1)S(1)} %collective-permute-done.15.rest_2_), channel_id=1, source_target_pairs={{0,2},{1,3},{4,0},{5,1},{8,4},{9,5},{12,8},{13,9},{14,12},{15,13},... | collective-permute-start | bytes 1572872 | tf_op jit(solution)/shard_map/ppermute | solution.py:269
  73.5 12.7 %collective-permute-start.13 = (bf16[64,4096]{1,0:T(8,128)(2,1)S(1)}, bf16[64,4096]{1,0:T(8,128)(2,1)S(1)}, u32[]{:S(2)}, u32[]{:S(2)}) collective-permute-start(bf16[64,4096]{1,0:T(8,128)(2,1)S(1)} %collective-permute-done.12.rest_0_), channel_id=1, source_target_pairs={{0,4},{1,5},{4,8},{5,9},{8,12},{9,13},{12,14},{13,15},{14,10},{15,... | collective-permute-start | bytes 1572872 | tf_op jit(solution)/shard_map/ppermute | solution.py:269
  75.2 12.8 %collective-permute-start.17 = (bf16[64,4096]{1,0:T(8,128)(2,1)}, bf16[64,4096]{1,0:T(8,128)(2,1)S(1)}, u32[]{:S(2)}, u32[]{:S(2)}) collective-permute-start(bf16[64,4096]{1,0:T(8,128)(2,1)} %collective-permute-done.16.rest_1_), channel_id=1, source_target_pairs={{0,2},{1,3},{4,0},{5,1},{8,4},{9,5},{12,8},{13,9},{14,12},{15,13},... | collective-permute-start | bytes 1572872 | tf_op jit(solution)/shard_map/ppermute | solution.py:269
  75.8 12.7 %collective-permute-start = (s32[1,1024]{1,0:T(1,128)S(1)}, s32[1,1024]{1,0:T(1,128)S(1)}, u32[]{:S(2)}, u32[]{:S(2)}) collective-permute-start(s32[1,1024]{1,0:T(1,128)S(1)} %reshape.69.own_route), channel_id=1, source_target_pairs={{0,1},{1,0},{2,3},{3,2},{4,5},{5,4},{6,7},{7,6},{8,9},{9,8},{10,11... | collective-permute-start | bytes 12296 | tf_op jit(solution)/shard_map/ppermute | solution.py:269
  86.3 26.5 %collective-permute-start.14 = (bf16[32,4096]{1,0:T(8,128)(2,1)S(1)}, bf16[32,4096]{1,0:T(8,128)(2,1)S(1)}, u32[]{:S(2)}, u32[]{:S(2)}) collective-permute-start(bf16[32,4096]{1,0:T(8,128)(2,1)S(1)} %slice.34), channel_id=1, source_target_pairs={{0,4},{1,5},{4,8},{5,9},{8,12},{9,13},{12,14},{13,15},{14,10},{15,... | collective-permute-start | bytes 786440 | tf_op jit(solution)/shard_map/ppermute | solution.py:269
  88.0 24.8 %collective-permute-start.18 = (bf16[32,4096]{1,0:T(8,128)(2,1)S(1)}, bf16[32,4096]{1,0:T(8,128)(2,1)S(1)}, u32[]{:S(2)}, u32[]{:S(2)}) collective-permute-start(bf16[32,4096]{1,0:T(8,128)(2,1)S(1)} %slice.35), channel_id=1, source_target_pairs={{0,2},{1,3},{4,0},{5,1},{8,4},{9,5},{12,8},{13,9},{14,12},{15,13},... | collective-permute-start | bytes 786440 | tf_op jit(solution)/shard_map/ppermute | solution.py:269
  88.7 3.4 %copy-start = (bf16[128,8,4096]{2,1,0:T(8,128)(2,1)S(1)}, bf16[128,8,4096]{2,1,0:T(8,128)(2,1)}, u32[]{:S(2)}) copy-start(bf16[128,8,4096]{2,1,0:T(8,128)(2,1)} %param.13) | copy-start | bytes 25165828
  92.1 10.2 %copy-start.1 = (bf16[128,8,4096]{2,1,0:T(8,128)(2,1)S(1)}, bf16[128,8,4096]{2,1,0:T(8,128)(2,1)}, u32[]{:S(2)}) copy-start(bf16[128,8,4096]{2,1,0:T(8,128)(2,1)} %param.13) | copy-start | bytes 25165828
  122.7 1.3 %collective-permute-start.19 = (f32[64,128]{1,0:T(8,128)S(1)}, f32[64,128]{1,0:T(8,128)S(1)}, u32[]{:S(2)}, u32[]{:S(2)}) collective-permute-start(f32[64,128]{1,0:T(8,128)S(1)} %get-tuple-element.16), channel_id=1, source_target_pairs={{0,1},{1,0},{2,3},{3,2},{4,5},{5,4},{6,7},{7,6},{8,9},{9,8},{10,11... | collective-permute-start | bytes 98312 | tf_op jit(solution)/shard_map/ppermute | solution.py:269

commit v2 on v1

v2 whole, which is shorter than its diff:
```python
import functools

import jax
import jax.numpy as jnp
import numpy as np
from jax import lax
from jax.experimental import pallas as pl
from jax.experimental.pallas import tpu as pltpu
from jax.sharding import PartitionSpec as P

DAMPING = 0.01
F32, BF16 = jnp.float32, jnp.bfloat16
RAW_HOPS = 1
STRIDE = 65
GROUP = 32
TILE = 512
MIB = 2**20


def split(x):
    hi = x.astype(BF16)
    return hi, (x - hi.astype(F32)).astype(BF16)


def swap(x):
    return pltpu.roll(x, 64, 1)


def prepare_kernel(experts, mine, sib, tab_a, tab_at, tab_s, tab_st, scale):
    half = experts // 2
    left64 = lax.broadcasted_iota(jnp.int32, (64, 128), 1) < 64
    left = left64[:32]

    def prepare(e, src, at):
        base = pl.multiple_of(e * 96, 32)

        def twice(f):
            r = swap(f)
            return jnp.concatenate([jnp.where(left, f, r), jnp.where(left, r, f)], 0)

        s = twice(src[pl.ds(base, 32), :])
        a = twice(src[pl.ds(base + 32, 32), :])
        scale[at + e] = 1.0 / (twice(src[pl.ds(base + 64, 32), :]) + DAMPING)
        t = jnp.concatenate([s, a], 0).T[:64]
        r = swap(t)
        st, a_t = jnp.where(left64, t, r), jnp.where(left64, r, t)
        for ref, m in ((tab_s, s), (tab_st, st)):
            hi, lo = split(m)
            ref[at + e, :, :128] = hi
            ref[at + e, :, 128:] = lo
        for ref, m in ((tab_a, a), (tab_at, a_t)):
            for w in (0, 1):
                hi, lo = split(jnp.where(left64 if w == 0 else ~left64, m, 0.0))
                ref[at + e, w, :64] = hi
                ref[at + e, w, 64:] = lo

    def both(e, unused):
        prepare(e, mine, 0)
        prepare(e, sib, half)
        return 0

    lax.fori_loop(0, half, both, 0, unroll=2)


def prepare(mine, sib, experts):
    vm = pl.BlockSpec(memory_space=pltpu.VMEM)
    return pl.pallas_call(
        functools.partial(prepare_kernel, experts),
        out_shape=[
            jax.ShapeDtypeStruct((experts, 2, 128, 128), BF16),
            jax.ShapeDtypeStruct((experts, 2, 128, 128), BF16),
            jax.ShapeDtypeStruct((experts, 64, 256), BF16),
            jax.ShapeDtypeStruct((experts, 64, 256), BF16),
            jax.ShapeDtypeStruct((experts, 64, 128), F32),
        ],
        in_specs=[vm] * 2,
        out_specs=[vm] * 5,
        compiler_params=pltpu.CompilerParams(vmem_limit_bytes=32 * MIB),
        cost_estimate=pl.CostEstimate(flops=2 * 10**9, bytes_accessed=8 * MIB, transcendentals=0),
        name="prepare",
    )(mine, sib)


def precondition_kernel(units, routes, owner, info, tab_a, tab_at, tab_s, tab_st, scale, *rest):
    chunks = len(units)
    experts = owner.shape[0]
    raws, outs = rest[:chunks], rest[chunks : 2 * chunks]
    xs, ys = rest[2 * chunks :]
    left64 = lax.broadcasted_iota(jnp.int32, (64, 128), 1) < 64
    left = left64[:32]

    def pair(tab, e1, e2, three):
        hi = [tab[e1, 0, :64], tab[e2, 1, :64]]
        lo = [tab[e1, 0, 64:], tab[e2, 1, 64:]]
        return jnp.concatenate(hi + (hi if three else []) + lo, 0)

    def cross(tab, e1, e2, x):
        hi, lo = split(x)
        o = jnp.dot(
            jnp.concatenate([tab[e1], tab[e2]], 0),
            jnp.concatenate([hi, lo, hi, lo], 0),
            preferred_element_type=F32,
        )
        return jnp.where(left64, o[:64], o[64:])

    for ch in range(chunks):
        raw, out = raws[ch], outs[ch]
        first = info[experts + units[ch]] * 8
        for c in range(32):
            xs[pl.ds(c * STRIDE, 64), :] = raw[:, c * 128 : (c + 1) * 128].astype(F32)

        def group(b, unused):
            es, g, x = [], [], []
            for i in range(GROUP):
                row = b * GROUP + i
                es.append(info[owner[routes[first + row // 8, row % 8]]])
                g.append(xs[pl.ds(row, 32, stride=STRIDE), :])
            n = GROUP // 2
            ee = [(es[2 * p], es[2 * p + 1]) for p in range(n)]
            for p in range(n):
                g1, g2 = g[2 * p], g[2 * p + 1]
                h = [jnp.where(left, g1, swap(g2)), jnp.where(left, swap(g1), g2)]
                h = jnp.concatenate(h, 0).astype(BF16)
                h = jnp.concatenate([h, h], 1)
                x.append(jnp.dot(h, pair(tab_a, *ee[p], False), preferred_element_type=F32))
            x = [
                cross(tab_st, *ee[p], x[p]) * jnp.where(left64, scale[ee[p][0]], scale[ee[p][1]])
                for p in range(n)
            ]
            x = [cross(tab_s, *ee[p], x[p]) for p in range(n)]
            for p in range(n):
                hi, lo = split(x[p])
                h = jnp.concatenate([hi, lo, hi], 1)
                y = jnp.dot(h, pair(tab_at, *ee[p], True), preferred_element_type=F32)
                top, low = y[:32], y[32:]
                for w, v in enumerate((jnp.where(left, top, swap(low)), jnp.where(left, swap(top), low))):
                    row = b * GROUP + 2 * p + w
                    ys[pl.ds((row % 8) * 8 + row // 8, 32, stride=STRIDE), :] = v
            return 0

        lax.fori_loop(0, 64 // GROUP, group, 0)
        for c in range(32):
            out[:, c * 128 : (c + 1) * 128] = ys[pl.ds(c * STRIDE, 64), :].astype(BF16)


def precondition(routes, owner, info, tables, raws, units):
    chunks = len(raws)
    sm = pl.BlockSpec(memory_space=pltpu.SMEM)
    vm = pl.BlockSpec(memory_space=pltpu.VMEM)
    return pl.pallas_call(
        functools.partial(precondition_kernel, units),
        out_shape=[jax.ShapeDtypeStruct(r.shape, BF16) for r in raws],
        in_specs=[sm] * 3 + [vm] * (5 + chunks),
        out_specs=[vm] * chunks,
        scratch_shapes=[pltpu.VMEM((32 * STRIDE, 128), F32), pltpu.VMEM((32 * STRIDE, 128), F32)],
        compiler_params=pltpu.CompilerParams(vmem_limit_bytes=24 * MIB),
        cost_estimate=pl.CostEstimate(
            flops=10**9 * 3 * chunks, bytes_accessed=10**6 * (7 + chunks), transcendentals=0
        ),
        name="precondition",
    )(routes, owner, info, *tables, *raws)


def products_kernel(units, placed, shapes, experts, info, route, query_route, train, *rest):
    n_in = len(shapes)
    n_old = 0 if placed is None else len(placed)
    parts, old = rest[:n_in], rest[n_in : n_in + n_old]
    out, held, total = rest[n_in + n_old :]
    blocks = sum(shapes) // 64
    train_rows = train.shape[0]
    at = 0
    for part, r in zip(parts, shapes):
        held[at : at + r, :] = part[...]
        at += r

    def tile(i, unused):
        here = pl.ds(pl.multiple_of(i * TILE, TILE), TILE)
        g = lax.dot_general(held[...], train[here, :], (((1,), (1,)), ((), ())), preferred_element_type=F32)
        there = route[:, here]
        for u in range(blocks):
            first = pl.multiple_of(info[experts + units[u]] * 64, 64)
            want = jnp.concatenate([query_route[pl.ds(first, 64), :]] * (TILE // 128), 1)
            hit = jnp.where(want == there, g[u * 64 : (u + 1) * 64], 0.0)
            total[u * 8 : (u + 1) * 8, here] = jnp.sum(hit.reshape(8, 8, TILE), axis=0)
        return 0

    lax.fori_loop(0, train_rows // TILE, tile, 0)
    row = lax.broadcasted_iota(jnp.int32, (train_rows, 128), 0)
    col = lax.broadcasted_iota(jnp.int32, (train_rows, 128), 1)
    fold = (lax.shift_right_logical(row, 3) == col).astype(BF16)
    x = total[...]
    hi = x.astype(BF16)
    left = x - hi.astype(F32)
    mid = left.astype(BF16)
    low = (left - mid.astype(F32)).astype(BF16)
    y = jnp.dot(jnp.concatenate([hi, mid, low], 0), fold, preferred_element_type=F32)
    n = blocks * 8
    y = y[:n] + y[n : 2 * n] + y[2 * n :]
    if placed is None:
        out[...] = y
        return
    todo = [(y, units)] + list(zip(old, placed))
    for values, names in todo:
        for u, name in enumerate(names):
            first = pl.multiple_of(info[experts + name] * 8, 8)
            out[pl.ds(first, 8), :] = values[u * 8 : (u + 1) * 8]


def products(info, experts, route, query_route, train, parts, units, old=None, placed=None, queries=0):
    shapes = [p.shape[0] for p in parts]
    blocks = sum(shapes) // 64
    train_rows, width = train.shape
    sm = pl.BlockSpec(memory_space=pltpu.SMEM)
    vm = pl.BlockSpec(memory_space=pltpu.VMEM)
    old = list(old or [])
    return pl.pallas_call(
        functools.partial(products_kernel, units, placed, shapes, experts),
        out_shape=jax.ShapeDtypeStruct((queries if placed else blocks * 8, 128), F32),
        in_specs=[sm] + [vm] * (3 + len(parts) + len(old)),
        out_specs=vm,
        scratch_shapes=[pltpu.VMEM((sum(shapes), width), BF16), pltpu.VMEM((blocks * 8, train_rows), F32)],
        compiler_params=pltpu.CompilerParams(vmem_limit_bytes=24 * MIB),
        cost_estimate=pl.CostEstimate(
            flops=4 * 128 * max(2, blocks) * train_rows * width // 2,
            bytes_accessed=2 * train_rows * width,
            transcendentals=0,
        ),
        name="products",
    )(info, route, query_route, train, *parts, *old)


def tables_of(devices, slots):
    chips = devices // 2
    far = chips // 2
    ring = [2 * z for z in range(far)] + [2 * z + 1 for z in reversed(range(far))]
    spot = [ring.index(c) for c in range(chips)]
    rows = []
    for me in range(devices):
        place = []
        for slot in range(devices * slots):
            rel = (spot[slot // slots // 2] - spot[me // 2]) % chips
            order = chips - 1 if rel == far else 2 * (chips - rel) - 1 if rel > far else 2 * rel
            across = (slot // slots) % 2 != me % 2
            place.append((across * chips + order) * slots + slot % slots)
        near = [2 * ring[(spot[me // 2] + d) % chips] + me % 2 for d in range(chips)]
        rows.append(place + near + [d ^ 1 for d in near])
    return ring, np.array(rows, np.int32)


def tie(value, other):
    return lax.optimization_barrier((value, other))[0]


def local(
    query_grads,
    query_routes,
    train_grads,
    train_routes,
    train_counts,
    owner_slot,
    basis_s,
    basis_a,
    eigenvalues,
):
    devices = lax.axis_size("shard")
    me = lax.axis_index("shard")
    experts = owner_slot.shape[0]
    queries, top = query_routes.shape
    width = query_grads.shape[2]
    train_dev = train_grads.shape[0]
    slots = basis_s.shape[0]
    chips = devices // 2
    far = chips // 2
    ring, constants = tables_of(devices, slots)
    info = lax.dynamic_index_in_dim(jnp.asarray(constants), me, 0, keepdims=False)

    def shift(step):
        return [
            (2 * c + k, 2 * ring[(i + step) % chips] + k) for i, c in enumerate(ring) for k in range(2)
        ]

    ahead, back = shift(1), shift(-1)
    across = [(d, d ^ 1) for d in range(devices)]
    send = lambda v, way: lax.ppermute(v, "shard", way)
    near = lambda distance: distance % chips
    other = lambda distance: chips + distance % chips

    raw = query_grads.reshape(-1, width)

    halves = lambda m: jnp.concatenate([m[:, :32], m[:, 32:]], axis=-1)
    pack = jnp.stack([basis_s.reshape(slots, 32, 128), halves(basis_a), halves(eigenvalues)], axis=1)
    pack = pack.reshape(slots * 96, 128)
    got, up, down = [pack], pack, pack
    for _ in range(far - 1):
        up, down = send(up, ahead), send(down, back)
        got += [up, down]
    cut = pack.shape[0] // 2
    got += [send(up[:cut], ahead), send(down[cut:], back)]
    mine = jnp.concatenate(got, axis=0)
    tables = prepare(mine, send(mine, across), experts)

    live = jnp.arange(train_dev, dtype=jnp.int32) < train_counts[0]
    route = jnp.where(live[:, None], train_routes, -1).reshape(1, train_dev * top)
    train = train_grads.reshape(train_dev * top, width)
    query_route = query_routes.reshape(devices, 8, top).transpose(0, 2, 1).reshape(queries * top, 1)
    query_route = jnp.broadcast_to(query_route, (queries * top, 128))

    pre = lambda raws, names: precondition(query_routes, owner_slot, info, tables, raws, names)
    multiply = lambda parts, names, **more: products(
        info, experts, route, query_route, train, parts, names, **more
    )
    if RAW_HOPS:
        up, down = send(raw, ahead), send(raw, back)
        up, down = pre([up, down], [near(-1), near(1)])
        held, names = [up, down], [near(-1), near(1)]
    else:
        (own,) = pre([raw], [near(0)])
        up, down = own, own
        held, names = [own], [near(0)]
    done, placed = [], []
    for step in range(1 + RAW_HOPS, far + 1):
        if done:
            up, down = tie((up, down), done[-1])
        if step == far:
            up, down = send(up[:32], ahead), send(down[32:], back)
        else:
            up, down = send(up, ahead), send(down, back)
        if RAW_HOPS and step == 2:
            (own,) = pre([raw], [near(0)])
            held, names = held + [own], names + [near(0)]
        parts = held + [send(v, across) for v in held]
        names = names + [n + chips for n in names]
        done.append(multiply(parts, names))
        placed.append(names)
        held, names = [up, down], [near(-step), near(step)]
    last = jnp.concatenate([up, down], axis=0)
    return multiply(
        [last, send(last, across)], [near(far), other(far)], old=done, placed=placed, queries=queries
    )


def solution(mesh):
    placed = (
        P(("groups", "shard"), None, None),
        P("groups", None),
        P(("groups", "shard"), None, None),
        P(("groups", "shard"), None),
        P(("groups", "shard")),
        P(),
        P("shard", None, None),
        P("shard", None, None),
        P("shard", None, None),
    )
    return jax.shard_map(
        local, mesh=mesh, in_specs=placed, out_specs=P("groups", "shard"), check_vma=False
    )
```

time: 126 us -> 107 us (0.85)
  between operations: 12.4 us -> 0.91 us
  Pallas kernels: 38 us -> 32.7 us
  local copies, waits for them, and re-layouts: 9.94 us -> 14.5 us
  other arithmetic: 4.37 us -> 0.1 us
  waiting for transfers between devices: 42.3 us -> 39.4 us
  starting transfers between devices: 17.6 us -> 19.2 us
    pallas_call x4 -> x7, Pallas kernels: 38 us -> 32.7 us  [the longest x4 16.9 us: products(): pl.pallas_call(functools.partial(products_kernel, units, placed, shapes,...]
    unnamed x21 -> x30, local copies, waits for them, and re-layouts: 5.94 us -> 10.6 us
    ppermute x20 -> x25, waiting for transfers between devices: 42.3 us -> 39.4 us  [local(): send = lambda v, way: lax.ppermute(v, 'shard', way)]
    reduce_sum x2 -> x0, other arithmetic: 2.78 us -> none  [the longest x1 1.48 us: dev_at(): return 2 * jnp.sum(jnp.where(jnp.arange(chips) == at, rings, 0)) + me % 2]
    ppermute x20 -> x25, starting transfers between devices: 17.6 us -> 19.2 us  [local(): send = lambda v, way: lax.ppermute(v, 'shard', way)]
    add x2 -> x0, other arithmetic: 1.32 us -> none  [the longest x1 1.31 us: local(): rel = (jnp.repeat(spots, 2 * slots) - my_spot + chips) % chips]
  transfers between devices with their start and end apart: 20 -> 25, of which waited for: 9 -> 14; matrix products, arithmetic and copies ran while one was open for 7% -> 1% of each run, Pallas kernels for 23% -> 19%
where the time goes in v2:
time: 107 us
  waiting for transfers between devices  39.4 us (37%)
  Pallas kernels  32.7 us (31%)
  starting transfers between devices  19.2 us (18%)
  local copies, waits for them, and re-layouts  14.5 us (14%)
    ppermute x25, waiting for transfers between devices, local(): send = lambda v, way: lax.ppermute(v, 'shard', way)  39.4 us
    ppermute x25, starting transfers between devices, local(): send = lambda v, way: lax.ppermute(v, 'shard', way)  19.2 us
    pallas_call x4, Pallas kernels, products(): pl.pallas_call(functools.partial(products_kernel, units, placed, shapes,...  16.9 us
    pallas_call x2, Pallas kernels, precondition(): pl.pallas_call(functools.partial(precondition_kernel, units), out_shape=[...  13 us
    unnamed x30, local copies, waits for them, and re-layouts  10.6 us
    pallas_call x1, Pallas kernels, prepare(): pl.pallas_call(functools.partial(prepare_kernel, experts), out_shape=[jax...  2.81 us
  transfers between devices with their start and end apart: 25, of which 14 were waited for; matrix products, arithmetic and copies ran while one was open for 1% of the time, Pallas kernels for 19%

profile of v2, /device:TPU:0, one launch (start us, length us, event | category | flops | bytes accessed | tf_op | source)
XLA Modules:
  0.0 106.8 jit_solution(10034633059146612088)
XLA Ops:
  0.0 0.8 fusion
  0.8 0.8 fusion.1
  1.6 0.9 stack_reshape.3
  2.5 0.1 maximum_bitcast_fusion
  2.7 3.1 %collective-permute-start = (f32[192,128]{1,0:T(8,128)S(1)}, f32[192,128]{1,0:T(8,128)S(1)}, u32[]{:S(2)}, u32[]{:S(2)}) collective-permute-start(f32[192,128]{1,0:T(8,128)S(1)} %bitcast.21), channel_id=1, source_target_pairs={{0,4},{1,5},{4,8},{5,9},{8,12},{9,13},{12,14},{13,15},{14,10},{15,... | collective-permute-start | bytes 294920 | tf_op jit(solution)/shard_map/ppermute | solution.py:284
  5.7 0.0 collective-permute-start.1
  5.8 2.7 %collective-permute-done = f32[192,128]{1,0:T(8,128)S(1)} collective-permute-done((f32[192,128]{1,0:T(8,128)S(1)}, f32[192,128]{1,0:T(8,128)S(1)}, u32[]{:S(2)}, u32[]{:S(2)}) %collective-permute-start) | collective-permute-done | bytes 98336 | tf_op jit(solution)/shard_map/ppermute | solution.py:284
  8.5 1.9 %collective-permute-start.2 = (f32[192,128]{1,0:T(8,128)S(1)}, f32[192,128]{1,0:T(8,128)S(1)}, u32[]{:S(2)}, u32[]{:S(2)}) collective-permute-start(f32[192,128]{1,0:T(8,128)S(1)} %collective-permute-done), channel_id=1, source_target_pairs={{0,4},{1,5},{4,8},{5,9},{8,12},{9,13},{12,14},{13,15},{14,10},{15,... | collective-permute-start | bytes 294920 | tf_op jit(solution)/shard_map/ppermute | solution.py:284
  10.4 0.2 collective-permute-start.3
  10.6 2.5 %collective-permute-done.2 = f32[192,128]{1,0:T(8,128)S(1)} collective-permute-done((f32[192,128]{1,0:T(8,128)S(1)}, f32[192,128]{1,0:T(8,128)S(1)}, u32[]{:S(2)}, u32[]{:S(2)}) %collective-permute-start.2) | collective-permute-done | bytes 98336 | tf_op jit(solution)/shard_map/ppermute | solution.py:284
  13.1 1.9 %collective-permute-start.4 = (f32[192,128]{1,0:T(8,128)S(1)}, f32[192,128]{1,0:T(8,128)S(1)}, u32[]{:S(2)}, u32[]{:S(2)}) collective-permute-start(f32[192,128]{1,0:T(8,128)S(1)} %collective-permute-done.2), channel_id=1, source_target_pairs={{0,4},{1,5},{4,8},{5,9},{8,12},{9,13},{12,14},{13,15},{14,10},{15,... | collective-permute-start | bytes 294920 | tf_op jit(solution)/shard_map/ppermute | solution.py:284
  15.0 0.1 collective-permute-done.3
  15.0 0.1 collective-permute-start.5
  15.2 2.6 %collective-permute-done.4 = f32[192,128]{1,0:T(8,128)S(1)} collective-permute-done((f32[192,128]{1,0:T(8,128)S(1)}, f32[192,128]{1,0:T(8,128)S(1)}, u32[]{:S(2)}, u32[]{:S(2)}) %collective-permute-start.4) | collective-permute-done | bytes 98336 | tf_op jit(solution)/shard_map/ppermute | solution.py:284
  17.8 2.3 %collective-permute-start.6 = (f32[96,128]{1,0:T(8,128)S(1)}, f32[96,128]{1,0:T(8,128)S(1)}, u32[]{:S(2)}, u32[]{:S(2)}) collective-permute-start(f32[96,128]{1,0:T(8,128)S(1)} %slice.32), channel_id=1, source_target_pairs={{0,4},{1,5},{4,8},{5,9},{8,12},{9,13},{12,14},{13,15},{14,10},{15,... | collective-permute-start | bytes 147464 | tf_op jit(solution)/shard_map/ppermute | solution.py:284
  20.1 0.1 collective-permute-done.5
  20.2 0.1 collective-permute-start.7
  20.3 1.8 %collective-permute-done.6 = f32[96,128]{1,0:T(8,128)S(1)} collective-permute-done((f32[96,128]{1,0:T(8,128)S(1)}, f32[96,128]{1,0:T(8,128)S(1)}, u32[]{:S(2)}, u32[]{:S(2)}) %collective-permute-start.6) | collective-permute-done | bytes 49184 | tf_op jit(solution)/shard_map/ppermute | solution.py:284
  22.1 2.1 %collective-permute-done.7 = f32[96,128]{1,0:T(8,128)S(1)} collective-permute-done((f32[96,128]{1,0:T(8,128)S(1)}, f32[96,128]{1,0:T(8,128)S(1)}, u32[]{:S(2)}, u32[]{:S(2)}) %collective-permute-start.7) | collective-permute-done | bytes 49184 | tf_op jit(solution)/shard_map/ppermute | solution.py:284
  24.3 0.0 collective-permute-start.8
  24.3 0.1 collective-permute-start.10
  24.5 1.9 %collective-permute-start.9 = (bf16[64,4096]{1,0:T(8,128)(2,1)S(1)}, bf16[64,4096]{1,0:T(8,128)(2,1)S(1)}, u32[]{:S(2)}, u32[]{:S(2)}) collective-permute-start(bf16[64,4096]{1,0:T(8,128)(2,1)S(1)} %bitcast.19), channel_id=1, source_target_pairs={{0,4},{1,5},{4,8},{5,9},{8,12},{9,13},{12,14},{13,15},{14,10},{15,... | collective-permute-start | bytes 1572872 | tf_op jit(solution)/shard_map/ppermute | solution.py:284
  26.4 0.1 copy.18.routes
  26.5 0.7 dynamic-slice_bitcast_fusion.info
  27.2 0.0 collective-permute-done.8.sib
  27.2 2.8 %prepare.1 = (bf16[32,2,128,128]{3,2,1,0:T(8,128)(2,1)S(1)}, bf16[32,2,128,128]{3,2,1,0:T(8,128)(2,1)S(1)}, bf16[32,64,256]{2,1,0:T(8,128)(2,1)S(1)}, bf16[32,64,256]{2,1,0:T(8,128)(2,1)S(1)}, f32[32,64,128]{2,1,0:T(8,128)S(1)}) custom-call(f32[1536,128]{1,0:T(8,128)S(1)} %constant_dynamic-update-slice_fusion.mine, f32[1536,128]{1,0:T(8,128)S(1)} %collective-permute-done.8.sib), custom_call_target="tpu_custom_call" | custom-call | flops 2000000000 | bytes 8388608 | tf_op jit(solution)/shard_map/prepare/pallas_call | solution.py:67
  30.0 8.6 %collective-permute-done.10.rest_1_ = bf16[64,4096]{1,0:T(8,128)(2,1)S(1)} collective-permute-done((bf16[64,4096]{1,0:T(8,128)(2,1)S(1)}, bf16[64,4096]{1,0:T(8,128)(2,1)S(1)}, u32[]{:S(2)}, u32[]{:S(2)}) %collective-permute-start.10) | collective-permute-done | bytes 524320 | tf_op jit(solution)/shard_map/ppermute | solution.py:284
  38.6 0.8 copy-done.3
  39.4 0.0 collective-permute-done.9.rest_0_
  39.5 0.8 copy-done.5
  40.2 1.0 copy-done.4
  41.3 1.0 copy-done.6
  42.3 7.6 %precondition.2 = (bf16[64,4096]{1,0:T(8,128)(2,1)S(1)}, bf16[64,4096]{1,0:T(8,128)(2,1)S(1)}) custom-call(s32[128,8]{1,0:T(8,128)S(1)} %copy.18.routes, s32[32]{0:T(128)S(1)} %copy-done.7, s32[48]{0:T(128)S(1)} %dynamic-slice_bitcast_fusion.info, bf16[32,2,128,128]{3,2,1,0:T(8,128)(2,1)S(1)} %get-tuple-element.16.tab_a, ...), custom_call_target="tpu_custom_call" | custom-call | flops 6000000000 | bytes 9000000 | tf_op jit(solution)/shard_map/precondition/pallas_call | solution.py:150
  49.9 1.6 %collective-permute-start.11 = (bf16[64,4096]{1,0:T(8,128)(2,1)S(1)}, bf16[64,4096]{1,0:T(8,128)(2,1)S(1)}, u32[]{:S(2)}, u32[]{:S(2)}) collective-permute-start(bf16[64,4096]{1,0:T(8,128)(2,1)S(1)} %get-tuple-element.21.rest_0_), channel_id=1, source_target_pairs={{0,4},{1,5},{4,8},{5,9},{8,12},{9,13},{12,14},{13,15},{14,10},{15,... | collective-permute-start | bytes 1572872 | tf_op jit(solution)/shard_map/ppermute | solution.py:284
  51.6 0.4 collective-permute-start.12
  52.0 5.4 %precondition.3.rest_2_ = bf16[64,4096]{1,0:T(8,128)(2,1)} custom-call(s32[128,8]{1,0:T(8,128)S(1)} %copy.18.routes, s32[32]{0:T(128)S(1)} %copy-done.7, s32[48]{0:T(128)S(1)} %dynamic-slice_bitcast_fusion.info, bf16[32,2,128,128]{3,2,1,0:T(8,128)(2,1)S(1)} %get-tuple-element.16.tab_a, bf16[32,2,128,128]{3,2,1,0:T(8,128)(2,1)S(1)} %get-tuple-element.17.tab_at, ...), custom_call_target="tpu_custom_call" | custom-call | flops 3000000000 | bytes 8000000 | tf_op jit(solution)/shard_map/precondition/pallas_call | solution.py:150
  57.5 0.5 collective-permute-start.13
  58.0 0.0 collective-permute-start.14
  58.0 0.1 reshape.22
  58.1 0.1 broadcast_in_dim.22
  58.9 0.1 copy.15
  59.0 0.1 reshape.21.route
  59.1 4.4 %collective-permute-done.11.rest_0_ = bf16[64,4096]{1,0:T(8,128)(2,1)S(1)} collective-permute-done((bf16[64,4096]{1,0:T(8,128)(2,1)S(1)}, bf16[64,4096]{1,0:T(8,128)(2,1)S(1)}, u32[]{:S(2)}, u32[]{:S(2)}) %collective-permute-start.11) | collective-permute-done | bytes 524320 | tf_op jit(solution)/shard_map/ppermute | solution.py:284
  63.5 1.3 %collective-permute-done.12.rest_1_ = bf16[64,4096]{1,0:T(8,128)(2,1)S(1)} collective-permute-done((bf16[64,4096]{1,0:T(8,128)(2,1)S(1)}, bf16[64,4096]{1,0:T(8,128)(2,1)S(1)}, u32[]{:S(2)}, u32[]{:S(2)}) %collective-permute-start.12) | collective-permute-done | bytes 524320 | tf_op jit(solution)/shard_map/ppermute | solution.py:284
  64.8 0.0 collective-permute-done.13.rest_3_
  64.8 0.0 collective-permute-done.14.rest_4_
  64.8 0.2 broadcast_in_dim.23.query_route
  65.0 0.0 copy-start
  65.0 3.4 %copy-done = bf16[128,8,4096]{2,1,0:T(8,128)(2,1)S(1)} copy-done((bf16[128,8,4096]{2,1,0:T(8,128)(2,1)S(1)}, bf16[128,8,4096]{2,1,0:T(8,128)(2,1)}, u32[]{:S(2)}) %copy-start) | copy-done | bytes 8388632
  68.4 5.5 %products.4.rest_2_ = f32[48,128]{1,0:T(8,128)S(1)} custom-call(s32[48]{0:T(128)S(1)} %dynamic-slice_bitcast_fusion.info, s32[1,1024]{1,0:T(1,128)S(1)} %reshape.21.route, s32[1024,128]{1,0:T(8,128)S(1)} %broadcast_in_dim.23.query_route, bf16[1024,4096]{1,0:T(8,128)(2,1)S(1)} %bitcast.14, bf16[64,4096]{1,0:T(8,128)(2,1)S(1)} %get-tuple-element.21.rest_0_, ...), custom_call_target="tpu_custom_call" | custom-call | flops 6442450944 | bytes 8388608 | tf_op jit(solution)/shard_map/products/pallas_call | solution.py:216
  73.9 1.6 %collective-permute-start.16 = (bf16[64,4096]{1,0:T(8,128)(2,1)S(1)}, bf16[64,4096]{1,0:T(8,128)(2,1)S(1)}, u32[]{:S(2)}, u32[]{:S(2)}) collective-permute-start(bf16[64,4096]{1,0:T(8,128)(2,1)S(1)} %collective-permute-done.11.rest_0_), channel_id=1, source_target_pairs={{0,4},{1,5},{4,8},{5,9},{8,12},{9,13},{12,14},{13,15},{14,10},{15,... | collective-permute-start | bytes 1572872 | tf_op jit(solution)/shard_map/ppermute | solution.py:284
  75.5 0.4 collective-permute-start.17
  76.0 3.4 %copy-done.1 = bf16[128,8,4096]{2,1,0:T(8,128)(2,1)S(1)} copy-done((bf16[128,8,4096]{2,1,0:T(8,128)(2,1)S(1)}, bf16[128,8,4096]{2,1,0:T(8,128)(2,1)}, u32[]{:S(2)}) %copy-start.1) | copy-done | bytes 8388632
  79.4 3.4 %products.5.rest_3_ = f32[32,128]{1,0:T(8,128)S(1)} custom-call(s32[48]{0:T(128)S(1)} %dynamic-slice_bitcast_fusion.info, s32[1,1024]{1,0:T(1,128)S(1)} %reshape.21.route, s32[1024,128]{1,0:T(8,128)S(1)} %broadcast_in_dim.23.query_route, bf16[1024,4096]{1,0:T(8,128)(2,1)S(1)} %bitcast.15, bf16[64,4096]{1,0:T(8,128)(2,1)S(1)} %collective-permute-done.11.rest_0_, ...), custom_call_target="tpu_custom_call" | custom-call | flops 4294967296 | bytes 8388608 | tf_op jit(solution)/shard_map/products/pallas_call | solution.py:216
  82.8 5.5 %collective-permute-done.16.rest_0_ = bf16[64,4096]{1,0:T(8,128)(2,1)S(1)} collective-permute-done((bf16[64,4096]{1,0:T(8,128)(2,1)S(1)}, bf16[64,4096]{1,0:T(8,128)(2,1)S(1)}, u32[]{:S(2)}, u32[]{:S(2)}) %collective-permute-start.16) | collective-permute-done | bytes 524320 | tf_op jit(solution)/shard_map/ppermute | solution.py:284
  88.3 1.3 %collective-permute-done.17.rest_1_ = bf16[64,4096]{1,0:T(8,128)(2,1)S(1)} collective-permute-done((bf16[64,4096]{1,0:T(8,128)(2,1)S(1)}, bf16[64,4096]{1,0:T(8,128)(2,1)S(1)}, u32[]{:S(2)}, u32[]{:S(2)}) %collective-permute-start.17) | collective-permute-done | bytes 524320 | tf_op jit(solution)/shard_map/ppermute | solution.py:284
  89.6 1.6 %collective-permute-start.20 = (bf16[32,4096]{1,0:T(8,128)(2,1)S(1)}, bf16[32,4096]{1,0:T(8,128)(2,1)S(1)}, u32[]{:S(2)}, u32[]{:S(2)}) collective-permute-start(bf16[32,4096]{1,0:T(8,128)(2,1)S(1)} %slice.30), channel_id=1, source_target_pairs={{0,4},{1,5},{4,8},{5,9},{8,12},{9,13},{12,14},{13,15},{14,10},{15,... | collective-permute-start | bytes 786440 | tf_op jit(solution)/shard_map/ppermute | solution.py:284
  91.2 0.7 collective-permute-start.21
  91.9 0.5 collective-permute-start.24
  92.4 4.8 %collective-permute-done.20 = bf16[32,4096]{1,0:T(8,128)(2,1)S(1)} collective-permute-done((bf16[32,4096]{1,0:T(8,128)(2,1)S(1)}, bf16[32,4096]{1,0:T(8,128)(2,1)S(1)}, u32[]{:S(2)}, u32[]{:S(2)}) %collective-permute-start.20) | collective-permute-done | bytes 262176 | tf_op jit(solution)/shard_map/ppermute | solution.py:284
  97.3 1.5 %collective-permute-done.21 = bf16[32,4096]{1,0:T(8,128)(2,1)S(1)} collective-permute-done((bf16[32,4096]{1,0:T(8,128)(2,1)S(1)}, bf16[32,4096]{1,0:T(8,128)(2,1)S(1)}, u32[]{:S(2)}, u32[]{:S(2)}) %collective-permute-start.21) | collective-permute-done | bytes 262176 | tf_op jit(solution)/shard_map/ppermute | solution.py:284
  98.8 0.1 collective-permute-start.22
  98.9 3.5 %products.6.rest_4_ = f32[32,128]{1,0:T(8,128)S(1)} custom-call(s32[48]{0:T(128)S(1)} %dynamic-slice_bitcast_fusion.info, s32[1,1024]{1,0:T(1,128)S(1)} %reshape.21.route, s32[1024,128]{1,0:T(8,128)S(1)} %broadcast_in_dim.23.query_route, bf16[1024,4096]{1,0:T(8,128)(2,1)S(1)} %bitcast.16, bf16[64,4096]{1,0:T(8,128)(2,1)S(1)} %collective-permute-done.16.rest_0_, ...), custom_call_target="tpu_custom_call" | custom-call | flops 4294967296 | bytes 8388608 | tf_op jit(solution)/shard_map/products/pallas_call | solution.py:216
  102.3 4.5 %products.7 = f32[128,128]{1,0:T(8,128)} custom-call(s32[48]{0:T(128)S(1)} %dynamic-slice_bitcast_fusion.info, s32[1,1024]{1,0:T(1,128)S(1)} %reshape.21.route, s32[1024,128]{1,0:T(8,128)S(1)} %broadcast_in_dim.23.query_route, bf16[1024,4096]{1,0:T(8,128)(2,1)S(1)} %bitcast.17, bf16[64,4096]{1,0:T(8,128)(2,1)S(1)} %constant_dynamic-update-slice_fusion.9.rest_0_, ...), custom_call_target="tpu_custom_call" | custom-call | flops 2147483648 | bytes 8388608 | tf_op jit(solution)/shard_map/products/pallas_call | solution.py:216
  (44 shorter events, 0.2 us)
Async XLA Ops:
  0.0 24.3 %copy-start.2 = (bf16[8,8,4096]{2,1,0:T(8,128)(2,1)S(1)}, bf16[8,8,4096]{2,1,0:T(8,128)(2,1)}, u32[]{:S(2)}) copy-start(bf16[8,8,4096]{2,1,0:T(8,128)(2,1)} %param.10) | copy-start | bytes 1572868
  0.0 26.4 %copy-start.8 = (s32[128,8]{0,1:T(8,128)S(1)}, s32[128,8]{0,1:T(8,128)}, u32[]{:S(2)}) copy-start(s32[128,8]{0,1:T(8,128)} %param.11) | copy-start | bytes 12292
  2.7 5.8 %collective-permute-start = (f32[192,128]{1,0:T(8,128)S(1)}, f32[192,128]{1,0:T(8,128)S(1)}, u32[]{:S(2)}, u32[]{:S(2)}) collective-permute-start(f32[192,128]{1,0:T(8,128)S(1)} %bitcast.21), channel_id=1, source_target_pairs={{0,4},{1,5},{4,8},{5,9},{8,12},{9,13},{12,14},{13,15},{14,10},{15,... | collective-permute-start | bytes 294920 | tf_op jit(solution)/shard_map/ppermute | solution.py:284
  5.7 4.6 %collective-permute-start.1 = (f32[192,128]{1,0:T(8,128)S(1)}, f32[192,128]{1,0:T(8,128)S(1)}, u32[]{:S(2)}, u32[]{:S(2)}) collective-permute-start(f32[192,128]{1,0:T(8,128)S(1)} %bitcast.22), channel_id=1, source_target_pairs={{0,2},{1,3},{4,0},{5,1},{8,4},{9,5},{12,8},{13,9},{14,12},{15,13},... | collective-permute-start | bytes 294920 | tf_op jit(solution)/shard_map/ppermute | solution.py:284
  8.5 4.6 %collective-permute-start.2 = (f32[192,128]{1,0:T(8,128)S(1)}, f32[192,128]{1,0:T(8,128)S(1)}, u32[]{:S(2)}, u32[]{:S(2)}) collective-permute-start(f32[192,128]{1,0:T(8,128)S(1)} %collective-permute-done), channel_id=1, source_target_pairs={{0,4},{1,5},{4,8},{5,9},{8,12},{9,13},{12,14},{13,15},{14,10},{15,... | collective-permute-start | bytes 294920 | tf_op jit(solution)/shard_map/ppermute | solution.py:284
  10.4 4.7 %collective-permute-start.3 = (f32[192,128]{1,0:T(8,128)S(1)}, f32[192,128]{1,0:T(8,128)S(1)}, u32[]{:S(2)}, u32[]{:S(2)}) collective-permute-start(f32[192,128]{1,0:T(8,128)S(1)} %collective-permute-done.1), channel_id=1, source_target_pairs={{0,2},{1,3},{4,0},{5,1},{8,4},{9,5},{12,8},{13,9},{14,12},{15,13},... | collective-permute-start | bytes 294920 | tf_op jit(solution)/shard_map/ppermute | solution.py:284
  13.1 4.7 %collective-permute-start.4 = (f32[192,128]{1,0:T(8,128)S(1)}, f32[192,128]{1,0:T(8,128)S(1)}, u32[]{:S(2)}, u32[]{:S(2)}) collective-permute-start(f32[192,128]{1,0:T(8,128)S(1)} %collective-permute-done.2), channel_id=1, source_target_pairs={{0,4},{1,5},{4,8},{5,9},{8,12},{9,13},{12,14},{13,15},{14,10},{15,... | collective-permute-start | bytes 294920 | tf_op jit(solution)/shard_map/ppermute | solution.py:284
  15.0 5.1 %collective-permute-start.5 = (f32[192,128]{1,0:T(8,128)S(1)}, f32[192,128]{1,0:T(8,128)S(1)}, u32[]{:S(2)}, u32[]{:S(2)}) collective-permute-start(f32[192,128]{1,0:T(8,128)S(1)} %collective-permute-done.3), channel_id=1, source_target_pairs={{0,2},{1,3},{4,0},{5,1},{8,4},{9,5},{12,8},{13,9},{14,12},{15,13},... | collective-permute-start | bytes 294920 | tf_op jit(solution)/shard_map/ppermute | solution.py:284
  17.8 4.3 %collective-permute-start.6 = (f32[96,128]{1,0:T(8,128)S(1)}, f32[96,128]{1,0:T(8,128)S(1)}, u32[]{:S(2)}, u32[]{:S(2)}) collective-permute-start(f32[96,128]{1,0:T(8,128)S(1)} %slice.32), channel_id=1, source_target_pairs={{0,4},{1,5},{4,8},{5,9},{8,12},{9,13},{12,14},{13,15},{14,10},{15,... | collective-permute-start | bytes 147464 | tf_op jit(solution)/shard_map/ppermute | solution.py:284
  20.2 4.1 %collective-permute-start.7 = (f32[96,128]{1,0:T(8,128)S(1)}, f32[96,128]{1,0:T(8,128)S(1)}, u32[]{:S(2)}, u32[]{:S(2)}) collective-permute-start(f32[96,128]{1,0:T(8,128)S(1)} %slice.33), channel_id=1, source_target_pairs={{0,2},{1,3},{4,0},{5,1},{8,4},{9,5},{12,8},{13,9},{14,12},{15,13},... | collective-permute-start | bytes 147464 | tf_op jit(solution)/shard_map/ppermute | solution.py:284
  24.3 2.9 %collective-permute-start.8 = (f32[1536,128]{1,0:T(8,128)S(1)}, f32[1536,128]{1,0:T(8,128)S(1)}, u32[]{:S(2)}, u32[]{:S(2)}) collective-permute-start(f32[1536,128]{1,0:T(8,128)S(1)} %constant_dynamic-update-slice_fusion.mine), channel_id=1, source_target_pairs={{0,1},{1,0},{2,3},{3,2},{4,5},{5,4},{6,7},{7,6},{8,9},{9,8},{10,11... | collective-permute-start | bytes 2359304 | tf_op jit(solution)/shard_map/ppermute | solution.py:284
  24.3 14.3 %collective-permute-start.10 = (bf16[64,4096]{1,0:T(8,128)(2,1)S(1)}, bf16[64,4096]{1,0:T(8,128)(2,1)S(1)}, u32[]{:S(2)}, u32[]{:S(2)}) collective-permute-start(bf16[64,4096]{1,0:T(8,128)(2,1)S(1)} %bitcast.18), channel_id=1, source_target_pairs={{0,2},{1,3},{4,0},{5,1},{8,4},{9,5},{12,8},{13,9},{14,12},{15,13},... | collective-permute-start | bytes 1572872 | tf_op jit(solution)/shard_map/ppermute | solution.py:284
  24.5 15.0 %collective-permute-start.9 = (bf16[64,4096]{1,0:T(8,128)(2,1)S(1)}, bf16[64,4096]{1,0:T(8,128)(2,1)S(1)}, u32[]{:S(2)}, u32[]{:S(2)}) collective-permute-start(bf16[64,4096]{1,0:T(8,128)(2,1)S(1)} %bitcast.19), channel_id=1, source_target_pairs={{0,4},{1,5},{4,8},{5,9},{8,12},{9,13},{12,14},{13,15},{14,10},{15,... | collective-permute-start | bytes 1572872 | tf_op jit(solution)/shard_map/ppermute | solution.py:284
  27.2 13.1 %copy-start.7 = (s32[32]{0:T(128)S(1)}, s32[32]{0:T(128)}, u32[]{:S(2)}) copy-start(s32[32]{0:T(128)} %owner.3) | copy-start | bytes 388
  38.6 0.8 copy-start.3
  39.4 0.8 copy-start.5
  40.2 1.0 copy-start.4
  41.3 1.0 copy-start.6
  49.9 13.5 %collective-permute-start.11 = (bf16[64,4096]{1,0:T(8,128)(2,1)S(1)}, bf16[64,4096]{1,0:T(8,128)(2,1)S(1)}, u32[]{:S(2)}, u32[]{:S(2)}) collective-permute-start(bf16[64,4096]{1,0:T(8,128)(2,1)S(1)} %get-tuple-element.21.rest_0_), channel_id=1, source_target_pairs={{0,4},{1,5},{4,8},{5,9},{8,12},{9,13},{12,14},{13,15},{14,10},{15,... | collective-permute-start | bytes 1572872 | tf_op jit(solution)/shard_map/ppermute | solution.py:284
  51.6 7.3 %copy-start.9 = (s32[128,8]{0,1:T(8,128)S(1)}, s32[128,8]{0,1:T(8,128)}, u32[]{:S(2)}) copy-start(s32[128,8]{0,1:T(8,128)} %param.13) | copy-start | bytes 12292
  51.6 13.2 %collective-permute-start.12 = (bf16[64,4096]{1,0:T(8,128)(2,1)S(1)}, bf16[64,4096]{1,0:T(8,128)(2,1)S(1)}, u32[]{:S(2)}, u32[]{:S(2)}) collective-permute-start(bf16[64,4096]{1,0:T(8,128)(2,1)S(1)} %get-tuple-element.22.rest_1_), channel_id=1, source_target_pairs={{0,2},{1,3},{4,0},{5,1},{8,4},{9,5},{12,8},{13,9},{14,12},{15,13},... | collective-permute-start | bytes 1572872 | tf_op jit(solution)/shard_map/ppermute | solution.py:284
  57.4 7.3 %collective-permute-start.15 = (bf16[64,4096]{1,0:T(8,128)(2,1)}, bf16[64,4096]{1,0:T(8,128)(2,1)S(1)}, u32[]{:S(2)}, u32[]{:S(2)}) collective-permute-start(bf16[64,4096]{1,0:T(8,128)(2,1)} %precondition.3.rest_2_), channel_id=1, source_target_pairs={{0,1},{1,0},{2,3},{3,2},{4,5},{5,4},{6,7},{7,6},{8,9},{9,8},{10,11... | collective-permute-start | bytes 1572872 | tf_op jit(solution)/shard_map/ppermute | solution.py:284
  57.5 7.3 %collective-permute-start.13 = (bf16[64,4096]{1,0:T(8,128)(2,1)S(1)}, bf16[64,4096]{1,0:T(8,128)(2,1)}, u32[]{:S(2)}, u32[]{:S(2)}) collective-permute-start(bf16[64,4096]{1,0:T(8,128)(2,1)S(1)} %get-tuple-element.21.rest_0_), channel_id=1, source_target_pairs={{0,1},{1,0},{2,3},{3,2},{4,5},{5,4},{6,7},{7,6},{8,9},{9,8},{10,11... | collective-permute-start | bytes 1572872 | tf_op jit(solution)/shard_map/ppermute | solution.py:284
  58.0 6.8 %collective-permute-start.14 = (bf16[64,4096]{1,0:T(8,128)(2,1)S(1)}, bf16[64,4096]{1,0:T(8,128)(2,1)}, u32[]{:S(2)}, u32[]{:S(2)}) collective-permute-start(bf16[64,4096]{1,0:T(8,128)(2,1)S(1)} %get-tuple-element.22.rest_1_), channel_id=1, source_target_pairs={{0,1},{1,0},{2,3},{3,2},{4,5},{5,4},{6,7},{7,6},{8,9},{9,8},{10,11... | collective-permute-start | bytes 1572872 | tf_op jit(solution)/shard_map/ppermute | solution.py:284
  63.5 12.5 %collective-permute-start.18 = (bf16[64,4096]{1,0:T(8,128)(2,1)S(1)}, bf16[64,4096]{1,0:T(8,128)(2,1)S(1)}, u32[]{:S(2)}, u32[]{:S(2)}) collective-permute-start(bf16[64,4096]{1,0:T(8,128)(2,1)S(1)} %collective-permute-done.11.rest_0_), channel_id=1, source_target_pairs={{0,1},{1,0},{2,3},{3,2},{4,5},{5,4},{6,7},{7,6},{8,9},{9,8},{10,11... | collective-permute-start | bytes 1572872 | tf_op jit(solution)/shard_map/ppermute | solution.py:284
  64.8 11.2 %collective-permute-start.19 = (bf16[64,4096]{1,0:T(8,128)(2,1)S(1)}, bf16[64,4096]{1,0:T(8,128)(2,1)S(1)}, u32[]{:S(2)}, u32[]{:S(2)}) collective-permute-start(bf16[64,4096]{1,0:T(8,128)(2,1)S(1)} %collective-permute-done.12.rest_1_), channel_id=1, source_target_pairs={{0,1},{1,0},{2,3},{3,2},{4,5},{5,4},{6,7},{7,6},{8,9},{9,8},{10,11... | collective-permute-start | bytes 1572872 | tf_op jit(solution)/shard_map/ppermute | solution.py:284
  65.0 3.4 %copy-start = (bf16[128,8,4096]{2,1,0:T(8,128)(2,1)S(1)}, bf16[128,8,4096]{2,1,0:T(8,128)(2,1)}, u32[]{:S(2)}) copy-start(bf16[128,8,4096]{2,1,0:T(8,128)(2,1)} %param.12) | copy-start | bytes 25165828
  73.9 14.4 %collective-permute-start.16 = (bf16[64,4096]{1,0:T(8,128)(2,1)S(1)}, bf16[64,4096]{1,0:T(8,128)(2,1)S(1)}, u32[]{:S(2)}, u32[]{:S(2)}) collective-permute-start(bf16[64,4096]{1,0:T(8,128)(2,1)S(1)} %collective-permute-done.11.rest_0_), channel_id=1, source_target_pairs={{0,4},{1,5},{4,8},{5,9},{8,12},{9,13},{12,14},{13,15},{14,10},{15,... | collective-permute-start | bytes 1572872 | tf_op jit(solution)/shard_map/ppermute | solution.py:284
  75.5 14.0 %collective-permute-start.17 = (bf16[64,4096]{1,0:T(8,128)(2,1)S(1)}, bf16[64,4096]{1,0:T(8,128)(2,1)S(1)}, u32[]{:S(2)}, u32[]{:S(2)}) collective-permute-start(bf16[64,4096]{1,0:T(8,128)(2,1)S(1)} %collective-permute-done.12.rest_1_), channel_id=1, source_target_pairs={{0,2},{1,3},{4,0},{5,1},{8,4},{9,5},{12,8},{13,9},{14,12},{15,13},... | collective-permute-start | bytes 1572872 | tf_op jit(solution)/shard_map/ppermute | solution.py:284
  76.0 3.4 %copy-start.1 = (bf16[128,8,4096]{2,1,0:T(8,128)(2,1)S(1)}, bf16[128,8,4096]{2,1,0:T(8,128)(2,1)}, u32[]{:S(2)}) copy-start(bf16[128,8,4096]{2,1,0:T(8,128)(2,1)} %param.12) | copy-start | bytes 25165828
  89.6 7.7 %collective-permute-start.20 = (bf16[32,4096]{1,0:T(8,128)(2,1)S(1)}, bf16[32,4096]{1,0:T(8,128)(2,1)S(1)}, u32[]{:S(2)}, u32[]{:S(2)}) collective-permute-start(bf16[32,4096]{1,0:T(8,128)(2,1)S(1)} %slice.30), channel_id=1, source_target_pairs={{0,4},{1,5},{4,8},{5,9},{8,12},{9,13},{12,14},{13,15},{14,10},{15,... | collective-permute-start | bytes 786440 | tf_op jit(solution)/shard_map/ppermute | solution.py:284
  91.2 7.6 %collective-permute-start.21 = (bf16[32,4096]{1,0:T(8,128)(2,1)S(1)}, bf16[32,4096]{1,0:T(8,128)(2,1)S(1)}, u32[]{:S(2)}, u32[]{:S(2)}) collective-permute-start(bf16[32,4096]{1,0:T(8,128)(2,1)S(1)} %slice.31), channel_id=1, source_target_pairs={{0,2},{1,3},{4,0},{5,1},{8,4},{9,5},{12,8},{13,9},{14,12},{15,13},... | collective-permute-start | bytes 786440 | tf_op jit(solution)/shard_map/ppermute | solution.py:284
  91.9 6.9 %collective-permute-start.23 = (bf16[64,4096]{1,0:T(8,128)(2,1)S(1)}, bf16[64,4096]{1,0:T(8,128)(2,1)S(1)}, u32[]{:S(2)}, u32[]{:S(2)}) collective-permute-start(bf16[64,4096]{1,0:T(8,128)(2,1)S(1)} %collective-permute-done.16.rest_0_), channel_id=1, source_target_pairs={{0,1},{1,0},{2,3},{3,2},{4,5},{5,4},{6,7},{7,6},{8,9},{9,8},{10,11... | collective-permute-start | bytes 1572872 | tf_op jit(solution)/shard_map/ppermute | solution.py:284
  91.9 6.9 %collective-permute-start.24 = (bf16[64,4096]{1,0:T(8,128)(2,1)S(1)}, bf16[64,4096]{1,0:T(8,128)(2,1)S(1)}, u32[]{:S(2)}, u32[]{:S(2)}) collective-permute-start(bf16[64,4096]{1,0:T(8,128)(2,1)S(1)} %collective-permute-done.17.rest_1_), channel_id=1, source_target_pairs={{0,1},{1,0},{2,3},{3,2},{4,5},{5,4},{6,7},{7,6},{8,9},{9,8},{10,11... | collective-permute-start | bytes 1572872 | tf_op jit(solution)/shard_map/ppermute | solution.py:284
  98.8 3.6 %collective-permute-start.22 = (bf16[64,4096]{1,0:T(8,128)(2,1)S(1)}, bf16[64,4096]{1,0:T(8,128)(2,1)S(1)}, u32[]{:S(2)}, u32[]{:S(2)}) collective-permute-start(bf16[64,4096]{1,0:T(8,128)(2,1)S(1)} %constant_dynamic-update-slice_fusion.9.rest_0_), channel_id=1, source_target_pairs={{0,1},{1,0},{2,3},{3,2},{4,5},{5,4},{6,7},{7,6},{8,9},{9,8},{10,11... | collective-permute-start | bytes 1572872 | tf_op jit(solution)/shard_map/ppermute | solution.py:284

commit v3 on v2

--- a/solution.py
+++ b/solution.py
@@ -10,7 +10,7 @@
 
 DAMPING = 0.01
 F32, BF16 = jnp.float32, jnp.bfloat16
-RAW_HOPS = 1
+RAW_HOPS = 2
 STRIDE = 65
 GROUP = 32
 TILE = 512
@@ -29,37 +29,39 @@
 def prepare_kernel(experts, mine, sib, tab_a, tab_at, tab_s, tab_st, scale):
     half = experts // 2
     left64 = lax.broadcasted_iota(jnp.int32, (64, 128), 1) < 64
-    left = left64[:32]
 
     def prepare(e, src, at):
-        base = pl.multiple_of(e * 96, 32)
+        base = pl.multiple_of(e * 96, 96)
+        f_s = jnp.concatenate([src[pl.ds(base + h, 32, stride=2), :] for h in (0, 1)], 0)
+        f_a = src[pl.ds(base + 64, 64), :]
+        f_l = src[pl.ds(base + 128, 64), :]
 
         def twice(f):
             r = swap(f)
-            return jnp.concatenate([jnp.where(left, f, r), jnp.where(left, r, f)], 0)
-
-        s = twice(src[pl.ds(base, 32), :])
-        a = twice(src[pl.ds(base + 32, 32), :])
-        scale[at + e] = 1.0 / (twice(src[pl.ds(base + 64, 32), :]) + DAMPING)
-        t = jnp.concatenate([s, a], 0).T[:64]
-        r = swap(t)
-        st, a_t = jnp.where(left64, t, r), jnp.where(left64, r, t)
-        for ref, m in ((tab_s, s), (tab_st, st)):
-            hi, lo = split(m)
-            ref[at + e, :, :128] = hi
-            ref[at + e, :, 128:] = lo
-        for ref, m in ((tab_a, a), (tab_at, a_t)):
-            for w in (0, 1):
-                hi, lo = split(jnp.where(left64 if w == 0 else ~left64, m, 0.0))
-                ref[at + e, w, :64] = hi
-                ref[at + e, w, 64:] = lo
+            return jnp.where(left64, f, r), jnp.where(left64, r, f)
+
+        for w0, (s, a, lam) in enumerate(zip(twice(f_s), twice(f_a), twice(f_l))):
+            to = at + e + w0
+            scale[to] = 1.0 / (lam + DAMPING)
+            t = jnp.concatenate([s, a], 0).T[:64]
+            r = swap(t)
+            st, a_t = jnp.where(left64, t, r), jnp.where(left64, r, t)
+            for ref, m in ((tab_s, s), (tab_st, st)):
+                hi, lo = split(m)
+                ref[to, :, :128] = hi
+                ref[to, :, 128:] = lo
+            for ref, m in ((tab_a, a), (tab_at, a_t)):
+                for w in (0, 1):
+                    hi, lo = split(jnp.where(left64 if w == 0 else ~left64, m, 0.0))
+                    ref[to, w, :64] = hi
+                    ref[to, w, 64:] = lo
 
     def both(e, unused):
-        prepare(e, mine, 0)
-        prepare(e, sib, half)
+        prepare(2 * e, mine, 0)
+        prepare(2 * e, sib, half)
         return 0
 
-    lax.fori_loop(0, half, both, 0, unroll=2)
+    lax.fori_loop(0, half // 2, both, 0)
 
 
 def prepare(mine, sib, experts):
@@ -75,7 +77,7 @@
         ],
         in_specs=[vm] * 2,
         out_specs=[vm] * 5,
-        compiler_params=pltpu.CompilerParams(vmem_limit_bytes=32 * MIB),
+        compiler_params=pltpu.CompilerParams(vmem_limit_bytes=4 * MIB),
         cost_estimate=pl.CostEstimate(flops=2 * 10**9, bytes_accessed=8 * MIB, transcendentals=0),
         name="prepare",
     )(mine, sib)
@@ -153,7 +155,7 @@
         in_specs=[sm] * 3 + [vm] * (5 + chunks),
         out_specs=[vm] * chunks,
         scratch_shapes=[pltpu.VMEM((32 * STRIDE, 128), F32), pltpu.VMEM((32 * STRIDE, 128), F32)],
-        compiler_params=pltpu.CompilerParams(vmem_limit_bytes=24 * MIB),
+        compiler_params=pltpu.CompilerParams(vmem_limit_bytes=8 * MIB),
         cost_estimate=pl.CostEstimate(
             flops=10**9 * 3 * chunks, bytes_accessed=10**6 * (7 + chunks), transcendentals=0
         ),
@@ -219,7 +221,7 @@
         in_specs=[sm] + [vm] * (3 + len(parts) + len(old)),
         out_specs=vm,
         scratch_shapes=[pltpu.VMEM((sum(shapes), width), BF16), pltpu.VMEM((blocks * 8, train_rows), F32)],
-        compiler_params=pltpu.CompilerParams(vmem_limit_bytes=24 * MIB),
+        compiler_params=pltpu.CompilerParams(vmem_limit_bytes=14 * MIB),
         cost_estimate=pl.CostEstimate(
             flops=4 * 128 * max(2, blocks) * train_rows * width // 2,
             bytes_accessed=2 * train_rows * width,
@@ -287,17 +289,25 @@
 
     raw = query_grads.reshape(-1, width)
 
-    halves = lambda m: jnp.concatenate([m[:, :32], m[:, 32:]], axis=-1)
-    pack = jnp.stack([basis_s.reshape(slots, 32, 128), halves(basis_a), halves(eigenvalues)], axis=1)
-    pack = pack.reshape(slots * 96, 128)
+    raws = []
+    for _ in range(RAW_HOPS):
+        u, d = raws[-1] if raws else (raw, raw)
+        raws.append((send(u, ahead), send(d, back)))
+    pairs = lambda m: jnp.concatenate([m[0::2], m[1::2]], axis=-1)
+    pack = jnp.stack([pairs(basis_s), pairs(basis_a), pairs(eigenvalues)], axis=1).reshape(slots * 96, 128)
     got, up, down = [pack], pack, pack
     for _ in range(far - 1):
         up, down = send(up, ahead), send(down, back)
         got += [up, down]
+    if raws:
+        up, down = tie((up, down), raws[0])
     cut = pack.shape[0] // 2
     got += [send(up[:cut], ahead), send(down[cut:], back)]
     mine = jnp.concatenate(got, axis=0)
-    tables = prepare(mine, send(mine, across), experts)
+    sib = send(mine, across)
+    if len(raws) > 1:
+        sib = tie(sib, raws[-1])
+    tables = prepare(mine, sib, experts)
 
     live = jnp.arange(train_dev, dtype=jnp.int32) < train_counts[0]
     route = jnp.where(live[:, None], train_routes, -1).reshape(1, train_dev * top)
@@ -309,14 +319,17 @@
     multiply = lambda parts, names, **more: products(
         info, experts, route, query_route, train, parts, names, **more
     )
+    held, names, parts = [], [], [raw]
     if RAW_HOPS:
-        up, down = send(raw, ahead), send(raw, back)
-        up, down = pre([up, down], [near(-1), near(1)])
-        held, names = [up, down], [near(-1), near(1)]
-    else:
-        (own,) = pre([raw], [near(0)])
-        up, down = own, own
-        held, names = [own], [near(0)]
+        up, down = pre(list(raws[-1]), [near(-RAW_HOPS), near(RAW_HOPS)])
+        held, names = [up, down], [near(-RAW_HOPS), near(RAW_HOPS)]
+        parts = [raw] + [v for pair in raws[:-1] for v in pair]
+        parts = list(tie(tuple(parts), up))
+    kinds = [near(0)] + [near(d) for h in range(1, RAW_HOPS) for d in (-h, h)]
+    rest = pre(parts, kinds)
+    if not RAW_HOPS:
+        up, down = rest[0], rest[0]
+    held, names = held + list(rest), names + kinds
     done, placed = [], []
     for step in range(1 + RAW_HOPS, far + 1):
         if done:
@@ -325,9 +338,6 @@
             up, down = send(up[:32], ahead), send(down[32:], back)
         else:
             up, down = send(up, ahead), send(down, back)
-        if RAW_HOPS and step == 2:
-            (own,) = pre([raw], [near(0)])
-            held, names = held + [own], names + [near(0)]
         parts = held + [send(v, across) for v in held]
         names = names + [n + chips for n in names]
         done.append(multiply(parts, names))

time: 107 us -> 110 us (1.028)
  Pallas kernels: 32.7 us -> 38.1 us
  local copies, waits for them, and re-layouts: 14.5 us -> 11.7 us
    pallas_call x2, Pallas kernels: 13 us -> 19.3 us  [precondition(): pl.pallas_call(functools.partial(precondition_kernel, units), out_shape=[...]
    unnamed x30 -> x26, local copies, waits for them, and re-layouts: 10.6 us -> 7.99 us
    pallas_call x4 -> x3, Pallas kernels: 16.9 us -> 16.1 us  [products(): pl.pallas_call(functools.partial(products_kernel, units, placed, shapes,...]
    slice x2 -> x3, local copies, waits for them, and re-layouts: 1.62 us -> 2.35 us  [local(): pairs = lambda m: jnp.concatenate([m[0::2], m[1::2]], axis=-1)]
  transfers between devices with their start and end apart: 25 -> 25, of which waited for: 14 -> 12; matrix products, arithmetic and copies ran while one was open for 1% -> 1% of each run, Pallas kernels for 19% -> 11%
where the time goes in v3:
time: 110 us; the launch traced here: 109 us
  waiting for transfers between devices  38.9 us (35%)
  Pallas kernels  38.1 us (35%)
  starting transfers between devices  19.2 us (17%)
  local copies, waits for them, and re-layouts  11.7 us (11%)
    ppermute x25, waiting for transfers between devices, local(): send = lambda v, way: lax.ppermute(v, 'shard', way)  38.9 us
    pallas_call x2, Pallas kernels, precondition(): pl.pallas_call(functools.partial(precondition_kernel, units), out_shape=[...  19.3 us
    ppermute x25, starting transfers between devices, local(): send = lambda v, way: lax.ppermute(v, 'shard', way)  19.2 us
    pallas_call x3, Pallas kernels, products(): pl.pallas_call(functools.partial(products_kernel, units, placed, shapes,...  16.1 us
    unnamed x26, local copies, waits for them, and re-layouts  7.99 us
    pallas_call x1, Pallas kernels, prepare(): pl.pallas_call(functools.partial(prepare_kernel, experts), out_shape=[jax...  2.73 us
    slice x3, local copies, waits for them, and re-layouts, local(): pairs = lambda m: jnp.concatenate([m[0::2], m[1::2]], axis=-1)  2.35 us
  transfers between devices with their start and end apart: 25, of which 12 were waited for; matrix products, arithmetic and copies ran while one was open for 1% of the time, Pallas kernels for 11%

profile of v3, /device:TPU:0, one launch (start us, length us, event | category | flops | bytes accessed | tf_op | source)
XLA Modules:
  0.0 109.0 jit_solution(12815419877154341620)
XLA Ops:
  0.0 0.8 fusion
  0.8 0.8 fusion.1
  1.6 0.8 fusion.2
  2.4 0.1 maximum_bitcast_fusion.2
  2.4 0.1 maximum_bitcast_fusion
  2.5 3.0 %collective-permute-start.1 = (f32[192,128]{1,0:T(8,128)S(1)}, f32[192,128]{1,0:T(8,128)S(1)}, u32[]{:S(2)}, u32[]{:S(2)}) collective-permute-start(f32[192,128]{1,0:T(8,128)S(1)} %bitcast.22), channel_id=1, source_target_pairs={{0,2},{1,3},{4,0},{5,1},{8,4},{9,5},{12,8},{13,9},{14,12},{15,13},... | collective-permute-start | bytes 294920 | tf_op jit(solution)/shard_map/ppermute | solution.py:286
  5.6 0.1 collective-permute-start
  5.7 1.9 %collective-permute-start.7 = (bf16[64,4096]{1,0:T(8,128)(2,1)}, bf16[64,4096]{1,0:T(8,128)(2,1)S(1)}, u32[]{:S(2)}, u32[]{:S(2)}) collective-permute-start(bf16[64,4096]{1,0:T(8,128)(2,1)} %bitcast.19), channel_id=1, source_target_pairs={{0,2},{1,3},{4,0},{5,1},{8,4},{9,5},{12,8},{13,9},{14,12},{15,13},... | collective-permute-start | bytes 1572872 | tf_op jit(solution)/shard_map/ppermute | solution.py:286
  7.6 0.1 collective-permute-start.6
  7.7 1.1 collective-permute-done.1
  8.8 2.0 %collective-permute-start.3 = (f32[192,128]{1,0:T(8,128)S(1)}, f32[192,128]{1,0:T(8,128)S(1)}, u32[]{:S(2)}, u32[]{:S(2)}) collective-permute-start(f32[192,128]{1,0:T(8,128)S(1)} %collective-permute-done.1), channel_id=1, source_target_pairs={{0,2},{1,3},{4,0},{5,1},{8,4},{9,5},{12,8},{13,9},{14,12},{15,13},... | collective-permute-start | bytes 294920 | tf_op jit(solution)/shard_map/ppermute | solution.py:286
  10.8 0.2 collective-permute-done
  11.0 10.8 %collective-permute-done.3 = f32[192,128]{1,0:T(8,128)S(1)} collective-permute-done((f32[192,128]{1,0:T(8,128)S(1)}, f32[192,128]{1,0:T(8,128)S(1)}, u32[]{:S(2)}, u32[]{:S(2)}) %collective-permute-start.3) | collective-permute-done | bytes 98336 | tf_op jit(solution)/shard_map/ppermute | solution.py:286
  21.8 1.8 %collective-permute-start.5 = (f32[192,128]{1,0:T(8,128)S(1)}, f32[192,128]{1,0:T(8,128)S(1)}, u32[]{:S(2)}, u32[]{:S(2)}) collective-permute-start(f32[192,128]{1,0:T(8,128)S(1)} %collective-permute-done.3), channel_id=1, source_target_pairs={{0,2},{1,3},{4,0},{5,1},{8,4},{9,5},{12,8},{13,9},{14,12},{15,13},... | collective-permute-start | bytes 294920 | tf_op jit(solution)/shard_map/ppermute | solution.py:286
  23.5 0.0 collective-permute-done.2
  23.5 0.3 collective-permute-start.4
  23.8 4.3 %collective-permute-done.4 = f32[192,128]{1,0:T(8,128)S(1)} collective-permute-done((f32[192,128]{1,0:T(8,128)S(1)}, f32[192,128]{1,0:T(8,128)S(1)}, u32[]{:S(2)}, u32[]{:S(2)}) %collective-permute-start.4) | collective-permute-done | bytes 98336 | tf_op jit(solution)/shard_map/ppermute | solution.py:286
  28.2 0.0 collective-permute-done.5
  28.2 0.0 collective-permute-done.6.rest_1_
  28.2 0.3 collective-permute-start.8
  28.5 1.8 %collective-permute-start.9 = (f32[96,128]{1,0:T(8,128)S(1)}, f32[96,128]{1,0:T(8,128)S(1)}, u32[]{:S(2)}, u32[]{:S(2)}) collective-permute-start(f32[96,128]{1,0:T(8,128)S(1)} %slice.43), channel_id=1, source_target_pairs={{0,2},{1,3},{4,0},{5,1},{8,4},{9,5},{12,8},{13,9},{14,12},{15,13},... | collective-permute-start | bytes 147464 | tf_op jit(solution)/shard_map/ppermute | solution.py:286
  30.4 2.0 %collective-permute-done.8 = f32[96,128]{1,0:T(8,128)S(1)} collective-permute-done((f32[96,128]{1,0:T(8,128)S(1)}, f32[96,128]{1,0:T(8,128)S(1)}, u32[]{:S(2)}, u32[]{:S(2)}) %collective-permute-start.8) | collective-permute-done | bytes 49184 | tf_op jit(solution)/shard_map/ppermute | solution.py:286
  32.3 0.3 collective-permute-done.9
  32.7 0.0 collective-permute-start.10
  32.7 1.8 %collective-permute-start.12 = (bf16[64,4096]{1,0:T(8,128)(2,1)S(1)}, bf16[64,4096]{1,0:T(8,128)(2,1)S(1)}, u32[]{:S(2)}, u32[]{:S(2)}) collective-permute-start(bf16[64,4096]{1,0:T(8,128)(2,1)S(1)} %collective-permute-done.7.rest_2_), channel_id=1, source_target_pairs={{0,2},{1,3},{4,0},{5,1},{8,4},{9,5},{12,8},{13,9},{14,12},{15,13},... | collective-permute-start | bytes 1572872 | tf_op jit(solution)/shard_map/ppermute | solution.py:286
  34.5 0.3 collective-permute-start.11
  34.8 0.1 copy.16.routes
  34.9 0.7 dynamic-slice_bitcast_fusion.info
  35.6 11.5 %collective-permute-done.12.rest_1_ = bf16[64,4096]{1,0:T(8,128)(2,1)S(1)} collective-permute-done((bf16[64,4096]{1,0:T(8,128)(2,1)S(1)}, bf16[64,4096]{1,0:T(8,128)(2,1)S(1)}, u32[]{:S(2)}, u32[]{:S(2)}) %collective-permute-start.12) | collective-permute-done | bytes 524320 | tf_op jit(solution)/shard_map/ppermute | solution.py:286
  47.1 1.5 %collective-permute-done.11.rest_0_ = bf16[64,4096]{1,0:T(8,128)(2,1)} collective-permute-done((bf16[64,4096]{1,0:T(8,128)(2,1)S(1)}, bf16[64,4096]{1,0:T(8,128)(2,1)}, u32[]{:S(2)}, u32[]{:S(2)}) %collective-permute-start.11) | collective-permute-done | bytes 524320 | tf_op jit(solution)/shard_map/ppermute | solution.py:286
  48.6 0.0 collective-permute-done.10.sib
  48.6 2.7 %prepare.1 = (bf16[32,2,128,128]{3,2,1,0:T(8,128)(2,1)S(1)}, bf16[32,2,128,128]{3,2,1,0:T(8,128)(2,1)S(1)}, bf16[32,64,256]{2,1,0:T(8,128)(2,1)S(1)}, bf16[32,64,256]{2,1,0:T(8,128)(2,1)S(1)}, f32[32,64,128]{2,1,0:T(8,128)S(1)}) custom-call(f32[1536,128]{1,0:T(8,128)S(1)} %constant_dynamic-update-slice_fusion.mine, f32[1536,128]{1,0:T(8,128)S(1)} %collective-permute-done.10.sib), custom_call_target="tpu_custom_call" | custom-call | flops 2000000000 | bytes 8388608 | tf_op jit(solution)/shard_map/prepare/pallas_call | solution.py:69
  51.4 1.0 copy-done.4
  52.4 7.7 %precondition.2 = (bf16[64,4096]{1,0:T(8,128)(2,1)S(1)}, bf16[64,4096]{1,0:T(8,128)(2,1)S(1)}) custom-call(s32[128,8]{1,0:T(8,128)S(1)} %copy.16.routes, s32[32]{0:T(128)S(1)} %copy-done.5, s32[48]{0:T(128)S(1)} %dynamic-slice_bitcast_fusion.info, bf16[32,2,128,128]{3,2,1,0:T(8,128)(2,1)S(1)} %get-tuple-element.26.tab_a, ...), custom_call_target="tpu_custom_call" | custom-call | flops 6000000000 | bytes 9000000 | tf_op jit(solution)/shard_map/precondition/pallas_call | solution.py:152
  60.1 0.0 copy-start.7
  60.1 11.7 %precondition.3 = (bf16[64,4096]{1,0:T(8,128)(2,1)}, bf16[64,4096]{1,0:T(8,128)(2,1)}, bf16[64,4096]{1,0:T(8,128)(2,1)}) custom-call(s32[128,8]{1,0:T(8,128)S(1)} %copy.16.routes, s32[32]{0:T(128)S(1)} %copy-done.5, s32[48]{0:T(128)S(1)} %dynamic-slice_bitcast_fusion.info, bf16[32,2,128,128]{3,2,1,0:T(8,128)(2,1)S(1)} %get-tuple-element.26.tab_a, ...), custom_call_target="tpu_custom_call" | custom-call | flops 8999999488 | bytes 10000000 | tf_op jit(solution)/shard_map/precondition/pallas_call | solution.py:152
  71.8 0.0 collective-permute-start.17
  71.8 0.5 collective-permute-start.18
  72.3 0.0 collective-permute-start.19
  72.3 0.5 collective-permute-start.16
  72.8 0.1 reshape.22
  73.6 0.1 copy.14
  73.7 0.1 reshape.21.route
  73.8 0.1 broadcast_in_dim.22
  73.9 0.0 collective-permute-done.17.rest_7_
  73.9 1.6 %collective-permute-start.14 = (bf16[64,4096]{1,0:T(8,128)(2,1)S(1)}, bf16[64,4096]{1,0:T(8,128)(2,1)S(1)}, u32[]{:S(2)}, u32[]{:S(2)}) collective-permute-start(bf16[64,4096]{1,0:T(8,128)(2,1)S(1)} %get-tuple-element.32.rest_1_), channel_id=1, source_target_pairs={{0,2},{1,3},{4,0},{5,1},{8,4},{9,5},{12,8},{13,9},{14,12},{15,13},... | collective-permute-start | bytes 1572872 | tf_op jit(solution)/shard_map/ppermute | solution.py:286
  75.5 0.0 collective-permute-done.18.rest_8_
  75.5 0.4 collective-permute-start.13
  76.0 0.9 collective-permute-done.19.rest_9_
  76.9 0.2 broadcast_in_dim.23.query_route
  77.1 0.0 copy-start
  77.1 3.4 %copy-done = bf16[128,8,4096]{2,1,0:T(8,128)(2,1)S(1)} copy-done((bf16[128,8,4096]{2,1,0:T(8,128)(2,1)S(1)}, bf16[128,8,4096]{2,1,0:T(8,128)(2,1)}, u32[]{:S(2)}) %copy-start) | copy-done | bytes 8388632
  80.5 8.1 %products.3.rest_2_ = f32[80,128]{1,0:T(8,128)S(1)} custom-call(s32[48]{0:T(128)S(1)} %dynamic-slice_bitcast_fusion.info, s32[1,1024]{1,0:T(1,128)S(1)} %reshape.21.route, s32[1024,128]{1,0:T(8,128)S(1)} %broadcast_in_dim.23.query_route, bf16[1024,4096]{1,0:T(8,128)(2,1)S(1)} %bitcast.16, bf16[64,4096]{1,0:T(8,128)(2,1)S(1)} %get-tuple-element.31.rest_0_, ...), custom_call_target="tpu_custom_call" | custom-call | flops 10737418240 | bytes 8388608 | tf_op jit(solution)/shard_map/products/pallas_call | solution.py:218
  88.6 1.0 collective-permute-done.13.rest_0_
  89.6 0.5 collective-permute-start.20
  90.1 1.6 %collective-permute-start.21 = (bf16[32,4096]{1,0:T(8,128)(2,1)S(1)}, bf16[32,4096]{1,0:T(8,128)(2,1)S(1)}, u32[]{:S(2)}, u32[]{:S(2)}) collective-permute-start(bf16[32,4096]{1,0:T(8,128)(2,1)S(1)} %slice.45), channel_id=1, source_target_pairs={{0,2},{1,3},{4,0},{5,1},{8,4},{9,5},{12,8},{13,9},{14,12},{15,13},... | collective-permute-start | bytes 786440 | tf_op jit(solution)/shard_map/ppermute | solution.py:286
  91.8 0.5 collective-permute-start.23
  92.3 5.0 %collective-permute-done.20 = bf16[32,4096]{1,0:T(8,128)(2,1)S(1)} collective-permute-done((bf16[32,4096]{1,0:T(8,128)(2,1)S(1)}, bf16[32,4096]{1,0:T(8,128)(2,1)S(1)}, u32[]{:S(2)}, u32[]{:S(2)}) %collective-permute-start.20) | collective-permute-done | bytes 262176 | tf_op jit(solution)/shard_map/ppermute | solution.py:286
  97.3 0.2 collective-permute-done.21
  97.5 0.1 collective-permute-start.22
  97.6 0.0 copy-start.1
  97.7 3.4 %copy-done.1 = bf16[128,8,4096]{2,1,0:T(8,128)(2,1)S(1)} copy-done((bf16[128,8,4096]{2,1,0:T(8,128)(2,1)S(1)}, bf16[128,8,4096]{2,1,0:T(8,128)(2,1)}, u32[]{:S(2)}) %copy-start.1) | copy-done | bytes 8388632
  101.0 3.5 %products.4.rest_3_ = f32[32,128]{1,0:T(8,128)S(1)} custom-call(s32[48]{0:T(128)S(1)} %dynamic-slice_bitcast_fusion.info, s32[1,1024]{1,0:T(1,128)S(1)} %reshape.21.route, s32[1024,128]{1,0:T(8,128)S(1)} %broadcast_in_dim.23.query_route, bf16[1024,4096]{1,0:T(8,128)(2,1)S(1)} %bitcast.17, bf16[64,4096]{1,0:T(8,128)(2,1)S(1)} %collective-permute-done.13.rest_0_, ...), custom_call_target="tpu_custom_call" | custom-call | flops 4294967296 | bytes 8388608 | tf_op jit(solution)/shard_map/products/pallas_call | solution.py:218
  104.5 4.5 %products.5 = f32[128,128]{1,0:T(8,128)} custom-call(s32[48]{0:T(128)S(1)} %dynamic-slice_bitcast_fusion.info, s32[1,1024]{1,0:T(1,128)S(1)} %reshape.21.route, s32[1024,128]{1,0:T(8,128)S(1)} %broadcast_in_dim.23.query_route, bf16[1024,4096]{1,0:T(8,128)(2,1)S(1)} %bitcast.18, bf16[64,4096]{1,0:T(8,128)(2,1)S(1)} %constant_dynamic-update-slice_fusion.9.rest_0_, ...), custom_call_target="tpu_custom_call" | custom-call | flops 2147483648 | bytes 8388608 | tf_op jit(solution)/shard_map/products/pallas_call | solution.py:218
  (39 shorter events, 0.2 us)
Async XLA Ops:
  0.0 34.8 %copy-start.6 = (s32[128,8]{0,1:T(8,128)S(1)}, s32[128,8]{0,1:T(8,128)}, u32[]{:S(2)}) copy-start(s32[128,8]{0,1:T(8,128)} %param.11) | copy-start | bytes 12292
  2.5 6.3 %collective-permute-start.1 = (f32[192,128]{1,0:T(8,128)S(1)}, f32[192,128]{1,0:T(8,128)S(1)}, u32[]{:S(2)}, u32[]{:S(2)}) collective-permute-start(f32[192,128]{1,0:T(8,128)S(1)} %bitcast.22), channel_id=1, source_target_pairs={{0,2},{1,3},{4,0},{5,1},{8,4},{9,5},{12,8},{13,9},{14,12},{15,13},... | collective-permute-start | bytes 294920 | tf_op jit(solution)/shard_map/ppermute | solution.py:286
  5.6 5.4 %collective-permute-start = (f32[192,128]{1,0:T(8,128)S(1)}, f32[192,128]{1,0:T(8,128)S(1)}, u32[]{:S(2)}, u32[]{:S(2)}) collective-permute-start(f32[192,128]{1,0:T(8,128)S(1)} %bitcast.23), channel_id=1, source_target_pairs={{0,4},{1,5},{4,8},{5,9},{8,12},{9,13},{12,14},{13,15},{14,10},{15,... | collective-permute-start | bytes 294920 | tf_op jit(solution)/shard_map/ppermute | solution.py:286
  5.7 22.5 %collective-permute-start.7 = (bf16[64,4096]{1,0:T(8,128)(2,1)}, bf16[64,4096]{1,0:T(8,128)(2,1)S(1)}, u32[]{:S(2)}, u32[]{:S(2)}) collective-permute-start(bf16[64,4096]{1,0:T(8,128)(2,1)} %bitcast.19), channel_id=1, source_target_pairs={{0,2},{1,3},{4,0},{5,1},{8,4},{9,5},{12,8},{13,9},{14,12},{15,13},... | collective-permute-start | bytes 1572872 | tf_op jit(solution)/shard_map/ppermute | solution.py:286
  7.6 20.6 %collective-permute-start.6 = (bf16[64,4096]{1,0:T(8,128)(2,1)}, bf16[64,4096]{1,0:T(8,128)(2,1)S(1)}, u32[]{:S(2)}, u32[]{:S(2)}) collective-permute-start(bf16[64,4096]{1,0:T(8,128)(2,1)} %bitcast.20), channel_id=1, source_target_pairs={{0,4},{1,5},{4,8},{5,9},{8,12},{9,13},{12,14},{13,15},{14,10},{15,... | collective-permute-start | bytes 1572872 | tf_op jit(solution)/shard_map/ppermute | solution.py:286
  8.8 13.0 %collective-permute-start.3 = (f32[192,128]{1,0:T(8,128)S(1)}, f32[192,128]{1,0:T(8,128)S(1)}, u32[]{:S(2)}, u32[]{:S(2)}) collective-permute-start(f32[192,128]{1,0:T(8,128)S(1)} %collective-permute-done.1), channel_id=1, source_target_pairs={{0,2},{1,3},{4,0},{5,1},{8,4},{9,5},{12,8},{13,9},{14,12},{15,13},... | collective-permute-start | bytes 294920 | tf_op jit(solution)/shard_map/ppermute | solution.py:286
  11.0 12.6 %collective-permute-start.2 = (f32[192,128]{1,0:T(8,128)S(1)}, f32[192,128]{1,0:T(8,128)S(1)}, u32[]{:S(2)}, u32[]{:S(2)}) collective-permute-start(f32[192,128]{1,0:T(8,128)S(1)} %collective-permute-done), channel_id=1, source_target_pairs={{0,4},{1,5},{4,8},{5,9},{8,12},{9,13},{12,14},{13,15},{14,10},{15,... | collective-permute-start | bytes 294920 | tf_op jit(solution)/shard_map/ppermute | solution.py:286
  21.8 6.4 %collective-permute-start.5 = (f32[192,128]{1,0:T(8,128)S(1)}, f32[192,128]{1,0:T(8,128)S(1)}, u32[]{:S(2)}, u32[]{:S(2)}) collective-permute-start(f32[192,128]{1,0:T(8,128)S(1)} %collective-permute-done.3), channel_id=1, source_target_pairs={{0,2},{1,3},{4,0},{5,1},{8,4},{9,5},{12,8},{13,9},{14,12},{15,13},... | collective-permute-start | bytes 294920 | tf_op jit(solution)/shard_map/ppermute | solution.py:286
  23.5 4.6 %collective-permute-start.4 = (f32[192,128]{1,0:T(8,128)S(1)}, f32[192,128]{1,0:T(8,128)S(1)}, u32[]{:S(2)}, u32[]{:S(2)}) collective-permute-start(f32[192,128]{1,0:T(8,128)S(1)} %collective-permute-done.2), channel_id=1, source_target_pairs={{0,4},{1,5},{4,8},{5,9},{8,12},{9,13},{12,14},{13,15},{14,10},{15,... | collective-permute-start | bytes 294920 | tf_op jit(solution)/shard_map/ppermute | solution.py:286
  28.2 4.1 %collective-permute-start.8 = (f32[96,128]{1,0:T(8,128)S(1)}, f32[96,128]{1,0:T(8,128)S(1)}, u32[]{:S(2)}, u32[]{:S(2)}) collective-permute-start(f32[96,128]{1,0:T(8,128)S(1)} %slice.42), channel_id=1, source_target_pairs={{0,4},{1,5},{4,8},{5,9},{8,12},{9,13},{12,14},{13,15},{14,10},{15,... | collective-permute-start | bytes 147464 | tf_op jit(solution)/shard_map/ppermute | solution.py:286
  28.5 4.1 %collective-permute-start.9 = (f32[96,128]{1,0:T(8,128)S(1)}, f32[96,128]{1,0:T(8,128)S(1)}, u32[]{:S(2)}, u32[]{:S(2)}) collective-permute-start(f32[96,128]{1,0:T(8,128)S(1)} %slice.43), channel_id=1, source_target_pairs={{0,2},{1,3},{4,0},{5,1},{8,4},{9,5},{12,8},{13,9},{14,12},{15,13},... | collective-permute-start | bytes 147464 | tf_op jit(solution)/shard_map/ppermute | solution.py:286
  32.7 15.9 %collective-permute-start.10 = (f32[1536,128]{1,0:T(8,128)S(1)}, f32[1536,128]{1,0:T(8,128)S(1)}, u32[]{:S(2)}, u32[]{:S(2)}) collective-permute-start(f32[1536,128]{1,0:T(8,128)S(1)} %constant_dynamic-update-slice_fusion.mine), channel_id=1, source_target_pairs={{0,1},{1,0},{2,3},{3,2},{4,5},{5,4},{6,7},{7,6},{8,9},{9,8},{10,11... | collective-permute-start | bytes 2359304 | tf_op jit(solution)/shard_map/ppermute | solution.py:286
  32.7 14.4 %collective-permute-start.12 = (bf16[64,4096]{1,0:T(8,128)(2,1)S(1)}, bf16[64,4096]{1,0:T(8,128)(2,1)S(1)}, u32[]{:S(2)}, u32[]{:S(2)}) collective-permute-start(bf16[64,4096]{1,0:T(8,128)(2,1)S(1)} %collective-permute-done.7.rest_2_), channel_id=1, source_target_pairs={{0,2},{1,3},{4,0},{5,1},{8,4},{9,5},{12,8},{13,9},{14,12},{15,13},... | collective-permute-start | bytes 1572872 | tf_op jit(solution)/shard_map/ppermute | solution.py:286
  34.5 14.1 %collective-permute-start.11 = (bf16[64,4096]{1,0:T(8,128)(2,1)S(1)}, bf16[64,4096]{1,0:T(8,128)(2,1)}, u32[]{:S(2)}, u32[]{:S(2)}) collective-permute-start(bf16[64,4096]{1,0:T(8,128)(2,1)S(1)} %collective-permute-done.6.rest_1_), channel_id=1, source_target_pairs={{0,4},{1,5},{4,8},{5,9},{8,12},{9,13},{12,14},{13,15},{14,10},{15,... | collective-permute-start | bytes 1572872 | tf_op jit(solution)/shard_map/ppermute | solution.py:286
  35.6 15.8 %copy-start.5 = (s32[32]{0:T(128)S(1)}, s32[32]{0:T(128)}, u32[]{:S(2)}) copy-start(s32[32]{0:T(128)} %owner.3) | copy-start | bytes 388
  47.1 4.3 %copy-start.3 = (bf16[64,4096]{1,0:T(8,128)(2,1)}, bf16[64,4096]{1,0:T(8,128)(2,1)S(1)}, u32[]{:S(2)}) copy-start(bf16[64,4096]{1,0:T(8,128)(2,1)S(1)} %collective-permute-done.12.rest_1_) | copy-start | bytes 1572868
  51.4 1.0 copy-start.4
  52.4 7.7 %copy-start.2 = (bf16[8,8,4096]{2,1,0:T(8,128)(2,1)S(1)}, bf16[8,8,4096]{2,1,0:T(8,128)(2,1)}, u32[]{:S(2)}) copy-start(bf16[8,8,4096]{2,1,0:T(8,128)(2,1)} %param.10) | copy-start | bytes 1572868
  60.1 13.4 %copy-start.7 = (s32[128,8]{0,1:T(8,128)S(1)}, s32[128,8]{0,1:T(8,128)}, u32[]{:S(2)}) copy-start(s32[128,8]{0,1:T(8,128)} %param.13) | copy-start | bytes 12292
  71.8 2.1 %collective-permute-start.17 = (bf16[64,4096]{1,0:T(8,128)(2,1)}, bf16[64,4096]{1,0:T(8,128)(2,1)S(1)}, u32[]{:S(2)}, u32[]{:S(2)}) collective-permute-start(bf16[64,4096]{1,0:T(8,128)(2,1)} %get-tuple-element.36.rest_2_), channel_id=1, source_target_pairs={{0,1},{1,0},{2,3},{3,2},{4,5},{5,4},{6,7},{7,6},{8,9},{9,8},{10,11... | collective-permute-start | bytes 1572872 | tf_op jit(solution)/shard_map/ppermute | solution.py:286
  71.8 3.8 %collective-permute-start.18 = (bf16[64,4096]{1,0:T(8,128)(2,1)}, bf16[64,4096]{1,0:T(8,128)(2,1)S(1)}, u32[]{:S(2)}, u32[]{:S(2)}) collective-permute-start(bf16[64,4096]{1,0:T(8,128)(2,1)} %get-tuple-element.37.rest_3_), channel_id=1, source_target_pairs={{0,1},{1,0},{2,3},{3,2},{4,5},{5,4},{6,7},{7,6},{8,9},{9,8},{10,11... | collective-permute-start | bytes 1572872 | tf_op jit(solution)/shard_map/ppermute | solution.py:286
  72.3 4.6 %collective-permute-start.19 = (bf16[64,4096]{1,0:T(8,128)(2,1)}, bf16[64,4096]{1,0:T(8,128)(2,1)S(1)}, u32[]{:S(2)}, u32[]{:S(2)}) collective-permute-start(bf16[64,4096]{1,0:T(8,128)(2,1)} %get-tuple-element.38.rest_4_), channel_id=1, source_target_pairs={{0,1},{1,0},{2,3},{3,2},{4,5},{5,4},{6,7},{7,6},{8,9},{9,8},{10,11... | collective-permute-start | bytes 1572872 | tf_op jit(solution)/shard_map/ppermute | solution.py:286
  72.3 4.6 %collective-permute-start.16 = (bf16[64,4096]{1,0:T(8,128)(2,1)S(1)}, bf16[64,4096]{1,0:T(8,128)(2,1)}, u32[]{:S(2)}, u32[]{:S(2)}) collective-permute-start(bf16[64,4096]{1,0:T(8,128)(2,1)S(1)} %get-tuple-element.32.rest_1_), channel_id=1, source_target_pairs={{0,1},{1,0},{2,3},{3,2},{4,5},{5,4},{6,7},{7,6},{8,9},{9,8},{10,11... | collective-permute-start | bytes 1572872 | tf_op jit(solution)/shard_map/ppermute | solution.py:286
  72.8 4.1 %collective-permute-start.15 = (bf16[64,4096]{1,0:T(8,128)(2,1)S(1)}, bf16[64,4096]{1,0:T(8,128)(2,1)}, u32[]{:S(2)}, u32[]{:S(2)}) collective-permute-start(bf16[64,4096]{1,0:T(8,128)(2,1)S(1)} %get-tuple-element.31.rest_0_), channel_id=1, source_target_pairs={{0,1},{1,0},{2,3},{3,2},{4,5},{5,4},{6,7},{7,6},{8,9},{9,8},{10,11... | collective-permute-start | bytes 1572872 | tf_op jit(solution)/shard_map/ppermute | solution.py:286
  73.9 14.7 %collective-permute-start.14 = (bf16[64,4096]{1,0:T(8,128)(2,1)S(1)}, bf16[64,4096]{1,0:T(8,128)(2,1)S(1)}, u32[]{:S(2)}, u32[]{:S(2)}) collective-permute-start(bf16[64,4096]{1,0:T(8,128)(2,1)S(1)} %get-tuple-element.32.rest_1_), channel_id=1, source_target_pairs={{0,2},{1,3},{4,0},{5,1},{8,4},{9,5},{12,8},{13,9},{14,12},{15,13},... | collective-permute-start | bytes 1572872 | tf_op jit(solution)/shard_map/ppermute | solution.py:286
  75.5 14.1 %collective-permute-start.13 = (bf16[64,4096]{1,0:T(8,128)(2,1)S(1)}, bf16[64,4096]{1,0:T(8,128)(2,1)S(1)}, u32[]{:S(2)}, u32[]{:S(2)}) collective-permute-start(bf16[64,4096]{1,0:T(8,128)(2,1)S(1)} %get-tuple-element.31.rest_0_), channel_id=1, source_target_pairs={{0,4},{1,5},{4,8},{5,9},{8,12},{9,13},{12,14},{13,15},{14,10},{15,... | collective-permute-start | bytes 1572872 | tf_op jit(solution)/shard_map/ppermute | solution.py:286
  77.1 3.4 %copy-start = (bf16[128,8,4096]{2,1,0:T(8,128)(2,1)S(1)}, bf16[128,8,4096]{2,1,0:T(8,128)(2,1)}, u32[]{:S(2)}) copy-start(bf16[128,8,4096]{2,1,0:T(8,128)(2,1)} %param.12) | copy-start | bytes 25165828
  89.6 7.7 %collective-permute-start.20 = (bf16[32,4096]{1,0:T(8,128)(2,1)S(1)}, bf16[32,4096]{1,0:T(8,128)(2,1)S(1)}, u32[]{:S(2)}, u32[]{:S(2)}) collective-permute-start(bf16[32,4096]{1,0:T(8,128)(2,1)S(1)} %slice.44), channel_id=1, source_target_pairs={{0,4},{1,5},{4,8},{5,9},{8,12},{9,13},{12,14},{13,15},{14,10},{15,... | collective-permute-start | bytes 786440 | tf_op jit(solution)/shard_map/ppermute | solution.py:286
  90.1 7.4 %collective-permute-start.21 = (bf16[32,4096]{1,0:T(8,128)(2,1)S(1)}, bf16[32,4096]{1,0:T(8,128)(2,1)S(1)}, u32[]{:S(2)}, u32[]{:S(2)}) collective-permute-start(bf16[32,4096]{1,0:T(8,128)(2,1)S(1)} %slice.45), channel_id=1, source_target_pairs={{0,2},{1,3},{4,0},{5,1},{8,4},{9,5},{12,8},{13,9},{14,12},{15,13},... | collective-permute-start | bytes 786440 | tf_op jit(solution)/shard_map/ppermute | solution.py:286
  91.8 5.9 %collective-permute-start.24 = (bf16[64,4096]{1,0:T(8,128)(2,1)S(1)}, bf16[64,4096]{1,0:T(8,128)(2,1)S(1)}, u32[]{:S(2)}, u32[]{:S(2)}) collective-permute-start(bf16[64,4096]{1,0:T(8,128)(2,1)S(1)} %collective-permute-done.14.rest_1_), channel_id=1, source_target_pairs={{0,1},{1,0},{2,3},{3,2},{4,5},{5,4},{6,7},{7,6},{8,9},{9,8},{10,11... | collective-permute-start | bytes 1572872 | tf_op jit(solution)/shard_map/ppermute | solution.py:286
  91.8 5.9 %collective-permute-start.23 = (bf16[64,4096]{1,0:T(8,128)(2,1)S(1)}, bf16[64,4096]{1,0:T(8,128)(2,1)S(1)}, u32[]{:S(2)}, u32[]{:S(2)}) collective-permute-start(bf16[64,4096]{1,0:T(8,128)(2,1)S(1)} %collective-permute-done.13.rest_0_), channel_id=1, source_target_pairs={{0,1},{1,0},{2,3},{3,2},{4,5},{5,4},{6,7},{7,6},{8,9},{9,8},{10,11... | collective-permute-start | bytes 1572872 | tf_op jit(solution)/shard_map/ppermute | solution.py:286
  97.5 6.9 %collective-permute-start.22 = (bf16[64,4096]{1,0:T(8,128)(2,1)S(1)}, bf16[64,4096]{1,0:T(8,128)(2,1)S(1)}, u32[]{:S(2)}, u32[]{:S(2)}) collective-permute-start(bf16[64,4096]{1,0:T(8,128)(2,1)S(1)} %constant_dynamic-update-slice_fusion.9.rest_0_), channel_id=1, source_target_pairs={{0,1},{1,0},{2,3},{3,2},{4,5},{5,4},{6,7},{7,6},{8,9},{9,8},{10,11... | collective-permute-start | bytes 1572872 | tf_op jit(solution)/shard_map/ppermute | solution.py:286
  97.6 3.4 %copy-start.1 = (bf16[128,8,4096]{2,1,0:T(8,128)(2,1)S(1)}, bf16[128,8,4096]{2,1,0:T(8,128)(2,1)}, u32[]{:S(2)}) copy-start(bf16[128,8,4096]{2,1,0:T(8,128)(2,1)} %param.12) | copy-start | bytes 25165828

commit v4 on v3

--- a/solution.py
+++ b/solution.py
@@ -10,9 +10,8 @@
 
 DAMPING = 0.01
 F32, BF16 = jnp.float32, jnp.bfloat16
-RAW_HOPS = 2
 STRIDE = 65
-GROUP = 32
+GROUP = 64
 TILE = 512
 MIB = 2**20
 
@@ -26,12 +25,13 @@
     return pltpu.roll(x, 64, 1)
 
 
-def prepare_kernel(experts, mine, sib, tab_a, tab_at, tab_s, tab_st, scale):
-    half = experts // 2
+def prepare_kernel(at, count, src, *rest):
+    tab_a, tab_at, tab_s, tab_st, scale = rest[-5:]
     left64 = lax.broadcasted_iota(jnp.int32, (64, 128), 1) < 64
 
-    def prepare(e, src, at):
-        base = pl.multiple_of(e * 96, 96)
+    def both(pair, unused):
+        e = 2 * pair
+        base = pl.multiple_of(pair * 192, 192)
         f_s = jnp.concatenate([src[pl.ds(base + h, 32, stride=2), :] for h in (0, 1)], 0)
         f_a = src[pl.ds(base + 64, 64), :]
         f_l = src[pl.ds(base + 128, 64), :]
@@ -55,19 +55,15 @@
                     hi, lo = split(jnp.where(left64 if w == 0 else ~left64, m, 0.0))
                     ref[to, w, :64] = hi
                     ref[to, w, 64:] = lo
-
-    def both(e, unused):
-        prepare(2 * e, mine, 0)
-        prepare(2 * e, sib, half)
         return 0
 
-    lax.fori_loop(0, half // 2, both, 0)
-
-
-def prepare(mine, sib, experts):
+    lax.fori_loop(0, count // 2, both, 0, unroll=2)
+
+
+def prepare(src, experts, at, tables=()):
     vm = pl.BlockSpec(memory_space=pltpu.VMEM)
     return pl.pallas_call(
-        functools.partial(prepare_kernel, experts),
+        functools.partial(prepare_kernel, at, experts // 2),
         out_shape=[
             jax.ShapeDtypeStruct((experts, 2, 128, 128), BF16),
             jax.ShapeDtypeStruct((experts, 2, 128, 128), BF16),
@@ -75,12 +71,33 @@
             jax.ShapeDtypeStruct((experts, 64, 256), BF16),
             jax.ShapeDtypeStruct((experts, 64, 128), F32),
         ],
-        in_specs=[vm] * 2,
+        in_specs=[vm] * (1 + len(tables)),
         out_specs=[vm] * 5,
+        input_output_aliases={1 + i: i for i in range(len(tables))},
         compiler_params=pltpu.CompilerParams(vmem_limit_bytes=4 * MIB),
-        cost_estimate=pl.CostEstimate(flops=2 * 10**9, bytes_accessed=8 * MIB, transcendentals=0),
+        cost_estimate=pl.CostEstimate(flops=10**9, bytes_accessed=4 * MIB, transcendentals=0),
         name="prepare",
-    )(mine, sib)
+    )(src, *tables)
+
+
+def pack_kernel(s, a, lam, out):
+    for i, m in enumerate((s, a, lam)):
+        for p in range(m.shape[0] // 2):
+            first = (3 * p + i) * 64
+            out[first : first + 64, :] = jnp.concatenate([m[2 * p], m[2 * p + 1]], axis=1)
+
+
+def pack_factors(s, a, lam):
+    vm = pl.BlockSpec(memory_space=pltpu.VMEM)
+    return pl.pallas_call(
+        pack_kernel,
+        out_shape=jax.ShapeDtypeStruct((s.shape[0] * 96, 128), F32),
+        in_specs=[vm] * 3,
+        out_specs=vm,
+        compiler_params=pltpu.CompilerParams(vmem_limit_bytes=4 * MIB),
+        cost_estimate=pl.CostEstimate(flops=10**5, bytes_accessed=10**5, transcendentals=0),
+        name="pack",
+    )(s, a, lam)
 
 
 def precondition_kernel(units, routes, owner, info, tab_a, tab_at, tab_s, tab_st, scale, *rest):
@@ -115,7 +132,7 @@
             es, g, x = [], [], []
             for i in range(GROUP):
                 row = b * GROUP + i
-                es.append(info[owner[routes[first + row // 8, row % 8]]])
+                es.append(info[owner[routes[first + row % 8, row // 8]]])
                 g.append(xs[pl.ds(row, 32, stride=STRIDE), :])
             n = GROUP // 2
             ee = [(es[2 * p], es[2 * p + 1]) for p in range(n)]
@@ -137,7 +154,7 @@
                 top, low = y[:32], y[32:]
                 for w, v in enumerate((jnp.where(left, top, swap(low)), jnp.where(left, swap(top), low))):
                     row = b * GROUP + 2 * p + w
-                    ys[pl.ds((row % 8) * 8 + row // 8, 32, stride=STRIDE), :] = v
+                    ys[pl.ds(row, 32, stride=STRIDE), :] = v
             return 0
 
         lax.fori_loop(0, 64 // GROUP, group, 0)
@@ -146,13 +163,13 @@
 
 
 def precondition(routes, owner, info, tables, raws, units):
-    chunks = len(raws)
+    chunks = len(units)
     sm = pl.BlockSpec(memory_space=pltpu.SMEM)
     vm = pl.BlockSpec(memory_space=pltpu.VMEM)
     return pl.pallas_call(
         functools.partial(precondition_kernel, units),
-        out_shape=[jax.ShapeDtypeStruct(r.shape, BF16) for r in raws],
-        in_specs=[sm] * 3 + [vm] * (5 + chunks),
+        out_shape=[jax.ShapeDtypeStruct((64, raws[0].shape[1]), BF16)] * chunks,
+        in_specs=[sm] * 3 + [vm] * (5 + len(raws)),
         out_specs=[vm] * chunks,
         scratch_shapes=[pltpu.VMEM((32 * STRIDE, 128), F32), pltpu.VMEM((32 * STRIDE, 128), F32)],
         compiler_params=pltpu.CompilerParams(vmem_limit_bytes=8 * MIB),
@@ -220,7 +237,10 @@
         out_shape=jax.ShapeDtypeStruct((queries if placed else blocks * 8, 128), F32),
         in_specs=[sm] + [vm] * (3 + len(parts) + len(old)),
         out_specs=vm,
-        scratch_shapes=[pltpu.VMEM((sum(shapes), width), BF16), pltpu.VMEM((blocks * 8, train_rows), F32)],
+        scratch_shapes=[
+            pltpu.VMEM((sum(shapes), width), BF16),
+            pltpu.VMEM((blocks * 8, train_rows), F32),
+        ],
         compiler_params=pltpu.CompilerParams(vmem_limit_bytes=14 * MIB),
         cost_estimate=pl.CostEstimate(
             flops=4 * 128 * max(2, blocks) * train_rows * width // 2,
@@ -244,8 +264,12 @@
             order = chips - 1 if rel == far else 2 * (chips - rel) - 1 if rel > far else 2 * rel
             across = (slot // slots) % 2 != me % 2
             place.append((across * chips + order) * slots + slot % slots)
-        near = [2 * ring[(spot[me // 2] + d) % chips] + me % 2 for d in range(chips)]
-        rows.append(place + near + [d ^ 1 for d in near])
+        near = []
+        for d in range(far + 1):
+            for core in (me % 2, 1 - me % 2):
+                chip = ring[(spot[me // 2] + (d if core else -d)) % chips]
+                near += [2 * chip + core, 2 * chip + 1 - core]
+        rows.append(place + near)
     return ring, np.array(rows, np.int32)
 
 
@@ -276,38 +300,31 @@
     ring, constants = tables_of(devices, slots)
     info = lax.dynamic_index_in_dim(jnp.asarray(constants), me, 0, keepdims=False)
 
-    def shift(step):
+    def shift(steps):
         return [
-            (2 * c + k, 2 * ring[(i + step) % chips] + k) for i, c in enumerate(ring) for k in range(2)
+            (2 * c + k, 2 * ring[(i + steps[k]) % chips] + k) for i, c in enumerate(ring) for k in (0, 1)
         ]
 
-    ahead, back = shift(1), shift(-1)
+    ahead, back, stream = shift((1, 1)), shift((-1, -1)), shift((1, -1))
     across = [(d, d ^ 1) for d in range(devices)]
     send = lambda v, way: lax.ppermute(v, "shard", way)
-    near = lambda distance: distance % chips
-    other = lambda distance: chips + distance % chips
-
-    raw = query_grads.reshape(-1, width)
-
-    raws = []
-    for _ in range(RAW_HOPS):
-        u, d = raws[-1] if raws else (raw, raw)
-        raws.append((send(u, ahead), send(d, back)))
-    pairs = lambda m: jnp.concatenate([m[0::2], m[1::2]], axis=-1)
-    pack = jnp.stack([pairs(basis_s), pairs(basis_a), pairs(eigenvalues)], axis=1).reshape(slots * 96, 128)
+
+    raw = query_grads.transpose(1, 0, 2).reshape(-1, width)
+    other_raw = send(raw, across)
+
+    pack = pack_factors(basis_s, basis_a, eigenvalues)
     got, up, down = [pack], pack, pack
-    for _ in range(far - 1):
+    cut = pack.shape[0] // 2
+    for step in range(1, far + 1):
+        if step == far:
+            up, down = up[:cut], down[cut:]
+            raw, up = tie(raw, got[-1]), tie(up, other_raw)
         up, down = send(up, ahead), send(down, back)
         got += [up, down]
-    if raws:
-        up, down = tie((up, down), raws[0])
-    cut = pack.shape[0] // 2
-    got += [send(up[:cut], ahead), send(down[cut:], back)]
+    a = send(raw, stream)
     mine = jnp.concatenate(got, axis=0)
     sib = send(mine, across)
-    if len(raws) > 1:
-        sib = tie(sib, raws[-1])
-    tables = prepare(mine, sib, experts)
+    tables = prepare(sib, experts, experts // 2, prepare(mine, experts, 0))
 
     live = jnp.arange(train_dev, dtype=jnp.int32) < train_counts[0]
     route = jnp.where(live[:, None], train_routes, -1).reshape(1, train_dev * top)
@@ -319,34 +336,29 @@
     multiply = lambda parts, names, **more: products(
         info, experts, route, query_route, train, parts, names, **more
     )
-    held, names, parts = [], [], [raw]
-    if RAW_HOPS:
-        up, down = pre(list(raws[-1]), [near(-RAW_HOPS), near(RAW_HOPS)])
-        held, names = [up, down], [near(-RAW_HOPS), near(RAW_HOPS)]
-        parts = [raw] + [v for pair in raws[:-1] for v in pair]
-        parts = list(tie(tuple(parts), up))
-    kinds = [near(0)] + [near(d) for h in range(1, RAW_HOPS) for d in (-h, h)]
-    rest = pre(parts, kinds)
-    if not RAW_HOPS:
-        up, down = rest[0], rest[0]
-    held, names = held + list(rest), names + kinds
+    (b,) = pre([other_raw], [1])
+    held, names = [send(b, across), b], [0, 1]
+    (a,) = pre([tie(a, b)], [4])
+    b = send(b, stream)
     done, placed = [], []
-    for step in range(1 + RAW_HOPS, far + 1):
+    for step in range(1, far):
         if done:
-            up, down = tie((up, down), done[-1])
-        if step == far:
-            up, down = send(up[:32], ahead), send(down[32:], back)
-        else:
-            up, down = send(up, ahead), send(down, back)
-        parts = held + [send(v, across) for v in held]
-        names = names + [n + chips for n in names]
-        done.append(multiply(parts, names))
+            a = tie(a, done[-1])
+        next_a = send(a, stream)
+        held += [a, send(a, across)]
+        if step < far - 1:
+            next_b = send(b, stream)
+        held += [b, send(b, across)]
+        names += [4 * step, 4 * step + 2, 4 * step + 1, 4 * step + 3]
+        a, b = next_a, next_b
+        if step > 1 or far < 4:
+            pass
+        done.append(multiply(held, names))
         placed.append(names)
-        held, names = [up, down], [near(-step), near(step)]
-    last = jnp.concatenate([up, down], axis=0)
-    return multiply(
-        [last, send(last, across)], [near(far), other(far)], old=done, placed=placed, queries=queries
-    )
+        held, names = [], []
+    if done:
+        a = tie(a, done[-1])
+    return multiply([a, send(a, across)], [4 * far, 4 * far + 2], old=done, placed=placed, queries=queries)
 
 
 def solution(mesh):

time: 110 us -> 89.5 us (0.81)
  waiting for transfers between devices: 38.9 us -> 26.2 us
  Pallas kernels: 38.1 us -> 27.4 us
  starting transfers between devices: 19.2 us -> 22.5 us
    ppermute x25, waiting for transfers between devices: 38.9 us -> 26.2 us  [local(): send = lambda v, way: lax.ppermute(v, 'shard', way)]
    pallas_call x2, Pallas kernels: 19.3 us -> 7.99 us  [precondition(): pl.pallas_call(functools.partial(precondition_kernel, units), out_shape=[...]
    ppermute x25, starting transfers between devices: 19.2 us -> 22.5 us  [local(): send = lambda v, way: lax.ppermute(v, 'shard', way)]
    slice x7 -> x2, local copies, waits for them, and re-layouts: 2.4 us -> 0.01 us  [local(): up, down = (up[:cut], down[cut:])]
    unnamed x26 -> x25, local copies, waits for them, and re-layouts: 7.99 us -> 9.46 us
    transpose x0 -> x1, local copies, waits for them, and re-layouts: none -> 1.33 us  [local(): raw = query_grads.transpose(1, 0, 2).reshape(-1, width)]
    pallas_call x3 -> x4, Pallas kernels: 16.1 us -> 16.6 us  [products(): pl.pallas_call(functools.partial(products_kernel, units, placed, shapes,...]
    pallas_call x1 -> x3, Pallas kernels: 2.73 us -> 2.82 us  [the longest x2 2.73 us: prepare(): pl.pallas_call(functools.partial(prepare_kernel, at, experts // 2), out_s...]
  transfers between devices with their start and end apart: 25 -> 25, of which waited for: 12 -> 9; matrix products, arithmetic and copies ran while one was open for 1% -> 3% of each run, Pallas kernels for 11% -> 26%
where the time goes in v4:
time: 89.5 us; the launch traced here: 89.1 us
  Pallas kernels  27.4 us (31%)
  waiting for transfers between devices  26.2 us (29%)
  starting transfers between devices  22.5 us (25%)
  local copies, waits for them, and re-layouts  12.1 us (14%)
  between operations  0.95 us (1%)
    ppermute x25, waiting for transfers between devices, local(): send = lambda v, way: lax.ppermute(v, 'shard', way)  26.2 us
    ppermute x25, starting transfers between devices, local(): send = lambda v, way: lax.ppermute(v, 'shard', way)  22.5 us
    pallas_call x4, Pallas kernels, products(): pl.pallas_call(functools.partial(products_kernel, units, placed, shapes,...  16.6 us
    unnamed x25, local copies, waits for them, and re-layouts  9.46 us
    pallas_call x2, Pallas kernels, precondition(): pl.pallas_call(functools.partial(precondition_kernel, units), out_shape=[...  7.99 us
    pallas_call x2, Pallas kernels, prepare(): pl.pallas_call(functools.partial(prepare_kernel, at, experts // 2), out_s...  2.73 us
  transfers between devices with their start and end apart: 25, of which 9 were waited for; matrix products, arithmetic and copies ran while one was open for 3% of the time, Pallas kernels for 26%

profile of v4, /device:TPU:0, one launch (start us, length us, event | category | flops | bytes accessed | tf_op | source)
XLA Modules:
  0.0 89.1 jit_solution(5857763340468353778)
XLA Ops:
  0.0 0.8 copy-done.2
  0.8 0.8 copy-done.3
  1.7 0.8 copy-done.4
  2.5 0.1 pack.1
  2.6 3.1 %collective-permute-start = (f32[192,128]{1,0:T(8,128)S(1)}, f32[192,128]{1,0:T(8,128)S(1)}, u32[]{:S(2)}, u32[]{:S(2)}) collective-permute-start(f32[192,128]{1,0:T(8,128)S(1)} %pack.1), channel_id=1, source_target_pairs={{0,4},{1,5},{4,8},{5,9},{8,12},{9,13},{12,14},{13,15},{14,10},{15,... | collective-permute-start | bytes 294920 | tf_op jit(solution)/shard_map/ppermute | solution.py:310
  5.7 0.0 collective-permute-start.1
  5.7 1.3 %copy.26 = bf16[8,8,4096]{2,1,0:T(8,128)(2,1)S(1)} copy(bf16[8,8,4096]{2,0,1:T(8,128)(2,1)} %bitcast.16) | data formatting | bytes 1048576 | tf_op jit(solution)/shard_map/transpose | solution.py:312
  7.0 0.1 collective-permute-start.6
  7.1 1.3 %collective-permute-done = f32[192,128]{1,0:T(8,128)S(1)} collective-permute-done((f32[192,128]{1,0:T(8,128)S(1)}, f32[192,128]{1,0:T(8,128)S(1)}, u32[]{:S(2)}, u32[]{:S(2)}) %collective-permute-start) | collective-permute-done | bytes 98336 | tf_op jit(solution)/shard_map/ppermute | solution.py:310
  8.4 1.9 %collective-permute-start.2 = (f32[192,128]{1,0:T(8,128)S(1)}, f32[192,128]{1,0:T(8,128)S(1)}, u32[]{:S(2)}, u32[]{:S(2)}) collective-permute-start(f32[192,128]{1,0:T(8,128)S(1)} %collective-permute-done), channel_id=1, source_target_pairs={{0,4},{1,5},{4,8},{5,9},{8,12},{9,13},{12,14},{13,15},{14,10},{15,... | collective-permute-start | bytes 294920 | tf_op jit(solution)/shard_map/ppermute | solution.py:310
  10.3 0.1 collective-permute-start.3
  10.5 2.6 %collective-permute-done.2 = f32[192,128]{1,0:T(8,128)S(1)} collective-permute-done((f32[192,128]{1,0:T(8,128)S(1)}, f32[192,128]{1,0:T(8,128)S(1)}, u32[]{:S(2)}, u32[]{:S(2)}) %collective-permute-start.2) | collective-permute-done | bytes 98336 | tf_op jit(solution)/shard_map/ppermute | solution.py:310
  13.0 1.9 %collective-permute-start.4 = (f32[192,128]{1,0:T(8,128)S(1)}, f32[192,128]{1,0:T(8,128)S(1)}, u32[]{:S(2)}, u32[]{:S(2)}) collective-permute-start(f32[192,128]{1,0:T(8,128)S(1)} %collective-permute-done.2), channel_id=1, source_target_pairs={{0,4},{1,5},{4,8},{5,9},{8,12},{9,13},{12,14},{13,15},{14,10},{15,... | collective-permute-start | bytes 294920 | tf_op jit(solution)/shard_map/ppermute | solution.py:310
  14.9 0.0 collective-permute-done.3
  14.9 0.1 collective-permute-start.5
  15.1 4.5 %collective-permute-done.5 = f32[192,128]{1,0:T(8,128)S(1)} collective-permute-done((f32[192,128]{1,0:T(8,128)S(1)}, f32[192,128]{1,0:T(8,128)S(1)}, u32[]{:S(2)}, u32[]{:S(2)}) %collective-permute-start.5) | collective-permute-done | bytes 98336 | tf_op jit(solution)/shard_map/ppermute | solution.py:310
  19.6 0.1 collective-permute-start.8
  19.7 0.0 collective-permute-done.6.rest_0_
  19.7 2.0 %collective-permute-start.7 = (f32[96,128]{1,0:T(8,128)S(1)}, f32[96,128]{1,0:T(8,128)S(1)}, u32[]{:S(2)}, u32[]{:S(2)}) collective-permute-start(f32[96,128]{1,0:T(8,128)S(1)} %slice.8), channel_id=1, source_target_pairs={{0,4},{1,5},{4,8},{5,9},{8,12},{9,13},{12,14},{13,15},{14,10},{15,... | collective-permute-start | bytes 147464 | tf_op jit(solution)/shard_map/ppermute | solution.py:310
  21.7 2.5 %collective-permute-done.7 = f32[96,128]{1,0:T(8,128)S(1)} collective-permute-done((f32[96,128]{1,0:T(8,128)S(1)}, f32[96,128]{1,0:T(8,128)S(1)}, u32[]{:S(2)}, u32[]{:S(2)}) %collective-permute-start.7) | collective-permute-done | bytes 49184 | tf_op jit(solution)/shard_map/ppermute | solution.py:310
  24.2 0.0 collective-permute-done.8
  24.2 0.1 collective-permute-start.9
  24.3 0.1 copy.24.routes
  24.4 0.7 dynamic-slice_bitcast_fusion.info
  25.1 1.6 %collective-permute-start.10 = (bf16[64,4096]{1,0:T(8,128)(2,1)S(1)}, bf16[64,4096]{1,0:T(8,128)(2,1)S(1)}, u32[]{:S(2)}, u32[]{:S(2)}) collective-permute-start(bf16[64,4096]{1,0:T(8,128)(2,1)S(1)} %bitcast.18), channel_id=1, source_target_pairs={{0,4},{1,3},{4,8},{5,1},{8,12},{9,5},{12,14},{13,9},{14,10},{15,13... | collective-permute-start | bytes 1572872 | tf_op jit(solution)/shard_map/ppermute | solution.py:310
  26.7 1.4 %prepare.2 = (bf16[32,2,128,128]{3,2,1,0:T(8,128)(2,1)S(1)}, bf16[32,2,128,128]{3,2,1,0:T(8,128)(2,1)S(1)}, bf16[32,64,256]{2,1,0:T(8,128)(2,1)S(1)}, bf16[32,64,256]{2,1,0:T(8,128)(2,1)S(1)}, f32[32,64,128]{2,1,0:T(8,128)S(1)}) custom-call(f32[1536,128]{1,0:T(8,128)S(1)} %constant_dynamic-update-slice_fusion.src), custom_call_target="tpu_custom_call" | custom-call | flops 1000000000 | bytes 4194304 | tf_op jit(solution)/shard_map/prepare/pallas_call | solution.py:65
  28.1 0.0 copy-start.5
  28.1 1.4 %prepare.3 = (bf16[32,2,128,128]{3,2,1,0:T(8,128)(2,1)S(1)}, bf16[32,2,128,128]{3,2,1,0:T(8,128)(2,1)S(1)}, bf16[32,64,256]{2,1,0:T(8,128)(2,1)S(1)}, bf16[32,64,256]{2,1,0:T(8,128)(2,1)S(1)}, f32[32,64,128]{2,1,0:T(8,128)S(1)}) custom-call(f32[1536,128]{1,0:T(8,128)S(1)} %collective-permute-done, ...), custom_call_target="tpu_custom_call", output_to_operand_aliasing={{0}: (1, {}), {1}: (2, {}), {2}: (3, {}), {3}: (4, {}), {4}... | custom-call | flops 1000000000 | bytes 4194304 | tf_op jit(solution)/shard_map/prepare/pallas_call | solution.py:65
  29.5 4.0 %precondition.2.rest_1_ = bf16[64,4096]{1,0:T(8,128)(2,1)S(1)} custom-call(s32[128,8]{1,0:T(8,128)S(1)} %copy.24.routes, s32[32]{0:T(128)S(1)} %copy-done.5, s32[52]{0:T(128)S(1)} %dynamic-slice_bitcast_fusion.info, bf16[32,2,128,128]{3,2,1,0:T(8,128)(2,1)S(1)} %get-tuple-element.27.tab_a, bf16[32,2,128,128]{3,2,1,0:T(8,128)(2,1)S(1)} %get-tuple-element.28.tab_at, ...), custom_call_target="tpu_custom_call" | custom-call | flops 3000000000 | bytes 8000000 | tf_op jit(solution)/shard_map/precondition/pallas_call | solution.py:169
  33.5 0.0 copy-start.7
  33.5 1.9 %collective-permute-start.14 = (bf16[64,4096]{1,0:T(8,128)(2,1)S(1)}, bf16[64,4096]{1,0:T(8,128)(2,1)S(1)}, u32[]{:S(2)}, u32[]{:S(2)}) collective-permute-start(bf16[64,4096]{1,0:T(8,128)(2,1)S(1)} %precondition.2.rest_1_), channel_id=1, source_target_pairs={{0,4},{1,3},{4,8},{5,1},{8,12},{9,5},{12,14},{13,9},{14,10},{15,13... | collective-permute-start | bytes 1572872 | tf_op jit(solution)/shard_map/ppermute | solution.py:310
  35.4 0.1 collective-permute-start.12
  35.5 0.0 collective-permute-done.10.rest_0_
  35.5 4.0 %precondition.3.rest_2_ = bf16[64,4096]{1,0:T(8,128)(2,1)S(1)} custom-call(s32[128,8]{1,0:T(8,128)S(1)} %copy.24.routes, s32[32]{0:T(128)S(1)} %copy-done.5, s32[52]{0:T(128)S(1)} %dynamic-slice_bitcast_fusion.info, bf16[32,2,128,128]{3,2,1,0:T(8,128)(2,1)S(1)} %get-tuple-element.27.tab_a, bf16[32,2,128,128]{3,2,1,0:T(8,128)(2,1)S(1)} %get-tuple-element.28.tab_at, ...), custom_call_target="tpu_custom_call" | custom-call | flops 3000000000 | bytes 8000000 | tf_op jit(solution)/shard_map/precondition/pallas_call | solution.py:169
  39.5 0.5 collective-permute-start.13
  40.0 2.7 %collective-permute-done.14.rest_4_ = bf16[64,4096]{1,0:T(8,128)(2,1)S(1)} collective-permute-done((bf16[64,4096]{1,0:T(8,128)(2,1)S(1)}, bf16[64,4096]{1,0:T(8,128)(2,1)S(1)}, u32[]{:S(2)}, u32[]{:S(2)}) %collective-permute-start.14) | collective-permute-done | bytes 524320 | tf_op jit(solution)/shard_map/ppermute | solution.py:310
  42.7 0.0 collective-permute-start.15
  42.7 0.1 reshape.19
  42.8 0.1 broadcast_in_dim.22
  43.6 0.1 copy.20
  43.7 0.1 reshape.18.route
  43.8 1.9 %collective-permute-start.11 = (bf16[64,4096]{1,0:T(8,128)(2,1)S(1)}, bf16[64,4096]{1,0:T(8,128)(2,1)S(1)}, u32[]{:S(2)}, u32[]{:S(2)}) collective-permute-start(bf16[64,4096]{1,0:T(8,128)(2,1)S(1)} %precondition.3.rest_2_), channel_id=1, source_target_pairs={{0,4},{1,3},{4,8},{5,1},{8,12},{9,5},{12,14},{13,9},{14,10},{15,13... | collective-permute-start | bytes 1572872 | tf_op jit(solution)/shard_map/ppermute | solution.py:310
  45.8 1.6 %collective-permute-start.18 = (bf16[64,4096]{1,0:T(8,128)(2,1)S(1)}, bf16[64,4096]{1,0:T(8,128)(2,1)S(1)}, u32[]{:S(2)}, u32[]{:S(2)}) collective-permute-start(bf16[64,4096]{1,0:T(8,128)(2,1)S(1)} %collective-permute-done.14.rest_4_), channel_id=1, source_target_pairs={{0,4},{1,3},{4,8},{5,1},{8,12},{9,5},{12,14},{13,9},{14,10},{15,13... | collective-permute-start | bytes 1572872 | tf_op jit(solution)/shard_map/ppermute | solution.py:310
  47.3 0.0 collective-permute-done.12.rest_0_
  47.3 0.0 collective-permute-done.15.rest_5_
  47.4 0.2 broadcast_in_dim.23.query_route
  47.5 0.0 copy-start
  47.6 3.4 %copy-done = bf16[128,8,4096]{2,1,0:T(8,128)(2,1)S(1)} copy-done((bf16[128,8,4096]{2,1,0:T(8,128)(2,1)S(1)}, bf16[128,8,4096]{2,1,0:T(8,128)(2,1)}, u32[]{:S(2)}) %copy-start) | copy-done | bytes 8388632
  50.9 5.2 %products.4.rest_2_ = f32[48,128]{1,0:T(8,128)S(1)} custom-call(s32[52]{0:T(128)S(1)} %dynamic-slice_bitcast_fusion.info, s32[1,1024]{1,0:T(1,128)S(1)} %reshape.18.route, s32[1024,128]{1,0:T(8,128)S(1)} %broadcast_in_dim.23.query_route, bf16[1024,4096]{1,0:T(8,128)(2,1)S(1)} %bitcast.12, bf16[64,4096]{1,0:T(8,128)(2,1)S(1)} %collective-permute-done.12.rest_0_, ...), custom_call_target="tpu_custom_call" | custom-call | flops 6442450944 | bytes 8388608 | tf_op jit(solution)/shard_map/products/pallas_call | solution.py:235
  56.1 0.1 collective-permute-start.17
  56.2 2.5 %collective-permute-done.18.rest_2_ = bf16[64,4096]{1,0:T(8,128)(2,1)S(1)} collective-permute-done((bf16[64,4096]{1,0:T(8,128)(2,1)S(1)}, bf16[64,4096]{1,0:T(8,128)(2,1)S(1)}, u32[]{:S(2)}, u32[]{:S(2)}) %collective-permute-start.18) | collective-permute-done | bytes 524320 | tf_op jit(solution)/shard_map/ppermute | solution.py:310
  58.7 0.0 collective-permute-start.19
  58.7 1.9 %collective-permute-start.16 = (bf16[64,4096]{1,0:T(8,128)(2,1)S(1)}, bf16[64,4096]{1,0:T(8,128)(2,1)S(1)}, u32[]{:S(2)}, u32[]{:S(2)}) collective-permute-start(bf16[64,4096]{1,0:T(8,128)(2,1)S(1)} %collective-permute-done.11.rest_0_), channel_id=1, source_target_pairs={{0,4},{1,3},{4,8},{5,1},{8,12},{9,5},{12,14},{13,9},{14,10},{15,13... | collective-permute-start | bytes 1572872 | tf_op jit(solution)/shard_map/ppermute | solution.py:310
  60.6 1.6 %collective-permute-start.22 = (bf16[64,4096]{1,0:T(8,128)(2,1)S(1)}, bf16[64,4096]{1,0:T(8,128)(2,1)S(1)}, u32[]{:S(2)}, u32[]{:S(2)}) collective-permute-start(bf16[64,4096]{1,0:T(8,128)(2,1)S(1)} %collective-permute-done.18.rest_2_), channel_id=1, source_target_pairs={{0,4},{1,3},{4,8},{5,1},{8,12},{9,5},{12,14},{13,9},{14,10},{15,13... | collective-permute-start | bytes 1572872 | tf_op jit(solution)/shard_map/ppermute | solution.py:310
  62.2 3.4 %copy-done.1 = bf16[128,8,4096]{2,1,0:T(8,128)(2,1)S(1)} copy-done((bf16[128,8,4096]{2,1,0:T(8,128)(2,1)S(1)}, bf16[128,8,4096]{2,1,0:T(8,128)(2,1)}, u32[]{:S(2)}) %copy-start.1) | copy-done | bytes 8388632
  65.5 3.5 %products.5.rest_3_ = f32[32,128]{1,0:T(8,128)S(1)} custom-call(s32[52]{0:T(128)S(1)} %dynamic-slice_bitcast_fusion.info, s32[1,1024]{1,0:T(1,128)S(1)} %reshape.18.route, s32[1024,128]{1,0:T(8,128)S(1)} %broadcast_in_dim.23.query_route, bf16[1024,4096]{1,0:T(8,128)(2,1)S(1)} %bitcast.13, bf16[64,4096]{1,0:T(8,128)(2,1)S(1)} %collective-permute-done.11.rest_0_, ...), custom_call_target="tpu_custom_call" | custom-call | flops 4294967296 | bytes 8388608 | tf_op jit(solution)/shard_map/products/pallas_call | solution.py:235
  69.0 0.1 collective-permute-start.21
  69.1 4.4 %collective-permute-done.22.rest_2_ = bf16[64,4096]{1,0:T(8,128)(2,1)S(1)} collective-permute-done((bf16[64,4096]{1,0:T(8,128)(2,1)S(1)}, bf16[64,4096]{1,0:T(8,128)(2,1)S(1)}, u32[]{:S(2)}, u32[]{:S(2)}) %collective-permute-start.22) | collective-permute-done | bytes 524320 | tf_op jit(solution)/shard_map/ppermute | solution.py:310
  73.5 1.9 %collective-permute-start.20 = (bf16[64,4096]{1,0:T(8,128)(2,1)S(1)}, bf16[64,4096]{1,0:T(8,128)(2,1)S(1)}, u32[]{:S(2)}, u32[]{:S(2)}) collective-permute-start(bf16[64,4096]{1,0:T(8,128)(2,1)S(1)} %collective-permute-done.16.rest_0_), channel_id=1, source_target_pairs={{0,4},{1,3},{4,8},{5,1},{8,12},{9,5},{12,14},{13,9},{14,10},{15,13... | collective-permute-start | bytes 1572872 | tf_op jit(solution)/shard_map/ppermute | solution.py:310
  75.4 0.0 collective-permute-done.23.rest_3_
  75.4 3.5 %products.6.rest_4_ = f32[32,128]{1,0:T(8,128)S(1)} custom-call(s32[52]{0:T(128)S(1)} %dynamic-slice_bitcast_fusion.info, s32[1,1024]{1,0:T(1,128)S(1)} %reshape.18.route, s32[1024,128]{1,0:T(8,128)S(1)} %broadcast_in_dim.23.query_route, bf16[1024,4096]{1,0:T(8,128)(2,1)S(1)} %bitcast.14, bf16[64,4096]{1,0:T(8,128)(2,1)S(1)} %collective-permute-done.16.rest_0_, ...), custom_call_target="tpu_custom_call" | custom-call | flops 4294967296 | bytes 8388608 | tf_op jit(solution)/shard_map/products/pallas_call | solution.py:235
  78.8 3.8 %collective-permute-done.20.rest_0_ = bf16[64,4096]{1,0:T(8,128)(2,1)S(1)} collective-permute-done((bf16[64,4096]{1,0:T(8,128)(2,1)S(1)}, bf16[64,4096]{1,0:T(8,128)(2,1)S(1)}, u32[]{:S(2)}, u32[]{:S(2)}) %collective-permute-start.20) | collective-permute-done | bytes 524320 | tf_op jit(solution)/shard_map/ppermute | solution.py:310
  82.7 1.9 %collective-permute-done.24.rest_1_ = bf16[64,4096]{1,0:T(8,128)(2,1)S(1)} collective-permute-done((bf16[64,4096]{1,0:T(8,128)(2,1)S(1)}, bf16[64,4096]{1,0:T(8,128)(2,1)S(1)}, u32[]{:S(2)}, u32[]{:S(2)}) %collective-permute-start.24) | collective-permute-done | bytes 524320 | tf_op jit(solution)/shard_map/ppermute | solution.py:310
  84.6 4.5 %products.7 = f32[128,128]{1,0:T(8,128)} custom-call(s32[52]{0:T(128)S(1)} %dynamic-slice_bitcast_fusion.info, s32[1,1024]{1,0:T(1,128)S(1)} %reshape.18.route, s32[1024,128]{1,0:T(8,128)S(1)} %broadcast_in_dim.23.query_route, bf16[1024,4096]{1,0:T(8,128)(2,1)S(1)} %bitcast.15, bf16[64,4096]{1,0:T(8,128)(2,1)S(1)} %collective-permute-done.20.rest_0_, ...), custom_call_target="tpu_custom_call" | custom-call | flops 2147483648 | bytes 8388608 | tf_op jit(solution)/shard_map/products/pallas_call | solution.py:235
  (33 shorter events, 0.2 us)
Async XLA Ops:
  0.0 0.8 copy-start.2
  0.8 0.8 copy-start.3
  1.7 0.8 copy-start.4
  2.5 21.8 %copy-start.6 = (s32[128,8]{0,1:T(8,128)S(1)}, s32[128,8]{0,1:T(8,128)}, u32[]{:S(2)}) copy-start(s32[128,8]{0,1:T(8,128)} %param.11) | copy-start | bytes 12292
  2.6 5.8 %collective-permute-start = (f32[192,128]{1,0:T(8,128)S(1)}, f32[192,128]{1,0:T(8,128)S(1)}, u32[]{:S(2)}, u32[]{:S(2)}) collective-permute-start(f32[192,128]{1,0:T(8,128)S(1)} %pack.1), channel_id=1, source_target_pairs={{0,4},{1,5},{4,8},{5,9},{8,12},{9,13},{12,14},{13,15},{14,10},{15,... | collective-permute-start | bytes 294920 | tf_op jit(solution)/shard_map/ppermute | solution.py:310
  5.7 4.6 %collective-permute-start.1 = (f32[192,128]{1,0:T(8,128)S(1)}, f32[192,128]{1,0:T(8,128)S(1)}, u32[]{:S(2)}, u32[]{:S(2)}) collective-permute-start(f32[192,128]{1,0:T(8,128)S(1)} %pack.1), channel_id=1, source_target_pairs={{0,2},{1,3},{4,0},{5,1},{8,4},{9,5},{12,8},{13,9},{14,12},{15,13},... | collective-permute-start | bytes 294920 | tf_op jit(solution)/shard_map/ppermute | solution.py:310
  7.0 12.7 %collective-permute-start.6 = (bf16[64,4096]{1,0:T(8,128)(2,1)S(1)}, bf16[64,4096]{1,0:T(8,128)(2,1)S(1)}, u32[]{:S(2)}, u32[]{:S(2)}) collective-permute-start(bf16[64,4096]{1,0:T(8,128)(2,1)S(1)} %bitcast.17), channel_id=1, source_target_pairs={{0,1},{1,0},{2,3},{3,2},{4,5},{5,4},{6,7},{7,6},{8,9},{9,8},{10,11... | collective-permute-start | bytes 1572872 | tf_op jit(solution)/shard_map/ppermute | solution.py:310
  8.4 4.6 %collective-permute-start.2 = (f32[192,128]{1,0:T(8,128)S(1)}, f32[192,128]{1,0:T(8,128)S(1)}, u32[]{:S(2)}, u32[]{:S(2)}) collective-permute-start(f32[192,128]{1,0:T(8,128)S(1)} %collective-permute-done), channel_id=1, source_target_pairs={{0,4},{1,5},{4,8},{5,9},{8,12},{9,13},{12,14},{13,15},{14,10},{15,... | collective-permute-start | bytes 294920 | tf_op jit(solution)/shard_map/ppermute | solution.py:310
  10.3 4.6 %collective-permute-start.3 = (f32[192,128]{1,0:T(8,128)S(1)}, f32[192,128]{1,0:T(8,128)S(1)}, u32[]{:S(2)}, u32[]{:S(2)}) collective-permute-start(f32[192,128]{1,0:T(8,128)S(1)} %collective-permute-done.1), channel_id=1, source_target_pairs={{0,2},{1,3},{4,0},{5,1},{8,4},{9,5},{12,8},{13,9},{14,12},{15,13},... | collective-permute-start | bytes 294920 | tf_op jit(solution)/shard_map/ppermute | solution.py:310
  13.0 6.7 %collective-permute-start.4 = (f32[192,128]{1,0:T(8,128)S(1)}, f32[192,128]{1,0:T(8,128)S(1)}, u32[]{:S(2)}, u32[]{:S(2)}) collective-permute-start(f32[192,128]{1,0:T(8,128)S(1)} %collective-permute-done.2), channel_id=1, source_target_pairs={{0,4},{1,5},{4,8},{5,9},{8,12},{9,13},{12,14},{13,15},{14,10},{15,... | collective-permute-start | bytes 294920 | tf_op jit(solution)/shard_map/ppermute | solution.py:310
  14.9 4.6 %collective-permute-start.5 = (f32[192,128]{1,0:T(8,128)S(1)}, f32[192,128]{1,0:T(8,128)S(1)}, u32[]{:S(2)}, u32[]{:S(2)}) collective-permute-start(f32[192,128]{1,0:T(8,128)S(1)} %collective-permute-done.3), channel_id=1, source_target_pairs={{0,2},{1,3},{4,0},{5,1},{8,4},{9,5},{12,8},{13,9},{14,12},{15,13},... | collective-permute-start | bytes 294920 | tf_op jit(solution)/shard_map/ppermute | solution.py:310
  19.6 4.6 %collective-permute-start.8 = (f32[96,128]{1,0:T(8,128)S(1)}, f32[96,128]{1,0:T(8,128)S(1)}, u32[]{:S(2)}, u32[]{:S(2)}) collective-permute-start(f32[96,128]{1,0:T(8,128)S(1)} %slice.9), channel_id=1, source_target_pairs={{0,2},{1,3},{4,0},{5,1},{8,4},{9,5},{12,8},{13,9},{14,12},{15,13},... | collective-permute-start | bytes 147464 | tf_op jit(solution)/shard_map/ppermute | solution.py:310
  19.7 4.5 %collective-permute-start.7 = (f32[96,128]{1,0:T(8,128)S(1)}, f32[96,128]{1,0:T(8,128)S(1)}, u32[]{:S(2)}, u32[]{:S(2)}) collective-permute-start(f32[96,128]{1,0:T(8,128)S(1)} %slice.8), channel_id=1, source_target_pairs={{0,4},{1,5},{4,8},{5,9},{8,12},{9,13},{12,14},{13,15},{14,10},{15,... | collective-permute-start | bytes 147464 | tf_op jit(solution)/shard_map/ppermute | solution.py:310
  24.2 3.8 %collective-permute-start.9 = (f32[1536,128]{1,0:T(8,128)S(1)}, f32[1536,128]{1,0:T(8,128)S(1)}, u32[]{:S(2)}, u32[]{:S(2)}) collective-permute-start(f32[1536,128]{1,0:T(8,128)S(1)} %constant_dynamic-update-slice_fusion.src), channel_id=1, source_target_pairs={{0,1},{1,0},{2,3},{3,2},{4,5},{5,4},{6,7},{7,6},{8,9},{9,8},{10,11... | collective-permute-start | bytes 2359304 | tf_op jit(solution)/shard_map/ppermute | solution.py:310
  25.1 10.4 %collective-permute-start.10 = (bf16[64,4096]{1,0:T(8,128)(2,1)S(1)}, bf16[64,4096]{1,0:T(8,128)(2,1)S(1)}, u32[]{:S(2)}, u32[]{:S(2)}) collective-permute-start(bf16[64,4096]{1,0:T(8,128)(2,1)S(1)} %bitcast.18), channel_id=1, source_target_pairs={{0,4},{1,3},{4,8},{5,1},{8,12},{9,5},{12,14},{13,9},{14,10},{15,13... | collective-permute-start | bytes 1572872 | tf_op jit(solution)/shard_map/ppermute | solution.py:310
  28.1 1.4 %copy-start.5 = (s32[32]{0:T(128)S(1)}, s32[32]{0:T(128)}, u32[]{:S(2)}) copy-start(s32[32]{0:T(128)} %owner.3) | copy-start | bytes 388
  33.5 10.1 %copy-start.7 = (s32[128,8]{0,1:T(8,128)S(1)}, s32[128,8]{0,1:T(8,128)}, u32[]{:S(2)}) copy-start(s32[128,8]{0,1:T(8,128)} %param.13) | copy-start | bytes 12292
  33.5 9.2 %collective-permute-start.14 = (bf16[64,4096]{1,0:T(8,128)(2,1)S(1)}, bf16[64,4096]{1,0:T(8,128)(2,1)S(1)}, u32[]{:S(2)}, u32[]{:S(2)}) collective-permute-start(bf16[64,4096]{1,0:T(8,128)(2,1)S(1)} %precondition.2.rest_1_), channel_id=1, source_target_pairs={{0,4},{1,3},{4,8},{5,1},{8,12},{9,5},{12,14},{13,9},{14,10},{15,13... | collective-permute-start | bytes 1572872 | tf_op jit(solution)/shard_map/ppermute | solution.py:310
  35.4 11.9 %collective-permute-start.12 = (bf16[64,4096]{1,0:T(8,128)(2,1)S(1)}, bf16[64,4096]{1,0:T(8,128)(2,1)S(1)}, u32[]{:S(2)}, u32[]{:S(2)}) collective-permute-start(bf16[64,4096]{1,0:T(8,128)(2,1)S(1)} %precondition.2.rest_1_), channel_id=1, source_target_pairs={{0,1},{1,0},{2,3},{3,2},{4,5},{5,4},{6,7},{7,6},{8,9},{9,8},{10,11... | collective-permute-start | bytes 1572872 | tf_op jit(solution)/shard_map/ppermute | solution.py:310
  39.5 7.9 %collective-permute-start.13 = (bf16[64,4096]{1,0:T(8,128)(2,1)S(1)}, bf16[64,4096]{1,0:T(8,128)(2,1)S(1)}, u32[]{:S(2)}, u32[]{:S(2)}) collective-permute-start(bf16[64,4096]{1,0:T(8,128)(2,1)S(1)} %precondition.3.rest_2_), channel_id=1, source_target_pairs={{0,1},{1,0},{2,3},{3,2},{4,5},{5,4},{6,7},{7,6},{8,9},{9,8},{10,11... | collective-permute-start | bytes 1572872 | tf_op jit(solution)/shard_map/ppermute | solution.py:310
  42.7 4.6 %collective-permute-start.15 = (bf16[64,4096]{1,0:T(8,128)(2,1)S(1)}, bf16[64,4096]{1,0:T(8,128)(2,1)}, u32[]{:S(2)}, u32[]{:S(2)}) collective-permute-start(bf16[64,4096]{1,0:T(8,128)(2,1)S(1)} %collective-permute-done.14.rest_4_), channel_id=1, source_target_pairs={{0,1},{1,0},{2,3},{3,2},{4,5},{5,4},{6,7},{7,6},{8,9},{9,8},{10,11... | collective-permute-start | bytes 1572872 | tf_op jit(solution)/shard_map/ppermute | solution.py:310
  43.8 12.3 %collective-permute-start.11 = (bf16[64,4096]{1,0:T(8,128)(2,1)S(1)}, bf16[64,4096]{1,0:T(8,128)(2,1)S(1)}, u32[]{:S(2)}, u32[]{:S(2)}) collective-permute-start(bf16[64,4096]{1,0:T(8,128)(2,1)S(1)} %precondition.3.rest_2_), channel_id=1, source_target_pairs={{0,4},{1,3},{4,8},{5,1},{8,12},{9,5},{12,14},{13,9},{14,10},{15,13... | collective-permute-start | bytes 1572872 | tf_op jit(solution)/shard_map/ppermute | solution.py:310
  45.8 12.9 %collective-permute-start.18 = (bf16[64,4096]{1,0:T(8,128)(2,1)S(1)}, bf16[64,4096]{1,0:T(8,128)(2,1)S(1)}, u32[]{:S(2)}, u32[]{:S(2)}) collective-permute-start(bf16[64,4096]{1,0:T(8,128)(2,1)S(1)} %collective-permute-done.14.rest_4_), channel_id=1, source_target_pairs={{0,4},{1,3},{4,8},{5,1},{8,12},{9,5},{12,14},{13,9},{14,10},{15,13... | collective-permute-start | bytes 1572872 | tf_op jit(solution)/shard_map/ppermute | solution.py:310
  47.5 3.4 %copy-start = (bf16[128,8,4096]{2,1,0:T(8,128)(2,1)S(1)}, bf16[128,8,4096]{2,1,0:T(8,128)(2,1)}, u32[]{:S(2)}) copy-start(bf16[128,8,4096]{2,1,0:T(8,128)(2,1)} %param.12) | copy-start | bytes 25165828
  56.1 6.0 %collective-permute-start.17 = (bf16[64,4096]{1,0:T(8,128)(2,1)S(1)}, bf16[64,4096]{1,0:T(8,128)(2,1)S(1)}, u32[]{:S(2)}, u32[]{:S(2)}) collective-permute-start(bf16[64,4096]{1,0:T(8,128)(2,1)S(1)} %collective-permute-done.11.rest_0_), channel_id=1, source_target_pairs={{0,1},{1,0},{2,3},{3,2},{4,5},{5,4},{6,7},{7,6},{8,9},{9,8},{10,11... | collective-permute-start | bytes 1572872 | tf_op jit(solution)/shard_map/ppermute | solution.py:310
  58.7 3.5 %collective-permute-start.19 = (bf16[64,4096]{1,0:T(8,128)(2,1)S(1)}, bf16[64,4096]{1,0:T(8,128)(2,1)S(1)}, u32[]{:S(2)}, u32[]{:S(2)}) collective-permute-start(bf16[64,4096]{1,0:T(8,128)(2,1)S(1)} %collective-permute-done.18.rest_2_), channel_id=1, source_target_pairs={{0,1},{1,0},{2,3},{3,2},{4,5},{5,4},{6,7},{7,6},{8,9},{9,8},{10,11... | collective-permute-start | bytes 1572872 | tf_op jit(solution)/shard_map/ppermute | solution.py:310
  58.7 10.3 %collective-permute-start.16 = (bf16[64,4096]{1,0:T(8,128)(2,1)S(1)}, bf16[64,4096]{1,0:T(8,128)(2,1)S(1)}, u32[]{:S(2)}, u32[]{:S(2)}) collective-permute-start(bf16[64,4096]{1,0:T(8,128)(2,1)S(1)} %collective-permute-done.11.rest_0_), channel_id=1, source_target_pairs={{0,4},{1,3},{4,8},{5,1},{8,12},{9,5},{12,14},{13,9},{14,10},{15,13... | collective-permute-start | bytes 1572872 | tf_op jit(solution)/shard_map/ppermute | solution.py:310
  60.6 12.9 %collective-permute-start.22 = (bf16[64,4096]{1,0:T(8,128)(2,1)S(1)}, bf16[64,4096]{1,0:T(8,128)(2,1)S(1)}, u32[]{:S(2)}, u32[]{:S(2)}) collective-permute-start(bf16[64,4096]{1,0:T(8,128)(2,1)S(1)} %collective-permute-done.18.rest_2_), channel_id=1, source_target_pairs={{0,4},{1,3},{4,8},{5,1},{8,12},{9,5},{12,14},{13,9},{14,10},{15,13... | collective-permute-start | bytes 1572872 | tf_op jit(solution)/shard_map/ppermute | solution.py:310
  62.1 3.4 %copy-start.1 = (bf16[128,8,4096]{2,1,0:T(8,128)(2,1)S(1)}, bf16[128,8,4096]{2,1,0:T(8,128)(2,1)}, u32[]{:S(2)}) copy-start(bf16[128,8,4096]{2,1,0:T(8,128)(2,1)} %param.12) | copy-start | bytes 25165828
  69.0 6.4 %collective-permute-start.21 = (bf16[64,4096]{1,0:T(8,128)(2,1)S(1)}, bf16[64,4096]{1,0:T(8,128)(2,1)S(1)}, u32[]{:S(2)}, u32[]{:S(2)}) collective-permute-start(bf16[64,4096]{1,0:T(8,128)(2,1)S(1)} %collective-permute-done.16.rest_0_), channel_id=1, source_target_pairs={{0,1},{1,0},{2,3},{3,2},{4,5},{5,4},{6,7},{7,6},{8,9},{9,8},{10,11... | collective-permute-start | bytes 1572872 | tf_op jit(solution)/shard_map/ppermute | solution.py:310
  73.5 1.9 %collective-permute-start.23 = (bf16[64,4096]{1,0:T(8,128)(2,1)S(1)}, bf16[64,4096]{1,0:T(8,128)(2,1)S(1)}, u32[]{:S(2)}, u32[]{:S(2)}) collective-permute-start(bf16[64,4096]{1,0:T(8,128)(2,1)S(1)} %collective-permute-done.22.rest_2_), channel_id=1, source_target_pairs={{0,1},{1,0},{2,3},{3,2},{4,5},{5,4},{6,7},{7,6},{8,9},{9,8},{10,11... | collective-permute-start | bytes 1572872 | tf_op jit(solution)/shard_map/ppermute | solution.py:310
  73.5 9.2 %collective-permute-start.20 = (bf16[64,4096]{1,0:T(8,128)(2,1)S(1)}, bf16[64,4096]{1,0:T(8,128)(2,1)S(1)}, u32[]{:S(2)}, u32[]{:S(2)}) collective-permute-start(bf16[64,4096]{1,0:T(8,128)(2,1)S(1)} %collective-permute-done.16.rest_0_), channel_id=1, source_target_pairs={{0,4},{1,3},{4,8},{5,1},{8,12},{9,5},{12,14},{13,9},{14,10},{15,13... | collective-permute-start | bytes 1572872 | tf_op jit(solution)/shard_map/ppermute | solution.py:310
  82.7 1.9 %collective-permute-start.24 = (bf16[64,4096]{1,0:T(8,128)(2,1)S(1)}, bf16[64,4096]{1,0:T(8,128)(2,1)S(1)}, u32[]{:S(2)}, u32[]{:S(2)}) collective-permute-start(bf16[64,4096]{1,0:T(8,128)(2,1)S(1)} %collective-permute-done.20.rest_0_), channel_id=1, source_target_pairs={{0,1},{1,0},{2,3},{3,2},{4,5},{5,4},{6,7},{7,6},{8,9},{9,8},{10,11... | collective-permute-start | bytes 1572872 | tf_op jit(solution)/shard_map/ppermute | solution.py:310

commit v5 on v4

--- a/solution.py
+++ b/solution.py
@@ -75,29 +75,34 @@
         out_specs=[vm] * 5,
         input_output_aliases={1 + i: i for i in range(len(tables))},
         compiler_params=pltpu.CompilerParams(vmem_limit_bytes=4 * MIB),
-        cost_estimate=pl.CostEstimate(flops=10**9, bytes_accessed=4 * MIB, transcendentals=0),
+        cost_estimate=pl.CostEstimate(flops=1000, bytes_accessed=1000, transcendentals=0),
         name="prepare",
     )(src, *tables)
 
 
-def pack_kernel(s, a, lam, out):
-    for i, m in enumerate((s, a, lam)):
-        for p in range(m.shape[0] // 2):
+def pack_kernel(s, a, lam, out, held, sems):
+    copies = [pltpu.make_async_copy(m, held.at[i], sems.at[i]) for i, m in enumerate((s, a, lam))]
+    for copy in copies:
+        copy.start()
+    for i, copy in enumerate(copies):
+        copy.wait()
+        for p in range(s.shape[0] // 2):
             first = (3 * p + i) * 64
-            out[first : first + 64, :] = jnp.concatenate([m[2 * p], m[2 * p + 1]], axis=1)
-
-
-def pack_factors(s, a, lam):
-    vm = pl.BlockSpec(memory_space=pltpu.VMEM)
+            out[first : first + 64, :] = jnp.concatenate([held[i, 2 * p], held[i, 2 * p + 1]], axis=1)
+
+
+def pack_factors(*factors):
+    slots = factors[0].shape[0]
     return pl.pallas_call(
         pack_kernel,
-        out_shape=jax.ShapeDtypeStruct((s.shape[0] * 96, 128), F32),
-        in_specs=[vm] * 3,
-        out_specs=vm,
+        out_shape=jax.ShapeDtypeStruct((slots * 96, 128), F32),
+        in_specs=[pl.BlockSpec(memory_space=pltpu.HBM)] * 3,
+        out_specs=pl.BlockSpec(memory_space=pltpu.VMEM),
+        scratch_shapes=[pltpu.VMEM((3, slots, 64, 64), F32), pltpu.SemaphoreType.DMA((3,))],
         compiler_params=pltpu.CompilerParams(vmem_limit_bytes=4 * MIB),
-        cost_estimate=pl.CostEstimate(flops=10**5, bytes_accessed=10**5, transcendentals=0),
+        cost_estimate=pl.CostEstimate(flops=1000, bytes_accessed=1000, transcendentals=0),
         name="pack",
-    )(s, a, lam)
+    )(*[pltpu.with_memory_space_constraint(m, pltpu.HBM) for m in factors])
 
 
 def precondition_kernel(units, routes, owner, info, tab_a, tab_at, tab_s, tab_st, scale, *rest):
@@ -173,9 +178,7 @@
         out_specs=[vm] * chunks,
         scratch_shapes=[pltpu.VMEM((32 * STRIDE, 128), F32), pltpu.VMEM((32 * STRIDE, 128), F32)],
         compiler_params=pltpu.CompilerParams(vmem_limit_bytes=8 * MIB),
-        cost_estimate=pl.CostEstimate(
-            flops=10**9 * 3 * chunks, bytes_accessed=10**6 * (7 + chunks), transcendentals=0
-        ),
+        cost_estimate=pl.CostEstimate(flops=1000, bytes_accessed=1000, transcendentals=0),
         name="precondition",
     )(routes, owner, info, *tables, *raws)
 
@@ -242,11 +245,7 @@
             pltpu.VMEM((blocks * 8, train_rows), F32),
         ],
         compiler_params=pltpu.CompilerParams(vmem_limit_bytes=14 * MIB),
-        cost_estimate=pl.CostEstimate(
-            flops=4 * 128 * max(2, blocks) * train_rows * width // 2,
-            bytes_accessed=2 * train_rows * width,
-            transcendentals=0,
-        ),
+        cost_estimate=pl.CostEstimate(flops=1000, bytes_accessed=1000, transcendentals=0),
         name="products",
     )(info, route, query_route, train, *parts, *old)
 
@@ -312,13 +311,21 @@
     raw = query_grads.transpose(1, 0, 2).reshape(-1, width)
     other_raw = send(raw, across)
 
+    live = jnp.arange(train_dev, dtype=jnp.int32) < train_counts[0]
+    route = jnp.where(live[:, None], train_routes, -1).reshape(1, train_dev * top)
+    train = train_grads.reshape(train_dev * top, width)
+    query_route = query_routes.reshape(devices, 8, top).transpose(0, 2, 1).reshape(queries * top, 1)
+    query_route = jnp.broadcast_to(query_route, (queries * top, 128))
+
     pack = pack_factors(basis_s, basis_a, eigenvalues)
     got, up, down = [pack], pack, pack
     cut = pack.shape[0] // 2
     for step in range(1, far + 1):
+        if step == 3:
+            up = tie(up, (other_raw, info, route, query_route))
         if step == far:
             up, down = up[:cut], down[cut:]
-            raw, up = tie(raw, got[-1]), tie(up, other_raw)
+            raw = tie(raw, got[-1])
         up, down = send(up, ahead), send(down, back)
         got += [up, down]
     a = send(raw, stream)
@@ -326,39 +333,32 @@
     sib = send(mine, across)
     tables = prepare(sib, experts, experts // 2, prepare(mine, experts, 0))
 
-    live = jnp.arange(train_dev, dtype=jnp.int32) < train_counts[0]
-    route = jnp.where(live[:, None], train_routes, -1).reshape(1, train_dev * top)
-    train = train_grads.reshape(train_dev * top, width)
-    query_route = query_routes.reshape(devices, 8, top).transpose(0, 2, 1).reshape(queries * top, 1)
-    query_route = jnp.broadcast_to(query_route, (queries * top, 128))
-
-    pre = lambda raws, names: precondition(query_routes, owner_slot, info, tables, raws, names)
-    multiply = lambda parts, names, **more: products(
-        info, experts, route, query_route, train, parts, names, **more
-    )
+    pre = lambda *args: precondition(query_routes, owner_slot, info, tables, *args)
     (b,) = pre([other_raw], [1])
     held, names = [send(b, across), b], [0, 1]
     (a,) = pre([tie(a, b)], [4])
     b = send(b, stream)
+    multiply = lambda parts, names, **more: products(
+        info, experts, route, query_route, train, parts, names, **more
+    )
+    held += [a, send(a, across)]
+    names += [4, 6]
     done, placed = [], []
-    for step in range(1, far):
-        if done:
-            a = tie(a, done[-1])
-        next_a = send(a, stream)
-        held += [a, send(a, across)]
-        if step < far - 1:
-            next_b = send(b, stream)
-        held += [b, send(b, across)]
-        names += [4 * step, 4 * step + 2, 4 * step + 1, 4 * step + 3]
-        a, b = next_a, next_b
-        if step > 1 or far < 4:
-            pass
+    coming = [(b, 5), (send(a, stream), 8)]
+    while len(coming) > 1 or coming[0][1] < 4 * far:
+        (now, name), (after, after_name) = coming
+        if name // 4 < far - 1:
+            further = [(send(now, stream), name + 4)]
+        else:
+            further = [(send(now, stream), 4 * far)] if name % 4 == 0 else []
+        held[0] = tie(held[0], now)
         done.append(multiply(held, names))
         placed.append(names)
-        held, names = [], []
-    if done:
-        a = tie(a, done[-1])
-    return multiply([a, send(a, across)], [4 * far, 4 * far + 2], old=done, placed=placed, queries=queries)
+        held, names = [now, send(now, across)], [name, name + 2]
+        coming = [(tie(after, done[-1]), after_name)] + further
+    now, name = coming[0]
+    held += [now, send(now, across)]
+    return multiply(held, names + [name, name + 2], old=done, placed=placed, queries=queries)
 
 
 def solution(mesh):

time: 89.5 us -> 78.2 us (0.87)
  local copies, waits for them, and re-layouts: 12.1 us -> 3.51 us
  Pallas kernels: 27.4 us -> 34.9 us
  starting transfers between devices: 22.5 us -> 15.6 us
  waiting for transfers between devices: 26.2 us -> 22.2 us
    unnamed x25 -> x19, local copies, waits for them, and re-layouts: 9.46 us -> 0.19 us
    ppermute x25, starting transfers between devices: 22.5 us -> 15.6 us  [local(): send = lambda v, way: lax.ppermute(v, 'shard', way)]
    pallas_call x4 -> x6, Pallas kernels: 16.6 us -> 22.9 us  [products(): pl.pallas_call(functools.partial(products_kernel, units, placed, shapes,...]
    ppermute x25, waiting for transfers between devices: 26.2 us -> 22.2 us  [local(): send = lambda v, way: lax.ppermute(v, 'shard', way)]
    pallas_call x1, Pallas kernels: 0.09 us -> 1.11 us  [pack_factors(): pl.pallas_call(pack_kernel, out_shape=jax.ShapeDtypeStruct((slots * 96, 1...]
  transfers between devices with their start and end apart: 25 -> 25, of which waited for: 9 -> 14; matrix products, arithmetic and copies ran while one was open for 3% -> 5% of each run, Pallas kernels for 26% -> 38%
where the time goes in v5:
time: 78.2 us; the launch traced here: 77.9 us
  Pallas kernels  34.9 us (45%)
  waiting for transfers between devices  22.2 us (28%)
  starting transfers between devices  15.6 us (20%)
  local copies, waits for them, and re-layouts  3.51 us (4%)
  between operations  0.96 us (1%)
    pallas_call x6, Pallas kernels, products(): pl.pallas_call(functools.partial(products_kernel, units, placed, shapes,...  22.9 us
    ppermute x25, waiting for transfers between devices, local(): send = lambda v, way: lax.ppermute(v, 'shard', way)  22.2 us
    ppermute x25, starting transfers between devices, local(): send = lambda v, way: lax.ppermute(v, 'shard', way)  15.6 us
    pallas_call x2, Pallas kernels, precondition(): pl.pallas_call(functools.partial(precondition_kernel, units), out_shape=[...  8.09 us
    pallas_call x2, Pallas kernels, prepare(): pl.pallas_call(functools.partial(prepare_kernel, at, experts // 2), out_s...  2.73 us
  transfers between devices with their start and end apart: 25, of which 14 were waited for; matrix products, arithmetic and copies ran while one was open for 5% of the time, Pallas kernels for 38%

profile of v5, /device:TPU:0, one launch (start us, length us, event | category | flops | bytes accessed | tf_op | source)
XLA Modules:
  0.0 77.9 jit_solution(14350979291649926345)
XLA Ops:
  0.0 1.1 %pack.1 = f32[192,128]{1,0:T(8,128)S(1)} custom-call(f32[2,64,64]{2,1,0:T(8,128)} %s.1, f32[2,64,64]{2,1,0:T(8,128)} %a.1, f32[2,64,64]{2,1,0:T(8,128)} %lam.1), custom_call_target="tpu_custom_call" | custom-call | flops 1000 | bytes 1000 | tf_op jit(solution)/shard_map/pack/pallas_call | solution.py:96
  1.1 3.0 %collective-permute-start.1 = (f32[192,128]{1,0:T(8,128)S(1)}, f32[192,128]{1,0:T(8,128)S(1)}, u32[]{:S(2)}, u32[]{:S(2)}) collective-permute-start(f32[192,128]{1,0:T(8,128)S(1)} %pack.1), channel_id=1, source_target_pairs={{0,2},{1,3},{4,0},{5,1},{8,4},{9,5},{12,8},{13,9},{14,12},{15,13},... | collective-permute-start | bytes 294920 | tf_op jit(solution)/shard_map/ppermute | solution.py:309
  4.1 0.1 collective-permute-start
  4.3 1.3 %copy.26 = bf16[8,8,4096]{2,1,0:T(8,128)(2,1)S(1)} copy(bf16[8,8,4096]{2,0,1:T(8,128)(2,1)} %bitcast.20) | data formatting | bytes 1048576 | tf_op jit(solution)/shard_map/transpose | solution.py:311
  5.6 0.1 collective-permute-start.4
  6.4 0.7 broadcast_select_fusion
  7.1 0.1 copy.20
  7.2 0.1 reshape.18.route
  7.3 0.8 reshape.19
  8.1 0.1 broadcast_in_dim.22
  8.2 0.7 dynamic-slice_bitcast_fusion.info
  8.9 0.0 collective-permute-done.1
  8.9 1.9 %collective-permute-start.3 = (f32[192,128]{1,0:T(8,128)S(1)}, f32[192,128]{1,0:T(8,128)S(1)}, u32[]{:S(2)}, u32[]{:S(2)}) collective-permute-start(f32[192,128]{1,0:T(8,128)S(1)} %collective-permute-done.1), channel_id=1, source_target_pairs={{0,2},{1,3},{4,0},{5,1},{8,4},{9,5},{12,8},{13,9},{14,12},{15,13},... | collective-permute-start | bytes 294920 | tf_op jit(solution)/shard_map/ppermute | solution.py:309
  10.8 0.0 collective-permute-done
  10.8 0.1 collective-permute-start.2
  11.0 3.3 %collective-permute-done.3 = f32[192,128]{1,0:T(8,128)S(1)} collective-permute-done((f32[192,128]{1,0:T(8,128)S(1)}, f32[192,128]{1,0:T(8,128)S(1)}, u32[]{:S(2)}, u32[]{:S(2)}) %collective-permute-start.3) | collective-permute-done | bytes 98336 | tf_op jit(solution)/shard_map/ppermute | solution.py:309
  14.3 1.7 %collective-permute-start.6 = (f32[192,128]{1,0:T(8,128)S(1)}, f32[192,128]{1,0:T(8,128)S(1)}, u32[]{:S(2)}, u32[]{:S(2)}) collective-permute-start(f32[192,128]{1,0:T(8,128)S(1)} %collective-permute-done.3), channel_id=1, source_target_pairs={{0,2},{1,3},{4,0},{5,1},{8,4},{9,5},{12,8},{13,9},{14,12},{15,13},... | collective-permute-start | bytes 294920 | tf_op jit(solution)/shard_map/ppermute | solution.py:309
  16.0 0.0 collective-permute-done.2
  16.0 0.0 collective-permute-done.4.rest_0_
  16.0 0.2 broadcast_in_dim.23.query_route
  16.2 0.4 collective-permute-start.5
  16.6 2.3 %collective-permute-done.6 = f32[192,128]{1,0:T(8,128)S(1)} collective-permute-done((f32[192,128]{1,0:T(8,128)S(1)}, f32[192,128]{1,0:T(8,128)S(1)}, u32[]{:S(2)}, u32[]{:S(2)}) %collective-permute-start.6) | collective-permute-done | bytes 98336 | tf_op jit(solution)/shard_map/ppermute | solution.py:309
  18.9 1.7 %collective-permute-start.8 = (f32[96,128]{1,0:T(8,128)S(1)}, f32[96,128]{1,0:T(8,128)S(1)}, u32[]{:S(2)}, u32[]{:S(2)}) collective-permute-start(f32[96,128]{1,0:T(8,128)S(1)} %slice.9), channel_id=1, source_target_pairs={{0,2},{1,3},{4,0},{5,1},{8,4},{9,5},{12,8},{13,9},{14,12},{15,13},... | collective-permute-start | bytes 147464 | tf_op jit(solution)/shard_map/ppermute | solution.py:309
  20.6 0.3 collective-permute-done.5
  20.9 0.3 collective-permute-start.7
  21.2 3.7 %collective-permute-done.7 = f32[96,128]{1,0:T(8,128)S(1)} collective-permute-done((f32[96,128]{1,0:T(8,128)S(1)}, f32[96,128]{1,0:T(8,128)S(1)}, u32[]{:S(2)}, u32[]{:S(2)}) %collective-permute-start.7) | collective-permute-done | bytes 49184 | tf_op jit(solution)/shard_map/ppermute | solution.py:309
  25.0 0.0 collective-permute-done.8
  25.0 0.1 collective-permute-start.9
  25.1 0.4 collective-permute-start.12
  25.5 0.1 copy.23.routes
  25.6 1.4 %prepare.2 = (bf16[32,2,128,128]{3,2,1,0:T(8,128)(2,1)S(1)}, bf16[32,2,128,128]{3,2,1,0:T(8,128)(2,1)S(1)}, bf16[32,64,256]{2,1,0:T(8,128)(2,1)S(1)}, bf16[32,64,256]{2,1,0:T(8,128)(2,1)S(1)}, f32[32,64,128]{2,1,0:T(8,128)S(1)}) custom-call(f32[1536,128]{1,0:T(8,128)S(1)} %constant_dynamic-update-slice_fusion.src), custom_call_target="tpu_custom_call" | custom-call | flops 1000 | bytes 1000 | tf_op jit(solution)/shard_map/prepare/pallas_call | solution.py:65
  26.9 0.4 collective-permute-done.9.src
  27.3 1.4 %prepare.3 = (bf16[32,2,128,128]{3,2,1,0:T(8,128)(2,1)S(1)}, bf16[32,2,128,128]{3,2,1,0:T(8,128)(2,1)S(1)}, bf16[32,64,256]{2,1,0:T(8,128)(2,1)S(1)}, bf16[32,64,256]{2,1,0:T(8,128)(2,1)S(1)}, f32[32,64,128]{2,1,0:T(8,128)S(1)}) custom-call(f32[1536,128]{1,0:T(8,128)S(1)} %collective-permute-done, ...), custom_call_target="tpu_custom_call", output_to_operand_aliasing={{0}: (1, {}), {1}: (2, {}), {2}: (3, {}), {3}: (4, {}), {4}... | custom-call | flops 1000 | bytes 1000 | tf_op jit(solution)/shard_map/prepare/pallas_call | solution.py:65
  28.7 0.0 slice-start
  28.7 4.1 %precondition.2.rest_1_ = bf16[64,4096]{1,0:T(8,128)(2,1)S(1)} custom-call(s32[128,8]{1,0:T(8,128)S(1)} %copy.23.routes, s32[32]{0:T(128)S(1)} %copy-done, s32[52]{0:T(128)S(1)} %dynamic-slice_bitcast_fusion.info, bf16[32,2,128,128]{3,2,1,0:T(8,128)(2,1)S(1)} %get-tuple-element.34.tab_a, bf16[32,2,128,128]{3,2,1,0:T(8,128)(2,1)S(1)} %get-tuple-element.35.tab_at, ...), custom_call_target="tpu_custom_call" | custom-call | flops 1000 | bytes 1000 | tf_op jit(solution)/shard_map/precondition/pallas_call | solution.py:174
  32.8 0.0 slice-start.1
  32.8 1.1 %collective-permute-start.14 = (bf16[64,4096]{1,0:T(8,128)(2,1)S(1)}, bf16[64,4096]{1,0:T(8,128)(2,1)S(1)}, u32[]{:S(2)}, u32[]{:S(2)}) collective-permute-start(bf16[64,4096]{1,0:T(8,128)(2,1)S(1)} %precondition.2.rest_1_), channel_id=1, source_target_pairs={{0,1},{1,0},{2,3},{3,2},{4,5},{5,4},{6,7},{7,6},{8,9},{9,8},{10,11... | collective-permute-start | bytes 1572872 | tf_op jit(solution)/shard_map/ppermute | solution.py:309
  33.9 0.4 collective-permute-start.10
  34.3 0.2 collective-permute-done.12.rest_0_
  34.5 4.0 %precondition.3.rest_2_ = bf16[64,4096]{1,0:T(8,128)(2,1)S(1)} custom-call(s32[128,8]{1,0:T(8,128)S(1)} %copy.23.routes, s32[32]{0:T(128)S(1)} %copy-done, s32[52]{0:T(128)S(1)} %dynamic-slice_bitcast_fusion.info, bf16[32,2,128,128]{3,2,1,0:T(8,128)(2,1)S(1)} %get-tuple-element.34.tab_a, bf16[32,2,128,128]{3,2,1,0:T(8,128)(2,1)S(1)} %get-tuple-element.35.tab_at, ...), custom_call_target="tpu_custom_call" | custom-call | flops 1000 | bytes 1000 | tf_op jit(solution)/shard_map/precondition/pallas_call | solution.py:174
  38.6 0.8 %collective-permute-start.15 = (bf16[64,4096]{1,0:T(8,128)(2,1)S(1)}, bf16[64,4096]{1,0:T(8,128)(2,1)S(1)}, u32[]{:S(2)}, u32[]{:S(2)}) collective-permute-start(bf16[64,4096]{1,0:T(8,128)(2,1)S(1)} %precondition.3.rest_2_), channel_id=1, source_target_pairs={{0,1},{1,0},{2,3},{3,2},{4,5},{5,4},{6,7},{7,6},{8,9},{9,8},{10,11... | collective-permute-start | bytes 1572872 | tf_op jit(solution)/shard_map/ppermute | solution.py:309
  39.4 0.7 collective-permute-start.13
  40.1 0.0 collective-permute-done.14.rest_0_
  40.1 3.0 %collective-permute-done.10.rest_0_ = bf16[64,4096]{1,0:T(8,128)(2,1)S(1)} collective-permute-done((bf16[64,4096]{1,0:T(8,128)(2,1)S(1)}, bf16[64,4096]{1,0:T(8,128)(2,1)S(1)}, u32[]{:S(2)}, u32[]{:S(2)}) %collective-permute-start.10) | collective-permute-done | bytes 524320 | tf_op jit(solution)/shard_map/ppermute | solution.py:309
  43.1 0.4 collective-permute-start.11
  43.5 3.5 %products.6.rest_4_ = f32[32,128]{1,0:T(8,128)S(1)} custom-call(s32[52]{0:T(128)S(1)} %dynamic-slice_bitcast_fusion.info, s32[1,1024]{1,0:T(1,128)S(1)} %reshape.18.route, s32[1024,128]{1,0:T(8,128)S(1)} %broadcast_in_dim.23.query_route, bf16[1024,4096]{1,0:T(8,128)(2,1)S(1)} %bitcast.14, bf16[64,4096]{1,0:T(8,128)(2,1)S(1)} %collective-permute-done.14.rest_0_, ...), custom_call_target="tpu_custom_call" | custom-call | flops 1000 | bytes 1000 | tf_op jit(solution)/shard_map/products/pallas_call | solution.py:238
  47.0 1.7 %collective-permute-done.13.rest_0_ = bf16[64,4096]{1,0:T(8,128)(2,1)S(1)} collective-permute-done((bf16[64,4096]{1,0:T(8,128)(2,1)S(1)}, bf16[64,4096]{1,0:T(8,128)(2,1)S(1)}, u32[]{:S(2)}, u32[]{:S(2)}) %collective-permute-start.13) | collective-permute-done | bytes 524320 | tf_op jit(solution)/shard_map/ppermute | solution.py:309
  48.7 0.6 collective-permute-start.18
  49.3 3.8 %products.7.rest_5_ = f32[16,128]{1,0:T(8,128)S(1)} custom-call(s32[52]{0:T(128)S(1)} %dynamic-slice_bitcast_fusion.info, s32[1,1024]{1,0:T(1,128)S(1)} %reshape.18.route, s32[1024,128]{1,0:T(8,128)S(1)} %broadcast_in_dim.23.query_route, bf16[1024,4096]{1,0:T(8,128)(2,1)S(1)} %bitcast.15, bf16[64,4096]{1,0:T(8,128)(2,1)S(1)} %collective-permute-done.10.rest_0_, ...), custom_call_target="tpu_custom_call" | custom-call | flops 1000 | bytes 1000 | tf_op jit(solution)/shard_map/products/pallas_call | solution.py:238
  53.1 1.2 %collective-permute-done.11.rest_0_ = bf16[64,4096]{1,0:T(8,128)(2,1)S(1)} collective-permute-done((bf16[64,4096]{1,0:T(8,128)(2,1)S(1)}, bf16[64,4096]{1,0:T(8,128)(2,1)S(1)}, u32[]{:S(2)}, u32[]{:S(2)}) %collective-permute-start.11) | collective-permute-done | bytes 524320 | tf_op jit(solution)/shard_map/ppermute | solution.py:309
  54.3 0.1 collective-permute-start.20
  54.4 0.4 collective-permute-start.17
  54.9 3.8 %products.8.rest_6_ = f32[16,128]{1,0:T(8,128)S(1)} custom-call(s32[52]{0:T(128)S(1)} %dynamic-slice_bitcast_fusion.info, s32[1,1024]{1,0:T(1,128)S(1)} %reshape.18.route, s32[1024,128]{1,0:T(8,128)S(1)} %broadcast_in_dim.23.query_route, bf16[1024,4096]{1,0:T(8,128)(2,1)S(1)} %bitcast.16, bf16[64,4096]{1,0:T(8,128)(2,1)S(1)} %collective-permute-done.13.rest_0_, ...), custom_call_target="tpu_custom_call" | custom-call | flops 1000 | bytes 1000 | tf_op jit(solution)/shard_map/products/pallas_call | solution.py:238
  58.7 1.2 %collective-permute-done.18.rest_0_ = bf16[64,4096]{1,0:T(8,128)(2,1)S(1)} collective-permute-done((bf16[64,4096]{1,0:T(8,128)(2,1)S(1)}, bf16[64,4096]{1,0:T(8,128)(2,1)S(1)}, u32[]{:S(2)}, u32[]{:S(2)}) %collective-permute-start.18) | collective-permute-done | bytes 524320 | tf_op jit(solution)/shard_map/ppermute | solution.py:309
  59.9 0.1 collective-permute-start.23
  60.1 0.6 collective-permute-start.22
  60.6 3.8 %products.9.rest_7_ = f32[16,128]{1,0:T(8,128)S(1)} custom-call(s32[52]{0:T(128)S(1)} %dynamic-slice_bitcast_fusion.info, s32[1,1024]{1,0:T(1,128)S(1)} %reshape.18.route, s32[1024,128]{1,0:T(8,128)S(1)} %broadcast_in_dim.23.query_route, bf16[1024,4096]{1,0:T(8,128)(2,1)S(1)} %bitcast.17, bf16[64,4096]{1,0:T(8,128)(2,1)S(1)} %collective-permute-done.11.rest_0_, ...), custom_call_target="tpu_custom_call" | custom-call | flops 1000 | bytes 1000 | tf_op jit(solution)/shard_map/products/pallas_call | solution.py:238
  64.5 1.1 %collective-permute-done.17.rest_0_ = bf16[64,4096]{1,0:T(8,128)(2,1)S(1)} collective-permute-done((bf16[64,4096]{1,0:T(8,128)(2,1)S(1)}, bf16[64,4096]{1,0:T(8,128)(2,1)S(1)}, u32[]{:S(2)}, u32[]{:S(2)}) %collective-permute-start.17) | collective-permute-done | bytes 524320 | tf_op jit(solution)/shard_map/ppermute | solution.py:309
  65.5 3.8 %products.10.rest_8_ = f32[16,128]{1,0:T(8,128)S(1)} custom-call(s32[52]{0:T(128)S(1)} %dynamic-slice_bitcast_fusion.info, s32[1,1024]{1,0:T(1,128)S(1)} %reshape.18.route, s32[1024,128]{1,0:T(8,128)S(1)} %broadcast_in_dim.23.query_route, bf16[1024,4096]{1,0:T(8,128)(2,1)S(1)} %bitcast.18, bf16[64,4096]{1,0:T(8,128)(2,1)S(1)} %collective-permute-done.18.rest_0_, ...), custom_call_target="tpu_custom_call" | custom-call | flops 1000 | bytes 1000 | tf_op jit(solution)/shard_map/products/pallas_call | solution.py:238
  69.4 1.8 %collective-permute-done.22.rest_2_ = bf16[64,4096]{1,0:T(8,128)(2,1)S(1)} collective-permute-done((bf16[64,4096]{1,0:T(8,128)(2,1)S(1)}, bf16[64,4096]{1,0:T(8,128)(2,1)S(1)}, u32[]{:S(2)}, u32[]{:S(2)}) %collective-permute-start.22) | collective-permute-done | bytes 524320 | tf_op jit(solution)/shard_map/ppermute | solution.py:309
  71.2 0.5 collective-permute-start.21
  71.7 1.4 %collective-permute-done.24.rest_3_ = bf16[64,4096]{1,0:T(8,128)(2,1)S(1)} collective-permute-done((bf16[64,4096]{1,0:T(8,128)(2,1)S(1)}, bf16[64,4096]{1,0:T(8,128)(2,1)S(1)}, u32[]{:S(2)}, u32[]{:S(2)}) %collective-permute-start.24) | collective-permute-done | bytes 524320 | tf_op jit(solution)/shard_map/ppermute | solution.py:309
  73.1 0.7 collective-permute-done.21.rest_1_
  73.8 4.1 %products.11 = f32[128,128]{1,0:T(8,128)} custom-call(s32[52]{0:T(128)S(1)} %dynamic-slice_bitcast_fusion.info, s32[1,1024]{1,0:T(1,128)S(1)} %reshape.18.route, s32[1024,128]{1,0:T(8,128)S(1)} %broadcast_in_dim.23.query_route, bf16[1024,4096]{1,0:T(8,128)(2,1)S(1)} %bitcast.19, bf16[64,4096]{1,0:T(8,128)(2,1)S(1)} %collective-permute-done.17.rest_0_, ...), custom_call_target="tpu_custom_call" | custom-call | flops 1000 | bytes 1000 | tf_op jit(solution)/shard_map/products/pallas_call | solution.py:238
  (30 shorter events, 0.1 us)
Async XLA Ops:
  0.0 25.5 %copy-start.2 = (s32[128,8]{0,1:T(8,128)S(1)}, s32[128,8]{0,1:T(8,128)}, u32[]{:S(2)}) copy-start(s32[128,8]{0,1:T(8,128)} %param.11) | copy-start | bytes 12292
  1.1 7.8 %collective-permute-start.1 = (f32[192,128]{1,0:T(8,128)S(1)}, f32[192,128]{1,0:T(8,128)S(1)}, u32[]{:S(2)}, u32[]{:S(2)}) collective-permute-start(f32[192,128]{1,0:T(8,128)S(1)} %pack.1), channel_id=1, source_target_pairs={{0,2},{1,3},{4,0},{5,1},{8,4},{9,5},{12,8},{13,9},{14,12},{15,13},... | collective-permute-start | bytes 294920 | tf_op jit(solution)/shard_map/ppermute | solution.py:309
  4.1 6.7 %collective-permute-start = (f32[192,128]{1,0:T(8,128)S(1)}, f32[192,128]{1,0:T(8,128)S(1)}, u32[]{:S(2)}, u32[]{:S(2)}) collective-permute-start(f32[192,128]{1,0:T(8,128)S(1)} %pack.1), channel_id=1, source_target_pairs={{0,4},{1,5},{4,8},{5,9},{8,12},{9,13},{12,14},{13,15},{14,10},{15,... | collective-permute-start | bytes 294920 | tf_op jit(solution)/shard_map/ppermute | solution.py:309
  5.6 19.4 %copy-start.1 = (bf16[8,8,4096]{2,1,0:T(8,128)(2,1)}, bf16[8,8,4096]{2,1,0:T(8,128)(2,1)S(1)}, u32[]{:S(2)}) copy-start(bf16[8,8,4096]{2,1,0:T(8,128)(2,1)S(1)} %copy.26) | copy-start | bytes 1572868
  5.6 10.4 %collective-permute-start.4 = (bf16[64,4096]{1,0:T(8,128)(2,1)S(1)}, bf16[64,4096]{1,0:T(8,128)(2,1)S(1)}, u32[]{:S(2)}, u32[]{:S(2)}) collective-permute-start(bf16[64,4096]{1,0:T(8,128)(2,1)S(1)} %bitcast.21), channel_id=1, source_target_pairs={{0,1},{1,0},{2,3},{3,2},{4,5},{5,4},{6,7},{7,6},{8,9},{9,8},{10,11... | collective-permute-start | bytes 1572872 | tf_op jit(solution)/shard_map/ppermute | solution.py:309
  8.9 5.4 %collective-permute-start.3 = (f32[192,128]{1,0:T(8,128)S(1)}, f32[192,128]{1,0:T(8,128)S(1)}, u32[]{:S(2)}, u32[]{:S(2)}) collective-permute-start(f32[192,128]{1,0:T(8,128)S(1)} %collective-permute-done.1), channel_id=1, source_target_pairs={{0,2},{1,3},{4,0},{5,1},{8,4},{9,5},{12,8},{13,9},{14,12},{15,13},... | collective-permute-start | bytes 294920 | tf_op jit(solution)/shard_map/ppermute | solution.py:309
  10.8 5.2 %collective-permute-start.2 = (f32[192,128]{1,0:T(8,128)S(1)}, f32[192,128]{1,0:T(8,128)S(1)}, u32[]{:S(2)}, u32[]{:S(2)}) collective-permute-start(f32[192,128]{1,0:T(8,128)S(1)} %collective-permute-done), channel_id=1, source_target_pairs={{0,4},{1,5},{4,8},{5,9},{8,12},{9,13},{12,14},{13,15},{14,10},{15,... | collective-permute-start | bytes 294920 | tf_op jit(solution)/shard_map/ppermute | solution.py:309
  14.3 4.6 %collective-permute-start.6 = (f32[192,128]{1,0:T(8,128)S(1)}, f32[192,128]{1,0:T(8,128)S(1)}, u32[]{:S(2)}, u32[]{:S(2)}) collective-permute-start(f32[192,128]{1,0:T(8,128)S(1)} %collective-permute-done.3), channel_id=1, source_target_pairs={{0,2},{1,3},{4,0},{5,1},{8,4},{9,5},{12,8},{13,9},{14,12},{15,13},... | collective-permute-start | bytes 294920 | tf_op jit(solution)/shard_map/ppermute | solution.py:309
  16.2 4.7 %collective-permute-start.5 = (f32[192,128]{1,0:T(8,128)S(1)}, f32[192,128]{1,0:T(8,128)S(1)}, u32[]{:S(2)}, u32[]{:S(2)}) collective-permute-start(f32[192,128]{1,0:T(8,128)S(1)} %collective-permute-done.2), channel_id=1, source_target_pairs={{0,4},{1,5},{4,8},{5,9},{8,12},{9,13},{12,14},{13,15},{14,10},{15,... | collective-permute-start | bytes 294920 | tf_op jit(solution)/shard_map/ppermute | solution.py:309
  18.9 6.1 %collective-permute-start.8 = (f32[96,128]{1,0:T(8,128)S(1)}, f32[96,128]{1,0:T(8,128)S(1)}, u32[]{:S(2)}, u32[]{:S(2)}) collective-permute-start(f32[96,128]{1,0:T(8,128)S(1)} %slice.9), channel_id=1, source_target_pairs={{0,2},{1,3},{4,0},{5,1},{8,4},{9,5},{12,8},{13,9},{14,12},{15,13},... | collective-permute-start | bytes 147464 | tf_op jit(solution)/shard_map/ppermute | solution.py:309
  20.9 4.1 %collective-permute-start.7 = (f32[96,128]{1,0:T(8,128)S(1)}, f32[96,128]{1,0:T(8,128)S(1)}, u32[]{:S(2)}, u32[]{:S(2)}) collective-permute-start(f32[96,128]{1,0:T(8,128)S(1)} %slice.8), channel_id=1, source_target_pairs={{0,4},{1,5},{4,8},{5,9},{8,12},{9,13},{12,14},{13,15},{14,10},{15,... | collective-permute-start | bytes 147464 | tf_op jit(solution)/shard_map/ppermute | solution.py:309
  25.0 2.4 %collective-permute-start.9 = (f32[1536,128]{1,0:T(8,128)S(1)}, f32[1536,128]{1,0:T(8,128)S(1)}, u32[]{:S(2)}, u32[]{:S(2)}) collective-permute-start(f32[1536,128]{1,0:T(8,128)S(1)} %constant_dynamic-update-slice_fusion.src), channel_id=1, source_target_pairs={{0,1},{1,0},{2,3},{3,2},{4,5},{5,4},{6,7},{7,6},{8,9},{9,8},{10,11... | collective-permute-start | bytes 2359304 | tf_op jit(solution)/shard_map/ppermute | solution.py:309
  25.1 9.4 %collective-permute-start.12 = (bf16[64,4096]{1,0:T(8,128)(2,1)}, bf16[64,4096]{1,0:T(8,128)(2,1)S(1)}, u32[]{:S(2)}, u32[]{:S(2)}) collective-permute-start(bf16[64,4096]{1,0:T(8,128)(2,1)} %bitcast.22), channel_id=1, source_target_pairs={{0,4},{1,3},{4,8},{5,1},{8,12},{9,5},{12,14},{13,9},{14,10},{15,13... | collective-permute-start | bytes 1572872 | tf_op jit(solution)/shard_map/ppermute | solution.py:309
  27.3 1.4 %copy-start = (s32[32]{0:T(128)S(1)}, s32[32]{0:T(128)}, u32[]{:S(2)}) copy-start(s32[32]{0:T(128)} %owner.3) | copy-start | bytes 388
  28.7 14.8 %slice-start = ((s8[8388608]{0:T(1024)(128)(4,1)}), s8[4194304]{0:T(1024)(128)(4,1)S(1)}, s32[]{:S(2)}) async-start(s8[8388608]{0:T(1024)(128)(4,1)} %bitcast.12), calls=%async_computation | async-start | bytes 8388608
  32.8 10.7 %slice-start.1 = ((s8[8388608]{0:T(1024)(128)(4,1)}), s8[4194304]{0:T(1024)(128)(4,1)S(1)}, s32[]{:S(2)}) async-start(s8[8388608]{0:T(1024)(128)(4,1)} %bitcast.12), calls=%async_computation.1 | async-start | bytes 8388608
  32.8 7.3 %collective-permute-start.14 = (bf16[64,4096]{1,0:T(8,128)(2,1)S(1)}, bf16[64,4096]{1,0:T(8,128)(2,1)S(1)}, u32[]{:S(2)}, u32[]{:S(2)}) collective-permute-start(bf16[64,4096]{1,0:T(8,128)(2,1)S(1)} %precondition.2.rest_1_), channel_id=1, source_target_pairs={{0,1},{1,0},{2,3},{3,2},{4,5},{5,4},{6,7},{7,6},{8,9},{9,8},{10,11... | collective-permute-start | bytes 1572872 | tf_op jit(solution)/shard_map/ppermute | solution.py:309
  33.9 9.2 %collective-permute-start.10 = (bf16[64,4096]{1,0:T(8,128)(2,1)S(1)}, bf16[64,4096]{1,0:T(8,128)(2,1)S(1)}, u32[]{:S(2)}, u32[]{:S(2)}) collective-permute-start(bf16[64,4096]{1,0:T(8,128)(2,1)S(1)} %precondition.2.rest_1_), channel_id=1, source_target_pairs={{0,4},{1,3},{4,8},{5,1},{8,12},{9,5},{12,14},{13,9},{14,10},{15,13... | collective-permute-start | bytes 1572872 | tf_op jit(solution)/shard_map/ppermute | solution.py:309
  38.6 5.0 %collective-permute-start.15 = (bf16[64,4096]{1,0:T(8,128)(2,1)S(1)}, bf16[64,4096]{1,0:T(8,128)(2,1)S(1)}, u32[]{:S(2)}, u32[]{:S(2)}) collective-permute-start(bf16[64,4096]{1,0:T(8,128)(2,1)S(1)} %precondition.3.rest_2_), channel_id=1, source_target_pairs={{0,1},{1,0},{2,3},{3,2},{4,5},{5,4},{6,7},{7,6},{8,9},{9,8},{10,11... | collective-permute-start | bytes 1572872 | tf_op jit(solution)/shard_map/ppermute | solution.py:309
  39.4 9.3 %collective-permute-start.13 = (bf16[64,4096]{1,0:T(8,128)(2,1)S(1)}, bf16[64,4096]{1,0:T(8,128)(2,1)S(1)}, u32[]{:S(2)}, u32[]{:S(2)}) collective-permute-start(bf16[64,4096]{1,0:T(8,128)(2,1)S(1)} %precondition.3.rest_2_), channel_id=1, source_target_pairs={{0,4},{1,3},{4,8},{5,1},{8,12},{9,5},{12,14},{13,9},{14,10},{15,13... | collective-permute-start | bytes 1572872 | tf_op jit(solution)/shard_map/ppermute | solution.py:309
  43.1 6.2 %collective-permute-start.16 = (bf16[64,4096]{1,0:T(8,128)(2,1)S(1)}, bf16[64,4096]{1,0:T(8,128)(2,1)S(1)}, u32[]{:S(2)}, u32[]{:S(2)}) collective-permute-start(bf16[64,4096]{1,0:T(8,128)(2,1)S(1)} %collective-permute-done.10.rest_0_), channel_id=1, source_target_pairs={{0,1},{1,0},{2,3},{3,2},{4,5},{5,4},{6,7},{7,6},{8,9},{9,8},{10,11... | collective-permute-start | bytes 1572872 | tf_op jit(solution)/shard_map/ppermute | solution.py:309
  43.1 11.2 %collective-permute-start.11 = (bf16[64,4096]{1,0:T(8,128)(2,1)S(1)}, bf16[64,4096]{1,0:T(8,128)(2,1)S(1)}, u32[]{:S(2)}, u32[]{:S(2)}) collective-permute-start(bf16[64,4096]{1,0:T(8,128)(2,1)S(1)} %collective-permute-done.10.rest_0_), channel_id=1, source_target_pairs={{0,4},{1,3},{4,8},{5,1},{8,12},{9,5},{12,14},{13,9},{14,10},{15,13... | collective-permute-start | bytes 1572872 | tf_op jit(solution)/shard_map/ppermute | solution.py:309
  48.7 6.2 %collective-permute-start.19 = (bf16[64,4096]{1,0:T(8,128)(2,1)S(1)}, bf16[64,4096]{1,0:T(8,128)(2,1)S(1)}, u32[]{:S(2)}, u32[]{:S(2)}) collective-permute-start(bf16[64,4096]{1,0:T(8,128)(2,1)S(1)} %collective-permute-done.13.rest_0_), channel_id=1, source_target_pairs={{0,1},{1,0},{2,3},{3,2},{4,5},{5,4},{6,7},{7,6},{8,9},{9,8},{10,11... | collective-permute-start | bytes 1572872 | tf_op jit(solution)/shard_map/ppermute | solution.py:309
  48.7 11.2 %collective-permute-start.18 = (bf16[64,4096]{1,0:T(8,128)(2,1)S(1)}, bf16[64,4096]{1,0:T(8,128)(2,1)S(1)}, u32[]{:S(2)}, u32[]{:S(2)}) collective-permute-start(bf16[64,4096]{1,0:T(8,128)(2,1)S(1)} %collective-permute-done.13.rest_0_), channel_id=1, source_target_pairs={{0,4},{1,3},{4,8},{5,1},{8,12},{9,5},{12,14},{13,9},{14,10},{15,13... | collective-permute-start | bytes 1572872 | tf_op jit(solution)/shard_map/ppermute | solution.py:309
  54.3 6.3 %collective-permute-start.20 = (bf16[64,4096]{1,0:T(8,128)(2,1)S(1)}, bf16[64,4096]{1,0:T(8,128)(2,1)S(1)}, u32[]{:S(2)}, u32[]{:S(2)}) collective-permute-start(bf16[64,4096]{1,0:T(8,128)(2,1)S(1)} %collective-permute-done.11.rest_0_), channel_id=1, source_target_pairs={{0,1},{1,0},{2,3},{3,2},{4,5},{5,4},{6,7},{7,6},{8,9},{9,8},{10,11... | collective-permute-start | bytes 1572872 | tf_op jit(solution)/shard_map/ppermute | solution.py:309
  54.4 11.1 %collective-permute-start.17 = (bf16[64,4096]{1,0:T(8,128)(2,1)S(1)}, bf16[64,4096]{1,0:T(8,128)(2,1)S(1)}, u32[]{:S(2)}, u32[]{:S(2)}) collective-permute-start(bf16[64,4096]{1,0:T(8,128)(2,1)S(1)} %collective-permute-done.11.rest_0_), channel_id=1, source_target_pairs={{0,4},{1,3},{4,8},{5,1},{8,12},{9,5},{12,14},{13,9},{14,10},{15,13... | collective-permute-start | bytes 1572872 | tf_op jit(solution)/shard_map/ppermute | solution.py:309
  59.9 5.6 %collective-permute-start.23 = (bf16[64,4096]{1,0:T(8,128)(2,1)S(1)}, bf16[64,4096]{1,0:T(8,128)(2,1)S(1)}, u32[]{:S(2)}, u32[]{:S(2)}) collective-permute-start(bf16[64,4096]{1,0:T(8,128)(2,1)S(1)} %collective-permute-done.18.rest_0_), channel_id=1, source_target_pairs={{0,1},{1,0},{2,3},{3,2},{4,5},{5,4},{6,7},{7,6},{8,9},{9,8},{10,11... | collective-permute-start | bytes 1572872 | tf_op jit(solution)/shard_map/ppermute | solution.py:309
  60.1 11.1 %collective-permute-start.22 = (bf16[64,4096]{1,0:T(8,128)(2,1)S(1)}, bf16[64,4096]{1,0:T(8,128)(2,1)S(1)}, u32[]{:S(2)}, u32[]{:S(2)}) collective-permute-start(bf16[64,4096]{1,0:T(8,128)(2,1)S(1)} %collective-permute-done.18.rest_0_), channel_id=1, source_target_pairs={{0,4},{1,3},{4,8},{5,1},{8,12},{9,5},{12,14},{13,9},{14,10},{15,13... | collective-permute-start | bytes 1572872 | tf_op jit(solution)/shard_map/ppermute | solution.py:309
  71.2 1.9 %collective-permute-start.24 = (bf16[64,4096]{1,0:T(8,128)(2,1)S(1)}, bf16[64,4096]{1,0:T(8,128)(2,1)S(1)}, u32[]{:S(2)}, u32[]{:S(2)}) collective-permute-start(bf16[64,4096]{1,0:T(8,128)(2,1)S(1)} %collective-permute-done.22.rest_2_), channel_id=1, source_target_pairs={{0,1},{1,0},{2,3},{3,2},{4,5},{5,4},{6,7},{7,6},{8,9},{9,8},{10,11... | collective-permute-start | bytes 1572872 | tf_op jit(solution)/shard_map/ppermute | solution.py:309
  71.2 2.7 %collective-permute-start.21 = (bf16[64,4096]{1,0:T(8,128)(2,1)S(1)}, bf16[64,4096]{1,0:T(8,128)(2,1)S(1)}, u32[]{:S(2)}, u32[]{:S(2)}) collective-permute-start(bf16[64,4096]{1,0:T(8,128)(2,1)S(1)} %collective-permute-done.17.rest_0_), channel_id=1, source_target_pairs={{0,1},{1,0},{2,3},{3,2},{4,5},{5,4},{6,7},{7,6},{8,9},{9,8},{10,11... | collective-permute-start | bytes 1572872 | tf_op jit(solution)/shard_map/ppermute | solution.py:309

commit v6 on v5

--- a/solution.py
+++ b/solution.py
@@ -63,7 +63,7 @@
 def prepare(src, experts, at, tables=()):
     vm = pl.BlockSpec(memory_space=pltpu.VMEM)
     return pl.pallas_call(
-        functools.partial(prepare_kernel, at, experts // 2),
+        functools.partial(prepare_kernel, at, src.shape[0] // 96),
         out_shape=[
             jax.ShapeDtypeStruct((experts, 2, 128, 128), BF16),
             jax.ShapeDtypeStruct((experts, 2, 128, 128), BF16),
@@ -137,7 +137,7 @@
             es, g, x = [], [], []
             for i in range(GROUP):
                 row = b * GROUP + i
-                es.append(info[owner[routes[first + row % 8, row // 8]]])
+                es.append(info[owner[routes[first + row // 8, row % 8]]])
                 g.append(xs[pl.ds(row, 32, stride=STRIDE), :])
             n = GROUP // 2
             ee = [(es[2 * p], es[2 * p + 1]) for p in range(n)]
@@ -159,7 +159,7 @@
                 top, low = y[:32], y[32:]
                 for w, v in enumerate((jnp.where(left, top, swap(low)), jnp.where(left, swap(top), low))):
                     row = b * GROUP + 2 * p + w
-                    ys[pl.ds(row, 32, stride=STRIDE), :] = v
+                    ys[pl.ds((row % 8) * 8 + row // 8, 32, stride=STRIDE), :] = v
             return 0
 
         lax.fori_loop(0, 64 // GROUP, group, 0)
@@ -308,7 +308,7 @@
     across = [(d, d ^ 1) for d in range(devices)]
     send = lambda v, way: lax.ppermute(v, "shard", way)
 
-    raw = query_grads.transpose(1, 0, 2).reshape(-1, width)
+    raw = query_grads.reshape(-1, width)
     other_raw = send(raw, across)
 
     live = jnp.arange(train_dev, dtype=jnp.int32) < train_counts[0]
@@ -318,47 +318,65 @@
     query_route = jnp.broadcast_to(query_route, (queries * top, 128))
 
     pack = pack_factors(basis_s, basis_a, eigenvalues)
-    got, up, down = [pack], pack, pack
     cut = pack.shape[0] // 2
-    for step in range(1, far + 1):
-        if step == 3:
+    ahead2, back2 = shift((2, 2)), shift((-2, -2))
+    got, up, down, tables, crossed = [pack], pack, pack, (), 0
+    for first in range(1, far, 2):
+        if first == 3:
             up = tie(up, (other_raw, info, route, query_route))
-        if step == far:
-            up, down = up[:cut], down[cut:]
-            raw = tie(raw, got[-1])
-        up, down = send(up, ahead), send(down, back)
-        got += [up, down]
-    a = send(raw, stream)
-    mine = jnp.concatenate(got, axis=0)
-    sib = send(mine, across)
-    tables = prepare(sib, experts, experts // 2, prepare(mine, experts, 0))
+        got += [send(up, ahead), send(down, back)]
+        if first + 1 == far:
+            got += [send(up[:cut], ahead2), send(down[cut:], back2)]
+        else:
+            up, down = send(up, ahead2), send(down, back2)
+            got += [up, down]
+        if first > 1 and first + 1 < far:
+            continue
+        mine = jnp.concatenate(got, axis=0)
+        sib = send(mine, across)
+        tables = prepare(mine, experts, crossed, tables)
+        tables = prepare(sib, experts, experts // 2 + crossed, tables)
+        crossed += mine.shape[0] // 96
+        got = []
+    near = send(tie(raw, up), stream)
+    next_near = send(near, stream)
 
     pre = lambda *args: precondition(query_routes, owner_slot, info, tables, *args)
-    (b,) = pre([other_raw], [1])
-    held, names = [send(b, across), b], [0, 1]
-    (a,) = pre([tie(a, b)], [4])
+    (b,) = pre([tie(other_raw, near)], [1])
+    queue = [([send(b, across), b], [0, 1])]
+    (a,) = pre([tie(next_near, b)], [8])
     b = send(b, stream)
+    later = ([a, send(a, across)], [8, 10])
     multiply = lambda parts, names, **more: products(
         info, experts, route, query_route, train, parts, names, **more
     )
-    held += [a, send(a, across)]
-    names += [4, 6]
     done, placed = [], []
-    coming = [(b, 5), (send(a, stream), 8)]
-    while len(coming) > 1 or coming[0][1] < 4 * far:
+    coming = [(b, 5), (send(a, stream), 12)]
+    while len(coming) > 1:
         (now, name), (after, after_name) = coming
-        if name // 4 < far - 1:
-            further = [(send(now, stream), name + 4)]
+        last = 4 * far if name % 4 == 0 else 4 * far - 3
+        further = [(send(now, stream), name + 4)] if name < last else []
+        if name == 5:
+            (a,) = pre([tie(near, now)], [4])
+            queue += [([a, send(a, across)], [4, 6]), later]
+            barrier = a
         else:
-            further = [(send(now, stream), 4 * far)] if name % 4 == 0 else []
-        held[0] = tie(held[0], now)
-        done.append(multiply(held, names))
-        placed.append(names)
-        held, names = [now, send(now, across)], [name, name + 2]
-        coming = [(tie(after, done[-1]), after_name)] + further
+            parts, names = [], []
+            for p, n in queue[:2]:
+                parts, names = parts + p, names + n
+            parts[0] = tie(parts[0], now)
+            barrier = multiply(parts, names)
+            done.append(barrier)
+            placed.append(names)
+            queue = queue[2:]
+        queue.append(([now, send(now, across)], [name, name + 2]))
+        coming = [(tie(after, barrier), after_name)] + further
     now, name = coming[0]
-    held += [now, send(now, across)]
-    return multiply(held, names + [name, name + 2], old=done, placed=placed, queries=queries)
+    queue.append(([now, send(now, across)], [name, name + 2]))
+    parts, names = [], []
+    for p, n in queue:
+        parts, names = parts + p, names + n
+    return multiply(parts, names, old=done, placed=placed, queries=queries)
 
 
 def solution(mesh):

time: 78.2 us -> 73.6 us (0.941)
  starting transfers between devices: 15.6 us -> 22.8 us
  waiting for transfers between devices: 22.2 us -> 16.3 us
  Pallas kernels: 34.9 us -> 30.5 us
  local copies, waits for them, and re-layouts: 3.51 us -> 2.17 us
    pallas_call x6 -> x4, Pallas kernels: 22.9 us -> 14.5 us  [products(): pl.pallas_call(functools.partial(products_kernel, units, placed, shapes,...]
    ppermute x25 -> x26, starting transfers between devices: 15.6 us -> 22.8 us  [local(): send = lambda v, way: lax.ppermute(v, 'shard', way)]
    ppermute x25 -> x26, waiting for transfers between devices: 22.2 us -> 16.3 us  [local(): send = lambda v, way: lax.ppermute(v, 'shard', way)]
    pallas_call x2 -> x3, Pallas kernels: 8.09 us -> 12.1 us  [precondition(): pl.pallas_call(functools.partial(precondition_kernel, units), out_shape=[...]
    transpose x1 -> x0, local copies, waits for them, and re-layouts: 1.33 us -> none  [local(): raw = query_grads.transpose(1, 0, 2).reshape(-1, width)]
    pallas_call x2 -> x4, Pallas kernels: 2.73 us -> 2.83 us  [prepare(): pl.pallas_call(functools.partial(prepare_kernel, at, src.shape[0] // 96),...]
  transfers between devices with their start and end apart: 25 -> 26, of which waited for: 14 -> 13; matrix products, arithmetic and copies ran while one was open for 5% -> 4% of each run, Pallas kernels for 38% -> 35%
where the time goes in v6:
time: 73.6 us; the launch traced here: 73.4 us
  Pallas kernels  30.5 us (41%)
  starting transfers between devices  22.8 us (31%)
  waiting for transfers between devices  16.3 us (22%)
  local copies, waits for them, and re-layouts  2.17 us (3%)
  between operations  0.93 us (1%)
    ppermute x26, starting transfers between devices, local(): send = lambda v, way: lax.ppermute(v, 'shard', way)  22.8 us
    ppermute x26, waiting for transfers between devices, local(): send = lambda v, way: lax.ppermute(v, 'shard', way)  16.3 us
    pallas_call x4, Pallas kernels, products(): pl.pallas_call(functools.partial(products_kernel, units, placed, shapes,...  14.5 us
    pallas_call x3, Pallas kernels, precondition(): pl.pallas_call(functools.partial(precondition_kernel, units), out_shape=[...  12.1 us
    pallas_call x4, Pallas kernels, prepare(): pl.pallas_call(functools.partial(prepare_kernel, at, src.shape[0] // 96),...  2.83 us
  transfers between devices with their start and end apart: 26, of which 13 were waited for; matrix products, arithmetic and copies ran while one was open for 4% of the time, Pallas kernels for 35%

profile of v6, /device:TPU:0, one launch (start us, length us, event | category | flops | bytes accessed | tf_op | source)
XLA Modules:
  0.0 73.4 jit_solution(6831136236849966300)
XLA Ops:
  0.0 1.1 %pack.1 = f32[192,128]{1,0:T(8,128)S(1)} custom-call(f32[2,64,64]{2,1,0:T(8,128)} %s.1, f32[2,64,64]{2,1,0:T(8,128)} %a.1, f32[2,64,64]{2,1,0:T(8,128)} %lam.1), custom_call_target="tpu_custom_call" | custom-call | flops 1000 | bytes 1000 | tf_op jit(solution)/shard_map/pack/pallas_call | solution.py:96
  1.1 3.1 %collective-permute-start.8 = (f32[192,128]{1,0:T(8,128)S(1)}, f32[192,128]{1,0:T(8,128)S(1)}, u32[]{:S(2)}, u32[]{:S(2)}) collective-permute-start(f32[192,128]{1,0:T(8,128)S(1)} %pack.1), channel_id=1, source_target_pairs={{0,4},{1,5},{4,8},{5,9},{8,12},{9,13},{12,14},{13,15},{14,10},{15,... | collective-permute-start | bytes 294920 | tf_op jit(solution)/shard_map/ppermute | solution.py:309
  4.2 0.0 collective-permute-start.9
  4.2 3.0 %collective-permute-start = (f32[192,128]{1,0:T(8,128)S(1)}, f32[192,128]{1,0:T(8,128)S(1)}, u32[]{:S(2)}, u32[]{:S(2)}) collective-permute-start(f32[192,128]{1,0:T(8,128)S(1)} %pack.1), channel_id=1, source_target_pairs={{0,8},{1,9},{4,12},{5,13},{8,14},{9,15},{12,10},{13,11},{14,6},{15... | collective-permute-start | bytes 294920 | tf_op jit(solution)/shard_map/ppermute | solution.py:309
  7.2 0.0 collective-permute-start.3
  7.2 0.0 collective-permute-start.1
  7.2 0.8 %reshape.19 = s32[16,8,8]{1,0,2:T(8,128)S(1)} reshape(s32[128,8]{0,1:T(8,128)} %param.11) | data formatting | bytes 8192 | tf_op jit(solution)/shard_map/reshape | solution.py:317
  8.0 0.1 broadcast_in_dim.22
  8.8 0.7 broadcast_select_fusion
  9.5 0.1 copy.30
  9.6 0.1 reshape.18.route
  9.7 0.7 dynamic-slice_bitcast_fusion.info
  10.5 1.0 %collective-permute-done = f32[192,128]{1,0:T(8,128)S(1)} collective-permute-done((f32[192,128]{1,0:T(8,128)S(1)}, f32[192,128]{1,0:T(8,128)S(1)}, u32[]{:S(2)}, u32[]{:S(2)}) %collective-permute-start) | collective-permute-done | bytes 98336 | tf_op jit(solution)/shard_map/ppermute | solution.py:309
  11.4 0.2 broadcast_in_dim.23.query_route
  11.6 1.8 %collective-permute-start.2 = (f32[192,128]{1,0:T(8,128)S(1)}, f32[192,128]{1,0:T(8,128)S(1)}, u32[]{:S(2)}, u32[]{:S(2)}) collective-permute-start(f32[192,128]{1,0:T(8,128)S(1)} %collective-permute-done), channel_id=1, source_target_pairs={{0,4},{1,5},{4,8},{5,9},{8,12},{9,13},{12,14},{13,15},{14,10},{15,... | collective-permute-start | bytes 294920 | tf_op jit(solution)/shard_map/ppermute | solution.py:309
  13.5 0.1 collective-permute-done.3
  13.6 0.1 collective-permute-start.10
  13.7 2.2 %collective-permute-start.6 = (f32[96,128]{1,0:T(8,128)S(1)}, f32[96,128]{1,0:T(8,128)S(1)}, u32[]{:S(2)}, u32[]{:S(2)}) collective-permute-start(f32[96,128]{1,0:T(8,128)S(1)} %slice.8), channel_id=1, source_target_pairs={{0,6},{1,7},{4,2},{5,3},{8,0},{9,1},{12,4},{13,5},{14,8},{15,9},{1... | collective-permute-start | bytes 147464 | tf_op jit(solution)/shard_map/ppermute | solution.py:309
  15.9 0.3 collective-permute-start.4
  16.2 1.2 %collective-permute-start.5 = (f32[96,128]{1,0:T(8,128)S(1)}, f32[96,128]{1,0:T(8,128)S(1)}, u32[]{:S(2)}, u32[]{:S(2)}) collective-permute-start(f32[96,128]{1,0:T(8,128)S(1)} %slice.6), channel_id=1, source_target_pairs={{0,8},{1,9},{4,12},{5,13},{8,14},{9,15},{12,10},{13,11},{14,6},{15... | collective-permute-start | bytes 147464 | tf_op jit(solution)/shard_map/ppermute | solution.py:309
  17.4 0.0 collective-permute-done.2
  17.4 1.4 %collective-permute-start.11 = (bf16[64,4096]{1,0:T(8,128)(2,1)}, bf16[64,4096]{1,0:T(8,128)(2,1)S(1)}, u32[]{:S(2)}, u32[]{:S(2)}) collective-permute-start(bf16[64,4096]{1,0:T(8,128)(2,1)} %bitcast.4), channel_id=1, source_target_pairs={{0,4},{1,3},{4,8},{5,1},{8,12},{9,5},{12,14},{13,9},{14,10},{15,13... | collective-permute-start | bytes 1572872 | tf_op jit(solution)/shard_map/ppermute | solution.py:309
  18.7 2.9 %collective-permute-done.4 = f32[192,128]{1,0:T(8,128)S(1)} collective-permute-done((f32[192,128]{1,0:T(8,128)S(1)}, f32[192,128]{1,0:T(8,128)S(1)}, u32[]{:S(2)}, u32[]{:S(2)}) %collective-permute-start.4) | collective-permute-done | bytes 98336 | tf_op jit(solution)/shard_map/ppermute | solution.py:309
  21.7 0.2 collective-permute-done.5
  21.9 0.1 collective-permute-start.7
  22.0 0.1 copy.33.routes
  22.1 0.9 %prepare.4 = (bf16[32,2,128,128]{3,2,1,0:T(8,128)(2,1)S(1)}, bf16[32,2,128,128]{3,2,1,0:T(8,128)(2,1)S(1)}, bf16[32,64,256]{2,1,0:T(8,128)(2,1)S(1)}, bf16[32,64,256]{2,1,0:T(8,128)(2,1)S(1)}, f32[32,64,128]{2,1,0:T(8,128)S(1)}) custom-call(f32[960,128]{1,0:T(8,128)S(1)} %constant_dynamic-update-slice_fusion.4.src), custom_call_target="tpu_custom_call" | custom-call | flops 1000 | bytes 1000 | tf_op jit(solution)/shard_map/prepare/pallas_call | solution.py:65
  23.0 0.0 collective-permute-done.10.src
  23.1 0.9 %prepare.5 = (bf16[32,2,128,128]{3,2,1,0:T(8,128)(2,1)S(1)}, bf16[32,2,128,128]{3,2,1,0:T(8,128)(2,1)S(1)}, bf16[32,64,256]{2,1,0:T(8,128)(2,1)S(1)}, bf16[32,64,256]{2,1,0:T(8,128)(2,1)S(1)}, f32[32,64,128]{2,1,0:T(8,128)S(1)}) custom-call(f32[960,128]{1,0:T(8,128)S(1)} %collective-permute-done., ...), custom_call_target="tpu_custom_call", output_to_operand_aliasing={{0}: (1, {}), {1}: (2, {}), {2}: (3, {}), {3}: (4, {}), {4}... | custom-call | flops 1000 | bytes 1000 | tf_op jit(solution)/shard_map/prepare/pallas_call | solution.py:65
  24.0 0.5 prepare.6
  24.5 0.0 copy-start
  24.5 0.5 prepare.7
  25.0 1.9 %collective-permute-done.11.rest_0_ = bf16[64,4096]{1,0:T(8,128)(2,1)S(1)} collective-permute-done((bf16[64,4096]{1,0:T(8,128)(2,1)}, bf16[64,4096]{1,0:T(8,128)(2,1)S(1)}, u32[]{:S(2)}, u32[]{:S(2)}) %collective-permute-start.11) | collective-permute-done | bytes 524320 | tf_op jit(solution)/shard_map/ppermute | solution.py:309
  26.9 1.2 %collective-permute-start.12 = (bf16[64,4096]{1,0:T(8,128)(2,1)S(1)}, bf16[64,4096]{1,0:T(8,128)(2,1)S(1)}, u32[]{:S(2)}, u32[]{:S(2)}) collective-permute-start(bf16[64,4096]{1,0:T(8,128)(2,1)S(1)} %collective-permute-done.11.rest_0_), channel_id=1, source_target_pairs={{0,4},{1,3},{4,8},{5,1},{8,12},{9,5},{12,14},{13,9},{14,10},{15,13... | collective-permute-start | bytes 1572872 | tf_op jit(solution)/shard_map/ppermute | solution.py:309
  28.1 4.0 %precondition.3.rest_1_ = bf16[64,4096]{1,0:T(8,128)(2,1)S(1)} custom-call(s32[128,8]{1,0:T(8,128)S(1)} %copy.33.routes, s32[32]{0:T(128)S(1)} %copy-done, s32[52]{0:T(128)S(1)} %dynamic-slice_bitcast_fusion.info, bf16[32,2,128,128]{3,2,1,0:T(8,128)(2,1)S(1)} %get-tuple-element.53.tab_a, bf16[32,2,128,128]{3,2,1,0:T(8,128)(2,1)S(1)} %get-tuple-element.54.tab_at, ...), custom_call_target="tpu_custom_call" | custom-call | flops 1000 | bytes 1000 | tf_op jit(solution)/shard_map/precondition/pallas_call | solution.py:174
  32.2 1.8 %collective-permute-start.14 = (bf16[64,4096]{1,0:T(8,128)(2,1)S(1)}, bf16[64,4096]{1,0:T(8,128)(2,1)S(1)}, u32[]{:S(2)}, u32[]{:S(2)}) collective-permute-start(bf16[64,4096]{1,0:T(8,128)(2,1)S(1)} %precondition.3.rest_1_), channel_id=1, source_target_pairs={{0,4},{1,3},{4,8},{5,1},{8,12},{9,5},{12,14},{13,9},{14,10},{15,13... | collective-permute-start | bytes 1572872 | tf_op jit(solution)/shard_map/ppermute | solution.py:309
  33.9 2.5 %collective-permute-done.12.rest_0_ = bf16[64,4096]{1,0:T(8,128)(2,1)S(1)} collective-permute-done((bf16[64,4096]{1,0:T(8,128)(2,1)S(1)}, bf16[64,4096]{1,0:T(8,128)(2,1)S(1)}, u32[]{:S(2)}, u32[]{:S(2)}) %collective-permute-start.12) | collective-permute-done | bytes 524320 | tf_op jit(solution)/shard_map/ppermute | solution.py:309
  36.4 4.0 %precondition.4.rest_0_ = bf16[64,4096]{1,0:T(8,128)(2,1)S(1)} custom-call(s32[128,8]{1,0:T(8,128)S(1)} %copy.33.routes, s32[32]{0:T(128)S(1)} %copy-done, s32[52]{0:T(128)S(1)} %dynamic-slice_bitcast_fusion.info, bf16[32,2,128,128]{3,2,1,0:T(8,128)(2,1)S(1)} %get-tuple-element.53.tab_a, bf16[32,2,128,128]{3,2,1,0:T(8,128)(2,1)S(1)} %get-tuple-element.54.tab_at, ...), custom_call_target="tpu_custom_call" | custom-call | flops 1000 | bytes 1000 | tf_op jit(solution)/shard_map/precondition/pallas_call | solution.py:174
  40.5 0.0 slice-start.1
  40.5 1.0 %collective-permute-start.13 = (bf16[64,4096]{1,0:T(8,128)(2,1)S(1)}, bf16[64,4096]{1,0:T(8,128)(2,1)S(1)}, u32[]{:S(2)}, u32[]{:S(2)}) collective-permute-start(bf16[64,4096]{1,0:T(8,128)(2,1)S(1)} %precondition.4.rest_0_), channel_id=1, source_target_pairs={{0,4},{1,3},{4,8},{5,1},{8,12},{9,5},{12,14},{13,9},{14,10},{15,13... | collective-permute-start | bytes 1572872 | tf_op jit(solution)/shard_map/ppermute | solution.py:309
  41.4 0.0 collective-permute-start.17
  41.4 0.6 collective-permute-done.14.rest_2_
  42.0 4.0 %precondition.5.rest_2_ = bf16[64,4096]{1,0:T(8,128)(2,1)S(1)} custom-call(s32[128,8]{1,0:T(8,128)S(1)} %copy.33.routes, s32[32]{0:T(128)S(1)} %copy-done, s32[52]{0:T(128)S(1)} %dynamic-slice_bitcast_fusion.info, bf16[32,2,128,128]{3,2,1,0:T(8,128)(2,1)S(1)} %get-tuple-element.53.tab_a, bf16[32,2,128,128]{3,2,1,0:T(8,128)(2,1)S(1)} %get-tuple-element.54.tab_at, ...), custom_call_target="tpu_custom_call" | custom-call | flops 1000 | bytes 1000 | tf_op jit(solution)/shard_map/precondition/pallas_call | solution.py:174
  46.1 0.1 collective-permute-start.18
  46.2 1.6 %collective-permute-start.16 = (bf16[64,4096]{1,0:T(8,128)(2,1)S(1)}, bf16[64,4096]{1,0:T(8,128)(2,1)S(1)}, u32[]{:S(2)}, u32[]{:S(2)}) collective-permute-start(bf16[64,4096]{1,0:T(8,128)(2,1)S(1)} %collective-permute-done.14.rest_2_), channel_id=1, source_target_pairs={{0,4},{1,3},{4,8},{5,1},{8,12},{9,5},{12,14},{13,9},{14,10},{15,13... | collective-permute-start | bytes 1572872 | tf_op jit(solution)/shard_map/ppermute | solution.py:309
  47.8 0.6 collective-permute-start.20
  48.4 1.3 %collective-permute-done.13.rest_0_ = bf16[64,4096]{1,0:T(8,128)(2,1)S(1)} collective-permute-done((bf16[64,4096]{1,0:T(8,128)(2,1)S(1)}, bf16[64,4096]{1,0:T(8,128)(2,1)S(1)}, u32[]{:S(2)}, u32[]{:S(2)}) %collective-permute-start.13) | collective-permute-done | bytes 524320 | tf_op jit(solution)/shard_map/ppermute | solution.py:309
  49.7 0.9 %collective-permute-start.15 = (bf16[64,4096]{1,0:T(8,128)(2,1)S(1)}, bf16[64,4096]{1,0:T(8,128)(2,1)S(1)}, u32[]{:S(2)}, u32[]{:S(2)}) collective-permute-start(bf16[64,4096]{1,0:T(8,128)(2,1)S(1)} %collective-permute-done.13.rest_0_), channel_id=1, source_target_pairs={{0,4},{1,3},{4,8},{5,1},{8,12},{9,5},{12,14},{13,9},{14,10},{15,13... | collective-permute-start | bytes 1572872 | tf_op jit(solution)/shard_map/ppermute | solution.py:309
  50.6 0.0 collective-permute-done.18.rest_3_
  50.6 3.5 %products.4.rest_4_ = f32[32,128]{1,0:T(8,128)S(1)} custom-call(s32[52]{0:T(128)S(1)} %dynamic-slice_bitcast_fusion.info, s32[1,1024]{1,0:T(1,128)S(1)} %reshape.18.route, s32[1024,128]{1,0:T(8,128)S(1)} %broadcast_in_dim.23.query_route, bf16[1024,4096]{1,0:T(8,128)(2,1)S(1)} %bitcast.11, bf16[64,4096]{1,0:T(8,128)(2,1)S(1)} %collective-permute-done.17.rest_0_, ...), custom_call_target="tpu_custom_call" | custom-call | flops 1000 | bytes 1000 | tf_op jit(solution)/shard_map/products/pallas_call | solution.py:238
  54.1 1.3 %collective-permute-done.16.rest_2_ = bf16[64,4096]{1,0:T(8,128)(2,1)S(1)} collective-permute-done((bf16[64,4096]{1,0:T(8,128)(2,1)S(1)}, bf16[64,4096]{1,0:T(8,128)(2,1)S(1)}, u32[]{:S(2)}, u32[]{:S(2)}) %collective-permute-start.16) | collective-permute-done | bytes 524320 | tf_op jit(solution)/shard_map/ppermute | solution.py:309
  55.4 0.1 collective-permute-start.24
  55.5 0.4 collective-permute-start.23
  55.9 0.0 collective-permute-done.20.rest_3_
  55.9 1.6 %collective-permute-start.22 = (bf16[64,4096]{1,0:T(8,128)(2,1)S(1)}, bf16[64,4096]{1,0:T(8,128)(2,1)S(1)}, u32[]{:S(2)}, u32[]{:S(2)}) collective-permute-start(bf16[64,4096]{1,0:T(8,128)(2,1)S(1)} %collective-permute-done.16.rest_2_), channel_id=1, source_target_pairs={{0,4},{1,3},{4,8},{5,1},{8,12},{9,5},{12,14},{13,9},{14,10},{15,13... | collective-permute-start | bytes 1572872 | tf_op jit(solution)/shard_map/ppermute | solution.py:309
  57.5 0.0 collective-permute-done.19.rest_1_
  57.5 3.5 %products.5.rest_5_ = f32[32,128]{1,0:T(8,128)S(1)} custom-call(s32[52]{0:T(128)S(1)} %dynamic-slice_bitcast_fusion.info, s32[1,1024]{1,0:T(1,128)S(1)} %reshape.18.route, s32[1024,128]{1,0:T(8,128)S(1)} %broadcast_in_dim.23.query_route, bf16[1024,4096]{1,0:T(8,128)(2,1)S(1)} %bitcast.12, bf16[64,4096]{1,0:T(8,128)(2,1)S(1)} %precondition.4.rest_0_, ...), custom_call_target="tpu_custom_call" | custom-call | flops 1000 | bytes 1000 | tf_op jit(solution)/shard_map/products/pallas_call | solution.py:238
  60.9 0.1 collective-permute-done.15.rest_0_
  61.0 3.5 %products.6.rest_6_ = f32[32,128]{1,0:T(8,128)S(1)} custom-call(s32[52]{0:T(128)S(1)} %dynamic-slice_bitcast_fusion.info, s32[1,1024]{1,0:T(1,128)S(1)} %reshape.18.route, s32[1024,128]{1,0:T(8,128)S(1)} %broadcast_in_dim.23.query_route, bf16[1024,4096]{1,0:T(8,128)(2,1)S(1)} %bitcast.13, bf16[64,4096]{1,0:T(8,128)(2,1)S(1)} %collective-permute-done.13.rest_0_, ...), custom_call_target="tpu_custom_call" | custom-call | flops 1000 | bytes 1000 | tf_op jit(solution)/shard_map/products/pallas_call | solution.py:238
  64.5 2.1 %collective-permute-done.22.rest_2_ = bf16[64,4096]{1,0:T(8,128)(2,1)S(1)} collective-permute-done((bf16[64,4096]{1,0:T(8,128)(2,1)S(1)}, bf16[64,4096]{1,0:T(8,128)(2,1)S(1)}, u32[]{:S(2)}, u32[]{:S(2)}) %collective-permute-start.22) | collective-permute-done | bytes 524320 | tf_op jit(solution)/shard_map/ppermute | solution.py:309
  66.6 0.5 collective-permute-start.21
  67.1 1.4 %collective-permute-done.25.rest_3_ = bf16[64,4096]{1,0:T(8,128)(2,1)S(1)} collective-permute-done((bf16[64,4096]{1,0:T(8,128)(2,1)S(1)}, bf16[64,4096]{1,0:T(8,128)(2,1)S(1)}, u32[]{:S(2)}, u32[]{:S(2)}) %collective-permute-start.25) | collective-permute-done | bytes 524320 | tf_op jit(solution)/shard_map/ppermute | solution.py:309
  68.5 0.7 %collective-permute-done.21.rest_1_ = bf16[64,4096]{1,0:T(8,128)(2,1)S(1)} collective-permute-done((bf16[64,4096]{1,0:T(8,128)(2,1)S(1)}, bf16[64,4096]{1,0:T(8,128)(2,1)S(1)}, u32[]{:S(2)}, u32[]{:S(2)}) %collective-permute-start.21) | collective-permute-done | bytes 524320 | tf_op jit(solution)/shard_map/ppermute | solution.py:309
  69.3 4.1 %products.7 = f32[128,128]{1,0:T(8,128)} custom-call(s32[52]{0:T(128)S(1)} %dynamic-slice_bitcast_fusion.info, s32[1,1024]{1,0:T(1,128)S(1)} %reshape.18.route, s32[1024,128]{1,0:T(8,128)S(1)} %broadcast_in_dim.23.query_route, bf16[1024,4096]{1,0:T(8,128)(2,1)S(1)} %bitcast.14, bf16[64,4096]{1,0:T(8,128)(2,1)S(1)} %collective-permute-done.15.rest_0_, ...), custom_call_target="tpu_custom_call" | custom-call | flops 1000 | bytes 1000 | tf_op jit(solution)/shard_map/products/pallas_call | solution.py:238
  (30 shorter events, 0.1 us)
Async XLA Ops:
  0.0 22.0 %copy-start.1 = (s32[128,8]{0,1:T(8,128)S(1)}, s32[128,8]{0,1:T(8,128)}, u32[]{:S(2)}) copy-start(s32[128,8]{0,1:T(8,128)} %param.11) | copy-start | bytes 12292
  1.1 9.3 %collective-permute-start.8 = (f32[192,128]{1,0:T(8,128)S(1)}, f32[192,128]{1,0:T(8,128)S(1)}, u32[]{:S(2)}, u32[]{:S(2)}) collective-permute-start(f32[192,128]{1,0:T(8,128)S(1)} %pack.1), channel_id=1, source_target_pairs={{0,4},{1,5},{4,8},{5,9},{8,12},{9,13},{12,14},{13,15},{14,10},{15,... | collective-permute-start | bytes 294920 | tf_op jit(solution)/shard_map/ppermute | solution.py:309
  4.2 6.2 %collective-permute-start.9 = (f32[192,128]{1,0:T(8,128)S(1)}, f32[192,128]{1,0:T(8,128)S(1)}, u32[]{:S(2)}, u32[]{:S(2)}) collective-permute-start(f32[192,128]{1,0:T(8,128)S(1)} %pack.1), channel_id=1, source_target_pairs={{0,2},{1,3},{4,0},{5,1},{8,4},{9,5},{12,8},{13,9},{14,12},{15,13},... | collective-permute-start | bytes 294920 | tf_op jit(solution)/shard_map/ppermute | solution.py:309
  4.2 7.2 %collective-permute-start = (f32[192,128]{1,0:T(8,128)S(1)}, f32[192,128]{1,0:T(8,128)S(1)}, u32[]{:S(2)}, u32[]{:S(2)}) collective-permute-start(f32[192,128]{1,0:T(8,128)S(1)} %pack.1), channel_id=1, source_target_pairs={{0,8},{1,9},{4,12},{5,13},{8,14},{9,15},{12,10},{13,11},{14,6},{15... | collective-permute-start | bytes 294920 | tf_op jit(solution)/shard_map/ppermute | solution.py:309
  7.2 6.4 %collective-permute-start.3 = (f32[192,128]{1,0:T(8,128)S(1)}, f32[192,128]{1,0:T(8,128)S(1)}, u32[]{:S(2)}, u32[]{:S(2)}) collective-permute-start(f32[192,128]{1,0:T(8,128)S(1)} %pack.1), channel_id=1, source_target_pairs={{0,6},{1,7},{4,2},{5,3},{8,0},{9,1},{12,4},{13,5},{14,8},{15,9},{1... | collective-permute-start | bytes 294920 | tf_op jit(solution)/shard_map/ppermute | solution.py:309
  7.2 4.2 %collective-permute-start.1 = (bf16[64,4096]{1,0:T(8,128)(2,1)}, bf16[64,4096]{1,0:T(8,128)(2,1)S(1)}, u32[]{:S(2)}, u32[]{:S(2)}) collective-permute-start(bf16[64,4096]{1,0:T(8,128)(2,1)} %bitcast.4), channel_id=1, source_target_pairs={{0,1},{1,0},{2,3},{3,2},{4,5},{5,4},{6,7},{7,6},{8,9},{9,8},{10,11... | collective-permute-start | bytes 1572872 | tf_op jit(solution)/shard_map/ppermute | solution.py:309
  11.6 5.7 %collective-permute-start.2 = (f32[192,128]{1,0:T(8,128)S(1)}, f32[192,128]{1,0:T(8,128)S(1)}, u32[]{:S(2)}, u32[]{:S(2)}) collective-permute-start(f32[192,128]{1,0:T(8,128)S(1)} %collective-permute-done), channel_id=1, source_target_pairs={{0,4},{1,5},{4,8},{5,9},{8,12},{9,13},{12,14},{13,15},{14,10},{15,... | collective-permute-start | bytes 294920 | tf_op jit(solution)/shard_map/ppermute | solution.py:309
  13.6 9.4 %collective-permute-start.10 = (f32[960,128]{1,0:T(8,128)S(1)}, f32[960,128]{1,0:T(8,128)S(1)}, u32[]{:S(2)}, u32[]{:S(2)}) collective-permute-start(f32[960,128]{1,0:T(8,128)S(1)} %constant_dynamic-update-slice_fusion.4.src), channel_id=1, source_target_pairs={{0,1},{1,0},{2,3},{3,2},{4,5},{5,4},{6,7},{7,6},{8,9},{9,8},{10,11... | collective-permute-start | bytes 1474568 | tf_op jit(solution)/shard_map/ppermute | solution.py:309
  13.7 8.2 %collective-permute-start.6 = (f32[96,128]{1,0:T(8,128)S(1)}, f32[96,128]{1,0:T(8,128)S(1)}, u32[]{:S(2)}, u32[]{:S(2)}) collective-permute-start(f32[96,128]{1,0:T(8,128)S(1)} %slice.8), channel_id=1, source_target_pairs={{0,6},{1,7},{4,2},{5,3},{8,0},{9,1},{12,4},{13,5},{14,8},{15,9},{1... | collective-permute-start | bytes 147464 | tf_op jit(solution)/shard_map/ppermute | solution.py:309
  15.9 5.8 %collective-permute-start.4 = (f32[192,128]{1,0:T(8,128)S(1)}, f32[192,128]{1,0:T(8,128)S(1)}, u32[]{:S(2)}, u32[]{:S(2)}) collective-permute-start(f32[192,128]{1,0:T(8,128)S(1)} %collective-permute-done.3), channel_id=1, source_target_pairs={{0,2},{1,3},{4,0},{5,1},{8,4},{9,5},{12,8},{13,9},{14,12},{15,13},... | collective-permute-start | bytes 294920 | tf_op jit(solution)/shard_map/ppermute | solution.py:309
  16.2 5.7 %collective-permute-start.5 = (f32[96,128]{1,0:T(8,128)S(1)}, f32[96,128]{1,0:T(8,128)S(1)}, u32[]{:S(2)}, u32[]{:S(2)}) collective-permute-start(f32[96,128]{1,0:T(8,128)S(1)} %slice.6), channel_id=1, source_target_pairs={{0,8},{1,9},{4,12},{5,13},{8,14},{9,15},{12,10},{13,11},{14,6},{15... | collective-permute-start | bytes 147464 | tf_op jit(solution)/shard_map/ppermute | solution.py:309
  17.4 9.6 %collective-permute-start.11 = (bf16[64,4096]{1,0:T(8,128)(2,1)}, bf16[64,4096]{1,0:T(8,128)(2,1)S(1)}, u32[]{:S(2)}, u32[]{:S(2)}) collective-permute-start(bf16[64,4096]{1,0:T(8,128)(2,1)} %bitcast.4), channel_id=1, source_target_pairs={{0,4},{1,3},{4,8},{5,1},{8,12},{9,5},{12,14},{13,9},{14,10},{15,13... | collective-permute-start | bytes 1572872 | tf_op jit(solution)/shard_map/ppermute | solution.py:309
  21.9 2.6 %collective-permute-start.7 = (f32[576,128]{1,0:T(8,128)S(1)}, f32[576,128]{1,0:T(8,128)S(1)}, u32[]{:S(2)}, u32[]{:S(2)}) collective-permute-start(f32[576,128]{1,0:T(8,128)S(1)} %constant_dynamic-update-slice_fusion.src), channel_id=1, source_target_pairs={{0,1},{1,0},{2,3},{3,2},{4,5},{5,4},{6,7},{7,6},{8,9},{9,8},{10,11... | collective-permute-start | bytes 884744 | tf_op jit(solution)/shard_map/ppermute | solution.py:309
  24.5 3.6 %copy-start = (s32[32]{0:T(128)S(1)}, s32[32]{0:T(128)}, u32[]{:S(2)}) copy-start(s32[32]{0:T(128)} %owner.5) | copy-start | bytes 388
  26.9 9.5 %collective-permute-start.12 = (bf16[64,4096]{1,0:T(8,128)(2,1)S(1)}, bf16[64,4096]{1,0:T(8,128)(2,1)S(1)}, u32[]{:S(2)}, u32[]{:S(2)}) collective-permute-start(bf16[64,4096]{1,0:T(8,128)(2,1)S(1)} %collective-permute-done.11.rest_0_), channel_id=1, source_target_pairs={{0,4},{1,3},{4,8},{5,1},{8,12},{9,5},{12,14},{13,9},{14,10},{15,13... | collective-permute-start | bytes 1572872 | tf_op jit(solution)/shard_map/ppermute | solution.py:309
  32.2 9.9 %collective-permute-start.14 = (bf16[64,4096]{1,0:T(8,128)(2,1)S(1)}, bf16[64,4096]{1,0:T(8,128)(2,1)S(1)}, u32[]{:S(2)}, u32[]{:S(2)}) collective-permute-start(bf16[64,4096]{1,0:T(8,128)(2,1)S(1)} %precondition.3.rest_1_), channel_id=1, source_target_pairs={{0,4},{1,3},{4,8},{5,1},{8,12},{9,5},{12,14},{13,9},{14,10},{15,13... | collective-permute-start | bytes 1572872 | tf_op jit(solution)/shard_map/ppermute | solution.py:309
  36.4 14.2 %slice-start = ((s8[8388608]{0:T(1024)(128)(4,1)}), s8[4194304]{0:T(1024)(128)(4,1)S(1)}, s32[]{:S(2)}) async-start(s8[8388608]{0:T(1024)(128)(4,1)} %bitcast.9), calls=%async_computation | async-start | bytes 8388608
  40.5 10.2 %slice-start.1 = ((s8[8388608]{0:T(1024)(128)(4,1)}), s8[4194304]{0:T(1024)(128)(4,1)S(1)}, s32[]{:S(2)}) async-start(s8[8388608]{0:T(1024)(128)(4,1)} %bitcast.9), calls=%async_computation.1 | async-start | bytes 8388608
  40.5 9.2 %collective-permute-start.13 = (bf16[64,4096]{1,0:T(8,128)(2,1)S(1)}, bf16[64,4096]{1,0:T(8,128)(2,1)S(1)}, u32[]{:S(2)}, u32[]{:S(2)}) collective-permute-start(bf16[64,4096]{1,0:T(8,128)(2,1)S(1)} %precondition.4.rest_0_), channel_id=1, source_target_pairs={{0,4},{1,3},{4,8},{5,1},{8,12},{9,5},{12,14},{13,9},{14,10},{15,13... | collective-permute-start | bytes 1572872 | tf_op jit(solution)/shard_map/ppermute | solution.py:309
  41.4 8.3 %collective-permute-start.17 = (bf16[64,4096]{1,0:T(8,128)(2,1)S(1)}, bf16[64,4096]{1,0:T(8,128)(2,1)S(1)}, u32[]{:S(2)}, u32[]{:S(2)}) collective-permute-start(bf16[64,4096]{1,0:T(8,128)(2,1)S(1)} %precondition.3.rest_1_), channel_id=1, source_target_pairs={{0,1},{1,0},{2,3},{3,2},{4,5},{5,4},{6,7},{7,6},{8,9},{9,8},{10,11... | collective-permute-start | bytes 1572872 | tf_op jit(solution)/shard_map/ppermute | solution.py:309
  46.1 4.5 %collective-permute-start.18 = (bf16[64,4096]{1,0:T(8,128)(2,1)S(1)}, bf16[64,4096]{1,0:T(8,128)(2,1)S(1)}, u32[]{:S(2)}, u32[]{:S(2)}) collective-permute-start(bf16[64,4096]{1,0:T(8,128)(2,1)S(1)} %precondition.5.rest_2_), channel_id=1, source_target_pairs={{0,1},{1,0},{2,3},{3,2},{4,5},{5,4},{6,7},{7,6},{8,9},{9,8},{10,11... | collective-permute-start | bytes 1572872 | tf_op jit(solution)/shard_map/ppermute | solution.py:309
  46.2 9.2 %collective-permute-start.16 = (bf16[64,4096]{1,0:T(8,128)(2,1)S(1)}, bf16[64,4096]{1,0:T(8,128)(2,1)S(1)}, u32[]{:S(2)}, u32[]{:S(2)}) collective-permute-start(bf16[64,4096]{1,0:T(8,128)(2,1)S(1)} %collective-permute-done.14.rest_2_), channel_id=1, source_target_pairs={{0,4},{1,3},{4,8},{5,1},{8,12},{9,5},{12,14},{13,9},{14,10},{15,13... | collective-permute-start | bytes 1572872 | tf_op jit(solution)/shard_map/ppermute | solution.py:309
  47.8 8.1 %collective-permute-start.20 = (bf16[64,4096]{1,0:T(8,128)(2,1)S(1)}, bf16[64,4096]{1,0:T(8,128)(2,1)S(1)}, u32[]{:S(2)}, u32[]{:S(2)}) collective-permute-start(bf16[64,4096]{1,0:T(8,128)(2,1)S(1)} %collective-permute-done.14.rest_2_), channel_id=1, source_target_pairs={{0,1},{1,0},{2,3},{3,2},{4,5},{5,4},{6,7},{7,6},{8,9},{9,8},{10,11... | collective-permute-start | bytes 1572872 | tf_op jit(solution)/shard_map/ppermute | solution.py:309
  49.7 7.8 %collective-permute-start.19 = (bf16[64,4096]{1,0:T(8,128)(2,1)S(1)}, bf16[64,4096]{1,0:T(8,128)(2,1)S(1)}, u32[]{:S(2)}, u32[]{:S(2)}) collective-permute-start(bf16[64,4096]{1,0:T(8,128)(2,1)S(1)} %precondition.4.rest_0_), channel_id=1, source_target_pairs={{0,1},{1,0},{2,3},{3,2},{4,5},{5,4},{6,7},{7,6},{8,9},{9,8},{10,11... | collective-permute-start | bytes 1572872 | tf_op jit(solution)/shard_map/ppermute | solution.py:309
  49.7 11.3 %collective-permute-start.15 = (bf16[64,4096]{1,0:T(8,128)(2,1)S(1)}, bf16[64,4096]{1,0:T(8,128)(2,1)S(1)}, u32[]{:S(2)}, u32[]{:S(2)}) collective-permute-start(bf16[64,4096]{1,0:T(8,128)(2,1)S(1)} %collective-permute-done.13.rest_0_), channel_id=1, source_target_pairs={{0,4},{1,3},{4,8},{5,1},{8,12},{9,5},{12,14},{13,9},{14,10},{15,13... | collective-permute-start | bytes 1572872 | tf_op jit(solution)/shard_map/ppermute | solution.py:309
  55.4 5.6 %collective-permute-start.24 = (bf16[64,4096]{1,0:T(8,128)(2,1)S(1)}, bf16[64,4096]{1,0:T(8,128)(2,1)S(1)}, u32[]{:S(2)}, u32[]{:S(2)}) collective-permute-start(bf16[64,4096]{1,0:T(8,128)(2,1)S(1)} %collective-permute-done.16.rest_2_), channel_id=1, source_target_pairs={{0,1},{1,0},{2,3},{3,2},{4,5},{5,4},{6,7},{7,6},{8,9},{9,8},{10,11... | collective-permute-start | bytes 1572872 | tf_op jit(solution)/shard_map/ppermute | solution.py:309
  55.5 5.5 %collective-permute-start.23 = (bf16[64,4096]{1,0:T(8,128)(2,1)S(1)}, bf16[64,4096]{1,0:T(8,128)(2,1)S(1)}, u32[]{:S(2)}, u32[]{:S(2)}) collective-permute-start(bf16[64,4096]{1,0:T(8,128)(2,1)S(1)} %collective-permute-done.13.rest_0_), channel_id=1, source_target_pairs={{0,1},{1,0},{2,3},{3,2},{4,5},{5,4},{6,7},{7,6},{8,9},{9,8},{10,11... | collective-permute-start | bytes 1572872 | tf_op jit(solution)/shard_map/ppermute | solution.py:309
  55.9 10.7 %collective-permute-start.22 = (bf16[64,4096]{1,0:T(8,128)(2,1)S(1)}, bf16[64,4096]{1,0:T(8,128)(2,1)S(1)}, u32[]{:S(2)}, u32[]{:S(2)}) collective-permute-start(bf16[64,4096]{1,0:T(8,128)(2,1)S(1)} %collective-permute-done.16.rest_2_), channel_id=1, source_target_pairs={{0,4},{1,3},{4,8},{5,1},{8,12},{9,5},{12,14},{13,9},{14,10},{15,13... | collective-permute-start | bytes 1572872 | tf_op jit(solution)/shard_map/ppermute | solution.py:309
  66.6 1.9 %collective-permute-start.25 = (bf16[64,4096]{1,0:T(8,128)(2,1)S(1)}, bf16[64,4096]{1,0:T(8,128)(2,1)S(1)}, u32[]{:S(2)}, u32[]{:S(2)}) collective-permute-start(bf16[64,4096]{1,0:T(8,128)(2,1)S(1)} %collective-permute-done.22.rest_2_), channel_id=1, source_target_pairs={{0,1},{1,0},{2,3},{3,2},{4,5},{5,4},{6,7},{7,6},{8,9},{9,8},{10,11... | collective-permute-start | bytes 1572872 | tf_op jit(solution)/shard_map/ppermute | solution.py:309
  66.6 2.7 %collective-permute-start.21 = (bf16[64,4096]{1,0:T(8,128)(2,1)S(1)}, bf16[64,4096]{1,0:T(8,128)(2,1)S(1)}, u32[]{:S(2)}, u32[]{:S(2)}) collective-permute-start(bf16[64,4096]{1,0:T(8,128)(2,1)S(1)} %collective-permute-done.15.rest_0_), channel_id=1, source_target_pairs={{0,1},{1,0},{2,3},{3,2},{4,5},{5,4},{6,7},{7,6},{8,9},{9,8},{10,11... | collective-permute-start | bytes 1572872 | tf_op jit(solution)/shard_map/ppermute | solution.py:309

commit v7 on v6

--- a/solution.py
+++ b/solution.py
@@ -12,7 +12,7 @@
 F32, BF16 = jnp.float32, jnp.bfloat16
 STRIDE = 65
 GROUP = 64
-TILE = 512
+TILE = 1024
 MIB = 2**20
 
 
@@ -105,9 +105,8 @@
     )(*[pltpu.with_memory_space_constraint(m, pltpu.HBM) for m in factors])
 
 
-def precondition_kernel(units, routes, owner, info, tab_a, tab_at, tab_s, tab_st, scale, *rest):
+def precondition_kernel(units, experts, size, queries, info, tab_a, tab_at, tab_s, tab_st, scale, *rest):
     chunks = len(units)
-    experts = owner.shape[0]
     raws, outs = rest[:chunks], rest[chunks : 2 * chunks]
     xs, ys = rest[2 * chunks :]
     left64 = lax.broadcasted_iota(jnp.int32, (64, 128), 1) < 64
@@ -129,7 +128,7 @@
 
     for ch in range(chunks):
         raw, out = raws[ch], outs[ch]
-        first = info[experts + units[ch]] * 8
+        first = size + experts + info[experts + units[ch]] * 8
         for c in range(32):
             xs[pl.ds(c * STRIDE, 64), :] = raw[:, c * 128 : (c + 1) * 128].astype(F32)
 
@@ -137,7 +136,7 @@
             es, g, x = [], [], []
             for i in range(GROUP):
                 row = b * GROUP + i
-                es.append(info[owner[routes[first + row // 8, row % 8]]])
+                es.append(info[info[size + info[first + row % 8 * queries + row // 8]]])
                 g.append(xs[pl.ds(row, 32, stride=STRIDE), :])
             n = GROUP // 2
             ee = [(es[2 * p], es[2 * p + 1]) for p in range(n)]
@@ -167,20 +166,20 @@
             out[:, c * 128 : (c + 1) * 128] = ys[pl.ds(c * STRIDE, 64), :].astype(BF16)
 
 
-def precondition(routes, owner, info, tables, raws, units):
+def precondition(experts, size, queries, info, tables, raws, units):
     chunks = len(units)
     sm = pl.BlockSpec(memory_space=pltpu.SMEM)
     vm = pl.BlockSpec(memory_space=pltpu.VMEM)
     return pl.pallas_call(
-        functools.partial(precondition_kernel, units),
+        functools.partial(precondition_kernel, units, experts, size, queries),
         out_shape=[jax.ShapeDtypeStruct((64, raws[0].shape[1]), BF16)] * chunks,
-        in_specs=[sm] * 3 + [vm] * (5 + len(raws)),
+        in_specs=[sm] + [vm] * (5 + len(raws)),
         out_specs=[vm] * chunks,
         scratch_shapes=[pltpu.VMEM((32 * STRIDE, 128), F32), pltpu.VMEM((32 * STRIDE, 128), F32)],
         compiler_params=pltpu.CompilerParams(vmem_limit_bytes=8 * MIB),
         cost_estimate=pl.CostEstimate(flops=1000, bytes_accessed=1000, transcendentals=0),
         name="precondition",
-    )(routes, owner, info, *tables, *raws)
+    )(info, *tables, *raws)
 
 
 def products_kernel(units, placed, shapes, experts, info, route, query_route, train, *rest):
@@ -298,6 +297,8 @@
     far = chips // 2
     ring, constants = tables_of(devices, slots)
     info = lax.dynamic_index_in_dim(jnp.asarray(constants), me, 0, keepdims=False)
+    size = info.shape[0]
+    scalars = jnp.concatenate([info, owner_slot, query_routes.T.reshape(-1)])
 
     def shift(steps):
         return [
@@ -323,7 +324,7 @@
     got, up, down, tables, crossed = [pack], pack, pack, (), 0
     for first in range(1, far, 2):
         if first == 3:
-            up = tie(up, (other_raw, info, route, query_route))
+            up = tie(up, (other_raw, scalars, route, query_route))
         got += [send(up, ahead), send(down, back)]
         if first + 1 == far:
             got += [send(up[:cut], ahead2), send(down[cut:], back2)]
@@ -341,41 +342,47 @@
     near = send(tie(raw, up), stream)
     next_near = send(near, stream)
 
-    pre = lambda *args: precondition(query_routes, owner_slot, info, tables, *args)
-    (b,) = pre([tie(other_raw, near)], [1])
-    queue = [([send(b, across), b], [0, 1])]
-    (a,) = pre([tie(next_near, b)], [8])
-    b = send(b, stream)
-    later = ([a, send(a, across)], [8, 10])
+    pre = lambda *args: precondition(experts, size, queries, scalars, tables, *args)
     multiply = lambda parts, names, **more: products(
-        info, experts, route, query_route, train, parts, names, **more
+        scalars, experts, route, query_route, train, parts, names, **more
     )
     done, placed = [], []
-    coming = [(b, 5), (send(a, stream), 12)]
+
+    def work(units, after):
+        parts = [v for p, _ in units for v in p]
+        names = [n for _, ns in units for n in ns]
+        parts[0] = tie(parts[0], after)
+        done.append(multiply(parts, names))
+        placed.append(names)
+        return done[-1]
+
+    both = lambda v, name: ([v, send(v, across)], [name, name + 2])
+    (b,) = pre([tie(other_raw, near)], [1])
+    own = ([send(b, across), b], [0, 1])
+    b1 = send(b, stream)
+    (a1,) = pre([tie(near, b)], [4])
+    next_near = tie(next_near, a1)
+    a3 = send(next_near, stream)
+    (a2,) = pre([next_near], [8])
+    b1 = tie(b1, a2)
+    b2 = send(b1, stream)
+    a3 = tie(a3, work([own, both(a1, 4)], b1))
+    (a3,) = pre([a3], [12])
+    a4 = send(a3, stream)
+    b2 = tie(b2, work([both(a2, 8), both(b1, 5)], a3))
+    b3 = send(b2, stream)
+    b3 = tie(b3, work([both(a3, 12), both(b2, 9)], a4))
+    coming, queue = [(a4, 16), (b3, 13)], []
     while len(coming) > 1:
         (now, name), (after, after_name) = coming
         last = 4 * far if name % 4 == 0 else 4 * far - 3
         further = [(send(now, stream), name + 4)] if name < last else []
-        if name == 5:
-            (a,) = pre([tie(near, now)], [4])
-            queue += [([a, send(a, across)], [4, 6]), later]
-            barrier = a
-        else:
-            parts, names = [], []
-            for p, n in queue[:2]:
-                parts, names = parts + p, names + n
-            parts[0] = tie(parts[0], now)
-            barrier = multiply(parts, names)
-            done.append(barrier)
-            placed.append(names)
-            queue = queue[2:]
-        queue.append(([now, send(now, across)], [name, name + 2]))
-        coming = [(tie(after, barrier), after_name)] + further
-    now, name = coming[0]
-    queue.append(([now, send(now, across)], [name, name + 2]))
-    parts, names = [], []
-    for p, n in queue:
-        parts, names = parts + p, names + n
+        if queue:
+            after = tie(after, work(queue, now))
+        queue = [both(now, name)]
+        coming = [(after, after_name)] + further
+    units = queue + [both(*coming[0])]
+    parts, names = [v for p, _ in units for v in p], [n for _, ns in units for n in ns]
     return multiply(parts, names, old=done, placed=placed, queries=queries)
 
 

time: 73.6 us -> 72.1 us (0.980)
  Pallas kernels: 30.5 us -> 29.2 us
  waiting for transfers between devices: 16.3 us -> 15.5 us
    pallas_call x4, Pallas kernels: 14.5 us -> 13.1 us  [products(): pl.pallas_call(functools.partial(products_kernel, units, placed, shapes,...]
    ppermute x26, waiting for transfers between devices: 16.3 us -> 15.5 us  [local(): send = lambda v, way: lax.ppermute(v, 'shard', way)]
    concatenate x0 -> x1, local copies, waits for them, and re-layouts: none -> 0.78 us  [local(): scalars = jnp.concatenate([info, owner_slot, query_routes.T.reshape(-1)])]
    pallas_call x3 -> x4, Pallas kernels: 12.1 us -> 12.1 us  [precondition(): pl.pallas_call(functools.partial(precondition_kernel, units, experts, siz...]
  transfers between devices with their start and end apart: 26 -> 26, of which waited for: 13 -> 11; matrix products, arithmetic and copies ran while one was open for 4% -> 5% of each run, Pallas kernels for 35% -> 34%
where the time goes in v7:
time: 72.1 us; the launch traced here: 71.8 us
  Pallas kernels  29.2 us (40%)
  starting transfers between devices  22.7 us (31%)
  waiting for transfers between devices  15.5 us (21%)
  local copies, waits for them, and re-layouts  2.84 us (4%)
  between operations  0.91 us (1%)
    ppermute x26, starting transfers between devices, local(): send = lambda v, way: lax.ppermute(v, 'shard', way)  22.7 us
    ppermute x26, waiting for transfers between devices, local(): send = lambda v, way: lax.ppermute(v, 'shard', way)  15.5 us
    pallas_call x4, Pallas kernels, products(): pl.pallas_call(functools.partial(products_kernel, units, placed, shapes,...  13.1 us
    pallas_call x4, Pallas kernels, precondition(): pl.pallas_call(functools.partial(precondition_kernel, units, experts, siz...  12.1 us
    pallas_call x4, Pallas kernels, prepare(): pl.pallas_call(functools.partial(prepare_kernel, at, src.shape[0] // 96),...  2.83 us
  transfers between devices with their start and end apart: 26, of which 11 were waited for; matrix products, arithmetic and copies ran while one was open for 5% of the time, Pallas kernels for 34%

profile of v7, /device:TPU:0, one launch (start us, length us, event | category | flops | bytes accessed | tf_op | source)
XLA Modules:
  0.0 71.8 jit_solution(9565503733796052482)
XLA Ops:
  0.0 1.2 %pack.1 = f32[192,128]{1,0:T(8,128)S(1)} custom-call(f32[2,64,64]{2,1,0:T(8,128)} %s.1, f32[2,64,64]{2,1,0:T(8,128)} %a.1, f32[2,64,64]{2,1,0:T(8,128)} %lam.1), custom_call_target="tpu_custom_call" | custom-call | flops 1000 | bytes 1000 | tf_op jit(solution)/shard_map/pack/pallas_call | solution.py:96
  1.2 3.1 %collective-permute-start.8 = (f32[192,128]{1,0:T(8,128)S(1)}, f32[192,128]{1,0:T(8,128)S(1)}, u32[]{:S(2)}, u32[]{:S(2)}) collective-permute-start(f32[192,128]{1,0:T(8,128)S(1)} %pack.1), channel_id=1, source_target_pairs={{0,4},{1,5},{4,8},{5,9},{8,12},{9,13},{12,14},{13,15},{14,10},{15,... | collective-permute-start | bytes 294920 | tf_op jit(solution)/shard_map/ppermute | solution.py:310
  4.2 0.0 collective-permute-start.9
  4.2 3.0 %collective-permute-start = (f32[192,128]{1,0:T(8,128)S(1)}, f32[192,128]{1,0:T(8,128)S(1)}, u32[]{:S(2)}, u32[]{:S(2)}) collective-permute-start(f32[192,128]{1,0:T(8,128)S(1)} %pack.1), channel_id=1, source_target_pairs={{0,8},{1,9},{4,12},{5,13},{8,14},{9,15},{12,10},{13,11},{14,6},{15... | collective-permute-start | bytes 294920 | tf_op jit(solution)/shard_map/ppermute | solution.py:310
  7.3 0.0 collective-permute-start.3
  7.3 0.0 collective-permute-start.1
  7.3 0.8 %reshape.23 = s32[16,8,8]{1,0,2:T(8,128)S(1)} reshape(s32[128,8]{0,1:T(8,128)} %param.11) | data formatting | bytes 8192 | tf_op jit(solution)/shard_map/reshape | solution.py:318
  8.1 0.1 broadcast_in_dim.22
  8.8 0.7 broadcast_select_fusion
  9.5 0.1 copy.27
  9.6 0.1 reshape.22.route
  9.7 0.7 dynamic-slice_bitcast_fusion
  10.4 0.8 %concatenate.9.info = s32[1108]{0:T(1024)S(1)} concatenate(s32[52]{0:T(128)S(1)} %dynamic-slice_bitcast_fusion, s32[32]{0:T(128)} %param.15, s32[1024]{0:T(1024)} %bitcast.19), dimensions={0} | concatenate | bytes 8864 | tf_op jit(solution)/shard_map/concatenate | solution.py:301
  11.3 0.0 collective-permute-done.9
  11.3 0.2 collective-permute-done
  11.5 0.2 broadcast_in_dim.23.query_route
  11.7 1.8 %collective-permute-start.2 = (f32[192,128]{1,0:T(8,128)S(1)}, f32[192,128]{1,0:T(8,128)S(1)}, u32[]{:S(2)}, u32[]{:S(2)}) collective-permute-start(f32[192,128]{1,0:T(8,128)S(1)} %collective-permute-done), channel_id=1, source_target_pairs={{0,4},{1,5},{4,8},{5,9},{8,12},{9,13},{12,14},{13,15},{14,10},{15,... | collective-permute-start | bytes 294920 | tf_op jit(solution)/shard_map/ppermute | solution.py:310
  13.5 0.1 collective-permute-done.3
  13.7 0.1 collective-permute-start.10
  13.8 2.1 %collective-permute-start.6 = (f32[96,128]{1,0:T(8,128)S(1)}, f32[96,128]{1,0:T(8,128)S(1)}, u32[]{:S(2)}, u32[]{:S(2)}) collective-permute-start(f32[96,128]{1,0:T(8,128)S(1)} %slice.8), channel_id=1, source_target_pairs={{0,6},{1,7},{4,2},{5,3},{8,0},{9,1},{12,4},{13,5},{14,8},{15,9},{1... | collective-permute-start | bytes 147464 | tf_op jit(solution)/shard_map/ppermute | solution.py:310
  15.9 0.9 %collective-permute-start.4 = (f32[192,128]{1,0:T(8,128)S(1)}, f32[192,128]{1,0:T(8,128)S(1)}, u32[]{:S(2)}, u32[]{:S(2)}) collective-permute-start(f32[192,128]{1,0:T(8,128)S(1)} %collective-permute-done.3), channel_id=1, source_target_pairs={{0,2},{1,3},{4,0},{5,1},{8,4},{9,5},{12,8},{13,9},{14,12},{15,13},... | collective-permute-start | bytes 294920 | tf_op jit(solution)/shard_map/ppermute | solution.py:310
  16.8 0.6 collective-permute-start.5
  17.4 0.0 collective-permute-done.2
  17.4 1.4 %collective-permute-start.11 = (bf16[64,4096]{1,0:T(8,128)(2,1)S(1)}, bf16[64,4096]{1,0:T(8,128)(2,1)S(1)}, u32[]{:S(2)}, u32[]{:S(2)}) collective-permute-start(bf16[64,4096]{1,0:T(8,128)(2,1)S(1)} %bitcast.21), channel_id=1, source_target_pairs={{0,4},{1,3},{4,8},{5,1},{8,12},{9,5},{12,14},{13,9},{14,10},{15,13... | collective-permute-start | bytes 1572872 | tf_op jit(solution)/shard_map/ppermute | solution.py:310
  18.8 2.9 %collective-permute-done.4 = f32[192,128]{1,0:T(8,128)S(1)} collective-permute-done((f32[192,128]{1,0:T(8,128)S(1)}, f32[192,128]{1,0:T(8,128)S(1)}, u32[]{:S(2)}, u32[]{:S(2)}) %collective-permute-start.4) | collective-permute-done | bytes 98336 | tf_op jit(solution)/shard_map/ppermute | solution.py:310
  21.7 0.5 collective-permute-done.5
  22.2 0.0 collective-permute-done.6
  22.2 0.1 collective-permute-start.7
  22.3 0.9 %prepare.4 = (bf16[32,2,128,128]{3,2,1,0:T(8,128)(2,1)S(1)}, bf16[32,2,128,128]{3,2,1,0:T(8,128)(2,1)S(1)}, bf16[32,64,256]{2,1,0:T(8,128)(2,1)S(1)}, bf16[32,64,256]{2,1,0:T(8,128)(2,1)S(1)}, f32[32,64,128]{2,1,0:T(8,128)S(1)}) custom-call(f32[960,128]{1,0:T(8,128)S(1)} %constant_dynamic-update-slice_fusion.4.src), custom_call_target="tpu_custom_call" | custom-call | flops 1000 | bytes 1000 | tf_op jit(solution)/shard_map/prepare/pallas_call | solution.py:65
  23.2 0.0 collective-permute-done.10.src
  23.2 0.9 %prepare.5 = (bf16[32,2,128,128]{3,2,1,0:T(8,128)(2,1)S(1)}, bf16[32,2,128,128]{3,2,1,0:T(8,128)(2,1)S(1)}, bf16[32,64,256]{2,1,0:T(8,128)(2,1)S(1)}, bf16[32,64,256]{2,1,0:T(8,128)(2,1)S(1)}, f32[32,64,128]{2,1,0:T(8,128)S(1)}) custom-call(f32[960,128]{1,0:T(8,128)S(1)} %collective-permute-done., ...), custom_call_target="tpu_custom_call", output_to_operand_aliasing={{0}: (1, {}), {1}: (2, {}), {2}: (3, {}), {3}: (4, {}), {4}... | custom-call | flops 1000 | bytes 1000 | tf_op jit(solution)/shard_map/prepare/pallas_call | solution.py:65
  24.2 0.5 prepare.6
  24.7 0.5 prepare.7
  25.2 1.9 %collective-permute-done.11.rest_0_ = bf16[64,4096]{1,0:T(8,128)(2,1)S(1)} collective-permute-done((bf16[64,4096]{1,0:T(8,128)(2,1)S(1)}, bf16[64,4096]{1,0:T(8,128)(2,1)S(1)}, u32[]{:S(2)}, u32[]{:S(2)}) %collective-permute-start.11) | collective-permute-done | bytes 524320 | tf_op jit(solution)/shard_map/ppermute | solution.py:310
  27.1 0.8 %collective-permute-start.12 = (bf16[64,4096]{1,0:T(8,128)(2,1)S(1)}, bf16[64,4096]{1,0:T(8,128)(2,1)S(1)}, u32[]{:S(2)}, u32[]{:S(2)}) collective-permute-start(bf16[64,4096]{1,0:T(8,128)(2,1)S(1)} %collective-permute-done.11.rest_0_), channel_id=1, source_target_pairs={{0,4},{1,3},{4,8},{5,1},{8,12},{9,5},{12,14},{13,9},{14,10},{15,13... | collective-permute-start | bytes 1572872 | tf_op jit(solution)/shard_map/ppermute | solution.py:310
  28.0 3.0 %precondition.4.rest_1_ = bf16[64,4096]{1,0:T(8,128)(2,1)S(1)} custom-call(s32[1108]{0:T(1024)S(1)} %concatenate.9.info, bf16[32,2,128,128]{3,2,1,0:T(8,128)(2,1)S(1)} %get-tuple-element.53.tab_a, bf16[32,2,128,128]{3,2,1,0:T(8,128)(2,1)S(1)} %get-tuple-element.54.tab_at, bf16[32,64,256]{2,1,0:T(8,128)(2,1)S(1)} %get-tuple-element.55.tab_s, ...), custom_call_target="tpu_custom_call" | custom-call | flops 1000 | bytes 1000 | tf_op jit(solution)/shard_map/precondition/pallas_call | solution.py:173
  31.0 1.8 %collective-permute-start.15 = (bf16[64,4096]{1,0:T(8,128)(2,1)S(1)}, bf16[64,4096]{1,0:T(8,128)(2,1)S(1)}, u32[]{:S(2)}, u32[]{:S(2)}) collective-permute-start(bf16[64,4096]{1,0:T(8,128)(2,1)S(1)} %precondition.4.rest_1_), channel_id=1, source_target_pairs={{0,4},{1,3},{4,8},{5,1},{8,12},{9,5},{12,14},{13,9},{14,10},{15,13... | collective-permute-start | bytes 1572872 | tf_op jit(solution)/shard_map/ppermute | solution.py:310
  32.8 3.0 %precondition.5.rest_2_ = bf16[64,4096]{1,0:T(8,128)(2,1)S(1)} custom-call(s32[1108]{0:T(1024)S(1)} %concatenate.9.info, bf16[32,2,128,128]{3,2,1,0:T(8,128)(2,1)S(1)} %get-tuple-element.53.tab_a, bf16[32,2,128,128]{3,2,1,0:T(8,128)(2,1)S(1)} %get-tuple-element.54.tab_at, bf16[32,64,256]{2,1,0:T(8,128)(2,1)S(1)} %get-tuple-element.55.tab_s, ...), custom_call_target="tpu_custom_call" | custom-call | flops 1000 | bytes 1000 | tf_op jit(solution)/shard_map/precondition/pallas_call | solution.py:173
  35.8 0.0 slice-start.1
  35.8 0.6 collective-permute-start.16
  36.4 0.0 collective-permute-done.12.rest_0_
  36.4 1.4 %collective-permute-start.13 = (bf16[64,4096]{1,0:T(8,128)(2,1)S(1)}, bf16[64,4096]{1,0:T(8,128)(2,1)S(1)}, u32[]{:S(2)}, u32[]{:S(2)}) collective-permute-start(bf16[64,4096]{1,0:T(8,128)(2,1)S(1)} %collective-permute-done.12.rest_0_), channel_id=1, source_target_pairs={{0,4},{1,3},{4,8},{5,1},{8,12},{9,5},{12,14},{13,9},{14,10},{15,13... | collective-permute-start | bytes 1572872 | tf_op jit(solution)/shard_map/ppermute | solution.py:310
  37.8 3.0 %precondition.6.rest_0_ = bf16[64,4096]{1,0:T(8,128)(2,1)S(1)} custom-call(s32[1108]{0:T(1024)S(1)} %concatenate.9.info, bf16[32,2,128,128]{3,2,1,0:T(8,128)(2,1)S(1)} %get-tuple-element.53.tab_a, bf16[32,2,128,128]{3,2,1,0:T(8,128)(2,1)S(1)} %get-tuple-element.54.tab_at, bf16[32,64,256]{2,1,0:T(8,128)(2,1)S(1)} %get-tuple-element.55.tab_s, ...), custom_call_target="tpu_custom_call" | custom-call | flops 1000 | bytes 1000 | tf_op jit(solution)/shard_map/precondition/pallas_call | solution.py:173
  40.8 1.1 %collective-permute-done.15.rest_2_ = bf16[64,4096]{1,0:T(8,128)(2,1)S(1)} collective-permute-done((bf16[64,4096]{1,0:T(8,128)(2,1)S(1)}, bf16[64,4096]{1,0:T(8,128)(2,1)S(1)}, u32[]{:S(2)}, u32[]{:S(2)}) %collective-permute-start.15) | collective-permute-done | bytes 524320 | tf_op jit(solution)/shard_map/ppermute | solution.py:310
  41.9 0.0 collective-permute-start.21
  41.9 0.5 collective-permute-start.20
  42.4 0.8 %collective-permute-start.19 = (bf16[64,4096]{1,0:T(8,128)(2,1)S(1)}, bf16[64,4096]{1,0:T(8,128)(2,1)S(1)}, u32[]{:S(2)}, u32[]{:S(2)}) collective-permute-start(bf16[64,4096]{1,0:T(8,128)(2,1)S(1)} %collective-permute-done.15.rest_2_), channel_id=1, source_target_pairs={{0,4},{1,3},{4,8},{5,1},{8,12},{9,5},{12,14},{13,9},{14,10},{15,13... | collective-permute-start | bytes 1572872 | tf_op jit(solution)/shard_map/ppermute | solution.py:310
  43.3 3.1 %products.4.rest_4_ = f32[32,128]{1,0:T(8,128)S(1)} custom-call(s32[1108]{0:T(1024)S(1)} %concatenate.9.info, s32[1,1024]{1,0:T(1,128)S(1)} %reshape.22.route, s32[1024,128]{1,0:T(8,128)S(1)} %broadcast_in_dim.23.query_route, bf16[1024,4096]{1,0:T(8,128)(2,1)S(1)} %bitcast.14, bf16[64,4096]{1,0:T(8,128)(2,1)S(1)} %collective-permute-done.14.rest_0_, ...), custom_call_target="tpu_custom_call" | custom-call | flops 1000 | bytes 1000 | tf_op jit(solution)/shard_map/products/pallas_call | solution.py:237
  46.4 1.1 %collective-permute-done.13.rest_0_ = bf16[64,4096]{1,0:T(8,128)(2,1)S(1)} collective-permute-done((bf16[64,4096]{1,0:T(8,128)(2,1)S(1)}, bf16[64,4096]{1,0:T(8,128)(2,1)S(1)}, u32[]{:S(2)}, u32[]{:S(2)}) %collective-permute-start.13) | collective-permute-done | bytes 524320 | tf_op jit(solution)/shard_map/ppermute | solution.py:310
  47.5 3.0 %precondition.7.rest_0_ = bf16[64,4096]{1,0:T(8,128)(2,1)S(1)} custom-call(s32[1108]{0:T(1024)S(1)} %concatenate.9.info, bf16[32,2,128,128]{3,2,1,0:T(8,128)(2,1)S(1)} %get-tuple-element.53.tab_a, bf16[32,2,128,128]{3,2,1,0:T(8,128)(2,1)S(1)} %get-tuple-element.54.tab_at, bf16[32,64,256]{2,1,0:T(8,128)(2,1)S(1)} %get-tuple-element.55.tab_s, ...), custom_call_target="tpu_custom_call" | custom-call | flops 1000 | bytes 1000 | tf_op jit(solution)/shard_map/precondition/pallas_call | solution.py:173
  50.6 0.9 %collective-permute-start.17 = (bf16[64,4096]{1,0:T(8,128)(2,1)S(1)}, bf16[64,4096]{1,0:T(8,128)(2,1)S(1)}, u32[]{:S(2)}, u32[]{:S(2)}) collective-permute-start(bf16[64,4096]{1,0:T(8,128)(2,1)S(1)} %precondition.7.rest_0_), channel_id=1, source_target_pairs={{0,4},{1,3},{4,8},{5,1},{8,12},{9,5},{12,14},{13,9},{14,10},{15,13... | collective-permute-start | bytes 1572872 | tf_op jit(solution)/shard_map/ppermute | solution.py:310
  51.5 3.1 %products.5.rest_5_ = f32[32,128]{1,0:T(8,128)S(1)} custom-call(s32[1108]{0:T(1024)S(1)} %concatenate.9.info, s32[1,1024]{1,0:T(1,128)S(1)} %reshape.22.route, s32[1024,128]{1,0:T(8,128)S(1)} %broadcast_in_dim.23.query_route, bf16[1024,4096]{1,0:T(8,128)(2,1)S(1)} %bitcast.15, bf16[64,4096]{1,0:T(8,128)(2,1)S(1)} %precondition.6.rest_0_, ...), custom_call_target="tpu_custom_call" | custom-call | flops 1000 | bytes 1000 | tf_op jit(solution)/shard_map/products/pallas_call | solution.py:237
  54.6 0.0 collective-permute-done.19.rest_2_
  54.6 0.1 collective-permute-start.24
  54.7 0.5 collective-permute-start.23
  55.2 1.7 %collective-permute-start.22 = (bf16[64,4096]{1,0:T(8,128)(2,1)S(1)}, bf16[64,4096]{1,0:T(8,128)(2,1)S(1)}, u32[]{:S(2)}, u32[]{:S(2)}) collective-permute-start(bf16[64,4096]{1,0:T(8,128)(2,1)S(1)} %collective-permute-done.19.rest_2_), channel_id=1, source_target_pairs={{0,4},{1,3},{4,8},{5,1},{8,12},{9,5},{12,14},{13,9},{14,10},{15,13... | collective-permute-start | bytes 1572872 | tf_op jit(solution)/shard_map/ppermute | solution.py:310
  56.9 2.9 %collective-permute-done.17.rest_0_ = bf16[64,4096]{1,0:T(8,128)(2,1)S(1)} collective-permute-done((bf16[64,4096]{1,0:T(8,128)(2,1)S(1)}, bf16[64,4096]{1,0:T(8,128)(2,1)S(1)}, u32[]{:S(2)}, u32[]{:S(2)}) %collective-permute-start.17) | collective-permute-done | bytes 524320 | tf_op jit(solution)/shard_map/ppermute | solution.py:310
  59.8 0.0 collective-permute-done.24.rest_3_
  59.8 3.1 %products.6.rest_6_ = f32[32,128]{1,0:T(8,128)S(1)} custom-call(s32[1108]{0:T(1024)S(1)} %concatenate.9.info, s32[1,1024]{1,0:T(1,128)S(1)} %reshape.22.route, s32[1024,128]{1,0:T(8,128)S(1)} %broadcast_in_dim.23.query_route, bf16[1024,4096]{1,0:T(8,128)(2,1)S(1)} %bitcast.16, bf16[64,4096]{1,0:T(8,128)(2,1)S(1)} %precondition.7.rest_0_, ...), custom_call_target="tpu_custom_call" | custom-call | flops 1000 | bytes 1000 | tf_op jit(solution)/shard_map/products/pallas_call | solution.py:237
  62.9 2.5 %collective-permute-done.22.rest_2_ = bf16[64,4096]{1,0:T(8,128)(2,1)S(1)} collective-permute-done((bf16[64,4096]{1,0:T(8,128)(2,1)S(1)}, bf16[64,4096]{1,0:T(8,128)(2,1)S(1)}, u32[]{:S(2)}, u32[]{:S(2)}) %collective-permute-start.22) | collective-permute-done | bytes 524320 | tf_op jit(solution)/shard_map/ppermute | solution.py:310
  65.4 0.5 collective-permute-start.18
  65.9 1.4 %collective-permute-done.25.rest_3_ = bf16[64,4096]{1,0:T(8,128)(2,1)S(1)} collective-permute-done((bf16[64,4096]{1,0:T(8,128)(2,1)S(1)}, bf16[64,4096]{1,0:T(8,128)(2,1)S(1)}, u32[]{:S(2)}, u32[]{:S(2)}) %collective-permute-start.25) | collective-permute-done | bytes 524320 | tf_op jit(solution)/shard_map/ppermute | solution.py:310
  67.3 0.7 %collective-permute-done.18.rest_1_ = bf16[64,4096]{1,0:T(8,128)(2,1)S(1)} collective-permute-done((bf16[64,4096]{1,0:T(8,128)(2,1)S(1)}, bf16[64,4096]{1,0:T(8,128)(2,1)S(1)}, u32[]{:S(2)}, u32[]{:S(2)}) %collective-permute-start.18) | collective-permute-done | bytes 524320 | tf_op jit(solution)/shard_map/ppermute | solution.py:310
  68.1 3.8 %products.7 = f32[128,128]{1,0:T(8,128)} custom-call(s32[1108]{0:T(1024)S(1)} %concatenate.9.info, s32[1,1024]{1,0:T(1,128)S(1)} %reshape.22.route, s32[1024,128]{1,0:T(8,128)S(1)} %broadcast_in_dim.23.query_route, bf16[1024,4096]{1,0:T(8,128)(2,1)S(1)} %bitcast.17, bf16[64,4096]{1,0:T(8,128)(2,1)S(1)} %collective-permute-done.17.rest_0_, ...), custom_call_target="tpu_custom_call" | custom-call | flops 1000 | bytes 1000 | tf_op jit(solution)/shard_map/products/pallas_call | solution.py:237
  (29 shorter events, 0.1 us)
Async XLA Ops:
  0.0 17.4 %copy-start = (bf16[8,8,4096]{2,1,0:T(8,128)(2,1)S(1)}, bf16[8,8,4096]{2,1,0:T(8,128)(2,1)}, u32[]{:S(2)}) copy-start(bf16[8,8,4096]{2,1,0:T(8,128)(2,1)} %param.10) | copy-start | bytes 1572868
  1.2 10.1 %collective-permute-start.8 = (f32[192,128]{1,0:T(8,128)S(1)}, f32[192,128]{1,0:T(8,128)S(1)}, u32[]{:S(2)}, u32[]{:S(2)}) collective-permute-start(f32[192,128]{1,0:T(8,128)S(1)} %pack.1), channel_id=1, source_target_pairs={{0,4},{1,5},{4,8},{5,9},{8,12},{9,13},{12,14},{13,15},{14,10},{15,... | collective-permute-start | bytes 294920 | tf_op jit(solution)/shard_map/ppermute | solution.py:310
  4.2 7.0 %collective-permute-start.9 = (f32[192,128]{1,0:T(8,128)S(1)}, f32[192,128]{1,0:T(8,128)S(1)}, u32[]{:S(2)}, u32[]{:S(2)}) collective-permute-start(f32[192,128]{1,0:T(8,128)S(1)} %pack.1), channel_id=1, source_target_pairs={{0,2},{1,3},{4,0},{5,1},{8,4},{9,5},{12,8},{13,9},{14,12},{15,13},... | collective-permute-start | bytes 294920 | tf_op jit(solution)/shard_map/ppermute | solution.py:310
  4.2 7.2 %collective-permute-start = (f32[192,128]{1,0:T(8,128)S(1)}, f32[192,128]{1,0:T(8,128)S(1)}, u32[]{:S(2)}, u32[]{:S(2)}) collective-permute-start(f32[192,128]{1,0:T(8,128)S(1)} %pack.1), channel_id=1, source_target_pairs={{0,8},{1,9},{4,12},{5,13},{8,14},{9,15},{12,10},{13,11},{14,6},{15... | collective-permute-start | bytes 294920 | tf_op jit(solution)/shard_map/ppermute | solution.py:310
  7.3 6.4 %collective-permute-start.3 = (f32[192,128]{1,0:T(8,128)S(1)}, f32[192,128]{1,0:T(8,128)S(1)}, u32[]{:S(2)}, u32[]{:S(2)}) collective-permute-start(f32[192,128]{1,0:T(8,128)S(1)} %pack.1), channel_id=1, source_target_pairs={{0,6},{1,7},{4,2},{5,3},{8,0},{9,1},{12,4},{13,5},{14,8},{15,9},{1... | collective-permute-start | bytes 294920 | tf_op jit(solution)/shard_map/ppermute | solution.py:310
  7.3 4.2 %collective-permute-start.1 = (bf16[64,4096]{1,0:T(8,128)(2,1)}, bf16[64,4096]{1,0:T(8,128)(2,1)S(1)}, u32[]{:S(2)}, u32[]{:S(2)}) collective-permute-start(bf16[64,4096]{1,0:T(8,128)(2,1)} %bitcast.20), channel_id=1, source_target_pairs={{0,1},{1,0},{2,3},{3,2},{4,5},{5,4},{6,7},{7,6},{8,9},{9,8},{10,11... | collective-permute-start | bytes 1572872 | tf_op jit(solution)/shard_map/ppermute | solution.py:310
  11.7 5.7 %collective-permute-start.2 = (f32[192,128]{1,0:T(8,128)S(1)}, f32[192,128]{1,0:T(8,128)S(1)}, u32[]{:S(2)}, u32[]{:S(2)}) collective-permute-start(f32[192,128]{1,0:T(8,128)S(1)} %collective-permute-done), channel_id=1, source_target_pairs={{0,4},{1,5},{4,8},{5,9},{8,12},{9,13},{12,14},{13,15},{14,10},{15,... | collective-permute-start | bytes 294920 | tf_op jit(solution)/shard_map/ppermute | solution.py:310
  13.7 9.6 %collective-permute-start.10 = (f32[960,128]{1,0:T(8,128)S(1)}, f32[960,128]{1,0:T(8,128)S(1)}, u32[]{:S(2)}, u32[]{:S(2)}) collective-permute-start(f32[960,128]{1,0:T(8,128)S(1)} %constant_dynamic-update-slice_fusion.4.src), channel_id=1, source_target_pairs={{0,1},{1,0},{2,3},{3,2},{4,5},{5,4},{6,7},{7,6},{8,9},{9,8},{10,11... | collective-permute-start | bytes 1474568 | tf_op jit(solution)/shard_map/ppermute | solution.py:310
  13.8 8.4 %collective-permute-start.6 = (f32[96,128]{1,0:T(8,128)S(1)}, f32[96,128]{1,0:T(8,128)S(1)}, u32[]{:S(2)}, u32[]{:S(2)}) collective-permute-start(f32[96,128]{1,0:T(8,128)S(1)} %slice.8), channel_id=1, source_target_pairs={{0,6},{1,7},{4,2},{5,3},{8,0},{9,1},{12,4},{13,5},{14,8},{15,9},{1... | collective-permute-start | bytes 147464 | tf_op jit(solution)/shard_map/ppermute | solution.py:310
  15.9 5.8 %collective-permute-start.4 = (f32[192,128]{1,0:T(8,128)S(1)}, f32[192,128]{1,0:T(8,128)S(1)}, u32[]{:S(2)}, u32[]{:S(2)}) collective-permute-start(f32[192,128]{1,0:T(8,128)S(1)} %collective-permute-done.3), channel_id=1, source_target_pairs={{0,2},{1,3},{4,0},{5,1},{8,4},{9,5},{12,8},{13,9},{14,12},{15,13},... | collective-permute-start | bytes 294920 | tf_op jit(solution)/shard_map/ppermute | solution.py:310
  16.8 5.4 %collective-permute-start.5 = (f32[96,128]{1,0:T(8,128)S(1)}, f32[96,128]{1,0:T(8,128)S(1)}, u32[]{:S(2)}, u32[]{:S(2)}) collective-permute-start(f32[96,128]{1,0:T(8,128)S(1)} %slice.6), channel_id=1, source_target_pairs={{0,8},{1,9},{4,12},{5,13},{8,14},{9,15},{12,10},{13,11},{14,6},{15... | collective-permute-start | bytes 147464 | tf_op jit(solution)/shard_map/ppermute | solution.py:310
  17.4 9.7 %collective-permute-start.11 = (bf16[64,4096]{1,0:T(8,128)(2,1)S(1)}, bf16[64,4096]{1,0:T(8,128)(2,1)S(1)}, u32[]{:S(2)}, u32[]{:S(2)}) collective-permute-start(bf16[64,4096]{1,0:T(8,128)(2,1)S(1)} %bitcast.21), channel_id=1, source_target_pairs={{0,4},{1,3},{4,8},{5,1},{8,12},{9,5},{12,14},{13,9},{14,10},{15,13... | collective-permute-start | bytes 1572872 | tf_op jit(solution)/shard_map/ppermute | solution.py:310
  22.2 2.4 %collective-permute-start.7 = (f32[576,128]{1,0:T(8,128)S(1)}, f32[576,128]{1,0:T(8,128)S(1)}, u32[]{:S(2)}, u32[]{:S(2)}) collective-permute-start(f32[576,128]{1,0:T(8,128)S(1)} %constant_dynamic-update-slice_fusion.src), channel_id=1, source_target_pairs={{0,1},{1,0},{2,3},{3,2},{4,5},{5,4},{6,7},{7,6},{8,9},{9,8},{10,11... | collective-permute-start | bytes 884744 | tf_op jit(solution)/shard_map/ppermute | solution.py:310
  27.1 9.3 %collective-permute-start.12 = (bf16[64,4096]{1,0:T(8,128)(2,1)S(1)}, bf16[64,4096]{1,0:T(8,128)(2,1)S(1)}, u32[]{:S(2)}, u32[]{:S(2)}) collective-permute-start(bf16[64,4096]{1,0:T(8,128)(2,1)S(1)} %collective-permute-done.11.rest_0_), channel_id=1, source_target_pairs={{0,4},{1,3},{4,8},{5,1},{8,12},{9,5},{12,14},{13,9},{14,10},{15,13... | collective-permute-start | bytes 1572872 | tf_op jit(solution)/shard_map/ppermute | solution.py:310
  31.0 10.9 %collective-permute-start.15 = (bf16[64,4096]{1,0:T(8,128)(2,1)S(1)}, bf16[64,4096]{1,0:T(8,128)(2,1)S(1)}, u32[]{:S(2)}, u32[]{:S(2)}) collective-permute-start(bf16[64,4096]{1,0:T(8,128)(2,1)S(1)} %precondition.4.rest_1_), channel_id=1, source_target_pairs={{0,4},{1,3},{4,8},{5,1},{8,12},{9,5},{12,14},{13,9},{14,10},{15,13... | collective-permute-start | bytes 1572872 | tf_op jit(solution)/shard_map/ppermute | solution.py:310
  32.8 9.7 %collective-permute-start.14 = (bf16[64,4096]{1,0:T(8,128)(2,1)S(1)}, bf16[64,4096]{1,0:T(8,128)(2,1)S(1)}, u32[]{:S(2)}, u32[]{:S(2)}) collective-permute-start(bf16[64,4096]{1,0:T(8,128)(2,1)S(1)} %precondition.4.rest_1_), channel_id=1, source_target_pairs={{0,1},{1,0},{2,3},{3,2},{4,5},{5,4},{6,7},{7,6},{8,9},{9,8},{10,11... | collective-permute-start | bytes 1572872 | tf_op jit(solution)/shard_map/ppermute | solution.py:310
  32.8 10.5 %slice-start = ((s8[8388608]{0:T(1024)(128)(4,1)}), s8[4194304]{0:T(1024)(128)(4,1)S(1)}, s32[]{:S(2)}) async-start(s8[8388608]{0:T(1024)(128)(4,1)} %bitcast.12), calls=%async_computation | async-start | bytes 8388608
  35.8 7.5 %slice-start.1 = ((s8[8388608]{0:T(1024)(128)(4,1)}), s8[4194304]{0:T(1024)(128)(4,1)S(1)}, s32[]{:S(2)}) async-start(s8[8388608]{0:T(1024)(128)(4,1)} %bitcast.12), calls=%async_computation.1 | async-start | bytes 8388608
  35.8 7.5 %collective-permute-start.16 = (bf16[64,4096]{1,0:T(8,128)(2,1)S(1)}, bf16[64,4096]{1,0:T(8,128)(2,1)S(1)}, u32[]{:S(2)}, u32[]{:S(2)}) collective-permute-start(bf16[64,4096]{1,0:T(8,128)(2,1)S(1)} %precondition.5.rest_2_), channel_id=1, source_target_pairs={{0,1},{1,0},{2,3},{3,2},{4,5},{5,4},{6,7},{7,6},{8,9},{9,8},{10,11... | collective-permute-start | bytes 1572872 | tf_op jit(solution)/shard_map/ppermute | solution.py:310
  36.4 11.2 %collective-permute-start.13 = (bf16[64,4096]{1,0:T(8,128)(2,1)S(1)}, bf16[64,4096]{1,0:T(8,128)(2,1)S(1)}, u32[]{:S(2)}, u32[]{:S(2)}) collective-permute-start(bf16[64,4096]{1,0:T(8,128)(2,1)S(1)} %collective-permute-done.12.rest_0_), channel_id=1, source_target_pairs={{0,4},{1,3},{4,8},{5,1},{8,12},{9,5},{12,14},{13,9},{14,10},{15,13... | collective-permute-start | bytes 1572872 | tf_op jit(solution)/shard_map/ppermute | solution.py:310
  41.9 9.5 %collective-permute-start.21 = (bf16[64,4096]{1,0:T(8,128)(2,1)S(1)}, bf16[64,4096]{1,0:T(8,128)(2,1)S(1)}, u32[]{:S(2)}, u32[]{:S(2)}) collective-permute-start(bf16[64,4096]{1,0:T(8,128)(2,1)S(1)} %collective-permute-done.15.rest_2_), channel_id=1, source_target_pairs={{0,1},{1,0},{2,3},{3,2},{4,5},{5,4},{6,7},{7,6},{8,9},{9,8},{10,11... | collective-permute-start | bytes 1572872 | tf_op jit(solution)/shard_map/ppermute | solution.py:310
  41.9 9.5 %collective-permute-start.20 = (bf16[64,4096]{1,0:T(8,128)(2,1)S(1)}, bf16[64,4096]{1,0:T(8,128)(2,1)S(1)}, u32[]{:S(2)}, u32[]{:S(2)}) collective-permute-start(bf16[64,4096]{1,0:T(8,128)(2,1)S(1)} %precondition.6.rest_0_), channel_id=1, source_target_pairs={{0,1},{1,0},{2,3},{3,2},{4,5},{5,4},{6,7},{7,6},{8,9},{9,8},{10,11... | collective-permute-start | bytes 1572872 | tf_op jit(solution)/shard_map/ppermute | solution.py:310
  42.4 12.1 %collective-permute-start.19 = (bf16[64,4096]{1,0:T(8,128)(2,1)S(1)}, bf16[64,4096]{1,0:T(8,128)(2,1)S(1)}, u32[]{:S(2)}, u32[]{:S(2)}) collective-permute-start(bf16[64,4096]{1,0:T(8,128)(2,1)S(1)} %collective-permute-done.15.rest_2_), channel_id=1, source_target_pairs={{0,4},{1,3},{4,8},{5,1},{8,12},{9,5},{12,14},{13,9},{14,10},{15,13... | collective-permute-start | bytes 1572872 | tf_op jit(solution)/shard_map/ppermute | solution.py:310
  50.6 9.2 %collective-permute-start.17 = (bf16[64,4096]{1,0:T(8,128)(2,1)S(1)}, bf16[64,4096]{1,0:T(8,128)(2,1)S(1)}, u32[]{:S(2)}, u32[]{:S(2)}) collective-permute-start(bf16[64,4096]{1,0:T(8,128)(2,1)S(1)} %precondition.7.rest_0_), channel_id=1, source_target_pairs={{0,4},{1,3},{4,8},{5,1},{8,12},{9,5},{12,14},{13,9},{14,10},{15,13... | collective-permute-start | bytes 1572872 | tf_op jit(solution)/shard_map/ppermute | solution.py:310
  54.6 5.2 %collective-permute-start.24 = (bf16[64,4096]{1,0:T(8,128)(2,1)S(1)}, bf16[64,4096]{1,0:T(8,128)(2,1)S(1)}, u32[]{:S(2)}, u32[]{:S(2)}) collective-permute-start(bf16[64,4096]{1,0:T(8,128)(2,1)S(1)} %collective-permute-done.19.rest_2_), channel_id=1, source_target_pairs={{0,1},{1,0},{2,3},{3,2},{4,5},{5,4},{6,7},{7,6},{8,9},{9,8},{10,11... | collective-permute-start | bytes 1572872 | tf_op jit(solution)/shard_map/ppermute | solution.py:310
  54.7 5.1 %collective-permute-start.23 = (bf16[64,4096]{1,0:T(8,128)(2,1)S(1)}, bf16[64,4096]{1,0:T(8,128)(2,1)S(1)}, u32[]{:S(2)}, u32[]{:S(2)}) collective-permute-start(bf16[64,4096]{1,0:T(8,128)(2,1)S(1)} %precondition.7.rest_0_), channel_id=1, source_target_pairs={{0,1},{1,0},{2,3},{3,2},{4,5},{5,4},{6,7},{7,6},{8,9},{9,8},{10,11... | collective-permute-start | bytes 1572872 | tf_op jit(solution)/shard_map/ppermute | solution.py:310
  55.2 10.3 %collective-permute-start.22 = (bf16[64,4096]{1,0:T(8,128)(2,1)S(1)}, bf16[64,4096]{1,0:T(8,128)(2,1)S(1)}, u32[]{:S(2)}, u32[]{:S(2)}) collective-permute-start(bf16[64,4096]{1,0:T(8,128)(2,1)S(1)} %collective-permute-done.19.rest_2_), channel_id=1, source_target_pairs={{0,4},{1,3},{4,8},{5,1},{8,12},{9,5},{12,14},{13,9},{14,10},{15,13... | collective-permute-start | bytes 1572872 | tf_op jit(solution)/shard_map/ppermute | solution.py:310
  65.4 1.9 %collective-permute-start.25 = (bf16[64,4096]{1,0:T(8,128)(2,1)S(1)}, bf16[64,4096]{1,0:T(8,128)(2,1)S(1)}, u32[]{:S(2)}, u32[]{:S(2)}) collective-permute-start(bf16[64,4096]{1,0:T(8,128)(2,1)S(1)} %collective-permute-done.22.rest_2_), channel_id=1, source_target_pairs={{0,1},{1,0},{2,3},{3,2},{4,5},{5,4},{6,7},{7,6},{8,9},{9,8},{10,11... | collective-permute-start | bytes 1572872 | tf_op jit(solution)/shard_map/ppermute | solution.py:310
  65.4 2.7 %collective-permute-start.18 = (bf16[64,4096]{1,0:T(8,128)(2,1)S(1)}, bf16[64,4096]{1,0:T(8,128)(2,1)S(1)}, u32[]{:S(2)}, u32[]{:S(2)}) collective-permute-start(bf16[64,4096]{1,0:T(8,128)(2,1)S(1)} %collective-permute-done.17.rest_0_), channel_id=1, source_target_pairs={{0,1},{1,0},{2,3},{3,2},{4,5},{5,4},{6,7},{7,6},{8,9},{9,8},{10,11... | collective-permute-start | bytes 1572872 | tf_op jit(solution)/shard_map/ppermute | solution.py:310

commit v8 on v7

--- a/solution.py
+++ b/solution.py
@@ -128,7 +128,8 @@
 
     for ch in range(chunks):
         raw, out = raws[ch], outs[ch]
-        first = size + experts + info[experts + units[ch]] * 8
+        base = info[info.shape[0] - 1]
+        first = size + experts + info[base + experts + units[ch]] * 8
         for c in range(32):
             xs[pl.ds(c * STRIDE, 64), :] = raw[:, c * 128 : (c + 1) * 128].astype(F32)
 
@@ -136,7 +137,7 @@
             es, g, x = [], [], []
             for i in range(GROUP):
                 row = b * GROUP + i
-                es.append(info[info[size + info[first + row % 8 * queries + row // 8]]])
+                es.append(info[base + info[size + info[first + row % 8 * queries + row // 8]]])
                 g.append(xs[pl.ds(row, 32, stride=STRIDE), :])
             n = GROUP // 2
             ee = [(es[2 * p], es[2 * p + 1]) for p in range(n)]
@@ -189,6 +190,7 @@
     out, held, total = rest[n_in + n_old :]
     blocks = sum(shapes) // 64
     train_rows = train.shape[0]
+    base = info[info.shape[0] - 1]
     at = 0
     for part, r in zip(parts, shapes):
         held[at : at + r, :] = part[...]
@@ -199,7 +201,7 @@
         g = lax.dot_general(held[...], train[here, :], (((1,), (1,)), ((), ())), preferred_element_type=F32)
         there = route[:, here]
         for u in range(blocks):
-            first = pl.multiple_of(info[experts + units[u]] * 64, 64)
+            first = pl.multiple_of(info[base + experts + units[u]] * 64, 64)
             want = jnp.concatenate([query_route[pl.ds(first, 64), :]] * (TILE // 128), 1)
             hit = jnp.where(want == there, g[u * 64 : (u + 1) * 64], 0.0)
             total[u * 8 : (u + 1) * 8, here] = jnp.sum(hit.reshape(8, 8, TILE), axis=0)
@@ -223,7 +225,7 @@
     todo = [(y, units)] + list(zip(old, placed))
     for values, names in todo:
         for u, name in enumerate(names):
-            first = pl.multiple_of(info[experts + name] * 8, 8)
+            first = pl.multiple_of(info[base + experts + name] * 8, 8)
             out[pl.ds(first, 8), :] = values[u * 8 : (u + 1) * 8]
 
 
@@ -296,9 +298,9 @@
     chips = devices // 2
     far = chips // 2
     ring, constants = tables_of(devices, slots)
-    info = lax.dynamic_index_in_dim(jnp.asarray(constants), me, 0, keepdims=False)
-    size = info.shape[0]
-    scalars = jnp.concatenate([info, owner_slot, query_routes.T.reshape(-1)])
+    size = constants.size
+    mine_at = (me * constants.shape[1]).astype(jnp.int32).reshape(1)
+    scalars = jnp.concatenate([jnp.asarray(constants.reshape(-1)), owner_slot, query_routes.T.reshape(-1), mine_at])
 
     def shift(steps):
         return [
@@ -360,28 +362,19 @@
     (b,) = pre([tie(other_raw, near)], [1])
     own = ([send(b, across), b], [0, 1])
     b1 = send(b, stream)
-    (a1,) = pre([tie(near, b)], [4])
-    next_near = tie(next_near, a1)
-    a3 = send(next_near, stream)
-    (a2,) = pre([next_near], [8])
-    b1 = tie(b1, a2)
-    b2 = send(b1, stream)
-    a3 = tie(a3, work([own, both(a1, 4)], b1))
-    (a3,) = pre([a3], [12])
-    a4 = send(a3, stream)
-    b2 = tie(b2, work([both(a2, 8), both(b1, 5)], a3))
-    b3 = send(b2, stream)
-    b3 = tie(b3, work([both(a3, 12), both(b2, 9)], a4))
-    coming, queue = [(a4, 16), (b3, 13)], []
-    while len(coming) > 1:
-        (now, name), (after, after_name) = coming
-        last = 4 * far if name % 4 == 0 else 4 * far - 3
-        further = [(send(now, stream), name + 4)] if name < last else []
-        if queue:
-            after = tie(after, work(queue, now))
-        queue = [both(now, name)]
-        coming = [(after, after_name)] + further
-    units = queue + [both(*coming[0])]
+    (a,) = pre([tie(near, b)], [4])
+    raw_a, b, pending = tie(next_near, a), b1, [own, both(a, 4)]
+    for step in range(2, far):
+        next_a = send(raw_a, stream)
+        (a,) = pre([raw_a], [4 * step])
+        b = tie(b, a)
+        next_b = send(b, stream)
+        raw_a = tie(next_a, work(pending, b))
+        pending = [both(a, 4 * step), both(b, 4 * step - 3)]
+        b = next_b
+    (a,) = pre([raw_a], [4 * far])
+    b = tie(b, work(pending, a))
+    units = [both(a, 4 * far), both(b, 4 * far - 3)]
     parts, names = [v for p, _ in units for v in p], [n for _, ns in units for n in ns]
     return multiply(parts, names, old=done, placed=placed, queries=queries)
 

time: 72.1 us -> 71.8 us (level)
  Pallas kernels: 29.2 us -> 32.7 us
  waiting for transfers between devices: 15.5 us -> 13.1 us
    pallas_call x4 -> x5, Pallas kernels: 12.1 us -> 15.3 us  [precondition(): pl.pallas_call(functools.partial(precondition_kernel, units, experts, siz...]
    ppermute x26, waiting for transfers between devices: 15.5 us -> 13.1 us  [local(): send = lambda v, way: lax.ppermute(v, 'shard', way)]
    ppermute x26, starting transfers between devices: 22.7 us -> 22 us  [local(): send = lambda v, way: lax.ppermute(v, 'shard', way)]
  transfers between devices with their start and end apart: 26 -> 26, of which waited for: 11 -> 11; matrix products, arithmetic and copies ran while one was open for 5% -> 4% of each run, Pallas kernels for 34% -> 39%
where the time goes in v8:
time: 71.8 us; the launch traced here: 71.6 us
  Pallas kernels  32.7 us (46%)
  starting transfers between devices  22 us (31%)
  waiting for transfers between devices  13.1 us (18%)
  local copies, waits for them, and re-layouts  2.16 us (3%)
  between operations  0.95 us (1%)
    ppermute x26, starting transfers between devices, local(): send = lambda v, way: lax.ppermute(v, 'shard', way)  22 us
    pallas_call x5, Pallas kernels, precondition(): pl.pallas_call(functools.partial(precondition_kernel, units, experts, siz...  15.3 us
    pallas_call x4, Pallas kernels, products(): pl.pallas_call(functools.partial(products_kernel, units, placed, shapes,...  13.3 us
    ppermute x26, waiting for transfers between devices, local(): send = lambda v, way: lax.ppermute(v, 'shard', way)  13.1 us
    pallas_call x4, Pallas kernels, prepare(): pl.pallas_call(functools.partial(prepare_kernel, at, src.shape[0] // 96),...  2.83 us
  transfers between devices with their start and end apart: 26, of which 11 were waited for; matrix products, arithmetic and copies ran while one was open for 4% of the time, Pallas kernels for 39%

profile of v8, /device:TPU:0, one launch (start us, length us, event | category | flops | bytes accessed | tf_op | source)
XLA Modules:
  0.0 71.6 jit_solution(16271174485271764284)
XLA Ops:
  0.0 1.2 %pack.1 = f32[192,128]{1,0:T(8,128)S(1)} custom-call(f32[2,64,64]{2,1,0:T(8,128)} %s.1, f32[2,64,64]{2,1,0:T(8,128)} %a.1, f32[2,64,64]{2,1,0:T(8,128)} %lam.1), custom_call_target="tpu_custom_call" | custom-call | flops 1000 | bytes 1000 | tf_op jit(solution)/shard_map/pack/pallas_call | solution.py:96
  1.2 3.1 %collective-permute-start.8 = (f32[192,128]{1,0:T(8,128)S(1)}, f32[192,128]{1,0:T(8,128)S(1)}, u32[]{:S(2)}, u32[]{:S(2)}) collective-permute-start(f32[192,128]{1,0:T(8,128)S(1)} %pack.1), channel_id=1, source_target_pairs={{0,4},{1,5},{4,8},{5,9},{8,12},{9,13},{12,14},{13,15},{14,10},{15,... | collective-permute-start | bytes 294920 | tf_op jit(solution)/shard_map/ppermute | solution.py:312
  4.2 0.0 collective-permute-start.9
  4.2 3.0 %collective-permute-start = (f32[192,128]{1,0:T(8,128)S(1)}, f32[192,128]{1,0:T(8,128)S(1)}, u32[]{:S(2)}, u32[]{:S(2)}) collective-permute-start(f32[192,128]{1,0:T(8,128)S(1)} %pack.1), channel_id=1, source_target_pairs={{0,8},{1,9},{4,12},{5,13},{8,14},{9,15},{12,10},{13,11},{14,6},{15... | collective-permute-start | bytes 294920 | tf_op jit(solution)/shard_map/ppermute | solution.py:312
  7.9 0.7 broadcast_select_fusion
  8.6 0.8 %reshape.27 = s32[16,8,8]{1,0,2:T(8,128)S(1)} reshape(s32[128,8]{0,1:T(8,128)} %param.11) | data formatting | bytes 8192 | tf_op jit(solution)/shard_map/reshape | solution.py:320
  9.4 0.1 broadcast_in_dim.22
  9.5 0.1 copy.27
  9.6 0.1 reshape.26.route
  9.7 0.8 %concatenate.9.info = s32[1889]{0:T(1024)S(1)} concatenate(s32[832]{0:T(1024)} %constant.10.clone, s32[32]{0:T(128)} %param.15, s32[1024]{0:T(1024)} %bitcast.18, s32[1]{0:T(128)} %bitcast.2), dimensions={0} | concatenate | bytes 15112 | tf_op jit(solution)/shard_map/concatenate | solution.py:303
  10.6 0.0 collective-permute-done.9
  10.6 0.8 %collective-permute-done = f32[192,128]{1,0:T(8,128)S(1)} collective-permute-done((f32[192,128]{1,0:T(8,128)S(1)}, f32[192,128]{1,0:T(8,128)S(1)}, u32[]{:S(2)}, u32[]{:S(2)}) %collective-permute-start) | collective-permute-done | bytes 98336 | tf_op jit(solution)/shard_map/ppermute | solution.py:312
  11.5 0.0 collective-permute-done.1.rest_0_
  11.5 0.2 broadcast_in_dim.23.query_route
  11.7 1.8 %collective-permute-start.2 = (f32[192,128]{1,0:T(8,128)S(1)}, f32[192,128]{1,0:T(8,128)S(1)}, u32[]{:S(2)}, u32[]{:S(2)}) collective-permute-start(f32[192,128]{1,0:T(8,128)S(1)} %collective-permute-done), channel_id=1, source_target_pairs={{0,4},{1,5},{4,8},{5,9},{8,12},{9,13},{12,14},{13,15},{14,10},{15,... | collective-permute-start | bytes 294920 | tf_op jit(solution)/shard_map/ppermute | solution.py:312
  13.5 0.1 collective-permute-done.3
  13.7 0.1 collective-permute-start.10
  13.8 2.2 %collective-permute-start.6 = (f32[96,128]{1,0:T(8,128)S(1)}, f32[96,128]{1,0:T(8,128)S(1)}, u32[]{:S(2)}, u32[]{:S(2)}) collective-permute-start(f32[96,128]{1,0:T(8,128)S(1)} %slice.8), channel_id=1, source_target_pairs={{0,6},{1,7},{4,2},{5,3},{8,0},{9,1},{12,4},{13,5},{14,8},{15,9},{1... | collective-permute-start | bytes 147464 | tf_op jit(solution)/shard_map/ppermute | solution.py:312
  15.9 0.3 collective-permute-start.4
  16.2 1.2 %collective-permute-start.5 = (f32[96,128]{1,0:T(8,128)S(1)}, f32[96,128]{1,0:T(8,128)S(1)}, u32[]{:S(2)}, u32[]{:S(2)}) collective-permute-start(f32[96,128]{1,0:T(8,128)S(1)} %slice.6), channel_id=1, source_target_pairs={{0,8},{1,9},{4,12},{5,13},{8,14},{9,15},{12,10},{13,11},{14,6},{15... | collective-permute-start | bytes 147464 | tf_op jit(solution)/shard_map/ppermute | solution.py:312
  17.4 1.4 %collective-permute-start.11 = (bf16[64,4096]{1,0:T(8,128)(2,1)S(1)}, bf16[64,4096]{1,0:T(8,128)(2,1)S(1)}, u32[]{:S(2)}, u32[]{:S(2)}) collective-permute-start(bf16[64,4096]{1,0:T(8,128)(2,1)S(1)} %bitcast.20), channel_id=1, source_target_pairs={{0,4},{1,3},{4,8},{5,1},{8,12},{9,5},{12,14},{13,9},{14,10},{15,13... | collective-permute-start | bytes 1572872 | tf_op jit(solution)/shard_map/ppermute | solution.py:312
  18.8 2.9 %collective-permute-done.4 = f32[192,128]{1,0:T(8,128)S(1)} collective-permute-done((f32[192,128]{1,0:T(8,128)S(1)}, f32[192,128]{1,0:T(8,128)S(1)}, u32[]{:S(2)}, u32[]{:S(2)}) %collective-permute-start.4) | collective-permute-done | bytes 98336 | tf_op jit(solution)/shard_map/ppermute | solution.py:312
  21.7 0.2 collective-permute-done.5
  22.0 0.0 collective-permute-done.6
  22.0 0.1 collective-permute-start.7
  22.1 0.9 %prepare.4 = (bf16[32,2,128,128]{3,2,1,0:T(8,128)(2,1)S(1)}, bf16[32,2,128,128]{3,2,1,0:T(8,128)(2,1)S(1)}, bf16[32,64,256]{2,1,0:T(8,128)(2,1)S(1)}, bf16[32,64,256]{2,1,0:T(8,128)(2,1)S(1)}, f32[32,64,128]{2,1,0:T(8,128)S(1)}) custom-call(f32[960,128]{1,0:T(8,128)S(1)} %constant_dynamic-update-slice_fusion.4.src), custom_call_target="tpu_custom_call" | custom-call | flops 1000 | bytes 1000 | tf_op jit(solution)/shard_map/prepare/pallas_call | solution.py:65
  23.0 0.0 collective-permute-done.10.src
  23.0 0.9 %prepare.5 = (bf16[32,2,128,128]{3,2,1,0:T(8,128)(2,1)S(1)}, bf16[32,2,128,128]{3,2,1,0:T(8,128)(2,1)S(1)}, bf16[32,64,256]{2,1,0:T(8,128)(2,1)S(1)}, bf16[32,64,256]{2,1,0:T(8,128)(2,1)S(1)}, f32[32,64,128]{2,1,0:T(8,128)S(1)}) custom-call(f32[960,128]{1,0:T(8,128)S(1)} %collective-permute-done., ...), custom_call_target="tpu_custom_call", output_to_operand_aliasing={{0}: (1, {}), {1}: (2, {}), {2}: (3, {}), {3}: (4, {}), {4}... | custom-call | flops 1000 | bytes 1000 | tf_op jit(solution)/shard_map/prepare/pallas_call | solution.py:65
  23.9 0.5 prepare.6
  24.4 0.5 prepare.7
  24.9 2.0 %collective-permute-done.11.rest_0_ = bf16[64,4096]{1,0:T(8,128)(2,1)S(1)} collective-permute-done((bf16[64,4096]{1,0:T(8,128)(2,1)S(1)}, bf16[64,4096]{1,0:T(8,128)(2,1)S(1)}, u32[]{:S(2)}, u32[]{:S(2)}) %collective-permute-start.11) | collective-permute-done | bytes 524320 | tf_op jit(solution)/shard_map/ppermute | solution.py:312
  26.9 1.0 %collective-permute-start.12 = (bf16[64,4096]{1,0:T(8,128)(2,1)S(1)}, bf16[64,4096]{1,0:T(8,128)(2,1)S(1)}, u32[]{:S(2)}, u32[]{:S(2)}) collective-permute-start(bf16[64,4096]{1,0:T(8,128)(2,1)S(1)} %collective-permute-done.11.rest_0_), channel_id=1, source_target_pairs={{0,4},{1,3},{4,8},{5,1},{8,12},{9,5},{12,14},{13,9},{14,10},{15,13... | collective-permute-start | bytes 1572872 | tf_op jit(solution)/shard_map/ppermute | solution.py:312
  28.0 3.1 %precondition.5.rest_1_ = bf16[64,4096]{1,0:T(8,128)(2,1)S(1)} custom-call(s32[1889]{0:T(1024)S(1)} %concatenate.9.info, bf16[32,2,128,128]{3,2,1,0:T(8,128)(2,1)S(1)} %get-tuple-element.54.tab_a, bf16[32,2,128,128]{3,2,1,0:T(8,128)(2,1)S(1)} %get-tuple-element.55.tab_at, bf16[32,64,256]{2,1,0:T(8,128)(2,1)S(1)} %get-tuple-element.56.tab_s, ...), custom_call_target="tpu_custom_call" | custom-call | flops 1000 | bytes 1000 | tf_op jit(solution)/shard_map/precondition/pallas_call | solution.py:174
  31.0 1.8 %collective-permute-start.15 = (bf16[64,4096]{1,0:T(8,128)(2,1)S(1)}, bf16[64,4096]{1,0:T(8,128)(2,1)S(1)}, u32[]{:S(2)}, u32[]{:S(2)}) collective-permute-start(bf16[64,4096]{1,0:T(8,128)(2,1)S(1)} %precondition.5.rest_1_), channel_id=1, source_target_pairs={{0,4},{1,3},{4,8},{5,1},{8,12},{9,5},{12,14},{13,9},{14,10},{15,13... | collective-permute-start | bytes 1572872 | tf_op jit(solution)/shard_map/ppermute | solution.py:312
  32.8 3.1 %precondition.6.rest_2_ = bf16[64,4096]{1,0:T(8,128)(2,1)S(1)} custom-call(s32[1889]{0:T(1024)S(1)} %concatenate.9.info, bf16[32,2,128,128]{3,2,1,0:T(8,128)(2,1)S(1)} %get-tuple-element.54.tab_a, bf16[32,2,128,128]{3,2,1,0:T(8,128)(2,1)S(1)} %get-tuple-element.55.tab_at, bf16[32,64,256]{2,1,0:T(8,128)(2,1)S(1)} %get-tuple-element.56.tab_s, ...), custom_call_target="tpu_custom_call" | custom-call | flops 1000 | bytes 1000 | tf_op jit(solution)/shard_map/precondition/pallas_call | solution.py:174
  35.9 0.0 slice-start.1
  35.9 0.6 collective-permute-start.16
  36.5 1.3 %collective-permute-start.13 = (bf16[64,4096]{1,0:T(8,128)(2,1)S(1)}, bf16[64,4096]{1,0:T(8,128)(2,1)S(1)}, u32[]{:S(2)}, u32[]{:S(2)}) collective-permute-start(bf16[64,4096]{1,0:T(8,128)(2,1)S(1)} %collective-permute-done.12.rest_0_), channel_id=1, source_target_pairs={{0,4},{1,3},{4,8},{5,1},{8,12},{9,5},{12,14},{13,9},{14,10},{15,13... | collective-permute-start | bytes 1572872 | tf_op jit(solution)/shard_map/ppermute | solution.py:312
  37.8 3.1 %precondition.7.rest_0_ = bf16[64,4096]{1,0:T(8,128)(2,1)S(1)} custom-call(s32[1889]{0:T(1024)S(1)} %concatenate.9.info, bf16[32,2,128,128]{3,2,1,0:T(8,128)(2,1)S(1)} %get-tuple-element.54.tab_a, bf16[32,2,128,128]{3,2,1,0:T(8,128)(2,1)S(1)} %get-tuple-element.55.tab_at, bf16[32,64,256]{2,1,0:T(8,128)(2,1)S(1)} %get-tuple-element.56.tab_s, ...), custom_call_target="tpu_custom_call" | custom-call | flops 1000 | bytes 1000 | tf_op jit(solution)/shard_map/precondition/pallas_call | solution.py:174
  40.8 1.0 %collective-permute-done.15.rest_2_ = bf16[64,4096]{1,0:T(8,128)(2,1)S(1)} collective-permute-done((bf16[64,4096]{1,0:T(8,128)(2,1)S(1)}, bf16[64,4096]{1,0:T(8,128)(2,1)S(1)}, u32[]{:S(2)}, u32[]{:S(2)}) %collective-permute-start.15) | collective-permute-done | bytes 524320 | tf_op jit(solution)/shard_map/ppermute | solution.py:312
  41.9 0.9 %collective-permute-start.18 = (bf16[64,4096]{1,0:T(8,128)(2,1)S(1)}, bf16[64,4096]{1,0:T(8,128)(2,1)S(1)}, u32[]{:S(2)}, u32[]{:S(2)}) collective-permute-start(bf16[64,4096]{1,0:T(8,128)(2,1)S(1)} %collective-permute-done.15.rest_2_), channel_id=1, source_target_pairs={{0,4},{1,3},{4,8},{5,1},{8,12},{9,5},{12,14},{13,9},{14,10},{15,13... | collective-permute-start | bytes 1572872 | tf_op jit(solution)/shard_map/ppermute | solution.py:312
  42.8 0.0 collective-permute-start.20
  42.8 0.0 collective-permute-done.14.rest_0_
  42.8 0.5 collective-permute-start.19
  43.3 0.0 collective-permute-done.16.rest_3_
  43.3 3.2 %products.4.rest_4_ = f32[32,128]{1,0:T(8,128)S(1)} custom-call(s32[1889]{0:T(1024)S(1)} %concatenate.9.info, s32[1,1024]{1,0:T(1,128)S(1)} %reshape.26.route, s32[1024,128]{1,0:T(8,128)S(1)} %broadcast_in_dim.23.query_route, bf16[1024,4096]{1,0:T(8,128)(2,1)S(1)} %bitcast.13, bf16[64,4096]{1,0:T(8,128)(2,1)S(1)} %collective-permute-done.14.rest_0_, ...), custom_call_target="tpu_custom_call" | custom-call | flops 1000 | bytes 1000 | tf_op jit(solution)/shard_map/products/pallas_call | solution.py:239
  46.5 1.0 %collective-permute-done.13.rest_0_ = bf16[64,4096]{1,0:T(8,128)(2,1)S(1)} collective-permute-done((bf16[64,4096]{1,0:T(8,128)(2,1)S(1)}, bf16[64,4096]{1,0:T(8,128)(2,1)S(1)}, u32[]{:S(2)}, u32[]{:S(2)}) %collective-permute-start.13) | collective-permute-done | bytes 524320 | tf_op jit(solution)/shard_map/ppermute | solution.py:312
  47.5 0.9 %collective-permute-start.17 = (bf16[64,4096]{1,0:T(8,128)(2,1)S(1)}, bf16[64,4096]{1,0:T(8,128)(2,1)S(1)}, u32[]{:S(2)}, u32[]{:S(2)}) collective-permute-start(bf16[64,4096]{1,0:T(8,128)(2,1)S(1)} %collective-permute-done.13.rest_0_), channel_id=1, source_target_pairs={{0,4},{1,3},{4,8},{5,1},{8,12},{9,5},{12,14},{13,9},{14,10},{15,13... | collective-permute-start | bytes 1572872 | tf_op jit(solution)/shard_map/ppermute | solution.py:312
  48.4 3.1 %precondition.8.rest_0_ = bf16[64,4096]{1,0:T(8,128)(2,1)S(1)} custom-call(s32[1889]{0:T(1024)S(1)} %concatenate.9.info, bf16[32,2,128,128]{3,2,1,0:T(8,128)(2,1)S(1)} %get-tuple-element.54.tab_a, bf16[32,2,128,128]{3,2,1,0:T(8,128)(2,1)S(1)} %get-tuple-element.55.tab_at, bf16[32,64,256]{2,1,0:T(8,128)(2,1)S(1)} %get-tuple-element.56.tab_s, ...), custom_call_target="tpu_custom_call" | custom-call | flops 1000 | bytes 1000 | tf_op jit(solution)/shard_map/precondition/pallas_call | solution.py:174
  51.4 1.7 %collective-permute-done.18.rest_2_ = bf16[64,4096]{1,0:T(8,128)(2,1)S(1)} collective-permute-done((bf16[64,4096]{1,0:T(8,128)(2,1)S(1)}, bf16[64,4096]{1,0:T(8,128)(2,1)S(1)}, u32[]{:S(2)}, u32[]{:S(2)}) %collective-permute-start.18) | collective-permute-done | bytes 524320 | tf_op jit(solution)/shard_map/ppermute | solution.py:312
  53.1 0.0 collective-permute-start.24
  53.1 0.5 collective-permute-start.23
  53.6 0.9 %collective-permute-start.22 = (bf16[64,4096]{1,0:T(8,128)(2,1)S(1)}, bf16[64,4096]{1,0:T(8,128)(2,1)S(1)}, u32[]{:S(2)}, u32[]{:S(2)}) collective-permute-start(bf16[64,4096]{1,0:T(8,128)(2,1)S(1)} %collective-permute-done.18.rest_2_), channel_id=1, source_target_pairs={{0,4},{1,3},{4,8},{5,1},{8,12},{9,5},{12,14},{13,9},{14,10},{15,13... | collective-permute-start | bytes 1572872 | tf_op jit(solution)/shard_map/ppermute | solution.py:312
  54.5 3.2 %products.5.rest_5_ = f32[32,128]{1,0:T(8,128)S(1)} custom-call(s32[1889]{0:T(1024)S(1)} %concatenate.9.info, s32[1,1024]{1,0:T(1,128)S(1)} %reshape.26.route, s32[1024,128]{1,0:T(8,128)S(1)} %broadcast_in_dim.23.query_route, bf16[1024,4096]{1,0:T(8,128)(2,1)S(1)} %bitcast.14, bf16[64,4096]{1,0:T(8,128)(2,1)S(1)} %precondition.7.rest_0_, ...), custom_call_target="tpu_custom_call" | custom-call | flops 1000 | bytes 1000 | tf_op jit(solution)/shard_map/products/pallas_call | solution.py:239
  57.7 1.1 %collective-permute-done.17.rest_0_ = bf16[64,4096]{1,0:T(8,128)(2,1)S(1)} collective-permute-done((bf16[64,4096]{1,0:T(8,128)(2,1)S(1)}, bf16[64,4096]{1,0:T(8,128)(2,1)S(1)}, u32[]{:S(2)}, u32[]{:S(2)}) %collective-permute-start.17) | collective-permute-done | bytes 524320 | tf_op jit(solution)/shard_map/ppermute | solution.py:312
  58.7 3.1 %precondition.9.rest_0_ = bf16[64,4096]{1,0:T(8,128)(2,1)S(1)} custom-call(s32[1889]{0:T(1024)S(1)} %concatenate.9.info, bf16[32,2,128,128]{3,2,1,0:T(8,128)(2,1)S(1)} %get-tuple-element.54.tab_a, bf16[32,2,128,128]{3,2,1,0:T(8,128)(2,1)S(1)} %get-tuple-element.55.tab_at, bf16[32,64,256]{2,1,0:T(8,128)(2,1)S(1)} %get-tuple-element.56.tab_s, ...), custom_call_target="tpu_custom_call" | custom-call | flops 1000 | bytes 1000 | tf_op jit(solution)/shard_map/precondition/pallas_call | solution.py:174
  61.8 0.0 collective-permute-done.23.rest_1_
  61.8 3.2 %products.6.rest_6_ = f32[32,128]{1,0:T(8,128)S(1)} custom-call(s32[1889]{0:T(1024)S(1)} %concatenate.9.info, s32[1,1024]{1,0:T(1,128)S(1)} %reshape.26.route, s32[1024,128]{1,0:T(8,128)S(1)} %broadcast_in_dim.23.query_route, bf16[1024,4096]{1,0:T(8,128)(2,1)S(1)} %bitcast.15, bf16[64,4096]{1,0:T(8,128)(2,1)S(1)} %precondition.8.rest_0_, ...), custom_call_target="tpu_custom_call" | custom-call | flops 1000 | bytes 1000 | tf_op jit(solution)/shard_map/products/pallas_call | solution.py:239
  65.0 0.0 collective-permute-done.22.rest_2_
  65.0 0.1 collective-permute-start.25
  65.1 0.5 collective-permute-start.21
  65.6 1.4 %collective-permute-done.25.rest_3_ = bf16[64,4096]{1,0:T(8,128)(2,1)S(1)} collective-permute-done((bf16[64,4096]{1,0:T(8,128)(2,1)S(1)}, bf16[64,4096]{1,0:T(8,128)(2,1)S(1)}, u32[]{:S(2)}, u32[]{:S(2)}) %collective-permute-start.25) | collective-permute-done | bytes 524320 | tf_op jit(solution)/shard_map/ppermute | solution.py:312
  67.0 0.7 %collective-permute-done.21.rest_1_ = bf16[64,4096]{1,0:T(8,128)(2,1)S(1)} collective-permute-done((bf16[64,4096]{1,0:T(8,128)(2,1)S(1)}, bf16[64,4096]{1,0:T(8,128)(2,1)S(1)}, u32[]{:S(2)}, u32[]{:S(2)}) %collective-permute-start.21) | collective-permute-done | bytes 524320 | tf_op jit(solution)/shard_map/ppermute | solution.py:312
  67.7 3.8 %products.7 = f32[128,128]{1,0:T(8,128)} custom-call(s32[1889]{0:T(1024)S(1)} %concatenate.9.info, s32[1,1024]{1,0:T(1,128)S(1)} %reshape.26.route, s32[1024,128]{1,0:T(8,128)S(1)} %broadcast_in_dim.23.query_route, bf16[1024,4096]{1,0:T(8,128)(2,1)S(1)} %bitcast.16, bf16[64,4096]{1,0:T(8,128)(2,1)S(1)} %precondition.9.rest_0_, ...), custom_call_target="tpu_custom_call" | custom-call | flops 1000 | bytes 1000 | tf_op jit(solution)/shard_map/products/pallas_call | solution.py:239
  (29 shorter events, 0.1 us)
Async XLA Ops:
  0.0 17.4 %copy-start = (bf16[8,8,4096]{2,1,0:T(8,128)(2,1)S(1)}, bf16[8,8,4096]{2,1,0:T(8,128)(2,1)}, u32[]{:S(2)}) copy-start(bf16[8,8,4096]{2,1,0:T(8,128)(2,1)} %param.10) | copy-start | bytes 1572868
  1.2 9.4 %collective-permute-start.8 = (f32[192,128]{1,0:T(8,128)S(1)}, f32[192,128]{1,0:T(8,128)S(1)}, u32[]{:S(2)}, u32[]{:S(2)}) collective-permute-start(f32[192,128]{1,0:T(8,128)S(1)} %pack.1), channel_id=1, source_target_pairs={{0,4},{1,5},{4,8},{5,9},{8,12},{9,13},{12,14},{13,15},{14,10},{15,... | collective-permute-start | bytes 294920 | tf_op jit(solution)/shard_map/ppermute | solution.py:312
  4.2 6.3 %collective-permute-start.9 = (f32[192,128]{1,0:T(8,128)S(1)}, f32[192,128]{1,0:T(8,128)S(1)}, u32[]{:S(2)}, u32[]{:S(2)}) collective-permute-start(f32[192,128]{1,0:T(8,128)S(1)} %pack.1), channel_id=1, source_target_pairs={{0,2},{1,3},{4,0},{5,1},{8,4},{9,5},{12,8},{13,9},{14,12},{15,13},... | collective-permute-start | bytes 294920 | tf_op jit(solution)/shard_map/ppermute | solution.py:312
  4.2 7.2 %collective-permute-start = (f32[192,128]{1,0:T(8,128)S(1)}, f32[192,128]{1,0:T(8,128)S(1)}, u32[]{:S(2)}, u32[]{:S(2)}) collective-permute-start(f32[192,128]{1,0:T(8,128)S(1)} %pack.1), channel_id=1, source_target_pairs={{0,8},{1,9},{4,12},{5,13},{8,14},{9,15},{12,10},{13,11},{14,6},{15... | collective-permute-start | bytes 294920 | tf_op jit(solution)/shard_map/ppermute | solution.py:312
  7.3 6.4 %collective-permute-start.3 = (f32[192,128]{1,0:T(8,128)S(1)}, f32[192,128]{1,0:T(8,128)S(1)}, u32[]{:S(2)}, u32[]{:S(2)}) collective-permute-start(f32[192,128]{1,0:T(8,128)S(1)} %pack.1), channel_id=1, source_target_pairs={{0,6},{1,7},{4,2},{5,3},{8,0},{9,1},{12,4},{13,5},{14,8},{15,9},{1... | collective-permute-start | bytes 294920 | tf_op jit(solution)/shard_map/ppermute | solution.py:312
  7.3 4.2 %collective-permute-start.1 = (bf16[64,4096]{1,0:T(8,128)(2,1)}, bf16[64,4096]{1,0:T(8,128)(2,1)S(1)}, u32[]{:S(2)}, u32[]{:S(2)}) collective-permute-start(bf16[64,4096]{1,0:T(8,128)(2,1)} %bitcast.19), channel_id=1, source_target_pairs={{0,1},{1,0},{2,3},{3,2},{4,5},{5,4},{6,7},{7,6},{8,9},{9,8},{10,11... | collective-permute-start | bytes 1572872 | tf_op jit(solution)/shard_map/ppermute | solution.py:312
  11.7 5.7 %collective-permute-start.2 = (f32[192,128]{1,0:T(8,128)S(1)}, f32[192,128]{1,0:T(8,128)S(1)}, u32[]{:S(2)}, u32[]{:S(2)}) collective-permute-start(f32[192,128]{1,0:T(8,128)S(1)} %collective-permute-done), channel_id=1, source_target_pairs={{0,4},{1,5},{4,8},{5,9},{8,12},{9,13},{12,14},{13,15},{14,10},{15,... | collective-permute-start | bytes 294920 | tf_op jit(solution)/shard_map/ppermute | solution.py:312
  13.7 9.3 %collective-permute-start.10 = (f32[960,128]{1,0:T(8,128)S(1)}, f32[960,128]{1,0:T(8,128)S(1)}, u32[]{:S(2)}, u32[]{:S(2)}) collective-permute-start(f32[960,128]{1,0:T(8,128)S(1)} %constant_dynamic-update-slice_fusion.4.src), channel_id=1, source_target_pairs={{0,1},{1,0},{2,3},{3,2},{4,5},{5,4},{6,7},{7,6},{8,9},{9,8},{10,11... | collective-permute-start | bytes 1474568 | tf_op jit(solution)/shard_map/ppermute | solution.py:312
  13.8 8.2 %collective-permute-start.6 = (f32[96,128]{1,0:T(8,128)S(1)}, f32[96,128]{1,0:T(8,128)S(1)}, u32[]{:S(2)}, u32[]{:S(2)}) collective-permute-start(f32[96,128]{1,0:T(8,128)S(1)} %slice.8), channel_id=1, source_target_pairs={{0,6},{1,7},{4,2},{5,3},{8,0},{9,1},{12,4},{13,5},{14,8},{15,9},{1... | collective-permute-start | bytes 147464 | tf_op jit(solution)/shard_map/ppermute | solution.py:312
  15.9 5.8 %collective-permute-start.4 = (f32[192,128]{1,0:T(8,128)S(1)}, f32[192,128]{1,0:T(8,128)S(1)}, u32[]{:S(2)}, u32[]{:S(2)}) collective-permute-start(f32[192,128]{1,0:T(8,128)S(1)} %collective-permute-done.3), channel_id=1, source_target_pairs={{0,2},{1,3},{4,0},{5,1},{8,4},{9,5},{12,8},{13,9},{14,12},{15,13},... | collective-permute-start | bytes 294920 | tf_op jit(solution)/shard_map/ppermute | solution.py:312
  16.2 5.7 %collective-permute-start.5 = (f32[96,128]{1,0:T(8,128)S(1)}, f32[96,128]{1,0:T(8,128)S(1)}, u32[]{:S(2)}, u32[]{:S(2)}) collective-permute-start(f32[96,128]{1,0:T(8,128)S(1)} %slice.6), channel_id=1, source_target_pairs={{0,8},{1,9},{4,12},{5,13},{8,14},{9,15},{12,10},{13,11},{14,6},{15... | collective-permute-start | bytes 147464 | tf_op jit(solution)/shard_map/ppermute | solution.py:312
  17.4 9.5 %collective-permute-start.11 = (bf16[64,4096]{1,0:T(8,128)(2,1)S(1)}, bf16[64,4096]{1,0:T(8,128)(2,1)S(1)}, u32[]{:S(2)}, u32[]{:S(2)}) collective-permute-start(bf16[64,4096]{1,0:T(8,128)(2,1)S(1)} %bitcast.20), channel_id=1, source_target_pairs={{0,4},{1,3},{4,8},{5,1},{8,12},{9,5},{12,14},{13,9},{14,10},{15,13... | collective-permute-start | bytes 1572872 | tf_op jit(solution)/shard_map/ppermute | solution.py:312
  22.0 2.4 %collective-permute-start.7 = (f32[576,128]{1,0:T(8,128)S(1)}, f32[576,128]{1,0:T(8,128)S(1)}, u32[]{:S(2)}, u32[]{:S(2)}) collective-permute-start(f32[576,128]{1,0:T(8,128)S(1)} %constant_dynamic-update-slice_fusion.src), channel_id=1, source_target_pairs={{0,1},{1,0},{2,3},{3,2},{4,5},{5,4},{6,7},{7,6},{8,9},{9,8},{10,11... | collective-permute-start | bytes 884744 | tf_op jit(solution)/shard_map/ppermute | solution.py:312
  26.9 9.5 %collective-permute-start.12 = (bf16[64,4096]{1,0:T(8,128)(2,1)S(1)}, bf16[64,4096]{1,0:T(8,128)(2,1)S(1)}, u32[]{:S(2)}, u32[]{:S(2)}) collective-permute-start(bf16[64,4096]{1,0:T(8,128)(2,1)S(1)} %collective-permute-done.11.rest_0_), channel_id=1, source_target_pairs={{0,4},{1,3},{4,8},{5,1},{8,12},{9,5},{12,14},{13,9},{14,10},{15,13... | collective-permute-start | bytes 1572872 | tf_op jit(solution)/shard_map/ppermute | solution.py:312
  31.0 10.8 %collective-permute-start.15 = (bf16[64,4096]{1,0:T(8,128)(2,1)S(1)}, bf16[64,4096]{1,0:T(8,128)(2,1)S(1)}, u32[]{:S(2)}, u32[]{:S(2)}) collective-permute-start(bf16[64,4096]{1,0:T(8,128)(2,1)S(1)} %precondition.5.rest_1_), channel_id=1, source_target_pairs={{0,4},{1,3},{4,8},{5,1},{8,12},{9,5},{12,14},{13,9},{14,10},{15,13... | collective-permute-start | bytes 1572872 | tf_op jit(solution)/shard_map/ppermute | solution.py:312
  32.8 10.0 %collective-permute-start.14 = (bf16[64,4096]{1,0:T(8,128)(2,1)S(1)}, bf16[64,4096]{1,0:T(8,128)(2,1)S(1)}, u32[]{:S(2)}, u32[]{:S(2)}) collective-permute-start(bf16[64,4096]{1,0:T(8,128)(2,1)S(1)} %precondition.5.rest_1_), channel_id=1, source_target_pairs={{0,1},{1,0},{2,3},{3,2},{4,5},{5,4},{6,7},{7,6},{8,9},{9,8},{10,11... | collective-permute-start | bytes 1572872 | tf_op jit(solution)/shard_map/ppermute | solution.py:312
  32.8 10.5 %slice-start = ((s8[8388608]{0:T(1024)(128)(4,1)}), s8[4194304]{0:T(1024)(128)(4,1)S(1)}, s32[]{:S(2)}) async-start(s8[8388608]{0:T(1024)(128)(4,1)} %bitcast.11), calls=%async_computation | async-start | bytes 8388608
  35.9 7.4 %slice-start.1 = ((s8[8388608]{0:T(1024)(128)(4,1)}), s8[4194304]{0:T(1024)(128)(4,1)S(1)}, s32[]{:S(2)}) async-start(s8[8388608]{0:T(1024)(128)(4,1)} %bitcast.11), calls=%async_computation.1 | async-start | bytes 8388608
  35.9 7.4 %collective-permute-start.16 = (bf16[64,4096]{1,0:T(8,128)(2,1)S(1)}, bf16[64,4096]{1,0:T(8,128)(2,1)S(1)}, u32[]{:S(2)}, u32[]{:S(2)}) collective-permute-start(bf16[64,4096]{1,0:T(8,128)(2,1)S(1)} %precondition.6.rest_2_), channel_id=1, source_target_pairs={{0,1},{1,0},{2,3},{3,2},{4,5},{5,4},{6,7},{7,6},{8,9},{9,8},{10,11... | collective-permute-start | bytes 1572872 | tf_op jit(solution)/shard_map/ppermute | solution.py:312
  36.5 11.0 %collective-permute-start.13 = (bf16[64,4096]{1,0:T(8,128)(2,1)S(1)}, bf16[64,4096]{1,0:T(8,128)(2,1)S(1)}, u32[]{:S(2)}, u32[]{:S(2)}) collective-permute-start(bf16[64,4096]{1,0:T(8,128)(2,1)S(1)} %collective-permute-done.12.rest_0_), channel_id=1, source_target_pairs={{0,4},{1,3},{4,8},{5,1},{8,12},{9,5},{12,14},{13,9},{14,10},{15,13... | collective-permute-start | bytes 1572872 | tf_op jit(solution)/shard_map/ppermute | solution.py:312
  41.9 11.2 %collective-permute-start.18 = (bf16[64,4096]{1,0:T(8,128)(2,1)S(1)}, bf16[64,4096]{1,0:T(8,128)(2,1)S(1)}, u32[]{:S(2)}, u32[]{:S(2)}) collective-permute-start(bf16[64,4096]{1,0:T(8,128)(2,1)S(1)} %collective-permute-done.15.rest_2_), channel_id=1, source_target_pairs={{0,4},{1,3},{4,8},{5,1},{8,12},{9,5},{12,14},{13,9},{14,10},{15,13... | collective-permute-start | bytes 1572872 | tf_op jit(solution)/shard_map/ppermute | solution.py:312
  42.8 10.9 %collective-permute-start.20 = (bf16[64,4096]{1,0:T(8,128)(2,1)S(1)}, bf16[64,4096]{1,0:T(8,128)(2,1)S(1)}, u32[]{:S(2)}, u32[]{:S(2)}) collective-permute-start(bf16[64,4096]{1,0:T(8,128)(2,1)S(1)} %collective-permute-done.15.rest_2_), channel_id=1, source_target_pairs={{0,1},{1,0},{2,3},{3,2},{4,5},{5,4},{6,7},{7,6},{8,9},{9,8},{10,11... | collective-permute-start | bytes 1572872 | tf_op jit(solution)/shard_map/ppermute | solution.py:312
  42.8 11.7 %collective-permute-start.19 = (bf16[64,4096]{1,0:T(8,128)(2,1)S(1)}, bf16[64,4096]{1,0:T(8,128)(2,1)S(1)}, u32[]{:S(2)}, u32[]{:S(2)}) collective-permute-start(bf16[64,4096]{1,0:T(8,128)(2,1)S(1)} %precondition.7.rest_0_), channel_id=1, source_target_pairs={{0,1},{1,0},{2,3},{3,2},{4,5},{5,4},{6,7},{7,6},{8,9},{9,8},{10,11... | collective-permute-start | bytes 1572872 | tf_op jit(solution)/shard_map/ppermute | solution.py:312
  47.5 11.2 %collective-permute-start.17 = (bf16[64,4096]{1,0:T(8,128)(2,1)S(1)}, bf16[64,4096]{1,0:T(8,128)(2,1)S(1)}, u32[]{:S(2)}, u32[]{:S(2)}) collective-permute-start(bf16[64,4096]{1,0:T(8,128)(2,1)S(1)} %collective-permute-done.13.rest_0_), channel_id=1, source_target_pairs={{0,4},{1,3},{4,8},{5,1},{8,12},{9,5},{12,14},{13,9},{14,10},{15,13... | collective-permute-start | bytes 1572872 | tf_op jit(solution)/shard_map/ppermute | solution.py:312
  53.1 8.7 %collective-permute-start.24 = (bf16[64,4096]{1,0:T(8,128)(2,1)S(1)}, bf16[64,4096]{1,0:T(8,128)(2,1)S(1)}, u32[]{:S(2)}, u32[]{:S(2)}) collective-permute-start(bf16[64,4096]{1,0:T(8,128)(2,1)S(1)} %collective-permute-done.18.rest_2_), channel_id=1, source_target_pairs={{0,1},{1,0},{2,3},{3,2},{4,5},{5,4},{6,7},{7,6},{8,9},{9,8},{10,11... | collective-permute-start | bytes 1572872 | tf_op jit(solution)/shard_map/ppermute | solution.py:312
  53.1 8.7 %collective-permute-start.23 = (bf16[64,4096]{1,0:T(8,128)(2,1)S(1)}, bf16[64,4096]{1,0:T(8,128)(2,1)S(1)}, u32[]{:S(2)}, u32[]{:S(2)}) collective-permute-start(bf16[64,4096]{1,0:T(8,128)(2,1)S(1)} %precondition.8.rest_0_), channel_id=1, source_target_pairs={{0,1},{1,0},{2,3},{3,2},{4,5},{5,4},{6,7},{7,6},{8,9},{9,8},{10,11... | collective-permute-start | bytes 1572872 | tf_op jit(solution)/shard_map/ppermute | solution.py:312
  53.6 11.4 %collective-permute-start.22 = (bf16[64,4096]{1,0:T(8,128)(2,1)S(1)}, bf16[64,4096]{1,0:T(8,128)(2,1)S(1)}, u32[]{:S(2)}, u32[]{:S(2)}) collective-permute-start(bf16[64,4096]{1,0:T(8,128)(2,1)S(1)} %collective-permute-done.18.rest_2_), channel_id=1, source_target_pairs={{0,4},{1,3},{4,8},{5,1},{8,12},{9,5},{12,14},{13,9},{14,10},{15,13... | collective-permute-start | bytes 1572872 | tf_op jit(solution)/shard_map/ppermute | solution.py:312
  65.0 2.0 %collective-permute-start.25 = (bf16[64,4096]{1,0:T(8,128)(2,1)S(1)}, bf16[64,4096]{1,0:T(8,128)(2,1)S(1)}, u32[]{:S(2)}, u32[]{:S(2)}) collective-permute-start(bf16[64,4096]{1,0:T(8,128)(2,1)S(1)} %collective-permute-done.22.rest_2_), channel_id=1, source_target_pairs={{0,1},{1,0},{2,3},{3,2},{4,5},{5,4},{6,7},{7,6},{8,9},{9,8},{10,11... | collective-permute-start | bytes 1572872 | tf_op jit(solution)/shard_map/ppermute | solution.py:312
  65.1 2.6 %collective-permute-start.21 = (bf16[64,4096]{1,0:T(8,128)(2,1)S(1)}, bf16[64,4096]{1,0:T(8,128)(2,1)S(1)}, u32[]{:S(2)}, u32[]{:S(2)}) collective-permute-start(bf16[64,4096]{1,0:T(8,128)(2,1)S(1)} %precondition.9.rest_0_), channel_id=1, source_target_pairs={{0,1},{1,0},{2,3},{3,2},{4,5},{5,4},{6,7},{7,6},{8,9},{9,8},{10,11... | collective-permute-start | bytes 1572872 | tf_op jit(solution)/shard_map/ppermute | solution.py:312
